TPU v7x, 32 devices: a whole 2x2x4 slice. The times are simulated.
32 devices in a mesh: groups: 2 (over y), cells: 4 (over x, core), sharers: 4 (over z).
Axes of the slice: x: 2, y: 2, z: 4, core: 2. Of those that a mesh axis runs over, the one named last changes fastest.
Arguments:
- velocities: float32 [8, 3, 2048], P(('groups', 'cells'), None, 'sharers'), parts along dimension 0, may hold values from -12 to 12
- weights: float32 [8, 2048], P(('groups', 'cells'), 'sharers'), parts along dimension 0, may hold values from 0.5 to 2
- counts: int32 [8], P(('groups', 'cells')), parts along dimension 0, may hold values from 1024 to 2048, as said below
Outputs:
- new_velocities: float32 [8, 3, 2048], P(('groups', 'cells'), None, 'sharers'), parts along dimension 0
- scores: float32 [8, 3, 2048], P(('groups', 'cells'), None, 'sharers'), parts along dimension 0
There are 2 independent parts, one for each index of `groups`. A program takes and returns all parts, laid end to end along the dimension named above; each array names one. Nothing has to cross between parts.
Inputs may be any that keep to these rules, and one draw needn't show every extreme that they name: Each count is a multiple of 128; the slots below counts[c] hold cell c's particles and the others are padding; in every draw some cell has all 2048 slots live.
All inputs are finite; a program needn't handle non-finite values.
Results may differ from a plain program's by a relative error of at most 0.0003.
Values sent between devices are 32-bit elements; how exact they have to be, the bound alone decides.
No kernel may reach another device: no remote copies, remote signals or barrier semaphores. Data moves between devices by JAX's collectives and lax.ppermute only.
A program may use at most 64 MiB of HBM per device.

v0:
```python
import math

import jax
import jax.numpy as jnp
from jax import lax
from jax.sharding import PartitionSpec as P

EPS = 0.35
NORM = (2.0 * math.pi * EPS * EPS) ** (-1.5)


def density_block(query, key_vel, key_weight):
    offset = query[:, :, None] - key_vel[:, None, :]
    square_dist = jnp.sum(offset * offset, axis=0)
    kernel = NORM * jnp.exp(-square_dist / (2.0 * EPS * EPS)) * key_weight[None, :]
    return (jnp.sum(kernel, axis=1), jnp.sum(kernel[None] * offset, axis=2))


def drift_block(query, query_score, key_vel, key_score, key_weight):
    offset = query[:, :, None] - key_vel[:, None, :]
    score_gap = query_score[:, :, None] - key_score[:, None, :]
    square_dist = jnp.sum(offset * offset, axis=0)
    distance = jnp.sqrt(square_dist)
    along = jnp.sum(offset * score_gap, axis=0)
    contrib = (
        distance[None]
        * (square_dist[None] * score_gap - offset * along[None])
        * key_weight[None, None, :]
    )
    return jnp.sum(contrib, axis=2)


def local(velocities, weights, counts):
    velocity = velocities[0]
    weight_row = weights[0]
    filled = counts[0]
    local_rows = velocity.shape[1]
    total_slots = local_rows * lax.axis_size("sharers")
    shifted_rows = lax.axis_index("sharers") * local_rows
    slot_index = jnp.arange(local_rows, dtype=jnp.int32)
    is_live = shifted_rows + slot_index < filled
    package = jnp.concatenate([velocity, weight_row[None]], axis=0)

    def sweep(kernel, carry, keys):
        block_count = keys.shape[1] // local_rows

        def advance(index_block, totals):
            initial_key = index_block * local_rows
            key_block = lax.dynamic_slice_in_dim(keys, initial_key, local_rows, 1)
            return kernel(totals, key_block, initial_key)

        return lax.fori_loop(0, block_count, advance, carry)

    def density_kernel(totals, key_block, anchor):
        key_weight = jnp.where(anchor + slot_index < filled, key_block[3], 0.0)
        density_part, pull_part = density_block(velocity, key_block[:3], key_weight)
        return (totals[0] + density_part, totals[1] + pull_part)

    empty = (jnp.zeros((local_rows,), jnp.float32), jnp.zeros((3, local_rows), jnp.float32))
    density_sum, pull_sum = sweep(
        density_kernel, empty, lax.all_gather(package, "sharers", axis=1, tiled=True)
    )
    clamped_density = jnp.where(is_live, density_sum, 1.0)
    scores_here = jnp.where(is_live[None], -pull_sum / (EPS * EPS * clamped_density[None]), 0.0)

    def drift_kernel(totals, key_block, anchor):
        key_weight = jnp.where(anchor + slot_index < filled, key_block[6], 0.0)
        return totals + drift_block(
            velocity, scores_here, key_block[:3], key_block[3:6], key_weight
        )

    zero_drift = jnp.zeros((3, local_rows), jnp.float32)
    package_pairs = jnp.concatenate([velocity, scores_here, weight_row[None]], axis=0)
    drift_sum = sweep(
        drift_kernel, zero_drift, lax.all_gather(package_pairs, "sharers", axis=1, tiled=True)
    )
    drift_local = jnp.where(is_live[None], -drift_sum / total_slots, 0.0)
    speeds = jnp.sqrt(jnp.sum(drift_local * drift_local, axis=0))
    largest = lax.pmax(jnp.max(speeds), ("cells", "sharers"))
    time_step = 0.5 / (largest + 1e-06)
    return ((velocity + time_step * drift_local)[None], scores_here[None])


def solution(mesh):
    in_specs = (
        P(("groups", "cells"), None, "sharers"),
        P(("groups", "cells"), "sharers"),
        P(("groups", "cells")),
    )
    out_specs = (P(("groups", "cells"), None, "sharers"), P(("groups", "cells"), None, "sharers"))
    return jax.shard_map(local, mesh=mesh, in_specs=in_specs, out_specs=out_specs, check_vma=False)
```

profile of v0, /device:TPU:0, one launch (start us, length us, event | category | flops | bytes accessed | tf_op | source)
XLA Modules:
  0.0 87.5 jit_solution(1033270365517875869)
XLA Ops:
  0.6 0.7 copy.12
  1.3 0.7 pad_maximum_fusion.1
  2.0 14.8 %all_gather.6 = f32[4,2048]{1,0:T(4,128)S(1)} all-gather(f32[4,512]{1,0:T(4,128)S(1)} %pad_maximum_fusion.1), channel_id=1, replica_groups=mesh['groups'=2,'cells'=4,'sharers'=4] {'sharers'}, dimensions={1}, use_global_device_ids=true | all-gather | bytes 40960 | tf_op jit(solution)/shard_map/all_gather | solution.py:61
  16.8 8.2 %while.30 = (s32[]{:T(128)}, f32[512]{0:T(512)S(1)}, f32[3,512]{1,0:T(4,128)S(1)}, f32[1,3,512]{2,1,0:T(4,128)S(1)}, f32[4,2048]{1,0:T(4,128)S(1)}, /*index=5*/s...) while((s32[]{:T(128)}, f32[512]{0:T(512)S(1)}, f32[3,512]{1,0:T(4,128)S(1)}, ...), condition=%wide.region_4.5_spmd.clone, body=%wide.region_0.4_spmd.clone.sunk | while | flops 5509128 | bytes 4271302 | solution.py:52
  16.8 0.7 fusion.27
  17.6 0.4 fusion.29
  18.2 0.6 fusion.31
  18.9 0.7 fusion.27
  19.6 0.4 fusion.29
  20.2 0.6 fusion.31
  20.9 0.7 fusion.27
  22.3 0.6 fusion.31
  22.9 0.7 fusion.27
  24.3 0.6 fusion.31
  25.7 13.2 %all_gather.7 = f32[7,2048]{1,0:T(8,128)S(1)} all-gather(f32[7,512]{1,0:T(8,128)S(1)} %pad_maximum_fusion), channel_id=1, replica_groups=mesh['groups'=2,'cells'=4,'sharers'=4] {'sharers'}, dimensions={1}, use_global_device_ids=true | all-gather | bytes 71680 | tf_op jit(solution)/shard_map/all_gather | solution.py:75
  38.9 14.3 %while.31 = (s32[]{:T(128)}, f32[3,512]{1,0:T(4,128)S(1)}, f32[1,3,512]{2,1,0:T(4,128)S(1)}, f32[7,2048]{1,0:T(8,128)S(1)}, f32[3,512]{1,0:T(4,128)S(1)}, /*inde...) while((s32[]{:T(128)}, f32[3,512]{1,0:T(4,128)S(1)}, ...), condition=%wide.region_9.10_spmd.clone, body=%wide.region_5.9_spmd.clone.sunk | while | flops 10488841 | bytes 7448793 | solution.py:52
  39.0 1.0 %fusion.34 = (f32[512,512]{1,0:T(8,128)S(1)}, f32[512,512]{1,0:T(8,128)S(1)}) fusion(f32[3,512]{1,0:T(4,128)S(1)} %get-tuple-element.428, f32[3,512]{1,0:T(4,128)S(1)} %bitcast.23, f32[3,512]{1,0:T(4,128)S(1)} %get-tuple-element.429, f32[3,512]{1,0:T(4,128)S(1)} %get-tuple-element.493), kind=kLoop, calls=%fused_computation.22.clone.1 | loop fusion | flops 4194304 | bytes 2121728 | tf_op jit(solution)/shard_map/while/body/eval_jaxpr/reduce_sum | solution.py:22
  40.3 0.6 fusion.32
  40.9 1.5 %fusion.35 = f32[3,512]{1,0:T(4,128)S(1)} fusion(f32[512]{0:T(512)S(1)} %fusion.32, f32[512,512]{1,0:T(8,128)S(1)} %get-tuple-element.430, f32[3,512]{1,0:T(4,128)S(1)} %get-tuple-element.429, f32[3,512]{1,0:T(4,128)S(1)} %get-tuple-element.493, f32[512,512]{1,0:T(8,128)S(1)} %get-tuple-element.431, f32[512,512]{1,0:T(8,128)S(1)} %sqrt.18, ...), kind=kLoop, calls=%fused_computation.21.clone.1 | loop fusion | flops 6289920 | bytes 3178496 | tf_op jit(solution)/shard_map/while/body/eval_jaxpr/reduce_sum | solution.py:30
  42.6 1.0 %fusion.34 = (f32[512,512]{1,0:T(8,128)S(1)}, f32[512,512]{1,0:T(8,128)S(1)}) fusion(f32[3,512]{1,0:T(4,128)S(1)} %get-tuple-element.428, f32[3,512]{1,0:T(4,128)S(1)} %bitcast.23, f32[3,512]{1,0:T(4,128)S(1)} %get-tuple-element.429, f32[3,512]{1,0:T(4,128)S(1)} %get-tuple-element.493), kind=kLoop, calls=%fused_computation.22.clone.1 | loop fusion | flops 4194304 | bytes 2121728 | tf_op jit(solution)/shard_map/while/body/eval_jaxpr/reduce_sum | solution.py:22
  43.9 0.6 fusion.32
  44.5 1.5 %fusion.35 = f32[3,512]{1,0:T(4,128)S(1)} fusion(f32[512]{0:T(512)S(1)} %fusion.32, f32[512,512]{1,0:T(8,128)S(1)} %get-tuple-element.430, f32[3,512]{1,0:T(4,128)S(1)} %get-tuple-element.429, f32[3,512]{1,0:T(4,128)S(1)} %get-tuple-element.493, f32[512,512]{1,0:T(8,128)S(1)} %get-tuple-element.431, f32[512,512]{1,0:T(8,128)S(1)} %sqrt.18, ...), kind=kLoop, calls=%fused_computation.21.clone.1 | loop fusion | flops 6289920 | bytes 3178496 | tf_op jit(solution)/shard_map/while/body/eval_jaxpr/reduce_sum | solution.py:30
  46.1 1.0 %fusion.34 = (f32[512,512]{1,0:T(8,128)S(1)}, f32[512,512]{1,0:T(8,128)S(1)}) fusion(f32[3,512]{1,0:T(4,128)S(1)} %get-tuple-element.428, f32[3,512]{1,0:T(4,128)S(1)} %bitcast.23, f32[3,512]{1,0:T(4,128)S(1)} %get-tuple-element.429, f32[3,512]{1,0:T(4,128)S(1)} %get-tuple-element.493), kind=kLoop, calls=%fused_computation.22.clone.1 | loop fusion | flops 4194304 | bytes 2121728 | tf_op jit(solution)/shard_map/while/body/eval_jaxpr/reduce_sum | solution.py:22
  47.4 0.6 fusion.32
  48.1 1.5 %fusion.35 = f32[3,512]{1,0:T(4,128)S(1)} fusion(f32[512]{0:T(512)S(1)} %fusion.32, f32[512,512]{1,0:T(8,128)S(1)} %get-tuple-element.430, f32[3,512]{1,0:T(4,128)S(1)} %get-tuple-element.429, f32[3,512]{1,0:T(4,128)S(1)} %get-tuple-element.493, f32[512,512]{1,0:T(8,128)S(1)} %get-tuple-element.431, f32[512,512]{1,0:T(8,128)S(1)} %sqrt.18, ...), kind=kLoop, calls=%fused_computation.21.clone.1 | loop fusion | flops 6289920 | bytes 3178496 | tf_op jit(solution)/shard_map/while/body/eval_jaxpr/reduce_sum | solution.py:30
  49.7 1.0 %fusion.34 = (f32[512,512]{1,0:T(8,128)S(1)}, f32[512,512]{1,0:T(8,128)S(1)}) fusion(f32[3,512]{1,0:T(4,128)S(1)} %get-tuple-element.428, f32[3,512]{1,0:T(4,128)S(1)} %bitcast.23, f32[3,512]{1,0:T(4,128)S(1)} %get-tuple-element.429, f32[3,512]{1,0:T(4,128)S(1)} %get-tuple-element.493), kind=kLoop, calls=%fused_computation.22.clone.1 | loop fusion | flops 4194304 | bytes 2121728 | tf_op jit(solution)/shard_map/while/body/eval_jaxpr/reduce_sum | solution.py:22
  51.0 0.6 fusion.32
  51.7 1.5 %fusion.35 = f32[3,512]{1,0:T(4,128)S(1)} fusion(f32[512]{0:T(512)S(1)} %fusion.32, f32[512,512]{1,0:T(8,128)S(1)} %get-tuple-element.430, f32[3,512]{1,0:T(4,128)S(1)} %get-tuple-element.429, f32[3,512]{1,0:T(4,128)S(1)} %get-tuple-element.493, f32[512,512]{1,0:T(8,128)S(1)} %get-tuple-element.431, f32[512,512]{1,0:T(8,128)S(1)} %sqrt.18, ...), kind=kLoop, calls=%fused_computation.21.clone.1 | loop fusion | flops 6289920 | bytes 3178496 | tf_op jit(solution)/shard_map/while/body/eval_jaxpr/reduce_sum | solution.py:30
  53.2 0.6 sqrt_reduce_fusion
  53.8 31.7 %pmax.7 = f32[]{:T(128)} all-reduce(f32[]{:T(128)} %sqrt_reduce_fusion), channel_id=1, replica_groups=mesh['groups'=2,'cells'=4,'sharers'=4] {'cells','sharers'}, use_global_device_ids=true, to_apply=%region_12.13 | all-reduce | flops 1 | bytes 8 | tf_op jit(solution)/shard_map/pmax | solution.py:79
  86.3 0.6 broadcast_in_dim.73
  86.9 0.6 broadcast_in_dim.74
  (50 shorter events, 3.9 us)
Async XLA Ops:
  16.8 8.8 %copy-start.1 = (f32[1,512]{1,0:T(1,128)S(1)}, f32[1,512]{1,0:T(1,128)}, u32[]{:S(2)}) copy-start(f32[1,512]{1,0:T(1,128)} %param.8) | copy-start | bytes 6148
  38.9 47.3 %copy-start = (f32[1,3,512]{2,0,1:T(1,128)S(1)}, f32[1,3,512]{2,0,1:T(1,128)}, u32[]{:S(2)}) copy-start(f32[1,3,512]{2,0,1:T(1,128)} %param.7) | copy-start | bytes 18436
where the time goes:
time: 87.8 us; the launch traced here: 87.5 us
  blocking collectives  59.8 us (68%)
  other arithmetic  21.8 us (25%)
  local copies, waits for them, and re-layouts  3.52 us (4%)
  between operations  2.04 us (2%)
    pmax x1, blocking collectives, local(): largest = lax.pmax(jnp.max(speeds), ('cells', 'sharers'))  31.7 us
    all_gather x1, blocking collectives, local(): lax.all_gather(package, 'sharers', axis=1, tiled=True)  14.8 us
    all_gather x1, blocking collectives, local(): lax.all_gather(package_pairs, 'sharers', axis=1, tiled=True)  13.2 us
    reduce_sum x4, other arithmetic, drift_block(): return jnp.sum(contrib, axis=2)  5.98 us
    reduce_sum x4, other arithmetic, drift_block(): square_dist = jnp.sum(offset * offset, axis=0)  3.82 us
    reduce_sum x8, other arithmetic, density_block(): return (jnp.sum(kernel, axis=1), jnp.sum(kernel[None] * offset, axis=2))  3.46 us
    lt x4, other arithmetic, density_kernel(): key_weight = jnp.where(anchor + slot_index < filled, key_block[3], 0.0)  2.62 us
    select_n x4, other arithmetic, drift_kernel(): key_weight = jnp.where(anchor + slot_index < filled, key_block[6], 0.0)  2.6 us

commit v1 on v0

v1 whole, which is shorter than its diff:
```python
import math

import jax
import jax.numpy as jnp
from jax import lax
from jax.sharding import PartitionSpec as P

EPS = 0.35
NORM = (2.0 * math.pi * EPS * EPS) ** (-1.5)


def density_block(query, key_vel, key_weight):
    offset = query[:, :, None] - key_vel[:, None, :]
    square_dist = jnp.sum(offset * offset, axis=0)
    kernel = NORM * jnp.exp(-square_dist / (2.0 * EPS * EPS)) * key_weight[None, :]
    return (jnp.sum(kernel, axis=1), jnp.sum(kernel[None] * offset, axis=2))


def drift_block(query, query_score, key_vel, key_score, key_weight):
    offset = query[:, :, None] - key_vel[:, None, :]
    score_gap = query_score[:, :, None] - key_score[:, None, :]
    square_dist = jnp.sum(offset * offset, axis=0)
    distance = jnp.sqrt(square_dist)
    along = jnp.sum(offset * score_gap, axis=0)
    contrib = (
        distance[None]
        * (square_dist[None] * score_gap - offset * along[None])
        * key_weight[None, None, :]
    )
    return jnp.sum(contrib, axis=2)


def exchange(value, axis):
    size = lax.axis_size(axis)
    blocks = [value]
    for shift in range(1, size):
        pairs = [(i, (i + shift) % size) for i in range(size)]
        blocks.append(lax.ppermute(value, axis, pairs))
    return blocks


def local(velocities, weights, counts):
    velocity = velocities[0]
    filled = counts[0]
    local_rows = velocity.shape[1]
    total_slots = local_rows * lax.axis_size("sharers")
    shifted_rows = lax.axis_index("sharers") * local_rows
    slot_index = jnp.arange(local_rows, dtype=jnp.int32)
    is_live = shifted_rows + slot_index < filled
    live_weight = jnp.where(is_live, weights[0], 0.0)

    density_sum = jnp.zeros((local_rows,), jnp.float32)
    pull_sum = jnp.zeros((3, local_rows), jnp.float32)
    key_blocks = exchange(jnp.concatenate([velocity, live_weight[None]], axis=0), "sharers")

    def density_step(totals, key_block):
        density_part, pull_part = density_block(velocity, key_block[:3], key_block[3])
        return (totals[0] + density_part, totals[1] + pull_part), None

    (density_sum, pull_sum), _ = lax.scan(
        density_step, (density_sum, pull_sum), jnp.stack(key_blocks)
    )
    clamped_density = jnp.where(is_live, density_sum, 1.0)
    scores_here = jnp.where(is_live[None], -pull_sum / (EPS * EPS * clamped_density[None]), 0.0)

    drift_sum = jnp.zeros((3, local_rows), jnp.float32)
    score_blocks = exchange(scores_here, "sharers")

    def drift_step(total, blocks):
        key_block, key_score = blocks
        part = drift_block(velocity, scores_here, key_block[:3], key_score, key_block[3])
        return total + part, None

    drift_sum, _ = lax.scan(
        drift_step, drift_sum, (jnp.stack(key_blocks), jnp.stack(score_blocks))
    )
    drift_local = jnp.where(is_live[None], -drift_sum / total_slots, 0.0)
    speeds = jnp.sqrt(jnp.sum(drift_local * drift_local, axis=0))
    largest = jnp.max(speeds).reshape(1, 1)
    for axis in ("sharers", "cells"):
        for other in exchange(largest, axis)[1:]:
            largest = jnp.maximum(largest, other)
    time_step = 0.5 / (largest + 1e-06)
    return ((velocity + time_step * drift_local)[None], scores_here[None])


def solution(mesh):
    in_specs = (
        P(("groups", "cells"), None, "sharers"),
        P(("groups", "cells"), "sharers"),
        P(("groups", "cells")),
    )
    out_specs = (P(("groups", "cells"), None, "sharers"), P(("groups", "cells"), None, "sharers"))
    return jax.shard_map(local, mesh=mesh, in_specs=in_specs, out_specs=out_specs, check_vma=False)
```

time: 87.8 us -> 53.3 us (0.61)
  blocking collectives: 59.8 us -> 0 us
  starting transfers between devices: 0 us -> 21.4 us
  waiting for transfers between devices: 0 us -> 6.47 us
  other arithmetic: 21.8 us -> 16.3 us
  between operations: 2.04 us -> 5.9 us
  local copies, waits for them, and re-layouts: 3.52 us -> 2.46 us
    pmax x1 -> x0, blocking collectives: 31.7 us -> none  [local(): largest = lax.pmax(jnp.max(speeds), ('cells', 'sharers'))]
    all_gather x2 -> x0, blocking collectives: 28 us -> none  [the longest x1 14.8 us: local(): lax.all_gather(package, 'sharers', axis=1, tiled=True)]
    ppermute x0 -> x12, starting transfers between devices: none -> 21.4 us  [exchange(): blocks.append(lax.ppermute(value, axis, pairs))]
    ppermute x0 -> x12, waiting for transfers between devices: none -> 6.47 us  [exchange(): blocks.append(lax.ppermute(value, axis, pairs))]
    lt x4 -> x0, other arithmetic: 2.62 us -> none  [density_kernel(): key_weight = jnp.where(anchor + slot_index < filled, key_block[3], 0.0)]
    select_n x4 -> x1, other arithmetic: 2.6 us -> 0.69 us  [local(): live_weight = jnp.where(is_live, weights[0], 0.0)]
  transfers between devices with their start and end apart: 0 -> 12, of which waited for: 0 -> 5; matrix products, arithmetic and copies ran while one was open for 0% -> 0% of each run, Pallas kernels for 0% -> 0%
where the time goes in v1:
time: 53.3 us; the launch traced here: 53 us
  starting transfers between devices  21.4 us (40%)
  other arithmetic  16.3 us (31%)
  waiting for transfers between devices  6.47 us (12%)
  between operations  5.9 us (11%)
  local copies, waits for them, and re-layouts  2.46 us (5%)
    ppermute x12, starting transfers between devices, exchange(): blocks.append(lax.ppermute(value, axis, pairs))  21.4 us
    ppermute x12, waiting for transfers between devices, exchange(): blocks.append(lax.ppermute(value, axis, pairs))  6.47 us
    reduce_sum x4, other arithmetic, drift_block(): return jnp.sum(contrib, axis=2)  5.98 us
    reduce_sum x4, other arithmetic, drift_block(): square_dist = jnp.sum(offset * offset, axis=0)  3.83 us
    reduce_sum x8, other arithmetic, density_block(): return (jnp.sum(kernel, axis=1), jnp.sum(kernel[None] * offset, axis=2))  3.47 us
    reduce_sum x4, other arithmetic, density_block(): square_dist = jnp.sum(offset * offset, axis=0)  1.45 us
  transfers between devices with their start and end apart: 12, of which 5 were waited for; matrix products, arithmetic and copies ran while one was open for 0% of the time, Pallas kernels for 0%

profile of v1, /device:TPU:0, one launch (start us, length us, event | category | flops | bytes accessed | tf_op | source)
XLA Modules:
  0.0 53.0 jit_solution(2806967233059799929)
XLA Ops:
  0.6 0.7 %copy.20 = f32[1,3,512]{2,1,0:T(4,128)S(1)} copy(f32[1,3,512]{2,0,1:T(1,128)} %param.7) | data formatting | bytes 12288
  2.0 0.7 %compare_select_fusion = f32[1,512]{1,0:T(1,128)S(1)} fusion(f32[1,512]{1,0:T(1,128)} %param.8, s32[]{:T(128)} %bitcast.38, s32[]{:T(128)S(6)} %mul.93), kind=kLoop, calls=%fused_computation.31 | loop fusion | flops 1536 | bytes 4104 | tf_op jit(solution)/shard_map/jit(_where)/select_n | solution.py:50
  2.7 3.1 %collective-permute-start = (f32[4,512]{1,0:T(4,128)S(1)}, f32[4,512]{1,0:T(4,128)S(1)}, u32[]{:S(2)}, u32[]{:S(2)}) collective-permute-start(f32[4,512]{1,0:T(4,128)S(1)} %pad_maximum_fusion.2), channel_id=1, source_target_pairs={{0,1},{1,2},{2,3},{3,0},{4,5},{5,6},{6,7},{7,4},{8,9},{9,10},{10,1... | collective-permute-start | bytes 24584 | tf_op jit(solution)/shard_map/ppermute | solution.py:38
  5.8 2.6 %collective-permute-start.1 = (f32[4,512]{1,0:T(4,128)S(1)}, f32[4,512]{1,0:T(4,128)S(1)}, u32[]{:S(2)}, u32[]{:S(2)}) collective-permute-start(f32[4,512]{1,0:T(4,128)S(1)} %pad_maximum_fusion.2), channel_id=1, source_target_pairs={{0,2},{1,3},{2,0},{3,1},{4,6},{5,7},{6,4},{7,5},{8,10},{9,11},{10,... | collective-permute-start | bytes 24584 | tf_op jit(solution)/shard_map/ppermute | solution.py:38
  8.3 1.3 %collective-permute-start.2 = (f32[4,512]{1,0:T(4,128)S(1)}, f32[4,512]{1,0:T(4,128)S(1)}, u32[]{:S(2)}, u32[]{:S(2)}) collective-permute-start(f32[4,512]{1,0:T(4,128)S(1)} %pad_maximum_fusion.2), channel_id=1, source_target_pairs={{0,3},{1,0},{2,1},{3,2},{4,7},{5,4},{6,5},{7,6},{8,11},{9,8},{10,9... | collective-permute-start | bytes 24584 | tf_op jit(solution)/shard_map/ppermute | solution.py:38
  9.7 0.7 %collective-permute-done.1 = f32[4,512]{1,0:T(4,128)S(1)} collective-permute-done((f32[4,512]{1,0:T(4,128)S(1)}, f32[4,512]{1,0:T(4,128)S(1)}, u32[]{:S(2)}, u32[]{:S(2)}) %collective-permute-start.1) | collective-permute-done | bytes 8224 | tf_op jit(solution)/shard_map/ppermute | solution.py:38
  10.4 1.6 %collective-permute-done.2 = f32[4,512]{1,0:T(4,128)S(1)} collective-permute-done((f32[4,512]{1,0:T(4,128)S(1)}, f32[4,512]{1,0:T(4,128)S(1)}, u32[]{:S(2)}, u32[]{:S(2)}) %collective-permute-start.2) | collective-permute-done | bytes 8224 | tf_op jit(solution)/shard_map/ppermute | solution.py:38
  12.0 5.3 %while.24 = (s32[]{:T(128)}, f32[512]{0:T(512)S(1)}, f32[3,512]{1,0:T(4,128)S(1)}, f32[1,3,512]{2,1,0:T(4,128)S(1)}, f32[4,4,512]{2,1,0:T(4,128)S(1)}, /*index=5*/s32[]{:T(128)}, s32[]{:T(128)}, s32[]{}) while((s32[]{:T(128)}, f32[512]{0:T(512)S(1)}, f32[3,512]{1,0:T(4,128)S(1)}, f32[1,3,512]{2,1,0:T(4,128)S(1)}, ...), condition=%wide.region_4.5_spmd.clone, body=%wide.region_0.4_spmd.clone.sunk | while | flops 5507588 | bytes 4270200 | solution.py:60
  12.7 0.6 %fusion.17 = f32[3,512]{1,0:T(4,128)S(1)} fusion(f32[512,512]{1,0:T(8,128)S(1)} %get-tuple-element.222, f32[3,512]{1,0:T(4,128)S(1)} %dynamic-slice_bitcast_fusion.4, f32[3,512]{1,0:T(4,128)S(1)} %bitcast.42), kind=kLoop, calls=%fused_computation.3.clone.1 | loop fusion | flops 2357760 | bytes 1067008 | tf_op jit(solution)/shard_map/while/body/eval_jaxpr/reduce_sum | solution.py:16
  14.0 0.6 %fusion.17 = f32[3,512]{1,0:T(4,128)S(1)} fusion(f32[512,512]{1,0:T(8,128)S(1)} %get-tuple-element.222, f32[3,512]{1,0:T(4,128)S(1)} %dynamic-slice_bitcast_fusion.4, f32[3,512]{1,0:T(4,128)S(1)} %bitcast.42), kind=kLoop, calls=%fused_computation.3.clone.1 | loop fusion | flops 2357760 | bytes 1067008 | tf_op jit(solution)/shard_map/while/body/eval_jaxpr/reduce_sum | solution.py:16
  15.3 0.6 %fusion.17 = f32[3,512]{1,0:T(4,128)S(1)} fusion(f32[512,512]{1,0:T(8,128)S(1)} %get-tuple-element.222, f32[3,512]{1,0:T(4,128)S(1)} %dynamic-slice_bitcast_fusion.4, f32[3,512]{1,0:T(4,128)S(1)} %bitcast.42), kind=kLoop, calls=%fused_computation.3.clone.1 | loop fusion | flops 2357760 | bytes 1067008 | tf_op jit(solution)/shard_map/while/body/eval_jaxpr/reduce_sum | solution.py:16
  16.7 0.6 %fusion.17 = f32[3,512]{1,0:T(4,128)S(1)} fusion(f32[512,512]{1,0:T(8,128)S(1)} %get-tuple-element.222, f32[3,512]{1,0:T(4,128)S(1)} %dynamic-slice_bitcast_fusion.4, f32[3,512]{1,0:T(4,128)S(1)} %bitcast.42), kind=kLoop, calls=%fused_computation.3.clone.1 | loop fusion | flops 2357760 | bytes 1067008 | tf_op jit(solution)/shard_map/while/body/eval_jaxpr/reduce_sum | solution.py:16
  17.4 1.0 %collective-permute-start.4 = (f32[3,512]{1,0:T(4,128)S(1)}, f32[3,512]{1,0:T(4,128)S(1)}, u32[]{:S(2)}, u32[]{:S(2)}) collective-permute-start(f32[3,512]{1,0:T(4,128)S(1)} %divide_select_fusion), channel_id=1, source_target_pairs={{0,2},{1,3},{2,0},{3,1},{4,6},{5,7},{6,4},{7,5},{8,10},{9,11},{10,... | collective-permute-start | bytes 18440 | tf_op jit(solution)/shard_map/ppermute | solution.py:38
  18.3 2.8 %collective-permute-start.3 = (f32[3,512]{1,0:T(4,128)S(1)}, f32[3,512]{1,0:T(4,128)S(1)}, u32[]{:S(2)}, u32[]{:S(2)}) collective-permute-start(f32[3,512]{1,0:T(4,128)S(1)} %divide_select_fusion), channel_id=1, source_target_pairs={{0,1},{1,2},{2,3},{3,0},{4,5},{5,6},{6,7},{7,4},{8,9},{9,10},{10,1... | collective-permute-start | bytes 18440 | tf_op jit(solution)/shard_map/ppermute | solution.py:38
  21.1 1.0 %collective-permute-start.5 = (f32[3,512]{1,0:T(4,128)S(1)}, f32[3,512]{1,0:T(4,128)S(1)}, u32[]{:S(2)}, u32[]{:S(2)}) collective-permute-start(f32[3,512]{1,0:T(4,128)S(1)} %divide_select_fusion), channel_id=1, source_target_pairs={{0,3},{1,0},{2,1},{3,2},{4,7},{5,4},{6,5},{7,6},{8,11},{9,8},{10,9... | collective-permute-start | bytes 18440 | tf_op jit(solution)/shard_map/ppermute | solution.py:38
  22.2 1.6 %collective-permute-done.3 = f32[3,512]{1,0:T(4,128)S(1)} collective-permute-done((f32[3,512]{1,0:T(4,128)S(1)}, f32[3,512]{1,0:T(4,128)S(1)}, u32[]{:S(2)}, u32[]{:S(2)}) %collective-permute-start.3) | collective-permute-done | bytes 6176 | tf_op jit(solution)/shard_map/ppermute | solution.py:38
  23.8 1.0 %collective-permute-done.5 = f32[3,512]{1,0:T(4,128)S(1)} collective-permute-done((f32[3,512]{1,0:T(4,128)S(1)}, f32[3,512]{1,0:T(4,128)S(1)}, u32[]{:S(2)}, u32[]{:S(2)}) %collective-permute-start.5) | collective-permute-done | bytes 6176 | tf_op jit(solution)/shard_map/ppermute | solution.py:38
  24.8 11.2 %while.25 = (s32[]{:T(128)}, f32[3,512]{1,0:T(4,128)S(1)}, f32[1,3,512]{2,1,0:T(4,128)S(1)}, f32[4,4,512]{2,1,0:T(4,128)S(1)}, f32[3,512]{1,0:T(4,128)S(1)}, /*i...) while((s32[]{:T(128)}, f32[3,512]{1,0:T(4,128)S(1)}, f32[1,3,512]{2,1,0:T(4,128)S(1)}, ...), condition=%wide.region_9.10_spmd.clone, body=%wide.region_5.9_spmd.clone.sunk | while | flops 10487300 | bytes 7456899 | solution.py:74
  24.9 1.0 %fusion.18 = (f32[512,512]{1,0:T(8,128)S(1)}, f32[512,512]{1,0:T(8,128)S(1)}) fusion(f32[3,512]{1,0:T(4,128)S(1)} %get-tuple-element.229, f32[3,512]{1,0:T(4,128)S(1)} %bitcast.43, f32[3,512]{1,0:T(4,128)S(1)} %get-tuple-element.230, f32[3,512]{1,0:T(4,128)S(1)} %get-tuple-element.279), kind=kLoop, calls=%fused_computation.17.clone.1 | loop fusion | flops 4194304 | bytes 2121728 | tf_op jit(solution)/shard_map/while/body/eval_jaxpr/reduce_sum | solution.py:22
  26.1 1.5 %fusion.19 = f32[3,512]{1,0:T(4,128)S(1)} fusion(f32[512]{0:T(512)S(1)} %bitcast.45, f32[512,512]{1,0:T(8,128)S(1)} %get-tuple-element.231, f32[3,512]{1,0:T(4,128)S(1)} %get-tuple-element.230, f32[3,512]{1,0:T(4,128)S(1)} %get-tuple-element.279, f32[512,512]{1,0:T(8,128)S(1)} %get-tuple-element.232, f32[512,512]{1,0:T(8,128)S(1)} %sqrt.14, ...), kind=kLoop, calls=%fused_computation.16.clone.1 | loop fusion | flops 6289920 | bytes 3178496 | tf_op jit(solution)/shard_map/while/body/eval_jaxpr/reduce_sum | solution.py:30
  27.7 1.0 %fusion.18 = (f32[512,512]{1,0:T(8,128)S(1)}, f32[512,512]{1,0:T(8,128)S(1)}) fusion(f32[3,512]{1,0:T(4,128)S(1)} %get-tuple-element.229, f32[3,512]{1,0:T(4,128)S(1)} %bitcast.43, f32[3,512]{1,0:T(4,128)S(1)} %get-tuple-element.230, f32[3,512]{1,0:T(4,128)S(1)} %get-tuple-element.279), kind=kLoop, calls=%fused_computation.17.clone.1 | loop fusion | flops 4194304 | bytes 2121728 | tf_op jit(solution)/shard_map/while/body/eval_jaxpr/reduce_sum | solution.py:22
  28.9 1.5 %fusion.19 = f32[3,512]{1,0:T(4,128)S(1)} fusion(f32[512]{0:T(512)S(1)} %bitcast.45, f32[512,512]{1,0:T(8,128)S(1)} %get-tuple-element.231, f32[3,512]{1,0:T(4,128)S(1)} %get-tuple-element.230, f32[3,512]{1,0:T(4,128)S(1)} %get-tuple-element.279, f32[512,512]{1,0:T(8,128)S(1)} %get-tuple-element.232, f32[512,512]{1,0:T(8,128)S(1)} %sqrt.14, ...), kind=kLoop, calls=%fused_computation.16.clone.1 | loop fusion | flops 6289920 | bytes 3178496 | tf_op jit(solution)/shard_map/while/body/eval_jaxpr/reduce_sum | solution.py:30
  30.5 1.0 %fusion.18 = (f32[512,512]{1,0:T(8,128)S(1)}, f32[512,512]{1,0:T(8,128)S(1)}) fusion(f32[3,512]{1,0:T(4,128)S(1)} %get-tuple-element.229, f32[3,512]{1,0:T(4,128)S(1)} %bitcast.43, f32[3,512]{1,0:T(4,128)S(1)} %get-tuple-element.230, f32[3,512]{1,0:T(4,128)S(1)} %get-tuple-element.279), kind=kLoop, calls=%fused_computation.17.clone.1 | loop fusion | flops 4194304 | bytes 2121728 | tf_op jit(solution)/shard_map/while/body/eval_jaxpr/reduce_sum | solution.py:22
  31.7 1.5 %fusion.19 = f32[3,512]{1,0:T(4,128)S(1)} fusion(f32[512]{0:T(512)S(1)} %bitcast.45, f32[512,512]{1,0:T(8,128)S(1)} %get-tuple-element.231, f32[3,512]{1,0:T(4,128)S(1)} %get-tuple-element.230, f32[3,512]{1,0:T(4,128)S(1)} %get-tuple-element.279, f32[512,512]{1,0:T(8,128)S(1)} %get-tuple-element.232, f32[512,512]{1,0:T(8,128)S(1)} %sqrt.14, ...), kind=kLoop, calls=%fused_computation.16.clone.1 | loop fusion | flops 6289920 | bytes 3178496 | tf_op jit(solution)/shard_map/while/body/eval_jaxpr/reduce_sum | solution.py:30
  33.3 1.0 %fusion.18 = (f32[512,512]{1,0:T(8,128)S(1)}, f32[512,512]{1,0:T(8,128)S(1)}) fusion(f32[3,512]{1,0:T(4,128)S(1)} %get-tuple-element.229, f32[3,512]{1,0:T(4,128)S(1)} %bitcast.43, f32[3,512]{1,0:T(4,128)S(1)} %get-tuple-element.230, f32[3,512]{1,0:T(4,128)S(1)} %get-tuple-element.279), kind=kLoop, calls=%fused_computation.17.clone.1 | loop fusion | flops 4194304 | bytes 2121728 | tf_op jit(solution)/shard_map/while/body/eval_jaxpr/reduce_sum | solution.py:22
  34.5 1.5 %fusion.19 = f32[3,512]{1,0:T(4,128)S(1)} fusion(f32[512]{0:T(512)S(1)} %bitcast.45, f32[512,512]{1,0:T(8,128)S(1)} %get-tuple-element.231, f32[3,512]{1,0:T(4,128)S(1)} %get-tuple-element.230, f32[3,512]{1,0:T(4,128)S(1)} %get-tuple-element.279, f32[512,512]{1,0:T(8,128)S(1)} %get-tuple-element.232, f32[512,512]{1,0:T(8,128)S(1)} %sqrt.14, ...), kind=kLoop, calls=%fused_computation.16.clone.1 | loop fusion | flops 6289920 | bytes 3178496 | tf_op jit(solution)/shard_map/while/body/eval_jaxpr/reduce_sum | solution.py:30
  36.1 0.6 %sqrt_reduce_fusion = f32[]{:T(128)} fusion(f32[512]{0:T(512)S(1)} %multiply_reduce_fusion), kind=kLoop, calls=%fused_computation.32 | loop fusion | flops 511 | bytes 2052 | tf_op jit(solution)/shard_map/reduce_max | solution.py:79
  36.7 3.4 %collective-permute-start.7 = (f32[1,1]{1,0:T(1,128)}, f32[1,1]{1,0:T(1,128)}, u32[]{:S(2)}, u32[]{:S(2)}) collective-permute-start(f32[1,1]{1,0:T(1,128)} %bitcast.7), channel_id=1, source_target_pairs={{0,2},{1,3},{2,0},{3,1},{4,6},{5,7},{6,4},{7,5},{8,10},{9,11},{10,... | collective-permute-start | bytes 20 | tf_op jit(solution)/shard_map/ppermute | solution.py:38
  40.5 1.6 %collective-permute-done.6 = f32[1,1]{1,0:T(1,128)} collective-permute-done((f32[1,1]{1,0:T(1,128)}, f32[1,1]{1,0:T(1,128)}, u32[]{:S(2)}, u32[]{:S(2)}) %collective-permute-start.6) | collective-permute-done | bytes 36 | tf_op jit(solution)/shard_map/ppermute | solution.py:38
  44.7 0.9 %collective-permute-start.9 = (f32[1,1]{1,0:T(1,128)}, f32[1,1]{1,0:T(1,128)}, u32[]{:S(2)}, u32[]{:S(2)}) collective-permute-start(f32[1,1]{1,0:T(1,128)} %max.20), channel_id=1, source_target_pairs={{0,4},{4,8},{8,12},{12,0},{1,5},{5,9},{9,13},{13,1},{2,6},{6,10},{... | collective-permute-start | bytes 20 | tf_op jit(solution)/shard_map/ppermute | solution.py:38
  45.5 2.8 %collective-permute-start.10 = (f32[1,1]{1,0:T(1,128)}, f32[1,1]{1,0:T(1,128)}, u32[]{:S(2)}, u32[]{:S(2)}) collective-permute-start(f32[1,1]{1,0:T(1,128)} %max.20), channel_id=1, source_target_pairs={{0,8},{4,12},{8,0},{12,4},{1,9},{5,13},{9,1},{13,5},{2,10},{6,14},... | collective-permute-start | bytes 20 | tf_op jit(solution)/shard_map/ppermute | solution.py:38
  48.3 2.1 %collective-permute-start.11 = (f32[1,1]{1,0:T(1,128)}, f32[1,1]{1,0:T(1,128)}, u32[]{:S(2)}, u32[]{:S(2)}) collective-permute-start(f32[1,1]{1,0:T(1,128)} %max.20), channel_id=1, source_target_pairs={{0,12},{4,0},{8,4},{12,8},{1,13},{5,1},{9,5},{13,9},{2,14},{6,2},{... | collective-permute-start | bytes 20 | tf_op jit(solution)/shard_map/ppermute | solution.py:38
  (73 shorter events, 5.0 us)
Async XLA Ops:
  2.7 7.0 %collective-permute-start = (f32[4,512]{1,0:T(4,128)S(1)}, f32[4,512]{1,0:T(4,128)S(1)}, u32[]{:S(2)}, u32[]{:S(2)}) collective-permute-start(f32[4,512]{1,0:T(4,128)S(1)} %pad_maximum_fusion.2), channel_id=1, source_target_pairs={{0,1},{1,2},{2,3},{3,0},{4,5},{5,6},{6,7},{7,4},{8,9},{9,10},{10,1... | collective-permute-start | bytes 24584 | tf_op jit(solution)/shard_map/ppermute | solution.py:38
  5.8 4.6 %collective-permute-start.1 = (f32[4,512]{1,0:T(4,128)S(1)}, f32[4,512]{1,0:T(4,128)S(1)}, u32[]{:S(2)}, u32[]{:S(2)}) collective-permute-start(f32[4,512]{1,0:T(4,128)S(1)} %pad_maximum_fusion.2), channel_id=1, source_target_pairs={{0,2},{1,3},{2,0},{3,1},{4,6},{5,7},{6,4},{7,5},{8,10},{9,11},{10,... | collective-permute-start | bytes 24584 | tf_op jit(solution)/shard_map/ppermute | solution.py:38
  8.3 3.7 %collective-permute-start.2 = (f32[4,512]{1,0:T(4,128)S(1)}, f32[4,512]{1,0:T(4,128)S(1)}, u32[]{:S(2)}, u32[]{:S(2)}) collective-permute-start(f32[4,512]{1,0:T(4,128)S(1)} %pad_maximum_fusion.2), channel_id=1, source_target_pairs={{0,3},{1,0},{2,1},{3,2},{4,7},{5,4},{6,5},{7,6},{8,11},{9,8},{10,9... | collective-permute-start | bytes 24584 | tf_op jit(solution)/shard_map/ppermute | solution.py:38
  17.4 4.8 %collective-permute-start.4 = (f32[3,512]{1,0:T(4,128)S(1)}, f32[3,512]{1,0:T(4,128)S(1)}, u32[]{:S(2)}, u32[]{:S(2)}) collective-permute-start(f32[3,512]{1,0:T(4,128)S(1)} %divide_select_fusion), channel_id=1, source_target_pairs={{0,2},{1,3},{2,0},{3,1},{4,6},{5,7},{6,4},{7,5},{8,10},{9,11},{10,... | collective-permute-start | bytes 18440 | tf_op jit(solution)/shard_map/ppermute | solution.py:38
  18.3 5.4 %collective-permute-start.3 = (f32[3,512]{1,0:T(4,128)S(1)}, f32[3,512]{1,0:T(4,128)S(1)}, u32[]{:S(2)}, u32[]{:S(2)}) collective-permute-start(f32[3,512]{1,0:T(4,128)S(1)} %divide_select_fusion), channel_id=1, source_target_pairs={{0,1},{1,2},{2,3},{3,0},{4,5},{5,6},{6,7},{7,4},{8,9},{9,10},{10,1... | collective-permute-start | bytes 18440 | tf_op jit(solution)/shard_map/ppermute | solution.py:38
  21.1 3.7 %collective-permute-start.5 = (f32[3,512]{1,0:T(4,128)S(1)}, f32[3,512]{1,0:T(4,128)S(1)}, u32[]{:S(2)}, u32[]{:S(2)}) collective-permute-start(f32[3,512]{1,0:T(4,128)S(1)} %divide_select_fusion), channel_id=1, source_target_pairs={{0,3},{1,0},{2,1},{3,2},{4,7},{5,4},{6,5},{7,6},{8,11},{9,8},{10,9... | collective-permute-start | bytes 18440 | tf_op jit(solution)/shard_map/ppermute | solution.py:38
  22.2 2.7 %copy-start = (f32[1,3,512]{2,0,1:T(1,128)}, f32[1,3,512]{2,0,1:T(1,128)S(1)}, u32[]{:S(2)}) copy-start(f32[1,3,512]{2,0,1:T(1,128)S(1)} %stack.40) | copy-start | bytes 18436
  24.8 27.6 %copy-start.1 = (f32[1,3,512]{2,0,1:T(1,128)S(1)}, f32[1,3,512]{2,0,1:T(1,128)}, u32[]{:S(2)}) copy-start(f32[1,3,512]{2,0,1:T(1,128)} %param.7) | copy-start | bytes 18436
  36.7 5.4 %collective-permute-start.6 = (f32[1,1]{1,0:T(1,128)}, f32[1,1]{1,0:T(1,128)}, u32[]{:S(2)}, u32[]{:S(2)}) collective-permute-start(f32[1,1]{1,0:T(1,128)} %bitcast.7), channel_id=1, source_target_pairs={{0,1},{1,2},{2,3},{3,0},{4,5},{5,6},{6,7},{7,4},{8,9},{9,10},{10,1... | collective-permute-start | bytes 20 | tf_op jit(solution)/shard_map/ppermute | solution.py:38
  36.7 6.7 %collective-permute-start.7 = (f32[1,1]{1,0:T(1,128)}, f32[1,1]{1,0:T(1,128)}, u32[]{:S(2)}, u32[]{:S(2)}) collective-permute-start(f32[1,1]{1,0:T(1,128)} %bitcast.7), channel_id=1, source_target_pairs={{0,2},{1,3},{2,0},{3,1},{4,6},{5,7},{6,4},{7,5},{8,10},{9,11},{10,... | collective-permute-start | bytes 20 | tf_op jit(solution)/shard_map/ppermute | solution.py:38
  40.1 4.0 %collective-permute-start.8 = (f32[1,1]{1,0:T(1,128)}, f32[1,1]{1,0:T(1,128)}, u32[]{:S(2)}, u32[]{:S(2)}) collective-permute-start(f32[1,1]{1,0:T(1,128)} %bitcast.7), channel_id=1, source_target_pairs={{0,3},{1,0},{2,1},{3,2},{4,7},{5,4},{6,5},{7,6},{8,11},{9,8},{10,9... | collective-permute-start | bytes 20 | tf_op jit(solution)/shard_map/ppermute | solution.py:38
  44.7 5.8 %collective-permute-start.9 = (f32[1,1]{1,0:T(1,128)}, f32[1,1]{1,0:T(1,128)}, u32[]{:S(2)}, u32[]{:S(2)}) collective-permute-start(f32[1,1]{1,0:T(1,128)} %max.20), channel_id=1, source_target_pairs={{0,4},{4,8},{8,12},{12,0},{1,5},{5,9},{9,13},{13,1},{2,6},{6,10},{... | collective-permute-start | bytes 20 | tf_op jit(solution)/shard_map/ppermute | solution.py:38
  45.5 5.6 %collective-permute-start.10 = (f32[1,1]{1,0:T(1,128)}, f32[1,1]{1,0:T(1,128)}, u32[]{:S(2)}, u32[]{:S(2)}) collective-permute-start(f32[1,1]{1,0:T(1,128)} %max.20), channel_id=1, source_target_pairs={{0,8},{4,12},{8,0},{12,4},{1,9},{5,13},{9,1},{13,5},{2,10},{6,14},... | collective-permute-start | bytes 20 | tf_op jit(solution)/shard_map/ppermute | solution.py:38
  48.3 3.4 %collective-permute-start.11 = (f32[1,1]{1,0:T(1,128)}, f32[1,1]{1,0:T(1,128)}, u32[]{:S(2)}, u32[]{:S(2)}) collective-permute-start(f32[1,1]{1,0:T(1,128)} %max.20), channel_id=1, source_target_pairs={{0,12},{4,0},{8,4},{12,8},{1,13},{5,1},{9,5},{13,9},{2,14},{6,2},{... | collective-permute-start | bytes 20 | tf_op jit(solution)/shard_map/ppermute | solution.py:38

commit v2 on v1

--- a/solution.py
+++ b/solution.py
@@ -31,12 +31,8 @@
 
 
 def exchange(value, axis):
-    size = lax.axis_size(axis)
-    blocks = [value]
-    for shift in range(1, size):
-        pairs = [(i, (i + shift) % size) for i in range(size)]
-        blocks.append(lax.ppermute(value, axis, pairs))
-    return blocks
+    copies = jnp.broadcast_to(value[None], (lax.axis_size(axis),) + value.shape)
+    return lax.all_to_all(copies, axis, 0, 0, tiled=True)
 
 
 def local(velocities, weights, counts):
@@ -58,7 +54,7 @@
         return (totals[0] + density_part, totals[1] + pull_part), None
 
     (density_sum, pull_sum), _ = lax.scan(
-        density_step, (density_sum, pull_sum), jnp.stack(key_blocks)
+        density_step, (density_sum, pull_sum), key_blocks
     )
     clamped_density = jnp.where(is_live, density_sum, 1.0)
     scores_here = jnp.where(is_live[None], -pull_sum / (EPS * EPS * clamped_density[None]), 0.0)
@@ -72,14 +68,11 @@
         return total + part, None
 
     drift_sum, _ = lax.scan(
-        drift_step, drift_sum, (jnp.stack(key_blocks), jnp.stack(score_blocks))
+        drift_step, drift_sum, (key_blocks, score_blocks)
     )
     drift_local = jnp.where(is_live[None], -drift_sum / total_slots, 0.0)
     speeds = jnp.sqrt(jnp.sum(drift_local * drift_local, axis=0))
-    largest = jnp.max(speeds).reshape(1, 1)
-    for axis in ("sharers", "cells"):
-        for other in exchange(largest, axis)[1:]:
-            largest = jnp.maximum(largest, other)
+    largest = jnp.max(exchange(jnp.max(speeds).reshape(1), ("cells", "sharers")))
     time_step = 0.5 / (largest + 1e-06)
     return ((velocity + time_step * drift_local)[None], scores_here[None])
 

time: 53.3 us -> 55.3 us (1.038)
  waiting for transfers between devices: 6.47 us -> 17 us
  starting transfers between devices: 21.4 us -> 13.1 us
  between operations: 5.9 us -> 2.06 us
  local copies, waits for them, and re-layouts: 2.46 us -> 5.42 us
  other arithmetic: 16.3 us -> 16.9 us
    ppermute x12 -> x0, starting transfers between devices: 21.4 us -> none  [exchange(): blocks.append(lax.ppermute(value, axis, pairs))]
    all_to_all x0 -> x3, waiting for transfers between devices: none -> 17 us  [exchange(): return lax.all_to_all(copies, axis, 0, 0, tiled=True)]
    all_to_all x0 -> x3, starting transfers between devices: none -> 13.1 us  [exchange(): return lax.all_to_all(copies, axis, 0, 0, tiled=True)]
    ppermute x12 -> x0, waiting for transfers between devices: 6.47 us -> none  [exchange(): blocks.append(lax.ppermute(value, axis, pairs))]
    broadcast_in_dim x0 -> x4, local copies, waits for them, and re-layouts: none -> 3.06 us  [exchange(): copies = jnp.broadcast_to(value[None], (lax.axis_size(axis),) + value.shape)]
    reduce_max x1 -> x2, other arithmetic: 0.61 us -> 1.23 us  [the longest x1 0.62 us: local(): jnp.max(exchange(jnp.max(speeds).reshape(1), ('cells', 'sharers')))]
  transfers between devices with their start and end apart: 12 -> 3, of which waited for: 5 -> 3; matrix products, arithmetic and copies ran while one was open for 0% -> 1% of each run, Pallas kernels for 0% -> 0%
where the time goes in v2:
time: 55.3 us; the launch traced here: 54.8 us
  waiting for transfers between devices  17 us (31%)
  other arithmetic  16.9 us (31%)
  starting transfers between devices  13.1 us (24%)
  local copies, waits for them, and re-layouts  5.42 us (10%)
  between operations  2.06 us (4%)
    all_to_all x3, waiting for transfers between devices, exchange(): return lax.all_to_all(copies, axis, 0, 0, tiled=True)  17 us
    all_to_all x3, starting transfers between devices, exchange(): return lax.all_to_all(copies, axis, 0, 0, tiled=True)  13.1 us
    reduce_sum x4, other arithmetic, drift_block(): return jnp.sum(contrib, axis=2)  5.98 us
    reduce_sum x4, other arithmetic, drift_block(): square_dist = jnp.sum(offset * offset, axis=0)  3.83 us
    reduce_sum x8, other arithmetic, density_block(): return (jnp.sum(kernel, axis=1), jnp.sum(kernel[None] * offset, axis=2))  3.47 us
    broadcast_in_dim x4, local copies, waits for them, and re-layouts, exchange(): copies = jnp.broadcast_to(value[None], (lax.axis_size(axis),) + value.shape)  3.06 us
    reduce_sum x4, other arithmetic, density_block(): square_dist = jnp.sum(offset * offset, axis=0)  1.45 us
  transfers between devices with their start and end apart: 3, of which 3 were waited for; matrix products, arithmetic and copies ran while one was open for 1% of the time, Pallas kernels for 0%

profile of v2, /device:TPU:0, one launch (start us, length us, event | category | flops | bytes accessed | tf_op | source)
XLA Modules:
  0.0 54.8 jit_solution(3787310579970878223)
XLA Ops:
  0.6 0.7 %copy.16 = f32[1,3,512]{2,1,0:T(4,128)S(1)} copy(f32[1,3,512]{2,0,1:T(1,128)} %param.7) | data formatting | bytes 12288
  2.0 0.7 %compare_select_fusion = f32[1,512]{1,0:T(1,128)S(1)} fusion(f32[1,512]{1,0:T(1,128)} %param.8, s32[]{:T(128)} %bitcast.29, s32[]{:T(128)S(6)} %mul.89), kind=kLoop, calls=%fused_computation.28 | loop fusion | flops 1536 | bytes 4104 | tf_op jit(solution)/shard_map/jit(_where)/select_n | solution.py:46
  2.7 0.6 %broadcast_in_dim.43 = f32[4,4,512]{2,1,0:T(4,128)} broadcast(f32[4,512]{1,0:T(4,128)S(1)} %pad_maximum_fusion), dimensions={1,2} | broadcast | bytes 40960 | tf_op jit(solution)/shard_map/broadcast_in_dim | solution.py:34
  3.3 6.3 %all-to-all-start = ((f32[4,4,512]{2,1,0:T(4,128)}), f32[4,4,512]{2,1,0:T(4,128)S(1)}, u32[]{:S(2)}, u32[]{:S(2)}) async-start(f32[4,4,512]{2,1,0:T(4,128)} %broadcast_in_dim.43), calls=%async_computation | async-start | bytes 65536 | tf_op jit(solution)/shard_map/all_to_all | solution.py:35
  9.6 5.7 %all-to-all-done = f32[4,4,512]{2,1,0:T(4,128)S(1)} async-done(((f32[4,4,512]{2,1,0:T(4,128)}), f32[4,4,512]{2,1,0:T(4,128)S(1)}, u32[]{:S(2)}, u32[]{:S(2)}) %all-to-all-start) | async-done | bytes 32800 | tf_op jit(solution)/shard_map/all_to_all | solution.py:35
  15.3 5.3 %while.24 = (s32[]{:T(128)}, f32[512]{0:T(512)S(1)}, f32[3,512]{1,0:T(4,128)S(1)}, f32[1,3,512]{2,1,0:T(4,128)S(1)}, f32[4,4,512]{2,1,0:T(4,128)S(1)}, /*index=5*/s32[]{:T(128)}, s32[]{:T(128)}, s32[]{}) while((s32[]{:T(128)}, f32[512]{0:T(512)S(1)}, f32[3,512]{1,0:T(4,128)S(1)}, f32[1,3,512]{2,1,0:T(4,128)S(1)}, ...), condition=%wide.region_4.5_spmd.clone, body=%wide.region_0.4_spmd.clone.sunk | while | flops 5507588 | bytes 4270200 | solution.py:56
  15.3 0.4 fusion.14
  15.9 0.6 %fusion.16 = f32[3,512]{1,0:T(4,128)S(1)} fusion(f32[512,512]{1,0:T(8,128)S(1)} %get-tuple-element.227, f32[3,512]{1,0:T(4,128)S(1)} %dynamic-slice_bitcast_fusion.5, f32[3,512]{1,0:T(4,128)S(1)} %bitcast.32), kind=kLoop, calls=%fused_computation.3.clone.1 | loop fusion | flops 2357760 | bytes 1067008 | tf_op jit(solution)/shard_map/while/body/eval_jaxpr/reduce_sum | solution.py:16
  16.6 0.4 fusion.14
  17.2 0.6 %fusion.16 = f32[3,512]{1,0:T(4,128)S(1)} fusion(f32[512,512]{1,0:T(8,128)S(1)} %get-tuple-element.227, f32[3,512]{1,0:T(4,128)S(1)} %dynamic-slice_bitcast_fusion.5, f32[3,512]{1,0:T(4,128)S(1)} %bitcast.32), kind=kLoop, calls=%fused_computation.3.clone.1 | loop fusion | flops 2357760 | bytes 1067008 | tf_op jit(solution)/shard_map/while/body/eval_jaxpr/reduce_sum | solution.py:16
  17.9 0.4 fusion.14
  18.6 0.6 %fusion.16 = f32[3,512]{1,0:T(4,128)S(1)} fusion(f32[512,512]{1,0:T(8,128)S(1)} %get-tuple-element.227, f32[3,512]{1,0:T(4,128)S(1)} %dynamic-slice_bitcast_fusion.5, f32[3,512]{1,0:T(4,128)S(1)} %bitcast.32), kind=kLoop, calls=%fused_computation.3.clone.1 | loop fusion | flops 2357760 | bytes 1067008 | tf_op jit(solution)/shard_map/while/body/eval_jaxpr/reduce_sum | solution.py:16
  19.9 0.6 %fusion.16 = f32[3,512]{1,0:T(4,128)S(1)} fusion(f32[512,512]{1,0:T(8,128)S(1)} %get-tuple-element.227, f32[3,512]{1,0:T(4,128)S(1)} %dynamic-slice_bitcast_fusion.5, f32[3,512]{1,0:T(4,128)S(1)} %bitcast.32), kind=kLoop, calls=%fused_computation.3.clone.1 | loop fusion | flops 2357760 | bytes 1067008 | tf_op jit(solution)/shard_map/while/body/eval_jaxpr/reduce_sum | solution.py:16
  20.6 0.6 %broadcast_in_dim.64 = f32[4,3,512]{2,1,0:T(4,128)} broadcast(f32[3,512]{1,0:T(4,128)S(1)} %divide_select_fusion), dimensions={1,2} | broadcast | bytes 30720 | tf_op jit(solution)/shard_map/broadcast_in_dim | solution.py:34
  21.2 3.3 %all-to-all-start.1 = ((f32[4,3,512]{2,1,0:T(4,128)}), f32[4,3,512]{2,1,0:T(4,128)S(1)}, u32[]{:S(2)}, u32[]{:S(2)}) async-start(f32[4,3,512]{2,1,0:T(4,128)} %broadcast_in_dim.64), calls=%async_computation.1 | async-start | bytes 65536 | tf_op jit(solution)/shard_map/all_to_all | solution.py:35
  24.5 5.6 %all-to-all-done.1 = f32[4,3,512]{2,1,0:T(4,128)S(1)} async-done(((f32[4,3,512]{2,1,0:T(4,128)}), f32[4,3,512]{2,1,0:T(4,128)S(1)}, u32[]{:S(2)}, u32[]{:S(2)}) %all-to-all-start.1) | async-done | bytes 24608 | tf_op jit(solution)/shard_map/all_to_all | solution.py:35
  30.1 11.1 %while.25 = (s32[]{:T(128)}, f32[3,512]{1,0:T(4,128)S(1)}, f32[1,3,512]{2,1,0:T(4,128)S(1)}, f32[4,4,512]{2,1,0:T(4,128)S(1)}, f32[3,512]{1,0:T(4,128)S(1)}, /*i...) while((s32[]{:T(128)}, f32[3,512]{1,0:T(4,128)S(1)}, f32[1,3,512]{2,1,0:T(4,128)S(1)}, ...), condition=%wide.region_9.10_spmd.clone, body=%wide.region_5.9_spmd.clone.sunk | while | flops 10487300 | bytes 7444607 | solution.py:70
  30.1 1.0 %fusion.17 = (f32[512,512]{1,0:T(8,128)S(1)}, f32[512,512]{1,0:T(8,128)S(1)}) fusion(f32[3,512]{1,0:T(4,128)S(1)} %get-tuple-element.234, f32[3,512]{1,0:T(4,128)S(1)} %bitcast.33, f32[3,512]{1,0:T(4,128)S(1)} %get-tuple-element.235, f32[3,512]{1,0:T(4,128)S(1)} %get-tuple-element.284), kind=kLoop, calls=%fused_computation.17.clone.1 | loop fusion | flops 4194304 | bytes 2121728 | tf_op jit(solution)/shard_map/while/body/eval_jaxpr/reduce_sum | solution.py:22
  31.3 1.5 %fusion.18 = f32[3,512]{1,0:T(4,128)S(1)} fusion(f32[512]{0:T(512)S(1)} %bitcast.35, f32[512,512]{1,0:T(8,128)S(1)} %get-tuple-element.236, f32[3,512]{1,0:T(4,128)S(1)} %get-tuple-element.235, f32[3,512]{1,0:T(4,128)S(1)} %get-tuple-element.284, f32[512,512]{1,0:T(8,128)S(1)} %get-tuple-element.237, f32[512,512]{1,0:T(8,128)S(1)} %sqrt.14, ...), kind=kLoop, calls=%fused_computation.16.clone.1 | loop fusion | flops 6289920 | bytes 3178496 | tf_op jit(solution)/shard_map/while/body/eval_jaxpr/reduce_sum | solution.py:30
  32.9 1.0 %fusion.17 = (f32[512,512]{1,0:T(8,128)S(1)}, f32[512,512]{1,0:T(8,128)S(1)}) fusion(f32[3,512]{1,0:T(4,128)S(1)} %get-tuple-element.234, f32[3,512]{1,0:T(4,128)S(1)} %bitcast.33, f32[3,512]{1,0:T(4,128)S(1)} %get-tuple-element.235, f32[3,512]{1,0:T(4,128)S(1)} %get-tuple-element.284), kind=kLoop, calls=%fused_computation.17.clone.1 | loop fusion | flops 4194304 | bytes 2121728 | tf_op jit(solution)/shard_map/while/body/eval_jaxpr/reduce_sum | solution.py:22
  34.1 1.5 %fusion.18 = f32[3,512]{1,0:T(4,128)S(1)} fusion(f32[512]{0:T(512)S(1)} %bitcast.35, f32[512,512]{1,0:T(8,128)S(1)} %get-tuple-element.236, f32[3,512]{1,0:T(4,128)S(1)} %get-tuple-element.235, f32[3,512]{1,0:T(4,128)S(1)} %get-tuple-element.284, f32[512,512]{1,0:T(8,128)S(1)} %get-tuple-element.237, f32[512,512]{1,0:T(8,128)S(1)} %sqrt.14, ...), kind=kLoop, calls=%fused_computation.16.clone.1 | loop fusion | flops 6289920 | bytes 3178496 | tf_op jit(solution)/shard_map/while/body/eval_jaxpr/reduce_sum | solution.py:30
  35.6 1.0 %fusion.17 = (f32[512,512]{1,0:T(8,128)S(1)}, f32[512,512]{1,0:T(8,128)S(1)}) fusion(f32[3,512]{1,0:T(4,128)S(1)} %get-tuple-element.234, f32[3,512]{1,0:T(4,128)S(1)} %bitcast.33, f32[3,512]{1,0:T(4,128)S(1)} %get-tuple-element.235, f32[3,512]{1,0:T(4,128)S(1)} %get-tuple-element.284), kind=kLoop, calls=%fused_computation.17.clone.1 | loop fusion | flops 4194304 | bytes 2121728 | tf_op jit(solution)/shard_map/while/body/eval_jaxpr/reduce_sum | solution.py:22
  36.9 1.5 %fusion.18 = f32[3,512]{1,0:T(4,128)S(1)} fusion(f32[512]{0:T(512)S(1)} %bitcast.35, f32[512,512]{1,0:T(8,128)S(1)} %get-tuple-element.236, f32[3,512]{1,0:T(4,128)S(1)} %get-tuple-element.235, f32[3,512]{1,0:T(4,128)S(1)} %get-tuple-element.284, f32[512,512]{1,0:T(8,128)S(1)} %get-tuple-element.237, f32[512,512]{1,0:T(8,128)S(1)} %sqrt.14, ...), kind=kLoop, calls=%fused_computation.16.clone.1 | loop fusion | flops 6289920 | bytes 3178496 | tf_op jit(solution)/shard_map/while/body/eval_jaxpr/reduce_sum | solution.py:30
  38.4 1.0 %fusion.17 = (f32[512,512]{1,0:T(8,128)S(1)}, f32[512,512]{1,0:T(8,128)S(1)}) fusion(f32[3,512]{1,0:T(4,128)S(1)} %get-tuple-element.234, f32[3,512]{1,0:T(4,128)S(1)} %bitcast.33, f32[3,512]{1,0:T(4,128)S(1)} %get-tuple-element.235, f32[3,512]{1,0:T(4,128)S(1)} %get-tuple-element.284), kind=kLoop, calls=%fused_computation.17.clone.1 | loop fusion | flops 4194304 | bytes 2121728 | tf_op jit(solution)/shard_map/while/body/eval_jaxpr/reduce_sum | solution.py:22
  39.7 1.5 %fusion.18 = f32[3,512]{1,0:T(4,128)S(1)} fusion(f32[512]{0:T(512)S(1)} %bitcast.35, f32[512,512]{1,0:T(8,128)S(1)} %get-tuple-element.236, f32[3,512]{1,0:T(4,128)S(1)} %get-tuple-element.235, f32[3,512]{1,0:T(4,128)S(1)} %get-tuple-element.284, f32[512,512]{1,0:T(8,128)S(1)} %get-tuple-element.237, f32[512,512]{1,0:T(8,128)S(1)} %sqrt.14, ...), kind=kLoop, calls=%fused_computation.16.clone.1 | loop fusion | flops 6289920 | bytes 3178496 | tf_op jit(solution)/shard_map/while/body/eval_jaxpr/reduce_sum | solution.py:30
  41.2 0.6 %sqrt_reduce_fusion = f32[]{:T(128)} fusion(f32[512]{0:T(512)S(1)} %multiply_reduce_fusion), kind=kLoop, calls=%fused_computation.29 | loop fusion | flops 511 | bytes 2052 | tf_op jit(solution)/shard_map/reduce_max | solution.py:75
  41.8 1.2 %broadcast_in_dim.65 = f32[16,1,1]{2,1,0:T(1,128)} broadcast(f32[]{:T(128)} %sqrt_reduce_fusion), dimensions={} | broadcast | bytes 68 | tf_op jit(solution)/shard_map/broadcast_in_dim | solution.py:34
  43.1 3.5 %all-to-all-start.2 = ((f32[16,1,1]{2,1,0:T(1,128)}), f32[16,1,1]{2,1,0:T(1,128)S(1)}, u32[]{:S(2)}, u32[]{:S(2)}) async-start(f32[16,1,1]{2,1,0:T(1,128)} %broadcast_in_dim.65), calls=%async_computation.2 | async-start | bytes 16384 | tf_op jit(solution)/shard_map/all_to_all | solution.py:35
  46.6 0.6 %broadcast_in_dim.67 = f32[1,3,512]{2,0,1:T(1,128)} reshape(f32[3,512]{1,0:T(4,128)S(1)} %get-tuple-element.290) | data formatting | bytes 12288 | tf_op jit(solution)/shard_map/broadcast_in_dim | solution.py:34
  47.2 5.7 %all-to-all-done.2 = f32[16,1,1]{2,1,0:T(1,128)S(1)} async-done(((f32[16,1,1]{2,1,0:T(1,128)}), f32[16,1,1]{2,1,0:T(1,128)S(1)}, u32[]{:S(2)}, u32[]{:S(2)}) %all-to-all-start.2) | async-done | bytes 96 | tf_op jit(solution)/shard_map/all_to_all | solution.py:35
  52.9 0.6 %reduce_max.19 = f32[]{:T(128)} reduce(f32[16,1,1]{2,1,0:T(1,128)S(1)} %all-to-all-done.2, f32[]{:T(128)} %constant.47.clone.1), dimensions={0,1,2}, to_apply=%region_12.13 | reduce | flops 15 | bytes 72 | tf_op jit(solution)/shard_map/reduce_max | solution.py:75
  54.2 0.6 %broadcast_in_dim.66 = f32[1,3,512]{2,0,1:T(1,128)} reshape(f32[3,512]{1,0:T(4,128)S(1)} %multiply_add_fusion) | data formatting | bytes 12288 | tf_op jit(solution)/shard_map/broadcast_in_dim | solution.py:77
  (47 shorter events, 2.7 us)
Async XLA Ops:
  3.3 12.0 %all-to-all-start = ((f32[4,4,512]{2,1,0:T(4,128)}), f32[4,4,512]{2,1,0:T(4,128)S(1)}, u32[]{:S(2)}, u32[]{:S(2)}) async-start(f32[4,4,512]{2,1,0:T(4,128)} %broadcast_in_dim.43), calls=%async_computation | async-start | bytes 65536 | tf_op jit(solution)/shard_map/all_to_all | solution.py:35
  21.2 8.9 %all-to-all-start.1 = ((f32[4,3,512]{2,1,0:T(4,128)}), f32[4,3,512]{2,1,0:T(4,128)S(1)}, u32[]{:S(2)}, u32[]{:S(2)}) async-start(f32[4,3,512]{2,1,0:T(4,128)} %broadcast_in_dim.64), calls=%async_computation.1 | async-start | bytes 65536 | tf_op jit(solution)/shard_map/all_to_all | solution.py:35
  30.1 24.1 %copy-start = (f32[1,3,512]{2,0,1:T(1,128)S(1)}, f32[1,3,512]{2,0,1:T(1,128)}, u32[]{:S(2)}) copy-start(f32[1,3,512]{2,0,1:T(1,128)} %param.7) | copy-start | bytes 18436
  43.1 9.8 %all-to-all-start.2 = ((f32[16,1,1]{2,1,0:T(1,128)}), f32[16,1,1]{2,1,0:T(1,128)S(1)}, u32[]{:S(2)}, u32[]{:S(2)}) async-start(f32[16,1,1]{2,1,0:T(1,128)} %broadcast_in_dim.65), calls=%async_computation.2 | async-start | bytes 16384 | tf_op jit(solution)/shard_map/all_to_all | solution.py:35

commit v3 on v2

v3 whole, which is shorter than its diff:
```python
import functools
import math

import jax
import jax.numpy as jnp
from jax import lax
from jax.experimental import pallas as pl
from jax.experimental.pallas import tpu as pltpu
from jax.sharding import PartitionSpec as P

EPS = 0.35
SCALE = math.sqrt(math.log2(math.e) / (2.0 * EPS * EPS))
GRID = 4.0
TINY = 1e-30
CHUNK = 256
FEATURES = 48
bf16, f32 = jnp.bfloat16, jnp.float32


def round_bf16(value):
    return value.astype(bf16).astype(f32)


def pieces(value, count):
    parts = []
    for _ in range(count):
        part = round_bf16(value)
        parts.append(part)
        value = value - part
    return parts


def padded(rows, height):
    filled = sum(row.shape[0] for row in rows)
    width = rows[0].shape[1]
    if filled < height:
        rows = rows + [jnp.zeros((height - filled, width), f32)]
    return jnp.concatenate(rows, axis=0)


def row_sum(value):
    return value[0:1] + value[1:2] + value[2:3]


def grid_parts(place):
    coarse = jnp.floor(place * GRID + 0.5) * (1.0 / GRID)
    return [coarse] + pieces(place - coarse, 2)


def distance_features(place):
    coarse, fine, rest = grid_parts(place)
    minor = place - coarse
    ones = jnp.ones_like(place)
    coarse_norm = jnp.concatenate(pieces(-row_sum(coarse * coarse), 3), axis=0)
    minor_norm = jnp.concatenate(
        pieces(-row_sum(minor * (2.0 * coarse + minor)), 3), axis=0
    )
    key_rows = [coarse, ones, coarse_norm, coarse, coarse, fine, rest, ones, minor_norm]
    key_rows += [fine, fine, rest, rest]
    query_rows = [coarse, coarse_norm, ones, fine, rest, coarse, coarse, minor_norm, ones]
    query_rows += [fine, rest, fine, rest]
    doubled = (0, 3, 4, 5, 6, 9, 10, 11, 12)
    query_rows = [row * 2.0 if i in doubled else row for i, row in enumerate(query_rows)]
    return padded(key_rows, FEATURES), padded(query_rows, FEATURES)


def along_key_features(place, score):
    coarse, fine, rest = grid_parts(place)
    first, second, third = pieces(score, 3)
    ones = jnp.ones_like(place)
    dot = jnp.concatenate(pieces(row_sum(place * score), 3), axis=0)
    rows = [ones, dot, -first, -second, -third, -first, -second, -first]
    rows += [coarse, coarse, coarse, fine, fine, rest]
    return padded(rows, FEATURES)


def along_query_features(place, score):
    coarse, fine, rest = grid_parts(place)
    first, second, third = pieces(score, 3)
    ones = jnp.ones_like(place)
    dot = jnp.concatenate(pieces(row_sum(place * score), 3), axis=0)
    rows = [dot, ones, coarse, coarse, coarse, fine, fine, rest]
    rows += [-first, -second, -third, -first, -second, -first]
    return padded(rows, FEATURES)


def weighted_rows(weight, value):
    whole = jnp.concatenate([weight, weight * value], axis=0)
    return padded(pieces(whole, 3), 16).astype(bf16)


def product(left, right):
    return jnp.dot(left, right, preferred_element_type=f32)


def split_product(left, matrix):
    upper = matrix.astype(bf16)
    lower = (matrix - upper.astype(f32)).astype(bf16)
    return product(left, upper) + product(left, lower)


def joined(total):
    return total[0:4] + total[4:8] + total[8:12]


def sweep_kernel(blocks, scores_out, drift_out, speed_out, place_ref, weight_ref,
                 key_ref, query_ref, own_ref, moment_ref, score_ref, along_ref, flux_ref):
    count, _, width = blocks.shape
    total_slots = count * width
    chunks = total_slots // CHUNK

    def columns(block):
        return pl.ds(pl.multiple_of(block * width, width), width)

    def build(block, carry):
        place = blocks[block, 0:3] * SCALE
        weight = blocks[block, 3:4]
        key, query = distance_features(place)
        place_ref[:, columns(block)] = place
        weight_ref[:, columns(block)] = weight
        key_ref[columns(block), :] = key.T.astype(bf16)
        query_ref[:, columns(block)] = query.astype(bf16)
        moment_ref[:, columns(block)] = weighted_rows(weight, place)
        return carry

    lax.fori_loop(0, count, build, 0, unroll=count <= 4)
    own_ref[...] = -query_ref[:, 0:width]

    def density(block, carry):
        query = query_ref[:, columns(block)]

        def add(chunk, total):
            keys = pl.ds(pl.multiple_of(chunk * CHUNK, CHUNK), CHUNK)
            blob = jnp.exp2(product(key_ref[keys, :], query))
            return total + split_product(moment_ref[:, keys], blob)

        total = lax.fori_loop(0, chunks, add, jnp.zeros((16, width), f32), unroll=8)
        sums = joined(total)
        place = place_ref[:, columns(block)]
        weight = weight_ref[:, columns(block)]
        live = weight > 0.0
        clamped = jnp.where(live, sums[0:1], 1.0)
        pull = place * sums[0:1] - sums[1:4]
        score = jnp.where(live, -pull / (SCALE * EPS * EPS * clamped), 0.0)
        score_ref[:, columns(block)] = score
        along_ref[columns(block), :] = along_key_features(place, score).T.astype(bf16)
        flux_ref[:, columns(block)] = weighted_rows(weight, score)
        return carry

    lax.fori_loop(0, count, density, 0)

    place = place_ref[:, 0:width]
    score = score_ref[:, 0:width]
    own = own_ref[...]
    own_along = along_query_features(place, score).astype(bf16)

    def add_drift(chunk, totals):
        keys = pl.ds(pl.multiple_of(chunk * CHUNK, CHUNK), CHUNK)
        square = jnp.maximum(product(key_ref[keys, :], own), TINY)
        along = product(along_ref[keys, :], own_along)
        distance = square * lax.rsqrt(square)
        return (
            totals[0] + split_product(flux_ref[:, keys], square * distance),
            totals[1] + split_product(moment_ref[:, keys], along * distance),
        )

    zero = jnp.zeros((16, width), f32)
    cubes, linear = lax.fori_loop(0, chunks, add_drift, (zero, zero), unroll=8)
    cubes, linear = joined(cubes), joined(linear)
    drift = score * cubes[0:1] - cubes[1:4] - place * linear[0:1] + linear[1:4]
    live = weight_ref[:, 0:width] > 0.0
    drift = jnp.where(live, drift * (-1.0 / (SCALE * SCALE * SCALE * total_slots)), 0.0)
    largest = jnp.max(row_sum(drift * drift), axis=1, keepdims=True)
    speed_out[...] = jnp.broadcast_to(jnp.sqrt(largest), speed_out.shape)
    for part in range(width // 128):
        lanes = slice(part * 128, part * 128 + 128)
        for axis in range(3):
            scores_out[axis, part : part + 1, :] = score[axis : axis + 1, lanes]
            drift_out[axis, part : part + 1, :] = drift[axis : axis + 1, lanes]


def sweep(blocks):
    count, _, width = blocks.shape
    slots = count * width
    parts = jax.ShapeDtypeStruct((3, width // 128, 128), f32)
    whole = pl.BlockSpec(memory_space=pltpu.VMEM)
    return pl.pallas_call(
        sweep_kernel,
        out_shape=(parts, parts, jax.ShapeDtypeStruct((8, 128), f32)),
        in_specs=[whole],
        out_specs=(whole, whole, whole),
        scratch_shapes=[
            pltpu.VMEM((3, slots), f32),
            pltpu.VMEM((1, slots), f32),
            pltpu.VMEM((slots, FEATURES), bf16),
            pltpu.VMEM((FEATURES, slots), bf16),
            pltpu.VMEM((FEATURES, width), bf16),
            pltpu.VMEM((16, slots), bf16),
            pltpu.VMEM((3, slots), f32),
            pltpu.VMEM((slots, FEATURES), bf16),
            pltpu.VMEM((16, slots), bf16),
        ],
        compiler_params=pltpu.CompilerParams(vmem_limit_bytes=48 * 1024 * 1024),
        name="sweep",
    )(blocks)


def swapped(value, axis, step):
    pairs = [(i, i ^ step) for i in range(lax.axis_size(axis))]
    return lax.ppermute(value, axis, pairs)


def steps(axis):
    step = 1
    while step < lax.axis_size(axis):
        yield step
        step *= 2


def local(velocities, weights, counts):
    velocity = velocities[0]
    width = velocity.shape[1]
    slot = lax.axis_index("sharers") * width + jnp.arange(width, dtype=jnp.int32)
    live_weight = jnp.where(slot < counts[0], weights[0], 0.0)
    blocks = jnp.concatenate([velocity, live_weight[None]], axis=0)[None]
    for step in steps("sharers"):
        blocks = jnp.concatenate([blocks, swapped(blocks, "sharers", step)], axis=0)
    scores, drift, largest = sweep(blocks)
    for axis in ("cells", "sharers"):
        for step in steps(axis):
            largest = jnp.maximum(largest, swapped(largest, axis, step))
    time_step = 0.5 / (largest[0:1, :] + 1e-06)
    moved = velocity.reshape(drift.shape) + time_step[None] * drift
    return moved.reshape(velocities.shape), scores.reshape(velocities.shape)


def solution(mesh):
    in_specs = (
        P(("groups", "cells"), None, "sharers"),
        P(("groups", "cells"), "sharers"),
        P(("groups", "cells")),
    )
    out_specs = (P(("groups", "cells"), None, "sharers"), P(("groups", "cells"), None, "sharers"))
    return jax.shard_map(local, mesh=mesh, in_specs=in_specs, out_specs=out_specs, check_vma=False)
```

time: 55.3 us -> 38.4 us (0.69)
  other arithmetic: 16.9 us -> 0.66 us
  Pallas kernels: 0 us -> 13.1 us
  waiting for transfers between devices: 17 us -> 9.57 us
  local copies, waits for them, and re-layouts: 5.42 us -> 0.7 us
  between operations: 2.06 us -> 1.32 us
    all_to_all x3 -> x0, waiting for transfers between devices: 17 us -> none  [exchange(): return lax.all_to_all(copies, axis, 0, 0, tiled=True)]
    reduce_sum x21 -> x0, other arithmetic: 14.7 us -> none  [the longest x4 5.98 us: drift_block(): return jnp.sum(contrib, axis=2)]
    pallas_call x0 -> x1, Pallas kernels: none -> 13.1 us  [sweep(): pl.pallas_call(sweep_kernel, out_shape=(parts, parts, jax.ShapeDtypeStruc...]
    all_to_all x3 -> x0, starting transfers between devices: 13.1 us -> none  [exchange(): return lax.all_to_all(copies, axis, 0, 0, tiled=True)]
    ppermute x0 -> x6, starting transfers between devices: none -> 12.8 us  [swapped(): return lax.ppermute(value, axis, pairs)]
    ppermute x0 -> x6, waiting for transfers between devices: none -> 9.57 us  [swapped(): return lax.ppermute(value, axis, pairs)]
    broadcast_in_dim x5 -> x0, local copies, waits for them, and re-layouts: 3.65 us -> none  [the longest x4 3.06 us: exchange(): copies = jnp.broadcast_to(value[None], (lax.axis_size(axis),) + value.shape)]
    reduce_max x2 -> x0, other arithmetic: 1.23 us -> none  [the longest x1 0.62 us: local(): jnp.max(exchange(jnp.max(speeds).reshape(1), ('cells', 'sharers')))]
  transfers between devices with their start and end apart: 3 -> 6, of which waited for: 3 -> 6; matrix products, arithmetic and copies ran while one was open for 1% -> 0% of each run, Pallas kernels for 0% -> 0%
where the time goes in v3:
time: 38.4 us; the launch traced here: 38.1 us
  Pallas kernels  13.1 us (34%)
  starting transfers between devices  12.8 us (33%)
  waiting for transfers between devices  9.57 us (25%)
  between operations  1.32 us (3%)
  local copies, waits for them, and re-layouts  0.7 us (2%)
  other arithmetic  0.66 us (2%)
    pallas_call x1, Pallas kernels, sweep(): pl.pallas_call(sweep_kernel, out_shape=(parts, parts, jax.ShapeDtypeStruc...  13.1 us
    ppermute x6, starting transfers between devices, swapped(): return lax.ppermute(value, axis, pairs)  12.8 us
    ppermute x6, waiting for transfers between devices, swapped(): return lax.ppermute(value, axis, pairs)  9.57 us
  transfers between devices with their start and end apart: 6, of which 6 were waited for; matrix products, arithmetic and copies ran while one was open for 0% of the time, Pallas kernels for 0%

profile of v3, /device:TPU:0, one launch (start us, length us, event | category | flops | bytes accessed | tf_op | source)
XLA Modules:
  0.0 38.1 jit_solution(5856221471483816178)
XLA Ops:
  0.6 0.0 copy-start
  1.3 0.0 copy-done
  1.3 0.0 copy-start.1
  1.3 0.7 %copy-done.1 = f32[1,512]{1,0:T(1,128)S(1)} copy-done((f32[1,512]{1,0:T(1,128)S(1)}, f32[1,512]{1,0:T(1,128)}, u32[]{:S(2)}) %copy-start.1) | copy-done | bytes 2072
  2.0 3.1 %collective-permute-start = (f32[1,4,512]{2,1,0:T(4,128)S(1)}, f32[1,4,512]{2,1,0:T(4,128)S(1)}, u32[]{:S(2)}, u32[]{:S(2)}) collective-permute-start(f32[1,4,512]{2,1,0:T(4,128)S(1)} %maximum_bitcast_fusion), channel_id=1, source_target_pairs={{0,1},{1,0},{2,3},{3,2},{4,5},{5,4},{6,7},{7,6},{8,9},{9,8},{10,11... | collective-permute-start | bytes 24584 | tf_op jit(solution)/shard_map/ppermute | solution.py:210
  5.1 1.6 %collective-permute-done = f32[1,4,512]{2,1,0:T(4,128)S(1)} collective-permute-done((f32[1,4,512]{2,1,0:T(4,128)S(1)}, f32[1,4,512]{2,1,0:T(4,128)S(1)}, u32[]{:S(2)}, u32[]{:S(2)}) %collective-permute-start) | collective-permute-done | bytes 8224 | tf_op jit(solution)/shard_map/ppermute | solution.py:210
  6.8 3.0 %collective-permute-start.1 = (f32[2,4,512]{2,1,0:T(4,128)S(1)}, f32[2,4,512]{2,1,0:T(4,128)S(1)}, u32[]{:S(2)}, u32[]{:S(2)}) collective-permute-start(f32[2,4,512]{2,1,0:T(4,128)S(1)} %pad_maximum_fusion.1), channel_id=1, source_target_pairs={{0,2},{1,3},{2,0},{3,1},{4,6},{5,7},{6,4},{7,5},{8,10},{9,11},{10,... | collective-permute-start | bytes 49160 | tf_op jit(solution)/shard_map/ppermute | solution.py:210
  9.8 1.7 %collective-permute-done.1 = f32[2,4,512]{2,1,0:T(4,128)S(1)} collective-permute-done((f32[2,4,512]{2,1,0:T(4,128)S(1)}, f32[2,4,512]{2,1,0:T(4,128)S(1)}, u32[]{:S(2)}, u32[]{:S(2)}) %collective-permute-start.1) | collective-permute-done | bytes 16416 | tf_op jit(solution)/shard_map/ppermute | solution.py:210
  11.5 13.1 %sweep.1 = (f32[3,4,128]{2,1,0:T(4,128)}, f32[3,4,128]{2,1,0:T(4,128)S(1)}, f32[8,128]{1,0:T(8,128)S(1)}) custom-call(f32[4,4,512]{2,1,0:T(4,128)S(1)} %pad_maximum_fusion.blocks), custom_call_target="tpu_custom_call" | custom-call | tf_op jit(solution)/shard_map/sweep/pallas_call | solution.py:187
  24.6 0.0 collective-permute-start.2
  24.6 1.2 %collective-permute-done.2 = f32[8,128]{1,0:T(8,128)S(1)} collective-permute-done((f32[8,128]{1,0:T(8,128)S(1)}, f32[8,128]{1,0:T(8,128)S(1)}, u32[]{:S(2)}, u32[]{:S(2)}) %collective-permute-start.2) | collective-permute-done | bytes 4128 | tf_op jit(solution)/shard_map/ppermute | solution.py:210
  25.8 1.8 %collective-permute-start.3 = (f32[8,128]{1,0:T(8,128)S(1)}, f32[8,128]{1,0:T(8,128)S(1)}, u32[]{:S(2)}, u32[]{:S(2)}) collective-permute-start(f32[8,128]{1,0:T(8,128)S(1)} %max.12), channel_id=1, source_target_pairs={{0,8},{4,12},{8,0},{12,4},{1,9},{5,13},{9,1},{13,5},{2,10},{6,14},... | collective-permute-start | bytes 12296 | tf_op jit(solution)/shard_map/ppermute | solution.py:210
  27.6 1.8 %collective-permute-done.3 = f32[8,128]{1,0:T(8,128)S(1)} collective-permute-done((f32[8,128]{1,0:T(8,128)S(1)}, f32[8,128]{1,0:T(8,128)S(1)}, u32[]{:S(2)}, u32[]{:S(2)}) %collective-permute-start.3) | collective-permute-done | bytes 4128 | tf_op jit(solution)/shard_map/ppermute | solution.py:210
  29.4 1.9 %collective-permute-start.4 = (f32[8,128]{1,0:T(8,128)S(1)}, f32[8,128]{1,0:T(8,128)S(1)}, u32[]{:S(2)}, u32[]{:S(2)}) collective-permute-start(f32[8,128]{1,0:T(8,128)S(1)} %max.13), channel_id=1, source_target_pairs={{0,1},{1,0},{2,3},{3,2},{4,5},{5,4},{6,7},{7,6},{8,9},{9,8},{10,11... | collective-permute-start | bytes 12296 | tf_op jit(solution)/shard_map/ppermute | solution.py:210
  31.3 1.7 %collective-permute-done.4 = f32[8,128]{1,0:T(8,128)S(1)} collective-permute-done((f32[8,128]{1,0:T(8,128)S(1)}, f32[8,128]{1,0:T(8,128)S(1)}, u32[]{:S(2)}, u32[]{:S(2)}) %collective-permute-start.4) | collective-permute-done | bytes 4128 | tf_op jit(solution)/shard_map/ppermute | solution.py:210
  33.0 2.9 %collective-permute-start.5 = (f32[8,128]{1,0:T(8,128)S(1)}, f32[8,128]{1,0:T(8,128)S(1)}, u32[]{:S(2)}, u32[]{:S(2)}) collective-permute-start(f32[8,128]{1,0:T(8,128)S(1)} %max.14), channel_id=1, source_target_pairs={{0,2},{1,3},{2,0},{3,1},{4,6},{5,7},{6,4},{7,5},{8,10},{9,11},{10,... | collective-permute-start | bytes 12296 | tf_op jit(solution)/shard_map/ppermute | solution.py:210
  35.9 1.6 %collective-permute-done.5 = f32[8,128]{1,0:T(8,128)S(1)} collective-permute-done((f32[8,128]{1,0:T(8,128)S(1)}, f32[8,128]{1,0:T(8,128)S(1)}, u32[]{:S(2)}, u32[]{:S(2)}) %collective-permute-start.5) | collective-permute-done | bytes 4128 | tf_op jit(solution)/shard_map/ppermute | solution.py:210
  37.5 0.6 %multiply_add_fusion = f32[3,4,128]{2,1,0:T(4,128)} fusion(f32[3,4,128]{2,1,0:T(4,128)S(1)} %bitcast.13, f32[3,4,128]{2,1,0:T(4,128)S(1)} %get-tuple-element.6, f32[128]{0:T(128)S(1)} %divide_bitcast_fusion), kind=kLoop, calls=%fused_computation.5 | loop fusion | flops 3072 | bytes 18944 | tf_op jit(solution)/shard_map/add | solution.py:233
  (10 shorter events, 0.1 us)
Async XLA Ops:
  0.6 0.7 %copy-start = (f32[1,3,512]{2,0,1:T(1,128)S(1)}, f32[1,3,512]{2,0,1:T(1,128)}, u32[]{:S(2)}) copy-start(f32[1,3,512]{2,0,1:T(1,128)} %param.3) | copy-start | bytes 18436
  1.3 0.7 %copy-start.1 = (f32[1,512]{1,0:T(1,128)S(1)}, f32[1,512]{1,0:T(1,128)}, u32[]{:S(2)}) copy-start(f32[1,512]{1,0:T(1,128)} %param.4) | copy-start | bytes 6148
  2.0 4.7 %collective-permute-start = (f32[1,4,512]{2,1,0:T(4,128)S(1)}, f32[1,4,512]{2,1,0:T(4,128)S(1)}, u32[]{:S(2)}, u32[]{:S(2)}) collective-permute-start(f32[1,4,512]{2,1,0:T(4,128)S(1)} %maximum_bitcast_fusion), channel_id=1, source_target_pairs={{0,1},{1,0},{2,3},{3,2},{4,5},{5,4},{6,7},{7,6},{8,9},{9,8},{10,11... | collective-permute-start | bytes 24584 | tf_op jit(solution)/shard_map/ppermute | solution.py:210
  6.8 4.7 %collective-permute-start.1 = (f32[2,4,512]{2,1,0:T(4,128)S(1)}, f32[2,4,512]{2,1,0:T(4,128)S(1)}, u32[]{:S(2)}, u32[]{:S(2)}) collective-permute-start(f32[2,4,512]{2,1,0:T(4,128)S(1)} %pad_maximum_fusion.1), channel_id=1, source_target_pairs={{0,2},{1,3},{2,0},{3,1},{4,6},{5,7},{6,4},{7,5},{8,10},{9,11},{10,... | collective-permute-start | bytes 49160 | tf_op jit(solution)/shard_map/ppermute | solution.py:210
  24.6 1.2 %collective-permute-start.2 = (f32[8,128]{1,0:T(8,128)S(1)}, f32[8,128]{1,0:T(8,128)S(1)}, u32[]{:S(2)}, u32[]{:S(2)}) collective-permute-start(f32[8,128]{1,0:T(8,128)S(1)} %get-tuple-element.5), channel_id=1, source_target_pairs={{0,4},{4,0},{8,12},{12,8},{1,5},{5,1},{9,13},{13,9},{2,6},{6,2},{1... | collective-permute-start | bytes 12296 | tf_op jit(solution)/shard_map/ppermute | solution.py:210
  25.8 3.6 %collective-permute-start.3 = (f32[8,128]{1,0:T(8,128)S(1)}, f32[8,128]{1,0:T(8,128)S(1)}, u32[]{:S(2)}, u32[]{:S(2)}) collective-permute-start(f32[8,128]{1,0:T(8,128)S(1)} %max.12), channel_id=1, source_target_pairs={{0,8},{4,12},{8,0},{12,4},{1,9},{5,13},{9,1},{13,5},{2,10},{6,14},... | collective-permute-start | bytes 12296 | tf_op jit(solution)/shard_map/ppermute | solution.py:210
  29.4 3.6 %collective-permute-start.4 = (f32[8,128]{1,0:T(8,128)S(1)}, f32[8,128]{1,0:T(8,128)S(1)}, u32[]{:S(2)}, u32[]{:S(2)}) collective-permute-start(f32[8,128]{1,0:T(8,128)S(1)} %max.13), channel_id=1, source_target_pairs={{0,1},{1,0},{2,3},{3,2},{4,5},{5,4},{6,7},{7,6},{8,9},{9,8},{10,11... | collective-permute-start | bytes 12296 | tf_op jit(solution)/shard_map/ppermute | solution.py:210
  33.0 4.5 %collective-permute-start.5 = (f32[8,128]{1,0:T(8,128)S(1)}, f32[8,128]{1,0:T(8,128)S(1)}, u32[]{:S(2)}, u32[]{:S(2)}) collective-permute-start(f32[8,128]{1,0:T(8,128)S(1)} %max.14), channel_id=1, source_target_pairs={{0,2},{1,3},{2,0},{3,1},{4,6},{5,7},{6,4},{7,5},{8,10},{9,11},{10,... | collective-permute-start | bytes 12296 | tf_op jit(solution)/shard_map/ppermute | solution.py:210

commit v4 on v3

--- a/solution.py
+++ b/solution.py
@@ -1,3 +1,4 @@
+import functools
 import functools
 import math
 
@@ -13,6 +14,7 @@
 GRID = 4.0
 TINY = 1e-30
 CHUNK = 256
+TILE = 256
 FEATURES = 48
 bf16, f32 = jnp.bfloat16, jnp.float32
 
@@ -104,7 +106,8 @@
 
 
 def sweep_kernel(blocks, scores_out, drift_out, speed_out, place_ref, weight_ref,
-                 key_ref, query_ref, own_ref, moment_ref, score_ref, along_ref, flux_ref):
+                 key_ref, query_ref, own_ref, moment_ref, score_ref, along_ref, flux_ref,
+                 own_along_ref, sums_ref):
     count, _, width = blocks.shape
     total_slots = count * width
     chunks = total_slots // CHUNK
@@ -126,35 +129,35 @@
     lax.fori_loop(0, count, build, 0, unroll=count <= 4)
     own_ref[...] = -query_ref[:, 0:width]
 
-    def density(block, carry):
-        query = query_ref[:, columns(block)]
+    def density(tile, carry):
+        here = pl.ds(pl.multiple_of(tile * TILE, TILE), TILE)
+        query = query_ref[:, here]
 
         def add(chunk, total):
             keys = pl.ds(pl.multiple_of(chunk * CHUNK, CHUNK), CHUNK)
             blob = jnp.exp2(product(key_ref[keys, :], query))
             return total + split_product(moment_ref[:, keys], blob)
 
-        total = lax.fori_loop(0, chunks, add, jnp.zeros((16, width), f32), unroll=8)
+        total = lax.fori_loop(0, chunks, add, jnp.zeros((16, TILE), f32), unroll=8)
         sums = joined(total)
-        place = place_ref[:, columns(block)]
-        weight = weight_ref[:, columns(block)]
+        place = place_ref[:, here]
+        weight = weight_ref[:, here]
         live = weight > 0.0
         clamped = jnp.where(live, sums[0:1], 1.0)
         pull = place * sums[0:1] - sums[1:4]
         score = jnp.where(live, -pull / (SCALE * EPS * EPS * clamped), 0.0)
-        score_ref[:, columns(block)] = score
-        along_ref[columns(block), :] = along_key_features(place, score).T.astype(bf16)
-        flux_ref[:, columns(block)] = weighted_rows(weight, score)
+        score_ref[:, here] = score
+        along_ref[here, :] = along_key_features(place, score).T.astype(bf16)
+        flux_ref[:, here] = weighted_rows(weight, score)
         return carry
 
-    lax.fori_loop(0, count, density, 0)
+    lax.fori_loop(0, total_slots // TILE, density, 0)
 
     place = place_ref[:, 0:width]
     score = score_ref[:, 0:width]
-    own = own_ref[...]
-    own_along = along_query_features(place, score).astype(bf16)
-
-    def add_drift(chunk, totals):
+    own_along_ref[...] = along_query_features(place, score).astype(bf16)
+
+    def add_drift(own, own_along, chunk, totals):
         keys = pl.ds(pl.multiple_of(chunk * CHUNK, CHUNK), CHUNK)
         square = jnp.maximum(product(key_ref[keys, :], own), TINY)
         along = product(along_ref[keys, :], own_along)
@@ -164,9 +167,17 @@
             totals[1] + split_product(moment_ref[:, keys], along * distance),
         )
 
-    zero = jnp.zeros((16, width), f32)
-    cubes, linear = lax.fori_loop(0, chunks, add_drift, (zero, zero), unroll=8)
-    cubes, linear = joined(cubes), joined(linear)
+    def drift_tile(tile, carry):
+        here = pl.ds(pl.multiple_of(tile * TILE, TILE), TILE)
+        step = functools.partial(add_drift, own_ref[:, here], own_along_ref[:, here])
+        zero = jnp.zeros((16, TILE), f32)
+        cubes, linear = lax.fori_loop(0, chunks, step, (zero, zero), unroll=8)
+        sums_ref[0:4, here] = joined(cubes)
+        sums_ref[4:8, here] = joined(linear)
+        return carry
+
+    lax.fori_loop(0, width // TILE, drift_tile, 0)
+    cubes, linear = sums_ref[0:4, :], sums_ref[4:8, :]
     drift = score * cubes[0:1] - cubes[1:4] - place * linear[0:1] + linear[1:4]
     live = weight_ref[:, 0:width] > 0.0
     drift = jnp.where(live, drift * (-1.0 / (SCALE * SCALE * SCALE * total_slots)), 0.0)
@@ -199,38 +210,85 @@
             pltpu.VMEM((3, slots), f32),
             pltpu.VMEM((slots, FEATURES), bf16),
             pltpu.VMEM((16, slots), bf16),
+            pltpu.VMEM((FEATURES, width), bf16),
+            pltpu.VMEM((8, width), f32),
         ],
         compiler_params=pltpu.CompilerParams(vmem_limit_bytes=48 * 1024 * 1024),
         name="sweep",
     )(blocks)
 
 
+def pack_kernel(velocity, weight, place, filled, packed):
+    parts = velocity.shape[1]
+    lane = lax.broadcasted_iota(jnp.int32, (1, 128), 1)
+    first = place[0] * (parts * 128)
+    for part in range(parts):
+        lanes = slice(part * 128, part * 128 + 128)
+        live = first + part * 128 + lane < filled[0]
+        for axis in range(3):
+            packed[0, axis : axis + 1, lanes] = velocity[axis, part : part + 1, :]
+        packed[0, 3:4, lanes] = jnp.where(live, weight[part : part + 1, :], 0.0)
+
+
+def pack(velocities, weights, counts):
+    width = weights.shape[1]
+    place = lax.axis_index("sharers").astype(jnp.int32).reshape(1)
+    vector = pl.BlockSpec(memory_space=pltpu.VMEM)
+    scalar = pl.BlockSpec(memory_space=pltpu.SMEM)
+    return pl.pallas_call(
+        pack_kernel,
+        out_shape=jax.ShapeDtypeStruct((1, 4, width), f32),
+        in_specs=[vector, vector, scalar, scalar],
+        out_specs=vector,
+        name="pack",
+    )(velocities.reshape(3, width // 128, 128), weights.reshape(width // 128, 128), place, counts)
+
+
 def swapped(value, axis, step):
     pairs = [(i, i ^ step) for i in range(lax.axis_size(axis))]
     return lax.ppermute(value, axis, pairs)
 
 
-def steps(axis):
-    step = 1
-    while step < lax.axis_size(axis):
-        yield step
-        step *= 2
+def bits(size):
+    return [1 << bit for bit in range(size.bit_length() - 1)]
+
+
+def gathered(block):
+    size = lax.axis_size("sharers")
+    if size == 4:
+        third, first, second = (swapped(block, "sharers", step) for step in (3, 1, 2))
+        return jnp.concatenate([block, first, second, third], axis=0)
+    for step in bits(size):
+        block = jnp.concatenate([block, swapped(block, "sharers", step)], axis=0)
+    return block
+
+
+def group_maximum(value):
+    cells, sharers = lax.axis_size("cells"), lax.axis_size("sharers")
+    axes = ("cells", "sharers")
+    odd = [i for i in range(cells * sharers) if (i // sharers) % 2]
+
+    def among_odd(value, step):
+        return lax.ppermute(value, axes, [(i, i ^ step) for i in odd])
+
+    value = jnp.maximum(value, swapped(value, "cells", 1))
+    for step in bits(cells)[1:]:
+        value = jnp.maximum(value, among_odd(value, step * sharers))
+    if sharers == 4:
+        others = [among_odd(value, step) for step in (3, 1, 2)]
+        for other in others:
+            value = jnp.maximum(value, other)
+    else:
+        for step in bits(sharers):
+            value = jnp.maximum(value, among_odd(value, step))
+    back = lax.ppermute(value, "cells", [(i, i ^ 1) for i in range(1, cells, 2)])
+    return jnp.maximum(value, back)
 
 
 def local(velocities, weights, counts):
-    velocity = velocities[0]
-    width = velocity.shape[1]
-    slot = lax.axis_index("sharers") * width + jnp.arange(width, dtype=jnp.int32)
-    live_weight = jnp.where(slot < counts[0], weights[0], 0.0)
-    blocks = jnp.concatenate([velocity, live_weight[None]], axis=0)[None]
-    for step in steps("sharers"):
-        blocks = jnp.concatenate([blocks, swapped(blocks, "sharers", step)], axis=0)
-    scores, drift, largest = sweep(blocks)
-    for axis in ("cells", "sharers"):
-        for step in steps(axis):
-            largest = jnp.maximum(largest, swapped(largest, axis, step))
-    time_step = 0.5 / (largest[0:1, :] + 1e-06)
-    moved = velocity.reshape(drift.shape) + time_step[None] * drift
+    scores, drift, largest = sweep(gathered(pack(velocities, weights, counts)))
+    time_step = 0.5 / (group_maximum(largest)[0:1, :] + 1e-06)
+    moved = velocities.reshape(drift.shape) + time_step[None] * drift
     return moved.reshape(velocities.shape), scores.reshape(velocities.shape)
 
 

time: 38.4 us -> 46.8 us (1.22)
  waiting for transfers between devices: 9.57 us -> 19.6 us
  starting transfers between devices: 12.8 us -> 9.54 us
  Pallas kernels: 13.1 us -> 14.6 us
  local copies, waits for them, and re-layouts: 0.7 us -> 0.01 us
  other arithmetic: 0.66 us -> 1.34 us
    ppermute x0 -> x5, waiting for transfers between devices: none -> 14.3 us  [the longest x1 14.2 us: group_maximum(): lax.ppermute(value, 'cells', [(i, i ^ 1) for i in range(1, cells, 2)])]
    ppermute x6 -> x4, starting transfers between devices: 12.8 us -> 5.62 us  [swapped(): return lax.ppermute(value, axis, pairs)]
    ppermute x6 -> x4, waiting for transfers between devices: 9.57 us -> 5.36 us  [swapped(): return lax.ppermute(value, axis, pairs)]
    ppermute x0 -> x5, starting transfers between devices: none -> 3.93 us  [the longest x4 2.63 us: among_odd(): return lax.ppermute(value, axes, [(i, i ^ step) for i in odd])]
    pallas_call x0 -> x1, Pallas kernels: none -> 1.3 us  [pack(): pl.pallas_call(pack_kernel, out_shape=jax.ShapeDtypeStruct((1, 4, width),...]
    unnamed x5 -> x2, local copies, waits for them, and re-layouts: 0.7 us -> 0.01 us
    concatenate x2 -> x1, other arithmetic: 0.01 us -> 0.71 us  [gathered(): return jnp.concatenate([block, first, second, third], axis=0)]
  transfers between devices with their start and end apart: 6 -> 9, of which waited for: 6 -> 4; matrix products, arithmetic and copies ran while one was open for 0% -> 0% of each run, Pallas kernels for 0% -> 0%
where the time goes in v4:
time: 46.8 us; the launch traced here: 46.5 us
  waiting for transfers between devices  19.6 us (42%)
  Pallas kernels  14.6 us (31%)
  starting transfers between devices  9.54 us (20%)
  between operations  1.38 us (3%)
  other arithmetic  1.34 us (3%)
    ppermute x1, waiting for transfers between devices, group_maximum(): lax.ppermute(value, 'cells', [(i, i ^ 1) for i in range(1, cells, 2)])  14.2 us
    pallas_call x1, Pallas kernels, sweep(): pl.pallas_call(sweep_kernel, out_shape=(parts, parts, jax.ShapeDtypeStruc...  13.3 us
    ppermute x4, starting transfers between devices, swapped(): return lax.ppermute(value, axis, pairs)  5.62 us
    ppermute x4, waiting for transfers between devices, swapped(): return lax.ppermute(value, axis, pairs)  5.36 us
    ppermute x4, starting transfers between devices, among_odd(): return lax.ppermute(value, axes, [(i, i ^ step) for i in odd])  2.63 us
    pallas_call x1, Pallas kernels, pack(): pl.pallas_call(pack_kernel, out_shape=jax.ShapeDtypeStruct((1, 4, width),...  1.3 us
    ppermute x1, starting transfers between devices, group_maximum(): lax.ppermute(value, 'cells', [(i, i ^ 1) for i in range(1, cells, 2)])  1.29 us
  transfers between devices with their start and end apart: 9, of which 4 were waited for; matrix products, arithmetic and copies ran while one was open for 0% of the time, Pallas kernels for 0%

profile of v4, /device:TPU:0, one launch (start us, length us, event | category | flops | bytes accessed | tf_op | source)
XLA Modules:
  0.0 46.5 jit_solution(16957396552610318045)
XLA Ops:
  1.3 1.3 %pack.1 = f32[1,4,512]{2,1,0:T(4,128)} custom-call(f32[3,4,128]{2,1,0:T(4,128)} %bitcast.7, f32[4,128]{1,0:T(4,128)} %bitcast.10, s32[1]{0:T(128)} %bitcast.2.place, s32[1]{0:T(128)S(6)} %copy.9.filled), custom_call_target="tpu_custom_call" | custom-call | tf_op jit(solution)/shard_map/pack/pallas_call | solution.py:238
  2.6 5.0 %collective-permute-start.2 = (f32[1,4,512]{2,1,0:T(4,128)}, f32[1,4,512]{2,1,0:T(4,128)S(1)}, u32[]{:S(2)}, u32[]{:S(2)}) collective-permute-start(f32[1,4,512]{2,1,0:T(4,128)} %pack.1), channel_id=1, source_target_pairs={{0,3},{1,2},{2,1},{3,0},{4,7},{5,6},{6,5},{7,4},{8,11},{9,10},{10,... | collective-permute-start | bytes 24584 | tf_op jit(solution)/shard_map/ppermute | solution.py:249
  7.6 0.0 collective-permute-start.1
  7.6 0.6 %collective-permute-start = (f32[1,4,512]{2,1,0:T(4,128)}, f32[1,4,512]{2,1,0:T(4,128)S(1)}, u32[]{:S(2)}, u32[]{:S(2)}) collective-permute-start(f32[1,4,512]{2,1,0:T(4,128)} %pack.1), channel_id=1, source_target_pairs={{0,1},{1,0},{2,3},{3,2},{4,5},{5,4},{6,7},{7,6},{8,9},{9,8},{10,11... | collective-permute-start | bytes 24584 | tf_op jit(solution)/shard_map/ppermute | solution.py:249
  8.2 1.3 %collective-permute-done.2 = f32[1,4,512]{2,1,0:T(4,128)S(1)} collective-permute-done((f32[1,4,512]{2,1,0:T(4,128)}, f32[1,4,512]{2,1,0:T(4,128)S(1)}, u32[]{:S(2)}, u32[]{:S(2)}) %collective-permute-start.2) | collective-permute-done | bytes 8224 | tf_op jit(solution)/shard_map/ppermute | solution.py:249
  9.5 2.9 %collective-permute-done.1 = f32[1,4,512]{2,1,0:T(4,128)S(1)} collective-permute-done((f32[1,4,512]{2,1,0:T(4,128)}, f32[1,4,512]{2,1,0:T(4,128)S(1)}, u32[]{:S(2)}, u32[]{:S(2)}) %collective-permute-start.1) | collective-permute-done | bytes 8224 | tf_op jit(solution)/shard_map/ppermute | solution.py:249
  12.4 0.0 collective-permute-done
  12.4 0.7 %pad_maximum_fusion.blocks = f32[4,4,512]{2,1,0:T(4,128)S(1)} fusion(f32[1,4,512]{2,1,0:T(4,128)S(1)} %collective-permute-done.2, f32[1,4,512]{2,1,0:T(4,128)S(1)} %collective-permute-done.1, f32[1,4,512]{2,1,0:T(4,128)S(1)} %collective-permute-done, f32[1,4,512]{2,1,0:T(4,128)} %pack.1), kind=kLoop, calls=%fused_computation | loop fusion | flops 24576 | bytes 65536 | tf_op jit(solution)/shard_map/concatenate | solution.py:260
  13.1 13.3 %sweep.1 = (f32[3,4,128]{2,1,0:T(4,128)}, f32[3,4,128]{2,1,0:T(4,128)S(1)}, f32[8,128]{1,0:T(8,128)S(1)}) custom-call(f32[4,4,512]{2,1,0:T(4,128)S(1)} %pad_maximum_fusion.blocks), custom_call_target="tpu_custom_call" | custom-call | tf_op jit(solution)/shard_map/sweep/pallas_call | solution.py:198
  26.4 0.0 collective-permute-start.3
  26.4 1.2 %collective-permute-done.3 = f32[8,128]{1,0:T(8,128)S(1)} collective-permute-done((f32[8,128]{1,0:T(8,128)S(1)}, f32[8,128]{1,0:T(8,128)S(1)}, u32[]{:S(2)}, u32[]{:S(2)}) %collective-permute-start.3) | collective-permute-done | bytes 4128 | tf_op jit(solution)/shard_map/ppermute | solution.py:249
  27.5 0.7 %collective-permute-start.4 = (f32[8,128]{1,0:T(8,128)S(1)}, f32[8,128]{1,0:T(8,128)S(1)}, u32[]{:S(2)}, u32[]{:S(2)}) collective-permute-start(f32[8,128]{1,0:T(8,128)S(1)} %max.18), channel_id=1, source_target_pairs={{4,12},{5,13},{6,14},{7,15},{12,4},{13,5},{14,6},{15,7},{20,28},{2... | collective-permute-start | bytes 12296 | tf_op jit(solution)/shard_map/ppermute | solution.py:272
  28.2 0.0 collective-permute-done.4
  28.2 0.7 %collective-permute-start.7 = (f32[8,128]{1,0:T(8,128)S(1)}, f32[8,128]{1,0:T(8,128)S(1)}, u32[]{:S(2)}, u32[]{:S(2)}) collective-permute-start(f32[8,128]{1,0:T(8,128)S(1)} %max.19), channel_id=1, source_target_pairs={{4,6},{5,7},{6,4},{7,5},{12,14},{13,15},{14,12},{15,13},{20,22},{2... | collective-permute-start | bytes 12296 | tf_op jit(solution)/shard_map/ppermute | solution.py:272
  28.9 0.7 %collective-permute-start.6 = (f32[8,128]{1,0:T(8,128)S(1)}, f32[8,128]{1,0:T(8,128)S(1)}, u32[]{:S(2)}, u32[]{:S(2)}) collective-permute-start(f32[8,128]{1,0:T(8,128)S(1)} %max.19), channel_id=1, source_target_pairs={{4,5},{5,4},{6,7},{7,6},{12,13},{13,12},{14,15},{15,14},{20,21},{2... | collective-permute-start | bytes 12296 | tf_op jit(solution)/shard_map/ppermute | solution.py:272
  29.6 0.7 %collective-permute-start.5 = (f32[8,128]{1,0:T(8,128)S(1)}, f32[8,128]{1,0:T(8,128)S(1)}, u32[]{:S(2)}, u32[]{:S(2)}) collective-permute-start(f32[8,128]{1,0:T(8,128)S(1)} %max.19), channel_id=1, source_target_pairs={{4,7},{5,6},{6,5},{7,4},{12,15},{13,14},{14,13},{15,12},{20,23},{2... | collective-permute-start | bytes 12296 | tf_op jit(solution)/shard_map/ppermute | solution.py:272
  30.2 0.0 collective-permute-done.7
  30.2 0.0 collective-permute-done.6
  30.3 0.0 collective-permute-done.5
  30.3 0.0 copy-start
  30.3 1.3 %collective-permute-start.8 = (f32[8,128]{1,0:T(8,128)S(1)}, f32[8,128]{1,0:T(8,128)S(1)}, u32[]{:S(2)}, u32[]{:S(2)}) collective-permute-start(f32[8,128]{1,0:T(8,128)S(1)} %maximum_maximum_fusion), channel_id=1, source_target_pairs={{4,0},{12,8},{5,1},{13,9},{6,2},{14,10},{7,3},{15,11},{20,16},{28,... | collective-permute-start | bytes 12296 | tf_op jit(solution)/shard_map/ppermute | solution.py:284
  31.6 14.2 %collective-permute-done.8 = f32[8,128]{1,0:T(8,128)S(1)} collective-permute-done((f32[8,128]{1,0:T(8,128)S(1)}, f32[8,128]{1,0:T(8,128)S(1)}, u32[]{:S(2)}, u32[]{:S(2)}) %collective-permute-start.8) | collective-permute-done | bytes 4128 | tf_op jit(solution)/shard_map/ppermute | solution.py:284
  45.9 0.0 copy-done
  45.9 0.6 %multiply_add_fusion = f32[3,4,128]{2,1,0:T(4,128)} fusion(f32[3,4,128]{2,1,0:T(4,128)S(1)} %bitcast.8, f32[3,4,128]{2,1,0:T(4,128)S(1)} %get-tuple-element.6, f32[128]{0:T(128)S(1)} %divide_bitcast_fusion), kind=kLoop, calls=%fused_computation.1 | loop fusion | flops 3072 | bytes 18944 | tf_op jit(solution)/shard_map/add | solution.py:291
  (5 shorter events, 0.0 us)
Async XLA Ops:
  2.6 6.9 %collective-permute-start.2 = (f32[1,4,512]{2,1,0:T(4,128)}, f32[1,4,512]{2,1,0:T(4,128)S(1)}, u32[]{:S(2)}, u32[]{:S(2)}) collective-permute-start(f32[1,4,512]{2,1,0:T(4,128)} %pack.1), channel_id=1, source_target_pairs={{0,3},{1,2},{2,1},{3,0},{4,7},{5,6},{6,5},{7,4},{8,11},{9,10},{10,... | collective-permute-start | bytes 24584 | tf_op jit(solution)/shard_map/ppermute | solution.py:249
  7.6 4.8 %collective-permute-start.1 = (f32[1,4,512]{2,1,0:T(4,128)}, f32[1,4,512]{2,1,0:T(4,128)S(1)}, u32[]{:S(2)}, u32[]{:S(2)}) collective-permute-start(f32[1,4,512]{2,1,0:T(4,128)} %pack.1), channel_id=1, source_target_pairs={{0,2},{1,3},{2,0},{3,1},{4,6},{5,7},{6,4},{7,5},{8,10},{9,11},{10,... | collective-permute-start | bytes 24584 | tf_op jit(solution)/shard_map/ppermute | solution.py:249
  7.6 4.8 %collective-permute-start = (f32[1,4,512]{2,1,0:T(4,128)}, f32[1,4,512]{2,1,0:T(4,128)S(1)}, u32[]{:S(2)}, u32[]{:S(2)}) collective-permute-start(f32[1,4,512]{2,1,0:T(4,128)} %pack.1), channel_id=1, source_target_pairs={{0,1},{1,0},{2,3},{3,2},{4,5},{5,4},{6,7},{7,6},{8,9},{9,8},{10,11... | collective-permute-start | bytes 24584 | tf_op jit(solution)/shard_map/ppermute | solution.py:249
  26.4 1.2 %collective-permute-start.3 = (f32[8,128]{1,0:T(8,128)S(1)}, f32[8,128]{1,0:T(8,128)S(1)}, u32[]{:S(2)}, u32[]{:S(2)}) collective-permute-start(f32[8,128]{1,0:T(8,128)S(1)} %get-tuple-element.5), channel_id=1, source_target_pairs={{0,4},{4,0},{8,12},{12,8},{1,5},{5,1},{9,13},{13,9},{2,6},{6,2},{1... | collective-permute-start | bytes 12296 | tf_op jit(solution)/shard_map/ppermute | solution.py:249
  27.5 0.7 %collective-permute-start.4 = (f32[8,128]{1,0:T(8,128)S(1)}, f32[8,128]{1,0:T(8,128)S(1)}, u32[]{:S(2)}, u32[]{:S(2)}) collective-permute-start(f32[8,128]{1,0:T(8,128)S(1)} %max.18), channel_id=1, source_target_pairs={{4,12},{5,13},{6,14},{7,15},{12,4},{13,5},{14,6},{15,7},{20,28},{2... | collective-permute-start | bytes 12296 | tf_op jit(solution)/shard_map/ppermute | solution.py:272
  28.2 2.0 %collective-permute-start.7 = (f32[8,128]{1,0:T(8,128)S(1)}, f32[8,128]{1,0:T(8,128)S(1)}, u32[]{:S(2)}, u32[]{:S(2)}) collective-permute-start(f32[8,128]{1,0:T(8,128)S(1)} %max.19), channel_id=1, source_target_pairs={{4,6},{5,7},{6,4},{7,5},{12,14},{13,15},{14,12},{15,13},{20,22},{2... | collective-permute-start | bytes 12296 | tf_op jit(solution)/shard_map/ppermute | solution.py:272
  28.9 1.4 %collective-permute-start.6 = (f32[8,128]{1,0:T(8,128)S(1)}, f32[8,128]{1,0:T(8,128)S(1)}, u32[]{:S(2)}, u32[]{:S(2)}) collective-permute-start(f32[8,128]{1,0:T(8,128)S(1)} %max.19), channel_id=1, source_target_pairs={{4,5},{5,4},{6,7},{7,6},{12,13},{13,12},{14,15},{15,14},{20,21},{2... | collective-permute-start | bytes 12296 | tf_op jit(solution)/shard_map/ppermute | solution.py:272
  29.6 0.7 %collective-permute-start.5 = (f32[8,128]{1,0:T(8,128)S(1)}, f32[8,128]{1,0:T(8,128)S(1)}, u32[]{:S(2)}, u32[]{:S(2)}) collective-permute-start(f32[8,128]{1,0:T(8,128)S(1)} %max.19), channel_id=1, source_target_pairs={{4,7},{5,6},{6,5},{7,4},{12,15},{13,14},{14,13},{15,12},{20,23},{2... | collective-permute-start | bytes 12296 | tf_op jit(solution)/shard_map/ppermute | solution.py:272
  30.3 15.6 %copy-start = (f32[1,3,512]{2,0,1:T(1,128)S(1)}, f32[1,3,512]{2,0,1:T(1,128)}, u32[]{:S(2)}) copy-start(f32[1,3,512]{2,0,1:T(1,128)} %param.3) | copy-start | bytes 18436
  30.3 15.5 %collective-permute-start.8 = (f32[8,128]{1,0:T(8,128)S(1)}, f32[8,128]{1,0:T(8,128)S(1)}, u32[]{:S(2)}, u32[]{:S(2)}) collective-permute-start(f32[8,128]{1,0:T(8,128)S(1)} %maximum_maximum_fusion), channel_id=1, source_target_pairs={{4,0},{12,8},{5,1},{13,9},{6,2},{14,10},{7,3},{15,11},{20,16},{28,... | collective-permute-start | bytes 12296 | tf_op jit(solution)/shard_map/ppermute | solution.py:284

commit v5 on v4

--- a/solution.py
+++ b/solution.py
@@ -14,7 +14,7 @@
 GRID = 4.0
 TINY = 1e-30
 CHUNK = 256
-TILE = 256
+TILE = 512
 FEATURES = 48
 bf16, f32 = jnp.bfloat16, jnp.float32
 
@@ -105,60 +105,52 @@
     return total[0:4] + total[4:8] + total[8:12]
 
 
-def sweep_kernel(blocks, scores_out, drift_out, speed_out, place_ref, weight_ref,
-                 key_ref, query_ref, own_ref, moment_ref, score_ref, along_ref, flux_ref,
-                 own_along_ref, sums_ref):
-    count, _, width = blocks.shape
+def sweep_kernel(count, *refs):
+    blocks, refs = refs[:count], refs[count:]
+    scores_out, drift_out, speed_out, key_ref, query_ref, moment_ref, along_ref, flux_ref, sums_ref = refs
+    width = blocks[0].shape[2]
     total_slots = count * width
     chunks = total_slots // CHUNK
-
-    def columns(block):
-        return pl.ds(pl.multiple_of(block * width, width), width)
-
-    def build(block, carry):
-        place = blocks[block, 0:3] * SCALE
-        weight = blocks[block, 3:4]
-        key, query = distance_features(place)
-        place_ref[:, columns(block)] = place
-        weight_ref[:, columns(block)] = weight
-        key_ref[columns(block), :] = key.T.astype(bf16)
-        query_ref[:, columns(block)] = query.astype(bf16)
-        moment_ref[:, columns(block)] = weighted_rows(weight, place)
-        return carry
-
-    lax.fori_loop(0, count, build, 0, unroll=count <= 4)
-    own_ref[...] = -query_ref[:, 0:width]
+    tiles = total_slots // TILE
+    small = count <= 4
+
+    place = jnp.concatenate([block[0, 0:3] for block in blocks], axis=1) * SCALE
+    weight = jnp.concatenate([block[0, 3:4] for block in blocks], axis=1)
+    key, query = distance_features(place)
+    key_ref[...] = key.T.astype(bf16)
+    query_ref[...] = query.astype(bf16)
+    moment_ref[...] = weighted_rows(weight, place)
+
+    def slots(index, size):
+        return pl.ds(pl.multiple_of(index * size, size), size)
 
     def density(tile, carry):
-        here = pl.ds(pl.multiple_of(tile * TILE, TILE), TILE)
-        query = query_ref[:, here]
+        query = query_ref[:, slots(tile, TILE)]
 
         def add(chunk, total):
-            keys = pl.ds(pl.multiple_of(chunk * CHUNK, CHUNK), CHUNK)
+            keys = slots(chunk, CHUNK)
             blob = jnp.exp2(product(key_ref[keys, :], query))
             return total + split_product(moment_ref[:, keys], blob)
 
         total = lax.fori_loop(0, chunks, add, jnp.zeros((16, TILE), f32), unroll=8)
-        sums = joined(total)
-        place = place_ref[:, here]
-        weight = weight_ref[:, here]
-        live = weight > 0.0
-        clamped = jnp.where(live, sums[0:1], 1.0)
-        pull = place * sums[0:1] - sums[1:4]
-        score = jnp.where(live, -pull / (SCALE * EPS * EPS * clamped), 0.0)
-        score_ref[:, here] = score
-        along_ref[here, :] = along_key_features(place, score).T.astype(bf16)
-        flux_ref[:, here] = weighted_rows(weight, score)
+        sums_ref[:, slots(tile, TILE)] = joined(total)
         return carry
 
-    lax.fori_loop(0, total_slots // TILE, density, 0)
-
-    place = place_ref[:, 0:width]
-    score = score_ref[:, 0:width]
-    own_along_ref[...] = along_query_features(place, score).astype(bf16)
-
-    def add_drift(own, own_along, chunk, totals):
-        keys = pl.ds(pl.multiple_of(chunk * CHUNK, CHUNK), CHUNK)
+    lax.fori_loop(0, tiles, density, 0, unroll=small)
+    sums = sums_ref[...]
+    live = weight > 0.0
+    clamped = jnp.where(live, sums[0:1], 1.0)
+    pull = place * sums[0:1] - sums[1:4]
+    score = jnp.where(live, -pull / (SCALE * EPS * EPS * clamped), 0.0)
+    along_ref[...] = along_key_features(place, score).T.astype(bf16)
+    flux_ref[...] = weighted_rows(weight, score)
+
+    place, score, live = place[:, 0:width], score[:, 0:width], live[:, 0:width]
+    own_along = along_query_features(place, score).astype(bf16)
+    own = -query_ref[:, 0:width]
+
+    def add_drift(chunk, totals):
+        keys = slots(chunk, CHUNK)
         square = jnp.maximum(product(key_ref[keys, :], own), TINY)
         along = product(along_ref[keys, :], own_along)
         distance = square * lax.rsqrt(square)
@@ -167,19 +159,10 @@
             totals[1] + split_product(moment_ref[:, keys], along * distance),
         )
 
-    def drift_tile(tile, carry):
-        here = pl.ds(pl.multiple_of(tile * TILE, TILE), TILE)
-        step = functools.partial(add_drift, own_ref[:, here], own_along_ref[:, here])
-        zero = jnp.zeros((16, TILE), f32)
-        cubes, linear = lax.fori_loop(0, chunks, step, (zero, zero), unroll=8)
-        sums_ref[0:4, here] = joined(cubes)
-        sums_ref[4:8, here] = joined(linear)
-        return carry
-
-    lax.fori_loop(0, width // TILE, drift_tile, 0)
-    cubes, linear = sums_ref[0:4, :], sums_ref[4:8, :]
+    zero = jnp.zeros((16, width), f32)
+    cubes, linear = lax.fori_loop(0, chunks, add_drift, (zero, zero), unroll=8)
+    cubes, linear = joined(cubes), joined(linear)
     drift = score * cubes[0:1] - cubes[1:4] - place * linear[0:1] + linear[1:4]
-    live = weight_ref[:, 0:width] > 0.0
     drift = jnp.where(live, drift * (-1.0 / (SCALE * SCALE * SCALE * total_slots)), 0.0)
     largest = jnp.max(row_sum(drift * drift), axis=1, keepdims=True)
     speed_out[...] = jnp.broadcast_to(jnp.sqrt(largest), speed_out.shape)
@@ -191,37 +174,32 @@
 
 
 def sweep(blocks):
-    count, _, width = blocks.shape
+    count, width = len(blocks), blocks[0].shape[2]
     slots = count * width
     parts = jax.ShapeDtypeStruct((3, width // 128, 128), f32)
     whole = pl.BlockSpec(memory_space=pltpu.VMEM)
     return pl.pallas_call(
-        sweep_kernel,
+        functools.partial(sweep_kernel, count),
         out_shape=(parts, parts, jax.ShapeDtypeStruct((8, 128), f32)),
-        in_specs=[whole],
+        in_specs=[whole] * count,
         out_specs=(whole, whole, whole),
         scratch_shapes=[
-            pltpu.VMEM((3, slots), f32),
-            pltpu.VMEM((1, slots), f32),
             pltpu.VMEM((slots, FEATURES), bf16),
             pltpu.VMEM((FEATURES, slots), bf16),
-            pltpu.VMEM((FEATURES, width), bf16),
             pltpu.VMEM((16, slots), bf16),
-            pltpu.VMEM((3, slots), f32),
             pltpu.VMEM((slots, FEATURES), bf16),
             pltpu.VMEM((16, slots), bf16),
-            pltpu.VMEM((FEATURES, width), bf16),
-            pltpu.VMEM((8, width), f32),
+            pltpu.VMEM((4, slots), f32),
         ],
         compiler_params=pltpu.CompilerParams(vmem_limit_bytes=48 * 1024 * 1024),
         name="sweep",
-    )(blocks)
-
-
-def pack_kernel(velocity, weight, place, filled, packed):
+    )(*blocks)
+
+
+def pack_kernel(velocity, weight, filled, packed):
     parts = velocity.shape[1]
     lane = lax.broadcasted_iota(jnp.int32, (1, 128), 1)
-    first = place[0] * (parts * 128)
+    first = lax.axis_index("sharers") * (parts * 128)
     for part in range(parts):
         lanes = slice(part * 128, part * 128 + 128)
         live = first + part * 128 + lane < filled[0]
@@ -232,16 +210,15 @@
 
 def pack(velocities, weights, counts):
     width = weights.shape[1]
-    place = lax.axis_index("sharers").astype(jnp.int32).reshape(1)
     vector = pl.BlockSpec(memory_space=pltpu.VMEM)
     scalar = pl.BlockSpec(memory_space=pltpu.SMEM)
     return pl.pallas_call(
         pack_kernel,
         out_shape=jax.ShapeDtypeStruct((1, 4, width), f32),
-        in_specs=[vector, vector, scalar, scalar],
+        in_specs=[vector, vector, scalar],
         out_specs=vector,
         name="pack",
-    )(velocities.reshape(3, width // 128, 128), weights.reshape(width // 128, 128), place, counts)
+    )(velocities.reshape(3, width // 128, 128), weights.reshape(width // 128, 128), counts)
 
 
 def swapped(value, axis, step):
@@ -256,20 +233,18 @@
 def gathered(block):
     size = lax.axis_size("sharers")
     if size == 4:
-        third, first, second = (swapped(block, "sharers", step) for step in (3, 1, 2))
-        return jnp.concatenate([block, first, second, third], axis=0)
+        return [block] + [swapped(block, "sharers", step) for step in (3, 1, 2)]
     for step in bits(size):
         block = jnp.concatenate([block, swapped(block, "sharers", step)], axis=0)
-    return block
+    return [block[i : i + 1] for i in range(size)]
 
 
 def group_maximum(value):
     cells, sharers = lax.axis_size("cells"), lax.axis_size("sharers")
-    axes = ("cells", "sharers")
-    odd = [i for i in range(cells * sharers) if (i // sharers) % 2]
 
     def among_odd(value, step):
-        return lax.ppermute(value, axes, [(i, i ^ step) for i in odd])
+        pairs = [(i, i ^ step if (i // sharers) % 2 else i) for i in range(cells * sharers)]
+        return lax.ppermute(value, ("cells", "sharers"), pairs)
 
     value = jnp.maximum(value, swapped(value, "cells", 1))
     for step in bits(cells)[1:]:
@@ -281,8 +256,7 @@
     else:
         for step in bits(sharers):
             value = jnp.maximum(value, among_odd(value, step))
-    back = lax.ppermute(value, "cells", [(i, i ^ 1) for i in range(1, cells, 2)])
-    return jnp.maximum(value, back)
+    return jnp.maximum(value, swapped(value, "cells", 1))
 
 
 def local(velocities, weights, counts):

time: 46.8 us -> 44.3 us (0.947)
  waiting for transfers between devices: 19.6 us -> 7.65 us
  starting transfers between devices: 9.54 us -> 20.3 us
  Pallas kernels: 14.6 us -> 13.3 us
  other arithmetic: 1.34 us -> 0.63 us
  local copies, waits for them, and re-layouts: 0.01 us -> 0.7 us
    ppermute x5 -> x4, waiting for transfers between devices: 14.3 us -> 0.01 us  [among_odd(): return lax.ppermute(value, ('cells', 'sharers'), pairs)]
    ppermute x4 -> x5, starting transfers between devices: 5.62 us -> 17.7 us  [swapped(): return lax.ppermute(value, axis, pairs)]
    ppermute x4 -> x5, waiting for transfers between devices: 5.36 us -> 7.64 us  [swapped(): return lax.ppermute(value, axis, pairs)]
    ppermute x5 -> x4, starting transfers between devices: 3.93 us -> 2.63 us  [among_odd(): return lax.ppermute(value, ('cells', 'sharers'), pairs)]
    pallas_call x1, Pallas kernels: 13.3 us -> 12 us  [sweep(): pl.pallas_call(functools.partial(sweep_kernel, count), out_shape=(parts,...]
    concatenate x1 -> x0, other arithmetic: 0.71 us -> none  [gathered(): return jnp.concatenate([block, first, second, third], axis=0)]
    unnamed x2 -> x4, local copies, waits for them, and re-layouts: 0.01 us -> 0.7 us
  transfers between devices with their start and end apart: 9 -> 9, of which waited for: 4 -> 5; matrix products, arithmetic and copies ran while one was open for 0% -> 0% of each run, Pallas kernels for 0% -> 0%
where the time goes in v5:
time: 44.3 us; the launch traced here: 43.9 us
  starting transfers between devices  20.3 us (46%)
  Pallas kernels  13.3 us (30%)
  waiting for transfers between devices  7.65 us (17%)
  between operations  1.37 us (3%)
  local copies, waits for them, and re-layouts  0.7 us (2%)
  other arithmetic  0.63 us (1%)
    ppermute x5, starting transfers between devices, swapped(): return lax.ppermute(value, axis, pairs)  17.7 us
    pallas_call x1, Pallas kernels, sweep(): pl.pallas_call(functools.partial(sweep_kernel, count), out_shape=(parts,...  12 us
    ppermute x5, waiting for transfers between devices, swapped(): return lax.ppermute(value, axis, pairs)  7.64 us
    ppermute x4, starting transfers between devices, among_odd(): return lax.ppermute(value, ('cells', 'sharers'), pairs)  2.63 us
    pallas_call x1, Pallas kernels, pack(): pl.pallas_call(pack_kernel, out_shape=jax.ShapeDtypeStruct((1, 4, width),...  1.3 us
  transfers between devices with their start and end apart: 9, of which 5 were waited for; matrix products, arithmetic and copies ran while one was open for 0% of the time, Pallas kernels for 0%

profile of v5, /device:TPU:0, one launch (start us, length us, event | category | flops | bytes accessed | tf_op | source)
XLA Modules:
  0.0 43.9 jit_solution(6700579205983881366)
XLA Ops:
  1.3 1.3 %pack.1.refs_0_ = f32[1,4,512]{2,1,0:T(4,128)} custom-call(f32[3,4,128]{2,1,0:T(4,128)} %bitcast.6, f32[4,128]{1,0:T(4,128)} %bitcast.9, s32[1]{0:T(128)S(6)} %copy.9.filled), custom_call_target="tpu_custom_call" | custom-call | tf_op jit(solution)/shard_map/pack/pallas_call | solution.py:215
  2.6 4.0 %collective-permute-start.2 = (f32[1,4,512]{2,1,0:T(4,128)}, f32[1,4,512]{2,1,0:T(4,128)S(1)}, u32[]{:S(2)}, u32[]{:S(2)}) collective-permute-start(f32[1,4,512]{2,1,0:T(4,128)} %pack.1.refs_0_), channel_id=1, source_target_pairs={{0,2},{1,3},{2,0},{3,1},{4,6},{5,7},{6,4},{7,5},{8,10},{9,11},{10,... | collective-permute-start | bytes 24584 | tf_op jit(solution)/shard_map/ppermute | solution.py:226
  6.6 1.6 %collective-permute-start.1 = (f32[1,4,512]{2,1,0:T(4,128)}, f32[1,4,512]{2,1,0:T(4,128)S(1)}, u32[]{:S(2)}, u32[]{:S(2)}) collective-permute-start(f32[1,4,512]{2,1,0:T(4,128)} %pack.1.refs_0_), channel_id=1, source_target_pairs={{0,1},{1,0},{2,3},{3,2},{4,5},{5,4},{6,7},{7,6},{8,9},{9,8},{10,11... | collective-permute-start | bytes 24584 | tf_op jit(solution)/shard_map/ppermute | solution.py:226
  8.2 0.0 collective-permute-start
  8.2 0.3 collective-permute-done.2.refs_3_
  8.5 2.0 %collective-permute-done.1.refs_2_ = f32[1,4,512]{2,1,0:T(4,128)S(1)} collective-permute-done((f32[1,4,512]{2,1,0:T(4,128)}, f32[1,4,512]{2,1,0:T(4,128)S(1)}, u32[]{:S(2)}, u32[]{:S(2)}) %collective-permute-start.1) | collective-permute-done | bytes 8224 | tf_op jit(solution)/shard_map/ppermute | solution.py:226
  10.5 3.4 %collective-permute-done.refs_1_ = f32[1,4,512]{2,1,0:T(4,128)S(1)} collective-permute-done((f32[1,4,512]{2,1,0:T(4,128)}, f32[1,4,512]{2,1,0:T(4,128)S(1)}, u32[]{:S(2)}, u32[]{:S(2)}) %collective-permute-start) | collective-permute-done | bytes 8224 | tf_op jit(solution)/shard_map/ppermute | solution.py:226
  13.9 0.0 copy-start
  13.9 0.7 %copy-done = f32[1,4,512]{2,1,0:T(4,128)S(1)} copy-done((f32[1,4,512]{2,1,0:T(4,128)S(1)}, f32[1,4,512]{2,1,0:T(4,128)}, u32[]{:S(2)}) %copy-start) | copy-done | bytes 8216
  14.5 12.0 %sweep.1 = (f32[3,4,128]{2,1,0:T(4,128)}, f32[3,4,128]{2,1,0:T(4,128)S(1)}, f32[8,128]{1,0:T(8,128)S(1)}) custom-call(f32[1,4,512]{2,1,0:T(4,128)S(1)} %copy-done, f32[1,4,512]{2,1,0:T(4,128)S(1)} %collective-permute-done.refs_1_, f32[1,4,512]{2,1,0:T(4,128)S(1)} %collective-permute-done.1.refs_2_, f32[1,4,512]{2,1,0:T(4,128)S(1)} %collective-permute-done.2.refs_3_), custom_call_target="tpu_custom_call" | custom-call | tf_op jit(solution)/shard_map/sweep/pallas_call | solution.py:181
  26.5 0.0 collective-permute-start.3
  26.5 1.2 %collective-permute-done.3 = f32[8,128]{1,0:T(8,128)S(1)} collective-permute-done((f32[8,128]{1,0:T(8,128)S(1)}, f32[8,128]{1,0:T(8,128)S(1)}, u32[]{:S(2)}, u32[]{:S(2)}) %collective-permute-start.3) | collective-permute-done | bytes 4128 | tf_op jit(solution)/shard_map/ppermute | solution.py:226
  27.7 0.7 %collective-permute-start.4 = (f32[8,128]{1,0:T(8,128)S(1)}, f32[8,128]{1,0:T(8,128)S(1)}, u32[]{:S(2)}, u32[]{:S(2)}) collective-permute-start(f32[8,128]{1,0:T(8,128)S(1)} %max.18), channel_id=1, source_target_pairs={{0,0},{1,1},{2,2},{3,3},{4,12},{5,13},{6,14},{7,15},{8,8},{9,9},{1... | collective-permute-start | bytes 12296 | tf_op jit(solution)/shard_map/ppermute | solution.py:247
  28.4 0.0 collective-permute-done.4
  28.4 0.7 %collective-permute-start.7 = (f32[8,128]{1,0:T(8,128)S(1)}, f32[8,128]{1,0:T(8,128)S(1)}, u32[]{:S(2)}, u32[]{:S(2)}) collective-permute-start(f32[8,128]{1,0:T(8,128)S(1)} %max.19), channel_id=1, source_target_pairs={{0,0},{1,1},{2,2},{3,3},{4,6},{5,7},{6,4},{7,5},{8,8},{9,9},{10,10... | collective-permute-start | bytes 12296 | tf_op jit(solution)/shard_map/ppermute | solution.py:247
  29.1 0.7 %collective-permute-start.6 = (f32[8,128]{1,0:T(8,128)S(1)}, f32[8,128]{1,0:T(8,128)S(1)}, u32[]{:S(2)}, u32[]{:S(2)}) collective-permute-start(f32[8,128]{1,0:T(8,128)S(1)} %max.19), channel_id=1, source_target_pairs={{0,0},{1,1},{2,2},{3,3},{4,5},{5,4},{6,7},{7,6},{8,8},{9,9},{10,10... | collective-permute-start | bytes 12296 | tf_op jit(solution)/shard_map/ppermute | solution.py:247
  29.7 0.7 %collective-permute-start.5 = (f32[8,128]{1,0:T(8,128)S(1)}, f32[8,128]{1,0:T(8,128)S(1)}, u32[]{:S(2)}, u32[]{:S(2)}) collective-permute-start(f32[8,128]{1,0:T(8,128)S(1)} %max.19), channel_id=1, source_target_pairs={{0,0},{1,1},{2,2},{3,3},{4,7},{5,6},{6,5},{7,4},{8,8},{9,9},{10,10... | collective-permute-start | bytes 12296 | tf_op jit(solution)/shard_map/ppermute | solution.py:247
  30.4 0.0 collective-permute-done.7
  30.4 0.0 collective-permute-done.6
  30.4 0.0 collective-permute-done.5
  30.4 0.0 copy-start.1
  30.5 12.0 %collective-permute-start.8 = (f32[8,128]{1,0:T(8,128)S(1)}, f32[8,128]{1,0:T(8,128)S(1)}, u32[]{:S(2)}, u32[]{:S(2)}) collective-permute-start(f32[8,128]{1,0:T(8,128)S(1)} %maximum_maximum_fusion), channel_id=1, source_target_pairs={{0,4},{4,0},{8,12},{12,8},{1,5},{5,1},{9,13},{13,9},{2,6},{6,2},{1... | collective-permute-start | bytes 12296 | tf_op jit(solution)/shard_map/ppermute | solution.py:226
  42.5 0.8 %collective-permute-done.8 = f32[8,128]{1,0:T(8,128)S(1)} collective-permute-done((f32[8,128]{1,0:T(8,128)S(1)}, f32[8,128]{1,0:T(8,128)S(1)}, u32[]{:S(2)}, u32[]{:S(2)}) %collective-permute-start.8) | collective-permute-done | bytes 4128 | tf_op jit(solution)/shard_map/ppermute | solution.py:226
  43.3 0.0 copy-done.1
  43.3 0.6 %multiply_add_fusion = f32[3,4,128]{2,1,0:T(4,128)} fusion(f32[3,4,128]{2,1,0:T(4,128)S(1)} %bitcast.7, f32[3,4,128]{2,1,0:T(4,128)S(1)} %get-tuple-element.6, f32[128]{0:T(128)S(1)} %divide_bitcast_fusion), kind=kLoop, calls=%fused_computation | loop fusion | flops 3072 | bytes 18944 | tf_op jit(solution)/shard_map/add | solution.py:265
  (5 shorter events, 0.0 us)
Async XLA Ops:
  2.6 5.9 %collective-permute-start.2 = (f32[1,4,512]{2,1,0:T(4,128)}, f32[1,4,512]{2,1,0:T(4,128)S(1)}, u32[]{:S(2)}, u32[]{:S(2)}) collective-permute-start(f32[1,4,512]{2,1,0:T(4,128)} %pack.1.refs_0_), channel_id=1, source_target_pairs={{0,2},{1,3},{2,0},{3,1},{4,6},{5,7},{6,4},{7,5},{8,10},{9,11},{10,... | collective-permute-start | bytes 24584 | tf_op jit(solution)/shard_map/ppermute | solution.py:226
  6.6 3.9 %collective-permute-start.1 = (f32[1,4,512]{2,1,0:T(4,128)}, f32[1,4,512]{2,1,0:T(4,128)S(1)}, u32[]{:S(2)}, u32[]{:S(2)}) collective-permute-start(f32[1,4,512]{2,1,0:T(4,128)} %pack.1.refs_0_), channel_id=1, source_target_pairs={{0,1},{1,0},{2,3},{3,2},{4,5},{5,4},{6,7},{7,6},{8,9},{9,8},{10,11... | collective-permute-start | bytes 24584 | tf_op jit(solution)/shard_map/ppermute | solution.py:226
  8.2 5.7 %collective-permute-start = (f32[1,4,512]{2,1,0:T(4,128)}, f32[1,4,512]{2,1,0:T(4,128)S(1)}, u32[]{:S(2)}, u32[]{:S(2)}) collective-permute-start(f32[1,4,512]{2,1,0:T(4,128)} %pack.1.refs_0_), channel_id=1, source_target_pairs={{0,3},{1,2},{2,1},{3,0},{4,7},{5,6},{6,5},{7,4},{8,11},{9,10},{10,... | collective-permute-start | bytes 24584 | tf_op jit(solution)/shard_map/ppermute | solution.py:226
  13.9 0.7 %copy-start = (f32[1,4,512]{2,1,0:T(4,128)S(1)}, f32[1,4,512]{2,1,0:T(4,128)}, u32[]{:S(2)}) copy-start(f32[1,4,512]{2,1,0:T(4,128)} %pack.1.refs_0_) | copy-start | bytes 24580
  26.5 1.2 %collective-permute-start.3 = (f32[8,128]{1,0:T(8,128)S(1)}, f32[8,128]{1,0:T(8,128)S(1)}, u32[]{:S(2)}, u32[]{:S(2)}) collective-permute-start(f32[8,128]{1,0:T(8,128)S(1)} %get-tuple-element.5), channel_id=1, source_target_pairs={{0,4},{4,0},{8,12},{12,8},{1,5},{5,1},{9,13},{13,9},{2,6},{6,2},{1... | collective-permute-start | bytes 12296 | tf_op jit(solution)/shard_map/ppermute | solution.py:226
  27.7 0.7 %collective-permute-start.4 = (f32[8,128]{1,0:T(8,128)S(1)}, f32[8,128]{1,0:T(8,128)S(1)}, u32[]{:S(2)}, u32[]{:S(2)}) collective-permute-start(f32[8,128]{1,0:T(8,128)S(1)} %max.18), channel_id=1, source_target_pairs={{0,0},{1,1},{2,2},{3,3},{4,12},{5,13},{6,14},{7,15},{8,8},{9,9},{1... | collective-permute-start | bytes 12296 | tf_op jit(solution)/shard_map/ppermute | solution.py:247
  28.4 2.0 %collective-permute-start.7 = (f32[8,128]{1,0:T(8,128)S(1)}, f32[8,128]{1,0:T(8,128)S(1)}, u32[]{:S(2)}, u32[]{:S(2)}) collective-permute-start(f32[8,128]{1,0:T(8,128)S(1)} %max.19), channel_id=1, source_target_pairs={{0,0},{1,1},{2,2},{3,3},{4,6},{5,7},{6,4},{7,5},{8,8},{9,9},{10,10... | collective-permute-start | bytes 12296 | tf_op jit(solution)/shard_map/ppermute | solution.py:247
  29.1 1.4 %collective-permute-start.6 = (f32[8,128]{1,0:T(8,128)S(1)}, f32[8,128]{1,0:T(8,128)S(1)}, u32[]{:S(2)}, u32[]{:S(2)}) collective-permute-start(f32[8,128]{1,0:T(8,128)S(1)} %max.19), channel_id=1, source_target_pairs={{0,0},{1,1},{2,2},{3,3},{4,5},{5,4},{6,7},{7,6},{8,8},{9,9},{10,10... | collective-permute-start | bytes 12296 | tf_op jit(solution)/shard_map/ppermute | solution.py:247
  29.7 0.7 %collective-permute-start.5 = (f32[8,128]{1,0:T(8,128)S(1)}, f32[8,128]{1,0:T(8,128)S(1)}, u32[]{:S(2)}, u32[]{:S(2)}) collective-permute-start(f32[8,128]{1,0:T(8,128)S(1)} %max.19), channel_id=1, source_target_pairs={{0,0},{1,1},{2,2},{3,3},{4,7},{5,6},{6,5},{7,4},{8,8},{9,9},{10,10... | collective-permute-start | bytes 12296 | tf_op jit(solution)/shard_map/ppermute | solution.py:247
  30.4 12.9 %copy-start.1 = (f32[1,3,512]{2,0,1:T(1,128)S(1)}, f32[1,3,512]{2,0,1:T(1,128)}, u32[]{:S(2)}) copy-start(f32[1,3,512]{2,0,1:T(1,128)} %param.3) | copy-start | bytes 18436
  30.5 12.9 %collective-permute-start.8 = (f32[8,128]{1,0:T(8,128)S(1)}, f32[8,128]{1,0:T(8,128)S(1)}, u32[]{:S(2)}, u32[]{:S(2)}) collective-permute-start(f32[8,128]{1,0:T(8,128)S(1)} %maximum_maximum_fusion), channel_id=1, source_target_pairs={{0,4},{4,0},{8,12},{12,8},{1,5},{5,1},{9,13},{13,9},{2,6},{6,2},{1... | collective-permute-start | bytes 12296 | tf_op jit(solution)/shard_map/ppermute | solution.py:226

commit v6 on v5

v6 whole, which is shorter than its diff:
```python
import functools
import functools
import math

import jax
import jax.numpy as jnp
from jax import lax
from jax.experimental import pallas as pl
from jax.experimental.pallas import tpu as pltpu
from jax.sharding import PartitionSpec as P

EPS = 0.35
SCALE = math.sqrt(math.log2(math.e) / (2.0 * EPS * EPS))
GRID = 4.0
TINY = 1e-30
CHUNK = 256
FEATURES = 48
bf16, f32 = jnp.bfloat16, jnp.float32


def round_bf16(value):
    return value.astype(bf16).astype(f32)


def pieces(value, count):
    parts = []
    for _ in range(count):
        part = round_bf16(value)
        parts.append(part)
        value = value - part
    return parts


def padded(rows, height):
    filled = sum(row.shape[0] for row in rows)
    width = rows[0].shape[1]
    if filled < height:
        rows = rows + [jnp.zeros((height - filled, width), f32)]
    return jnp.concatenate(rows, axis=0)


def row_sum(value):
    return value[0:1] + value[1:2] + value[2:3]


def grid_parts(place):
    coarse = jnp.floor(place * GRID + 0.5) * (1.0 / GRID)
    return [coarse] + pieces(place - coarse, 2)


def distance_features(place):
    coarse, fine, rest = grid_parts(place)
    minor = place - coarse
    ones = jnp.ones_like(place)
    coarse_norm = jnp.concatenate(pieces(-row_sum(coarse * coarse), 3), axis=0)
    minor_norm = jnp.concatenate(
        pieces(-row_sum(minor * (2.0 * coarse + minor)), 3), axis=0
    )
    key_rows = [coarse, ones, coarse_norm, coarse, coarse, fine, rest, ones, minor_norm]
    key_rows += [fine, fine, rest, rest]
    query_rows = [coarse, coarse_norm, ones, fine, rest, coarse, coarse, minor_norm, ones]
    query_rows += [fine, rest, fine, rest]
    doubled = (0, 3, 4, 5, 6, 9, 10, 11, 12)
    query_rows = [row * 2.0 if i in doubled else row for i, row in enumerate(query_rows)]
    return padded(key_rows, FEATURES), padded(query_rows, FEATURES)


def along_key_features(place, score):
    coarse, fine, rest = grid_parts(place)
    first, second, third = pieces(score, 3)
    ones = jnp.ones_like(place)
    dot = jnp.concatenate(pieces(row_sum(place * score), 3), axis=0)
    rows = [ones, dot, -first, -second, -third, -first, -second, -first]
    rows += [coarse, coarse, coarse, fine, fine, rest]
    return padded(rows, FEATURES)


def along_query_features(place, score):
    coarse, fine, rest = grid_parts(place)
    first, second, third = pieces(score, 3)
    ones = jnp.ones_like(place)
    dot = jnp.concatenate(pieces(row_sum(place * score), 3), axis=0)
    rows = [dot, ones, coarse, coarse, coarse, fine, fine, rest]
    rows += [-first, -second, -third, -first, -second, -first]
    return padded(rows, FEATURES)


def weighted_rows(weight, value):
    whole = jnp.concatenate([weight, weight * value], axis=0)
    return padded(pieces(whole, 3), 16).astype(bf16)


def product(left, right):
    return jnp.dot(left, right, preferred_element_type=f32)


def split_product(left, matrix):
    upper = matrix.astype(bf16)
    lower = (matrix - upper.astype(f32)).astype(bf16)
    return product(left, upper) + product(left, lower)


def joined(total):
    return total[0:4] + total[4:8] + total[8:12]


def sweep_kernel(count, *refs):
    filled, blocks, refs = refs[0], refs[1 : count + 1], refs[count + 1 :]
    scores_out, drift_out, speed_out, key_ref, query_ref, moment_ref, along_ref, flux_ref = refs[:8]
    sums_ref, cubes_ref, linear_ref, even_ref, odd_ref, even_along_ref, odd_along_ref, own_ref = refs[8:]
    width = blocks[0].shape[2]
    total_slots = count * width
    chunks = total_slots // CHUNK
    steps = chunks * count
    here = lax.axis_index("sharers")

    def slots(index, size):
        return pl.ds(pl.multiple_of(index * size, size), size)

    lane = lax.broadcasted_iota(jnp.int32, (1, width), 1)
    live = [lane + (here ^ step) * width < filled[0] for step in range(count)]
    weight = jnp.concatenate(
        [jnp.where(on, block[0, 3:4], 0.0) for on, block in zip(live, blocks)], axis=1
    )
    place = jnp.concatenate([block[0, 0:3] for block in blocks], axis=1) * SCALE
    key, query = distance_features(place)
    key_ref[...] = key.T.astype(bf16)
    query_ref[...] = query.astype(bf16)
    moment_ref[...] = weighted_rows(weight, place)
    sums_ref[...] = jnp.zeros_like(sums_ref)

    def exponent(step):
        step = jnp.minimum(step, steps - 1)
        tile, chunk = step // chunks, step % chunks
        return product(key_ref[slots(chunk, CHUNK), :], query_ref[:, slots(tile, width)])

    def add_blobs(step, ref):
        tile, chunk = step // chunks, step % chunks
        sums_ref[:, slots(tile, width)] += split_product(
            moment_ref[:, slots(chunk, CHUNK)], jnp.exp2(ref[...])
        )

    even_ref[...] = exponent(0)

    def density(pair, carry):
        step = pair * 2
        odd_ref[...] = exponent(step + 1)
        add_blobs(step, even_ref)
        even_ref[...] = exponent(step + 2)
        add_blobs(step + 1, odd_ref)
        return carry

    lax.fori_loop(0, steps // 2, density, 0)

    sums = joined(sums_ref[...])
    live = weight > 0.0
    clamped = jnp.where(live, sums[0:1], 1.0)
    pull = place * sums[0:1] - sums[1:4]
    score = jnp.where(live, -pull / (SCALE * EPS * EPS * clamped), 0.0)
    along_ref[...] = along_key_features(place, score).T.astype(bf16)
    flux_ref[...] = weighted_rows(weight, score)

    place, score, live = place[:, 0:width], score[:, 0:width], live[:, 0:width]
    own_ref[0] = -query_ref[:, 0:width]
    own_ref[1] = along_query_features(place, score).astype(bf16)
    cubes_ref[...] = jnp.zeros_like(cubes_ref)
    linear_ref[...] = jnp.zeros_like(linear_ref)

    def pair_products(chunk, square_ref, dot_ref):
        keys = slots(jnp.minimum(chunk, chunks - 1), CHUNK)
        square_ref[...] = product(key_ref[keys, :], own_ref[0])
        dot_ref[...] = product(along_ref[keys, :], own_ref[1])

    def add_drift(chunk, square_ref, dot_ref):
        keys = slots(chunk, CHUNK)
        square = jnp.maximum(square_ref[...], TINY)
        distance = square * lax.rsqrt(square)
        cubes_ref[...] += split_product(flux_ref[:, keys], square * distance)
        linear_ref[...] += split_product(moment_ref[:, keys], dot_ref[...] * distance)

    pair_products(0, even_ref, even_along_ref)

    def drift_pair(pair, carry):
        chunk = pair * 2
        pair_products(chunk + 1, odd_ref, odd_along_ref)
        add_drift(chunk, even_ref, even_along_ref)
        pair_products(chunk + 2, even_ref, even_along_ref)
        add_drift(chunk + 1, odd_ref, odd_along_ref)
        return carry

    lax.fori_loop(0, chunks // 2, drift_pair, 0)
    cubes, linear = joined(cubes_ref[...]), joined(linear_ref[...])
    drift = score * cubes[0:1] - cubes[1:4] - place * linear[0:1] + linear[1:4]
    drift = jnp.where(live, drift * (-1.0 / (SCALE * SCALE * SCALE * total_slots)), 0.0)
    largest = jnp.max(row_sum(drift * drift), axis=1, keepdims=True)
    speed_out[...] = jnp.broadcast_to(jnp.sqrt(largest), speed_out.shape)
    for part in range(width // 128):
        lanes = slice(part * 128, part * 128 + 128)
        for axis in range(3):
            scores_out[axis, part : part + 1, :] = score[axis : axis + 1, lanes]
            drift_out[axis, part : part + 1, :] = drift[axis : axis + 1, lanes]


def sweep(counts, blocks, copies):
    count, width = len(blocks), blocks[0].shape[2]
    slots = count * width
    parts = jax.ShapeDtypeStruct((3, width // 128, 128), f32)
    whole = pl.BlockSpec(memory_space=pltpu.VMEM)
    return pl.pallas_call(
        functools.partial(sweep_kernel, count),
        out_shape=(parts, parts, jax.ShapeDtypeStruct((copies, 128), f32)),
        in_specs=[pl.BlockSpec(memory_space=pltpu.SMEM)] + [whole] * count,
        out_specs=(whole, whole, whole),
        scratch_shapes=[
            pltpu.VMEM((slots, FEATURES), bf16),
            pltpu.VMEM((FEATURES, slots), bf16),
            pltpu.VMEM((16, slots), bf16),
            pltpu.VMEM((slots, FEATURES), bf16),
            pltpu.VMEM((16, slots), bf16),
            pltpu.VMEM((16, slots), f32),
            pltpu.VMEM((16, width), f32),
            pltpu.VMEM((16, width), f32),
            pltpu.VMEM((CHUNK, width), f32),
            pltpu.VMEM((CHUNK, width), f32),
            pltpu.VMEM((CHUNK, width), f32),
            pltpu.VMEM((CHUNK, width), f32),
            pltpu.VMEM((2, FEATURES, width), bf16),
        ],
        compiler_params=pltpu.CompilerParams(vmem_limit_bytes=48 * 1024 * 1024),
        name="sweep",
    )(counts, *blocks)


def swapped(value, axis, step):
    pairs = [(i, i ^ step) for i in range(lax.axis_size(axis))]
    return lax.ppermute(value, axis, pairs)


def bits(size):
    return [1 << bit for bit in range(size.bit_length() - 1)]


def gathered(block):
    size = lax.axis_size("sharers")
    if size == 4:
        second, first, third = (swapped(block, "sharers", step) for step in (2, 1, 3))
        return [block, first, second, third]
    for step in bits(size):
        block = jnp.concatenate([block, swapped(block, "sharers", step)], axis=0)
    return [block[i : i + 1] for i in range(size)]


def local(velocities, weights, counts):
    axes = ("cells", "sharers")
    blocks = gathered(jnp.concatenate([velocities, weights[:, None]], axis=1))
    copies = lax.axis_size(axes)
    scores, drift, speeds = sweep(counts, blocks, copies)
    speeds = lax.all_to_all(speeds.reshape(copies, 1, 128), axes, 0, 0, tiled=True)
    time_step = 0.5 / (jnp.max(speeds, axis=0, keepdims=True) + 1e-06)
    moved = velocities.reshape(drift.shape) + time_step * drift
    return moved.reshape(velocities.shape), scores.reshape(velocities.shape)


def solution(mesh):
    in_specs = (
        P(("groups", "cells"), None, "sharers"),
        P(("groups", "cells"), "sharers"),
        P(("groups", "cells")),
    )
    out_specs = (P(("groups", "cells"), None, "sharers"), P(("groups", "cells"), None, "sharers"))
    return jax.shard_map(local, mesh=mesh, in_specs=in_specs, out_specs=out_specs, check_vma=False)
```

time: 44.3 us -> 34.5 us (0.78)
  starting transfers between devices: 20.3 us -> 5.76 us
  blocking collectives: 0 us -> 10.5 us
  waiting for transfers between devices: 7.65 us -> 3.26 us
  Pallas kernels: 13.3 us -> 11.4 us
  local copies, waits for them, and re-layouts: 0.7 us -> 1.35 us
    ppermute x5 -> x3, starting transfers between devices: 17.7 us -> 5.76 us  [swapped(): return lax.ppermute(value, axis, pairs)]
    all_to_all x0 -> x1, blocking collectives: none -> 10.5 us  [local(): lax.all_to_all(speeds.reshape(copies, 1, 128), axes, 0, 0, tiled=True)]
    ppermute x5 -> x3, waiting for transfers between devices: 7.64 us -> 3.26 us  [swapped(): return lax.ppermute(value, axis, pairs)]
    ppermute x4 -> x0, starting transfers between devices: 2.63 us -> none  [among_odd(): return lax.ppermute(value, ('cells', 'sharers'), pairs)]
    pallas_call x1 -> x0, Pallas kernels: 1.3 us -> none  [pack(): pl.pallas_call(pack_kernel, out_shape=jax.ShapeDtypeStruct((1, 4, width),...]
    unnamed x4 -> x5, local copies, waits for them, and re-layouts: 0.7 us -> 1.35 us
    pallas_call x1, Pallas kernels: 12 us -> 11.4 us  [sweep(): pl.pallas_call(functools.partial(sweep_kernel, count), out_shape=(parts,...]
  transfers between devices with their start and end apart: 9 -> 3, of which waited for: 5 -> 2; matrix products, arithmetic and copies ran while one was open for 0% -> 0% of each run, Pallas kernels for 0% -> 0%
where the time goes in v6:
time: 34.5 us; the launch traced here: 34.2 us
  Pallas kernels  11.4 us (33%)
  blocking collectives  10.5 us (30%)
  starting transfers between devices  5.76 us (17%)
  waiting for transfers between devices  3.26 us (9%)
  local copies, waits for them, and re-layouts  1.35 us (4%)
  between operations  1.3 us (4%)
  other arithmetic  0.65 us (2%)
    pallas_call x1, Pallas kernels, sweep(): pl.pallas_call(functools.partial(sweep_kernel, count), out_shape=(parts,...  11.4 us
    all_to_all x1, blocking collectives, local(): lax.all_to_all(speeds.reshape(copies, 1, 128), axes, 0, 0, tiled=True)  10.5 us
    ppermute x3, starting transfers between devices, swapped(): return lax.ppermute(value, axis, pairs)  5.76 us
    ppermute x3, waiting for transfers between devices, swapped(): return lax.ppermute(value, axis, pairs)  3.26 us
    unnamed x5, local copies, waits for them, and re-layouts  1.35 us
  transfers between devices with their start and end apart: 3, of which 2 were waited for; matrix products, arithmetic and copies ran while one was open for 0% of the time, Pallas kernels for 0%

profile of v6, /device:TPU:0, one launch (start us, length us, event | category | flops | bytes accessed | tf_op | source)
XLA Modules:
  0.0 34.2 jit_solution(15169852523862224681)
XLA Ops:
  0.6 0.0 copy-start.1
  0.6 0.7 %copy.11 = f32[1,3,512]{2,1,0:T(4,128)S(1)} copy(f32[1,3,512]{2,0,1:T(1,128)} %param.3) | data formatting | bytes 12288 | tf_op args[0]
  1.3 0.0 copy-done.1
  1.4 5.1 %collective-permute-start.2 = (f32[1,4,512]{2,1,0:T(4,128)S(1)}, f32[1,4,512]{2,1,0:T(4,128)S(1)}, u32[]{:S(2)}, u32[]{:S(2)}) collective-permute-start(f32[1,4,512]{2,1,0:T(4,128)S(1)} %pad_maximum_fusion.refs_1_), channel_id=1, source_target_pairs={{0,3},{1,2},{2,1},{3,0},{4,7},{5,6},{6,5},{7,4},{8,11},{9,10},{10,... | collective-permute-start | bytes 24584 | tf_op jit(solution)/shard_map/ppermute | solution.py:236
  6.5 0.0 collective-permute-start.1
  6.5 0.6 %collective-permute-start = (f32[1,4,512]{2,1,0:T(4,128)S(1)}, f32[1,4,512]{2,1,0:T(4,128)S(1)}, u32[]{:S(2)}, u32[]{:S(2)}) collective-permute-start(f32[1,4,512]{2,1,0:T(4,128)S(1)} %pad_maximum_fusion.refs_1_), channel_id=1, source_target_pairs={{0,1},{1,0},{2,3},{3,2},{4,5},{5,4},{6,7},{7,6},{8,9},{9,8},{10,11... | collective-permute-start | bytes 24584 | tf_op jit(solution)/shard_map/ppermute | solution.py:236
  7.8 0.3 collective-permute-done.2.refs_4_
  8.1 2.9 %collective-permute-done.1.refs_3_ = f32[1,4,512]{2,1,0:T(4,128)S(1)} collective-permute-done((f32[1,4,512]{2,1,0:T(4,128)S(1)}, f32[1,4,512]{2,1,0:T(4,128)S(1)}, u32[]{:S(2)}, u32[]{:S(2)}) %collective-permute-start.1) | collective-permute-done | bytes 8224 | tf_op jit(solution)/shard_map/ppermute | solution.py:236
  11.0 0.0 collective-permute-done.refs_2_
  11.0 11.4 %sweep.1 = (f32[3,4,128]{2,1,0:T(4,128)}, f32[3,4,128]{2,1,0:T(4,128)S(1)}, f32[16,128]{1,0:T(8,128)S(1)}) custom-call(s32[1]{0:T(128)S(6)} %copy.15.refs_0_, f32[1,4,512]{2,1,0:T(4,128)S(1)} %pad_maximum_fusion.refs_1_, f32[1,4,512]{2,1,0:T(4,128)S(1)} %collective-permute-done.refs_2_, f32[1,4,512]{2,1,0:T(4,128)S(1)} %collective-permute-done.1.refs_3_, ...), custom_call_target="tpu_custom_call" | custom-call | tf_op jit(solution)/shard_map/sweep/pallas_call | solution.py:209
  22.4 10.5 %all_to_all.5 = f32[16,1,128]{2,1,0:T(1,128)S(1)} all-to-all(f32[16,1,128]{2,1,0:T(1,128)S(1)} %bitcast.7), channel_id=1, replica_groups=mesh['groups'=2,'cells'=4,'sharers'=4] {'cells','sharers'}, dimensions={0} | all-to-all | bytes 16384 | tf_op jit(solution)/shard_map/all_to_all | solution.py:258
  32.9 0.0 copy-start
  33.0 0.6 %copy-done = f32[1,3,512]{2,0,1:T(1,128)S(1)} copy-done((f32[1,3,512]{2,0,1:T(1,128)S(1)}, f32[1,3,512]{2,0,1:T(1,128)}, u32[]{:S(2)}) %copy-start) | copy-done | bytes 6168
  33.6 0.6 %multiply_add_fusion = f32[3,4,128]{2,1,0:T(4,128)} fusion(f32[3,4,128]{2,1,0:T(4,128)S(1)} %bitcast.8, f32[3,4,128]{2,1,0:T(4,128)S(1)} %get-tuple-element.6, f32[128]{0:T(128)S(1)} %add_divide_fusion), kind=kLoop, calls=%fused_computation.1 | loop fusion | flops 3072 | bytes 18944 | tf_op jit(solution)/shard_map/add | solution.py:260
  (3 shorter events, 0.1 us)
Async XLA Ops:
  0.6 0.7 %copy-start.1 = (f32[1,512]{1,0:T(1,128)S(1)}, f32[1,512]{1,0:T(1,128)}, u32[]{:S(2)}) copy-start(f32[1,512]{1,0:T(1,128)} %param.4) | copy-start | bytes 6148
  1.4 6.7 %collective-permute-start.2 = (f32[1,4,512]{2,1,0:T(4,128)S(1)}, f32[1,4,512]{2,1,0:T(4,128)S(1)}, u32[]{:S(2)}, u32[]{:S(2)}) collective-permute-start(f32[1,4,512]{2,1,0:T(4,128)S(1)} %pad_maximum_fusion.refs_1_), channel_id=1, source_target_pairs={{0,3},{1,2},{2,1},{3,0},{4,7},{5,6},{6,5},{7,4},{8,11},{9,10},{10,... | collective-permute-start | bytes 24584 | tf_op jit(solution)/shard_map/ppermute | solution.py:236
  6.5 4.5 %collective-permute-start.1 = (f32[1,4,512]{2,1,0:T(4,128)S(1)}, f32[1,4,512]{2,1,0:T(4,128)S(1)}, u32[]{:S(2)}, u32[]{:S(2)}) collective-permute-start(f32[1,4,512]{2,1,0:T(4,128)S(1)} %pad_maximum_fusion.refs_1_), channel_id=1, source_target_pairs={{0,2},{1,3},{2,0},{3,1},{4,6},{5,7},{6,4},{7,5},{8,10},{9,11},{10,... | collective-permute-start | bytes 24584 | tf_op jit(solution)/shard_map/ppermute | solution.py:236
  6.5 4.5 %collective-permute-start = (f32[1,4,512]{2,1,0:T(4,128)S(1)}, f32[1,4,512]{2,1,0:T(4,128)S(1)}, u32[]{:S(2)}, u32[]{:S(2)}) collective-permute-start(f32[1,4,512]{2,1,0:T(4,128)S(1)} %pad_maximum_fusion.refs_1_), channel_id=1, source_target_pairs={{0,1},{1,0},{2,3},{3,2},{4,5},{5,4},{6,7},{7,6},{8,9},{9,8},{10,11... | collective-permute-start | bytes 24584 | tf_op jit(solution)/shard_map/ppermute | solution.py:236
  32.9 0.7 %copy-start = (f32[1,3,512]{2,0,1:T(1,128)S(1)}, f32[1,3,512]{2,0,1:T(1,128)}, u32[]{:S(2)}) copy-start(f32[1,3,512]{2,0,1:T(1,128)} %param.3) | copy-start | bytes 18436

commit v7 on v6

--- a/solution.py
+++ b/solution.py
@@ -13,7 +13,7 @@
 SCALE = math.sqrt(math.log2(math.e) / (2.0 * EPS * EPS))
 GRID = 4.0
 TINY = 1e-30
-CHUNK = 256
+CHUNK = 512
 FEATURES = 48
 bf16, f32 = jnp.bfloat16, jnp.float32
 
@@ -97,17 +97,21 @@
 def split_product(left, matrix):
     upper = matrix.astype(bf16)
     lower = (matrix - upper.astype(f32)).astype(bf16)
-    return product(left, upper) + product(left, lower)
+    return product(
+        jnp.concatenate([left, left], axis=1), jnp.concatenate([upper, lower], axis=0)
+    )
 
 
 def joined(total):
     return total[0:4] + total[4:8] + total[8:12]
 
 
-def sweep_kernel(count, *refs):
+def sweep_kernel(order, *refs):
+    count = len(order)
     filled, blocks, refs = refs[0], refs[1 : count + 1], refs[count + 1 :]
-    scores_out, drift_out, speed_out, key_ref, query_ref, moment_ref, along_ref, flux_ref = refs[:8]
-    sums_ref, cubes_ref, linear_ref, even_ref, odd_ref, even_along_ref, odd_along_ref, own_ref = refs[8:]
+    scores_out, drift_out, start_out, speed_out, key_ref, query_ref, moment_ref = refs[:7]
+    along_ref, flux_ref, sums_ref, cubes_ref, linear_ref, even_ref, odd_ref = refs[7:14]
+    even_along_ref, odd_along_ref, own_ref = refs[14:]
     width = blocks[0].shape[2]
     total_slots = count * width
     chunks = total_slots // CHUNK
@@ -118,7 +122,7 @@
         return pl.ds(pl.multiple_of(index * size, size), size)
 
     lane = lax.broadcasted_iota(jnp.int32, (1, width), 1)
-    live = [lane + (here ^ step) * width < filled[0] for step in range(count)]
+    live = [lane + (here ^ step) * width < filled[0] for step in order]
     weight = jnp.concatenate(
         [jnp.where(on, block[0, 3:4], 0.0) for on, block in zip(live, blocks)], axis=1
     )
@@ -199,18 +203,19 @@
         for axis in range(3):
             scores_out[axis, part : part + 1, :] = score[axis : axis + 1, lanes]
             drift_out[axis, part : part + 1, :] = drift[axis : axis + 1, lanes]
-
-
-def sweep(counts, blocks, copies):
+            start_out[axis, part : part + 1, :] = blocks[0][0, axis : axis + 1, lanes]
+
+
+def sweep(counts, blocks, order, copies):
     count, width = len(blocks), blocks[0].shape[2]
     slots = count * width
     parts = jax.ShapeDtypeStruct((3, width // 128, 128), f32)
     whole = pl.BlockSpec(memory_space=pltpu.VMEM)
     return pl.pallas_call(
-        functools.partial(sweep_kernel, count),
-        out_shape=(parts, parts, jax.ShapeDtypeStruct((copies, 128), f32)),
+        functools.partial(sweep_kernel, order),
+        out_shape=(parts, parts, parts, jax.ShapeDtypeStruct((copies, 128), f32)),
         in_specs=[pl.BlockSpec(memory_space=pltpu.SMEM)] + [whole] * count,
-        out_specs=(whole, whole, whole),
+        out_specs=(whole, whole, whole, whole),
         scratch_shapes=[
             pltpu.VMEM((slots, FEATURES), bf16),
             pltpu.VMEM((FEATURES, slots), bf16),
@@ -243,21 +248,21 @@
 def gathered(block):
     size = lax.axis_size("sharers")
     if size == 4:
-        second, first, third = (swapped(block, "sharers", step) for step in (2, 1, 3))
-        return [block, first, second, third]
+        order = [0, 2, 1, 3]
+        return [block] + [swapped(block, "sharers", step) for step in order[1:]], order
     for step in bits(size):
         block = jnp.concatenate([block, swapped(block, "sharers", step)], axis=0)
-    return [block[i : i + 1] for i in range(size)]
+    return [block[i : i + 1] for i in range(size)], list(range(size))
 
 
 def local(velocities, weights, counts):
     axes = ("cells", "sharers")
-    blocks = gathered(jnp.concatenate([velocities, weights[:, None]], axis=1))
+    blocks, order = gathered(jnp.concatenate([velocities, weights[:, None]], axis=1))
     copies = lax.axis_size(axes)
-    scores, drift, speeds = sweep(counts, blocks, copies)
+    scores, drift, start, speeds = sweep(counts, blocks, order, copies)
     speeds = lax.all_to_all(speeds.reshape(copies, 1, 128), axes, 0, 0, tiled=True)
     time_step = 0.5 / (jnp.max(speeds, axis=0, keepdims=True) + 1e-06)
-    moved = velocities.reshape(drift.shape) + time_step * drift
+    moved = start + time_step * drift
     return moved.reshape(velocities.shape), scores.reshape(velocities.shape)
 
 

time: 34.5 us -> 32.9 us (0.954)
  Pallas kernels: 11.4 us -> 10.5 us
  local copies, waits for them, and re-layouts: 1.35 us -> 0.7 us
    pallas_call x1, Pallas kernels: 11.4 us -> 10.5 us  [sweep(): pl.pallas_call(functools.partial(sweep_kernel, order), out_shape=(parts,...]
    unnamed x5 -> x3, local copies, waits for them, and re-layouts: 1.35 us -> 0.7 us
  transfers between devices with their start and end apart: 3 -> 3, of which waited for: 2 -> 3; matrix products, arithmetic and copies ran while one was open for 0% -> 0% of each run, Pallas kernels for 0% -> 0%
where the time goes in v7:
time: 32.9 us; the launch traced here: 32.7 us
  Pallas kernels  10.5 us (32%)
  blocking collectives  10.5 us (32%)
  starting transfers between devices  5.76 us (18%)
  waiting for transfers between devices  3.26 us (10%)
  between operations  1.3 us (4%)
  local copies, waits for them, and re-layouts  0.7 us (2%)
  other arithmetic  0.66 us (2%)
    pallas_call x1, Pallas kernels, sweep(): pl.pallas_call(functools.partial(sweep_kernel, order), out_shape=(parts,...  10.5 us
    all_to_all x1, blocking collectives, local(): lax.all_to_all(speeds.reshape(copies, 1, 128), axes, 0, 0, tiled=True)  10.5 us
    ppermute x3, starting transfers between devices, swapped(): return lax.ppermute(value, axis, pairs)  5.76 us
    ppermute x3, waiting for transfers between devices, swapped(): return lax.ppermute(value, axis, pairs)  3.26 us
    unnamed x3, local copies, waits for them, and re-layouts  0.7 us
  transfers between devices with their start and end apart: 3, of which 3 were waited for; matrix products, arithmetic and copies ran while one was open for 0% of the time, Pallas kernels for 0%

profile of v7, /device:TPU:0, one launch (start us, length us, event | category | flops | bytes accessed | tf_op | source)
XLA Modules:
  0.0 32.7 jit_solution(5923079739793690903)
XLA Ops:
  0.6 0.0 copy-start
  0.6 0.7 %copy.11 = f32[1,3,512]{2,1,0:T(4,128)S(1)} copy(f32[1,3,512]{2,0,1:T(1,128)} %param.3) | data formatting | bytes 12288 | tf_op args[0]
  1.3 0.0 copy-done
  1.4 5.1 %collective-permute-start.2 = (f32[1,4,512]{2,1,0:T(4,128)S(1)}, f32[1,4,512]{2,1,0:T(4,128)S(1)}, u32[]{:S(2)}, u32[]{:S(2)}) collective-permute-start(f32[1,4,512]{2,1,0:T(4,128)S(1)} %pad_maximum_fusion.refs_1_), channel_id=1, source_target_pairs={{0,3},{1,2},{2,1},{3,0},{4,7},{5,6},{6,5},{7,4},{8,11},{9,10},{10,... | collective-permute-start | bytes 24584 | tf_op jit(solution)/shard_map/ppermute | solution.py:241
  6.5 0.0 collective-permute-start.1
  6.5 0.6 %collective-permute-start = (f32[1,4,512]{2,1,0:T(4,128)S(1)}, f32[1,4,512]{2,1,0:T(4,128)S(1)}, u32[]{:S(2)}, u32[]{:S(2)}) collective-permute-start(f32[1,4,512]{2,1,0:T(4,128)S(1)} %pad_maximum_fusion.refs_1_), channel_id=1, source_target_pairs={{0,2},{1,3},{2,0},{3,1},{4,6},{5,7},{6,4},{7,5},{8,10},{9,11},{10,... | collective-permute-start | bytes 24584 | tf_op jit(solution)/shard_map/ppermute | solution.py:241
  7.8 0.3 %collective-permute-done.2.refs_4_ = f32[1,4,512]{2,1,0:T(4,128)S(1)} collective-permute-done((f32[1,4,512]{2,1,0:T(4,128)S(1)}, f32[1,4,512]{2,1,0:T(4,128)S(1)}, u32[]{:S(2)}, u32[]{:S(2)}) %collective-permute-start.2) | collective-permute-done | bytes 8224 | tf_op jit(solution)/shard_map/ppermute | solution.py:241
  8.1 2.0 %collective-permute-done.1.refs_3_ = f32[1,4,512]{2,1,0:T(4,128)S(1)} collective-permute-done((f32[1,4,512]{2,1,0:T(4,128)S(1)}, f32[1,4,512]{2,1,0:T(4,128)S(1)}, u32[]{:S(2)}, u32[]{:S(2)}) %collective-permute-start.1) | collective-permute-done | bytes 8224 | tf_op jit(solution)/shard_map/ppermute | solution.py:241
  10.1 0.9 %collective-permute-done.refs_2_ = f32[1,4,512]{2,1,0:T(4,128)S(1)} collective-permute-done((f32[1,4,512]{2,1,0:T(4,128)S(1)}, f32[1,4,512]{2,1,0:T(4,128)S(1)}, u32[]{:S(2)}, u32[]{:S(2)}) %collective-permute-start) | collective-permute-done | bytes 8224 | tf_op jit(solution)/shard_map/ppermute | solution.py:241
  11.0 10.5 %sweep.1 = (f32[3,4,128]{2,1,0:T(4,128)}, f32[3,4,128]{2,1,0:T(4,128)S(1)}, f32[3,4,128]{2,1,0:T(4,128)S(1)}, f32[16,128]{1,0:T(8,128)S(1)}) custom-call(s32[1]{0:T(128)S(6)} %copy.15.refs_0_, f32[1,4,512]{2,1,0:T(4,128)S(1)} %pad_maximum_fusion.refs_1_, f32[1,4,512]{2,1,0:T(4,128)S(1)} %collective-permute-done.refs_2_, ...), custom_call_target="tpu_custom_call" | custom-call | tf_op jit(solution)/shard_map/sweep/pallas_call | solution.py:214
  21.5 10.5 %all_to_all.5 = f32[16,1,128]{2,1,0:T(1,128)S(1)} all-to-all(f32[16,1,128]{2,1,0:T(1,128)S(1)} %bitcast.6), channel_id=1, replica_groups=mesh['groups'=2,'cells'=4,'sharers'=4] {'cells','sharers'}, dimensions={0} | all-to-all | bytes 16384 | tf_op jit(solution)/shard_map/all_to_all | solution.py:263
  32.1 0.6 %multiply_add_fusion = f32[3,4,128]{2,1,0:T(4,128)} fusion(f32[3,4,128]{2,1,0:T(4,128)S(1)} %get-tuple-element.6, f32[3,4,128]{2,1,0:T(4,128)S(1)} %get-tuple-element.8, f32[128]{0:T(128)S(1)} %add_divide_fusion), kind=kLoop, calls=%fused_computation.1 | loop fusion | flops 3072 | bytes 18944 | tf_op jit(solution)/shard_map/add | solution.py:265
  (3 shorter events, 0.1 us)
Async XLA Ops:
  0.6 0.7 %copy-start = (f32[1,512]{1,0:T(1,128)S(1)}, f32[1,512]{1,0:T(1,128)}, u32[]{:S(2)}) copy-start(f32[1,512]{1,0:T(1,128)} %param.4) | copy-start | bytes 6148
  1.4 6.7 %collective-permute-start.2 = (f32[1,4,512]{2,1,0:T(4,128)S(1)}, f32[1,4,512]{2,1,0:T(4,128)S(1)}, u32[]{:S(2)}, u32[]{:S(2)}) collective-permute-start(f32[1,4,512]{2,1,0:T(4,128)S(1)} %pad_maximum_fusion.refs_1_), channel_id=1, source_target_pairs={{0,3},{1,2},{2,1},{3,0},{4,7},{5,6},{6,5},{7,4},{8,11},{9,10},{10,... | collective-permute-start | bytes 24584 | tf_op jit(solution)/shard_map/ppermute | solution.py:241
  6.5 3.7 %collective-permute-start.1 = (f32[1,4,512]{2,1,0:T(4,128)S(1)}, f32[1,4,512]{2,1,0:T(4,128)S(1)}, u32[]{:S(2)}, u32[]{:S(2)}) collective-permute-start(f32[1,4,512]{2,1,0:T(4,128)S(1)} %pad_maximum_fusion.refs_1_), channel_id=1, source_target_pairs={{0,1},{1,0},{2,3},{3,2},{4,5},{5,4},{6,7},{7,6},{8,9},{9,8},{10,11... | collective-permute-start | bytes 24584 | tf_op jit(solution)/shard_map/ppermute | solution.py:241
  6.5 4.5 %collective-permute-start = (f32[1,4,512]{2,1,0:T(4,128)S(1)}, f32[1,4,512]{2,1,0:T(4,128)S(1)}, u32[]{:S(2)}, u32[]{:S(2)}) collective-permute-start(f32[1,4,512]{2,1,0:T(4,128)S(1)} %pad_maximum_fusion.refs_1_), channel_id=1, source_target_pairs={{0,2},{1,3},{2,0},{3,1},{4,6},{5,7},{6,4},{7,5},{8,10},{9,11},{10,... | collective-permute-start | bytes 24584 | tf_op jit(solution)/shard_map/ppermute | solution.py:241

commit v8 on v7

--- a/solution.py
+++ b/solution.py
@@ -13,7 +13,8 @@
 SCALE = math.sqrt(math.log2(math.e) / (2.0 * EPS * EPS))
 GRID = 4.0
 TINY = 1e-30
-CHUNK = 512
+DENSITY_CHUNK = 2048
+DRIFT_CHUNK = 1024
 FEATURES = 48
 bf16, f32 = jnp.bfloat16, jnp.float32
 
@@ -111,11 +112,14 @@
     filled, blocks, refs = refs[0], refs[1 : count + 1], refs[count + 1 :]
     scores_out, drift_out, start_out, speed_out, key_ref, query_ref, moment_ref = refs[:7]
     along_ref, flux_ref, sums_ref, cubes_ref, linear_ref, even_ref, odd_ref = refs[7:14]
-    even_along_ref, odd_along_ref, own_ref = refs[14:]
+    even_square_ref, odd_square_ref, even_along_ref, odd_along_ref, own_ref = refs[14:]
     width = blocks[0].shape[2]
     total_slots = count * width
-    chunks = total_slots // CHUNK
+    size = min(total_slots, DENSITY_CHUNK)
+    chunks = total_slots // size
     steps = chunks * count
+    drift_size = min(total_slots // 2, DRIFT_CHUNK)
+    drift_chunks = total_slots // drift_size
     here = lax.axis_index("sharers")
 
     def slots(index, size):
@@ -136,12 +140,12 @@
     def exponent(step):
         step = jnp.minimum(step, steps - 1)
         tile, chunk = step // chunks, step % chunks
-        return product(key_ref[slots(chunk, CHUNK), :], query_ref[:, slots(tile, width)])
+        return product(key_ref[slots(chunk, size), :], query_ref[:, slots(tile, width)])
 
     def add_blobs(step, ref):
         tile, chunk = step // chunks, step % chunks
         sums_ref[:, slots(tile, width)] += split_product(
-            moment_ref[:, slots(chunk, CHUNK)], jnp.exp2(ref[...])
+            moment_ref[:, slots(chunk, size)], jnp.exp2(ref[...])
         )
 
     even_ref[...] = exponent(0)
@@ -171,28 +175,28 @@
     linear_ref[...] = jnp.zeros_like(linear_ref)
 
     def pair_products(chunk, square_ref, dot_ref):
-        keys = slots(jnp.minimum(chunk, chunks - 1), CHUNK)
+        keys = slots(jnp.minimum(chunk, drift_chunks - 1), drift_size)
         square_ref[...] = product(key_ref[keys, :], own_ref[0])
         dot_ref[...] = product(along_ref[keys, :], own_ref[1])
 
     def add_drift(chunk, square_ref, dot_ref):
-        keys = slots(chunk, CHUNK)
+        keys = slots(chunk, drift_size)
         square = jnp.maximum(square_ref[...], TINY)
         distance = square * lax.rsqrt(square)
         cubes_ref[...] += split_product(flux_ref[:, keys], square * distance)
         linear_ref[...] += split_product(moment_ref[:, keys], dot_ref[...] * distance)
 
-    pair_products(0, even_ref, even_along_ref)
+    pair_products(0, even_square_ref, even_along_ref)
 
     def drift_pair(pair, carry):
         chunk = pair * 2
-        pair_products(chunk + 1, odd_ref, odd_along_ref)
-        add_drift(chunk, even_ref, even_along_ref)
-        pair_products(chunk + 2, even_ref, even_along_ref)
-        add_drift(chunk + 1, odd_ref, odd_along_ref)
+        pair_products(chunk + 1, odd_square_ref, odd_along_ref)
+        add_drift(chunk, even_square_ref, even_along_ref)
+        pair_products(chunk + 2, even_square_ref, even_along_ref)
+        add_drift(chunk + 1, odd_square_ref, odd_along_ref)
         return carry
 
-    lax.fori_loop(0, chunks // 2, drift_pair, 0)
+    lax.fori_loop(0, drift_chunks // 2, drift_pair, 0)
     cubes, linear = joined(cubes_ref[...]), joined(linear_ref[...])
     drift = score * cubes[0:1] - cubes[1:4] - place * linear[0:1] + linear[1:4]
     drift = jnp.where(live, drift * (-1.0 / (SCALE * SCALE * SCALE * total_slots)), 0.0)
@@ -225,10 +229,12 @@
             pltpu.VMEM((16, slots), f32),
             pltpu.VMEM((16, width), f32),
             pltpu.VMEM((16, width), f32),
-            pltpu.VMEM((CHUNK, width), f32),
-            pltpu.VMEM((CHUNK, width), f32),
-            pltpu.VMEM((CHUNK, width), f32),
-            pltpu.VMEM((CHUNK, width), f32),
+            pltpu.VMEM((min(slots, DENSITY_CHUNK), width), f32),
+            pltpu.VMEM((min(slots, DENSITY_CHUNK), width), f32),
+            pltpu.VMEM((min(slots // 2, DRIFT_CHUNK), width), f32),
+            pltpu.VMEM((min(slots // 2, DRIFT_CHUNK), width), f32),
+            pltpu.VMEM((min(slots // 2, DRIFT_CHUNK), width), f32),
+            pltpu.VMEM((min(slots // 2, DRIFT_CHUNK), width), f32),
             pltpu.VMEM((2, FEATURES, width), bf16),
         ],
         compiler_params=pltpu.CompilerParams(vmem_limit_bytes=48 * 1024 * 1024),

time: 32.9 us -> 33.1 us (level)
  no operation moved by 1% of the time
where the time goes in v8:
time: 33.1 us; the launch traced here: 32.8 us
  Pallas kernels  10.7 us (32%)
  blocking collectives  10.5 us (32%)
  starting transfers between devices  5.76 us (17%)
  waiting for transfers between devices  3.26 us (10%)
  between operations  1.3 us (4%)
  local copies, waits for them, and re-layouts  0.7 us (2%)
  other arithmetic  0.66 us (2%)
    pallas_call x1, Pallas kernels, sweep(): pl.pallas_call(functools.partial(sweep_kernel, order), out_shape=(parts,...  10.7 us
    all_to_all x1, blocking collectives, local(): lax.all_to_all(speeds.reshape(copies, 1, 128), axes, 0, 0, tiled=True)  10.5 us
    ppermute x3, starting transfers between devices, swapped(): return lax.ppermute(value, axis, pairs)  5.76 us
    ppermute x3, waiting for transfers between devices, swapped(): return lax.ppermute(value, axis, pairs)  3.26 us
    unnamed x3, local copies, waits for them, and re-layouts  0.7 us
  transfers between devices with their start and end apart: 3, of which 3 were waited for; matrix products, arithmetic and copies ran while one was open for 0% of the time, Pallas kernels for 0%

profile of v8, /device:TPU:0, one launch (start us, length us, event | category | flops | bytes accessed | tf_op | source)
XLA Modules:
  0.0 32.8 jit_solution(17081487884448927392)
XLA Ops:
  0.6 0.0 copy-start
  0.6 0.7 %copy.11 = f32[1,3,512]{2,1,0:T(4,128)S(1)} copy(f32[1,3,512]{2,0,1:T(1,128)} %param.3) | data formatting | bytes 12288 | tf_op args[0]
  1.3 0.0 copy-done
  1.4 5.1 %collective-permute-start.2 = (f32[1,4,512]{2,1,0:T(4,128)S(1)}, f32[1,4,512]{2,1,0:T(4,128)S(1)}, u32[]{:S(2)}, u32[]{:S(2)}) collective-permute-start(f32[1,4,512]{2,1,0:T(4,128)S(1)} %pad_maximum_fusion.refs_1_), channel_id=1, source_target_pairs={{0,3},{1,2},{2,1},{3,0},{4,7},{5,6},{6,5},{7,4},{8,11},{9,10},{10,... | collective-permute-start | bytes 24584 | tf_op jit(solution)/shard_map/ppermute | solution.py:247
  6.5 0.0 collective-permute-start.1
  6.5 0.6 %collective-permute-start = (f32[1,4,512]{2,1,0:T(4,128)S(1)}, f32[1,4,512]{2,1,0:T(4,128)S(1)}, u32[]{:S(2)}, u32[]{:S(2)}) collective-permute-start(f32[1,4,512]{2,1,0:T(4,128)S(1)} %pad_maximum_fusion.refs_1_), channel_id=1, source_target_pairs={{0,2},{1,3},{2,0},{3,1},{4,6},{5,7},{6,4},{7,5},{8,10},{9,11},{10,... | collective-permute-start | bytes 24584 | tf_op jit(solution)/shard_map/ppermute | solution.py:247
  7.8 0.3 %collective-permute-done.2.refs_4_ = f32[1,4,512]{2,1,0:T(4,128)S(1)} collective-permute-done((f32[1,4,512]{2,1,0:T(4,128)S(1)}, f32[1,4,512]{2,1,0:T(4,128)S(1)}, u32[]{:S(2)}, u32[]{:S(2)}) %collective-permute-start.2) | collective-permute-done | bytes 8224 | tf_op jit(solution)/shard_map/ppermute | solution.py:247
  8.1 2.0 %collective-permute-done.1.refs_3_ = f32[1,4,512]{2,1,0:T(4,128)S(1)} collective-permute-done((f32[1,4,512]{2,1,0:T(4,128)S(1)}, f32[1,4,512]{2,1,0:T(4,128)S(1)}, u32[]{:S(2)}, u32[]{:S(2)}) %collective-permute-start.1) | collective-permute-done | bytes 8224 | tf_op jit(solution)/shard_map/ppermute | solution.py:247
  10.1 0.9 %collective-permute-done.refs_2_ = f32[1,4,512]{2,1,0:T(4,128)S(1)} collective-permute-done((f32[1,4,512]{2,1,0:T(4,128)S(1)}, f32[1,4,512]{2,1,0:T(4,128)S(1)}, u32[]{:S(2)}, u32[]{:S(2)}) %collective-permute-start) | collective-permute-done | bytes 8224 | tf_op jit(solution)/shard_map/ppermute | solution.py:247
  11.0 10.7 %sweep.1 = (f32[3,4,128]{2,1,0:T(4,128)}, f32[3,4,128]{2,1,0:T(4,128)S(1)}, f32[3,4,128]{2,1,0:T(4,128)S(1)}, f32[16,128]{1,0:T(8,128)S(1)}) custom-call(s32[1]{0:T(128)S(6)} %copy.15.refs_0_, f32[1,4,512]{2,1,0:T(4,128)S(1)} %pad_maximum_fusion.refs_1_, f32[1,4,512]{2,1,0:T(4,128)S(1)} %collective-permute-done.refs_2_, ...), custom_call_target="tpu_custom_call" | custom-call | tf_op jit(solution)/shard_map/sweep/pallas_call | solution.py:218
  21.7 10.5 %all_to_all.5 = f32[16,1,128]{2,1,0:T(1,128)S(1)} all-to-all(f32[16,1,128]{2,1,0:T(1,128)S(1)} %bitcast.6), channel_id=1, replica_groups=mesh['groups'=2,'cells'=4,'sharers'=4] {'cells','sharers'}, dimensions={0} | all-to-all | bytes 16384 | tf_op jit(solution)/shard_map/all_to_all | solution.py:269
  32.2 0.6 %multiply_add_fusion = f32[3,4,128]{2,1,0:T(4,128)} fusion(f32[3,4,128]{2,1,0:T(4,128)S(1)} %get-tuple-element.6, f32[3,4,128]{2,1,0:T(4,128)S(1)} %get-tuple-element.8, f32[128]{0:T(128)S(1)} %add_divide_fusion), kind=kLoop, calls=%fused_computation.1 | loop fusion | flops 3072 | bytes 18944 | tf_op jit(solution)/shard_map/add | solution.py:271
  (3 shorter events, 0.1 us)
Async XLA Ops:
  0.6 0.7 %copy-start = (f32[1,512]{1,0:T(1,128)S(1)}, f32[1,512]{1,0:T(1,128)}, u32[]{:S(2)}) copy-start(f32[1,512]{1,0:T(1,128)} %param.4) | copy-start | bytes 6148
  1.4 6.7 %collective-permute-start.2 = (f32[1,4,512]{2,1,0:T(4,128)S(1)}, f32[1,4,512]{2,1,0:T(4,128)S(1)}, u32[]{:S(2)}, u32[]{:S(2)}) collective-permute-start(f32[1,4,512]{2,1,0:T(4,128)S(1)} %pad_maximum_fusion.refs_1_), channel_id=1, source_target_pairs={{0,3},{1,2},{2,1},{3,0},{4,7},{5,6},{6,5},{7,4},{8,11},{9,10},{10,... | collective-permute-start | bytes 24584 | tf_op jit(solution)/shard_map/ppermute | solution.py:247
  6.5 3.7 %collective-permute-start.1 = (f32[1,4,512]{2,1,0:T(4,128)S(1)}, f32[1,4,512]{2,1,0:T(4,128)S(1)}, u32[]{:S(2)}, u32[]{:S(2)}) collective-permute-start(f32[1,4,512]{2,1,0:T(4,128)S(1)} %pad_maximum_fusion.refs_1_), channel_id=1, source_target_pairs={{0,1},{1,0},{2,3},{3,2},{4,5},{5,4},{6,7},{7,6},{8,9},{9,8},{10,11... | collective-permute-start | bytes 24584 | tf_op jit(solution)/shard_map/ppermute | solution.py:247
  6.5 4.5 %collective-permute-start = (f32[1,4,512]{2,1,0:T(4,128)S(1)}, f32[1,4,512]{2,1,0:T(4,128)S(1)}, u32[]{:S(2)}, u32[]{:S(2)}) collective-permute-start(f32[1,4,512]{2,1,0:T(4,128)S(1)} %pad_maximum_fusion.refs_1_), channel_id=1, source_target_pairs={{0,2},{1,3},{2,0},{3,1},{4,6},{5,7},{6,4},{7,5},{8,10},{9,11},{10,... | collective-permute-start | bytes 24584 | tf_op jit(solution)/shard_map/ppermute | solution.py:247

commit v9 on v7

--- a/solution.py
+++ b/solution.py
@@ -15,6 +15,8 @@
 TINY = 1e-30
 CHUNK = 512
 FEATURES = 48
+EXTRA_ROW = 39
+DEAD = -20000.0
 bf16, f32 = jnp.bfloat16, jnp.float32
 
 
@@ -48,25 +50,27 @@
     return [coarse] + pieces(place - coarse, 2)
 
 
-def distance_features(place):
-    coarse, fine, rest = grid_parts(place)
-    minor = place - coarse
+def distance_features(parts, extra):
+    coarse, fine, rest = parts
+    minor = fine + rest
+    place = coarse + minor
     ones = jnp.ones_like(place)
     coarse_norm = jnp.concatenate(pieces(-row_sum(coarse * coarse), 3), axis=0)
     minor_norm = jnp.concatenate(
         pieces(-row_sum(minor * (2.0 * coarse + minor)), 3), axis=0
     )
     key_rows = [coarse, ones, coarse_norm, coarse, coarse, fine, rest, ones, minor_norm]
-    key_rows += [fine, fine, rest, rest]
+    key_rows += [fine, fine, rest, rest] + pieces(extra, 3)
     query_rows = [coarse, coarse_norm, ones, fine, rest, coarse, coarse, minor_norm, ones]
-    query_rows += [fine, rest, fine, rest]
+    query_rows += [fine, rest, fine, rest, ones]
     doubled = (0, 3, 4, 5, 6, 9, 10, 11, 12)
     query_rows = [row * 2.0 if i in doubled else row for i, row in enumerate(query_rows)]
     return padded(key_rows, FEATURES), padded(query_rows, FEATURES)
 
 
-def along_key_features(place, score):
-    coarse, fine, rest = grid_parts(place)
+def along_key_features(parts, score):
+    coarse, fine, rest = parts
+    place = coarse + fine + rest
     first, second, third = pieces(score, 3)
     ones = jnp.ones_like(place)
     dot = jnp.concatenate(pieces(row_sum(place * score), 3), axis=0)
@@ -75,8 +79,9 @@
     return padded(rows, FEATURES)
 
 
-def along_query_features(place, score):
-    coarse, fine, rest = grid_parts(place)
+def along_query_features(parts, score):
+    coarse, fine, rest = parts
+    place = coarse + fine + rest
     first, second, third = pieces(score, 3)
     ones = jnp.ones_like(place)
     dot = jnp.concatenate(pieces(row_sum(place * score), 3), axis=0)
@@ -109,9 +114,9 @@
 def sweep_kernel(order, *refs):
     count = len(order)
     filled, blocks, refs = refs[0], refs[1 : count + 1], refs[count + 1 :]
-    scores_out, drift_out, start_out, speed_out, key_ref, query_ref, moment_ref = refs[:7]
+    scores_out, drift_out, start_out, speed_out, key_ref, query_ref, column_ref = refs[:7]
     along_ref, flux_ref, sums_ref, cubes_ref, linear_ref, even_ref, odd_ref = refs[7:14]
-    even_along_ref, odd_along_ref, own_ref = refs[14:]
+    even_along_ref, odd_along_ref, own_ref, moment_ref = refs[14:]
     width = blocks[0].shape[2]
     total_slots = count * width
     chunks = total_slots // CHUNK
@@ -126,11 +131,17 @@
     weight = jnp.concatenate(
         [jnp.where(on, block[0, 3:4], 0.0) for on, block in zip(live, blocks)], axis=1
     )
-    place = jnp.concatenate([block[0, 0:3] for block in blocks], axis=1) * SCALE
-    key, query = distance_features(place)
+    live = weight > 0.0
+    parts = grid_parts(jnp.concatenate([block[0, 0:3] for block in blocks], axis=1) * SCALE)
+    place = parts[0] + parts[1] + parts[2]
+    extra = jnp.where(live, jnp.log2(jnp.where(live, weight, 1.0)), DEAD)
+    key, query = distance_features(parts, extra)
     key_ref[...] = key.T.astype(bf16)
     query_ref[...] = query.astype(bf16)
     moment_ref[...] = weighted_rows(weight, place)
+    across = padded([place], 8).T
+    for axis in range(3):
+        column_ref[axis] = jnp.broadcast_to(across[:, axis : axis + 1], column_ref.shape[1:])
     sums_ref[...] = jnp.zeros_like(sums_ref)
 
     def exponent(step):
@@ -140,9 +151,12 @@
 
     def add_blobs(step, ref):
         tile, chunk = step // chunks, step % chunks
-        sums_ref[:, slots(tile, width)] += split_product(
-            moment_ref[:, slots(chunk, CHUNK)], jnp.exp2(ref[...])
-        )
+        columns = [column_ref[axis, slots(chunk, CHUNK), :] for axis in range(3)]
+        for part in range(width // 128):
+            blob = jnp.exp2(ref[:, part * 128 : part * 128 + 128])
+            lanes = pl.ds(pl.multiple_of(tile * width + part * 128, 128), 128)
+            for i, term in enumerate([blob] + [blob * column for column in columns]):
+                sums_ref[i, :, lanes] += jnp.sum(term.reshape(CHUNK // 8, 8, 128), axis=0)
 
     even_ref[...] = exponent(0)
 
@@ -156,17 +170,18 @@
 
     lax.fori_loop(0, steps // 2, density, 0)
 
-    sums = joined(sums_ref[...])
-    live = weight > 0.0
+    sums = jnp.sum(sums_ref[...], axis=1)
     clamped = jnp.where(live, sums[0:1], 1.0)
     pull = place * sums[0:1] - sums[1:4]
     score = jnp.where(live, -pull / (SCALE * EPS * EPS * clamped), 0.0)
-    along_ref[...] = along_key_features(place, score).T.astype(bf16)
+    along_ref[...] = along_key_features(parts, score).T.astype(bf16)
     flux_ref[...] = weighted_rows(weight, score)
 
     place, score, live = place[:, 0:width], score[:, 0:width], live[:, 0:width]
-    own_ref[0] = -query_ref[:, 0:width]
-    own_ref[1] = along_query_features(place, score).astype(bf16)
+    parts = [part[:, 0:width] for part in parts]
+    row = lax.broadcasted_iota(jnp.int32, (FEATURES, width), 0)
+    own_ref[0] = jnp.where(row < EXTRA_ROW, -query[:, 0:width], 0.0).astype(bf16)
+    own_ref[1] = along_query_features(parts, score).astype(bf16)
     cubes_ref[...] = jnp.zeros_like(cubes_ref)
     linear_ref[...] = jnp.zeros_like(linear_ref)
 
@@ -219,10 +234,10 @@
         scratch_shapes=[
             pltpu.VMEM((slots, FEATURES), bf16),
             pltpu.VMEM((FEATURES, slots), bf16),
-            pltpu.VMEM((16, slots), bf16),
+            pltpu.VMEM((3, slots, 128), f32),
             pltpu.VMEM((slots, FEATURES), bf16),
             pltpu.VMEM((16, slots), bf16),
-            pltpu.VMEM((16, slots), f32),
+            pltpu.VMEM((4, 8, slots), f32),
             pltpu.VMEM((16, width), f32),
             pltpu.VMEM((16, width), f32),
             pltpu.VMEM((CHUNK, width), f32),
@@ -230,8 +245,9 @@
             pltpu.VMEM((CHUNK, width), f32),
             pltpu.VMEM((CHUNK, width), f32),
             pltpu.VMEM((2, FEATURES, width), bf16),
+            pltpu.VMEM((16, slots), bf16),
         ],
-        compiler_params=pltpu.CompilerParams(vmem_limit_bytes=48 * 1024 * 1024),
+        compiler_params=pltpu.CompilerParams(vmem_limit_bytes=(16 << 20) + slots * 2688),
         name="sweep",
     )(counts, *blocks)
 

time: 32.9 us -> 34.7 us (1.055)
  Pallas kernels: 10.5 us -> 12.3 us
    pallas_call x1, Pallas kernels: 10.5 us -> 12.3 us  [sweep(): pl.pallas_call(functools.partial(sweep_kernel, order), out_shape=(parts,...]
where the time goes in v9:
time: 34.7 us; the launch traced here: 34.5 us
  Pallas kernels  12.3 us (35%)
  blocking collectives  10.5 us (30%)
  starting transfers between devices  5.76 us (17%)
  waiting for transfers between devices  3.26 us (9%)
  between operations  1.3 us (4%)
  local copies, waits for them, and re-layouts  0.7 us (2%)
  other arithmetic  0.66 us (2%)
    pallas_call x1, Pallas kernels, sweep(): pl.pallas_call(functools.partial(sweep_kernel, order), out_shape=(parts,...  12.3 us
    all_to_all x1, blocking collectives, local(): lax.all_to_all(speeds.reshape(copies, 1, 128), axes, 0, 0, tiled=True)  10.5 us
    ppermute x3, starting transfers between devices, swapped(): return lax.ppermute(value, axis, pairs)  5.76 us
    ppermute x3, waiting for transfers between devices, swapped(): return lax.ppermute(value, axis, pairs)  3.26 us
    unnamed x3, local copies, waits for them, and re-layouts  0.7 us
  transfers between devices with their start and end apart: 3, of which 3 were waited for; matrix products, arithmetic and copies ran while one was open for 0% of the time, Pallas kernels for 0%

profile of v9, /device:TPU:0, one launch (start us, length us, event | category | flops | bytes accessed | tf_op | source)
XLA Modules:
  0.0 34.5 jit_solution(3370526795969777283)
XLA Ops:
  0.6 0.0 copy-start
  0.6 0.7 %copy.11 = f32[1,3,512]{2,1,0:T(4,128)S(1)} copy(f32[1,3,512]{2,0,1:T(1,128)} %param.3) | data formatting | bytes 12288 | tf_op args[0]
  1.3 0.0 copy-done
  1.4 5.1 %collective-permute-start.2 = (f32[1,4,512]{2,1,0:T(4,128)S(1)}, f32[1,4,512]{2,1,0:T(4,128)S(1)}, u32[]{:S(2)}, u32[]{:S(2)}) collective-permute-start(f32[1,4,512]{2,1,0:T(4,128)S(1)} %pad_maximum_fusion.refs_1_), channel_id=1, source_target_pairs={{0,3},{1,2},{2,1},{3,0},{4,7},{5,6},{6,5},{7,4},{8,11},{9,10},{10,... | collective-permute-start | bytes 24584 | tf_op jit(solution)/shard_map/ppermute | solution.py:257
  6.5 0.0 collective-permute-start.1
  6.5 0.6 %collective-permute-start = (f32[1,4,512]{2,1,0:T(4,128)S(1)}, f32[1,4,512]{2,1,0:T(4,128)S(1)}, u32[]{:S(2)}, u32[]{:S(2)}) collective-permute-start(f32[1,4,512]{2,1,0:T(4,128)S(1)} %pad_maximum_fusion.refs_1_), channel_id=1, source_target_pairs={{0,2},{1,3},{2,0},{3,1},{4,6},{5,7},{6,4},{7,5},{8,10},{9,11},{10,... | collective-permute-start | bytes 24584 | tf_op jit(solution)/shard_map/ppermute | solution.py:257
  7.8 0.3 collective-permute-done.2.refs_4_
  8.1 2.0 %collective-permute-done.1.refs_3_ = f32[1,4,512]{2,1,0:T(4,128)S(1)} collective-permute-done((f32[1,4,512]{2,1,0:T(4,128)S(1)}, f32[1,4,512]{2,1,0:T(4,128)S(1)}, u32[]{:S(2)}, u32[]{:S(2)}) %collective-permute-start.1) | collective-permute-done | bytes 8224 | tf_op jit(solution)/shard_map/ppermute | solution.py:257
  10.1 0.9 %collective-permute-done.refs_2_ = f32[1,4,512]{2,1,0:T(4,128)S(1)} collective-permute-done((f32[1,4,512]{2,1,0:T(4,128)S(1)}, f32[1,4,512]{2,1,0:T(4,128)S(1)}, u32[]{:S(2)}, u32[]{:S(2)}) %collective-permute-start) | collective-permute-done | bytes 8224 | tf_op jit(solution)/shard_map/ppermute | solution.py:257
  11.0 12.3 %sweep.1 = (f32[3,4,128]{2,1,0:T(4,128)}, f32[3,4,128]{2,1,0:T(4,128)S(1)}, f32[3,4,128]{2,1,0:T(4,128)S(1)}, f32[16,128]{1,0:T(8,128)S(1)}) custom-call(s32[1]{0:T(128)S(6)} %copy.15.refs_0_, f32[1,4,512]{2,1,0:T(4,128)S(1)} %pad_maximum_fusion.refs_1_, f32[1,4,512]{2,1,0:T(4,128)S(1)} %collective-permute-done.refs_2_, ...), custom_call_target="tpu_custom_call" | custom-call | tf_op jit(solution)/shard_map/sweep/pallas_call | solution.py:229
  23.3 10.5 %all_to_all.5 = f32[16,1,128]{2,1,0:T(1,128)S(1)} all-to-all(f32[16,1,128]{2,1,0:T(1,128)S(1)} %bitcast.6), channel_id=1, replica_groups=mesh['groups'=2,'cells'=4,'sharers'=4] {'cells','sharers'}, dimensions={0} | all-to-all | bytes 16384 | tf_op jit(solution)/shard_map/all_to_all | solution.py:279
  33.9 0.6 %multiply_add_fusion = f32[3,4,128]{2,1,0:T(4,128)} fusion(f32[3,4,128]{2,1,0:T(4,128)S(1)} %get-tuple-element.6, f32[3,4,128]{2,1,0:T(4,128)S(1)} %get-tuple-element.8, f32[128]{0:T(128)S(1)} %add_divide_fusion), kind=kLoop, calls=%fused_computation.1 | loop fusion | flops 3072 | bytes 18944 | tf_op jit(solution)/shard_map/add | solution.py:281
  (3 shorter events, 0.1 us)
Async XLA Ops:
  0.6 0.7 %copy-start = (f32[1,512]{1,0:T(1,128)S(1)}, f32[1,512]{1,0:T(1,128)}, u32[]{:S(2)}) copy-start(f32[1,512]{1,0:T(1,128)} %param.4) | copy-start | bytes 6148
  1.4 6.7 %collective-permute-start.2 = (f32[1,4,512]{2,1,0:T(4,128)S(1)}, f32[1,4,512]{2,1,0:T(4,128)S(1)}, u32[]{:S(2)}, u32[]{:S(2)}) collective-permute-start(f32[1,4,512]{2,1,0:T(4,128)S(1)} %pad_maximum_fusion.refs_1_), channel_id=1, source_target_pairs={{0,3},{1,2},{2,1},{3,0},{4,7},{5,6},{6,5},{7,4},{8,11},{9,10},{10,... | collective-permute-start | bytes 24584 | tf_op jit(solution)/shard_map/ppermute | solution.py:257
  6.5 3.7 %collective-permute-start.1 = (f32[1,4,512]{2,1,0:T(4,128)S(1)}, f32[1,4,512]{2,1,0:T(4,128)S(1)}, u32[]{:S(2)}, u32[]{:S(2)}) collective-permute-start(f32[1,4,512]{2,1,0:T(4,128)S(1)} %pad_maximum_fusion.refs_1_), channel_id=1, source_target_pairs={{0,1},{1,0},{2,3},{3,2},{4,5},{5,4},{6,7},{7,6},{8,9},{9,8},{10,11... | collective-permute-start | bytes 24584 | tf_op jit(solution)/shard_map/ppermute | solution.py:257
  6.5 4.5 %collective-permute-start = (f32[1,4,512]{2,1,0:T(4,128)S(1)}, f32[1,4,512]{2,1,0:T(4,128)S(1)}, u32[]{:S(2)}, u32[]{:S(2)}) collective-permute-start(f32[1,4,512]{2,1,0:T(4,128)S(1)} %pad_maximum_fusion.refs_1_), channel_id=1, source_target_pairs={{0,2},{1,3},{2,0},{3,1},{4,6},{5,7},{6,4},{7,5},{8,10},{9,11},{10,... | collective-permute-start | bytes 24584 | tf_op jit(solution)/shard_map/ppermute | solution.py:257

commit v10 on v7

--- a/solution.py
+++ b/solution.py
@@ -111,7 +111,7 @@
     filled, blocks, refs = refs[0], refs[1 : count + 1], refs[count + 1 :]
     scores_out, drift_out, start_out, speed_out, key_ref, query_ref, moment_ref = refs[:7]
     along_ref, flux_ref, sums_ref, cubes_ref, linear_ref, even_ref, odd_ref = refs[7:14]
-    even_along_ref, odd_along_ref, own_ref = refs[14:]
+    own_exponent_ref, own_along_ref = refs[14:]
     width = blocks[0].shape[2]
     total_slots = count * width
     chunks = total_slots // CHUNK
@@ -144,17 +144,26 @@
             moment_ref[:, slots(chunk, CHUNK)], jnp.exp2(ref[...])
         )
 
-    even_ref[...] = exponent(0)
+    own_exponent_ref[slots(0, CHUNK), :] = exponent(0)
+
+    def own_density(chunk, carry):
+        later = jnp.minimum(chunk + 1, chunks - 1)
+        own_exponent_ref[slots(later, CHUNK), :] = exponent(later)
+        add_blobs(chunk, own_exponent_ref.at[slots(chunk, CHUNK), :])
+        return carry
+
+    lax.fori_loop(0, chunks, own_density, 0, unroll=count <= 4)
+    even_ref[...] = exponent(chunks)
 
     def density(pair, carry):
-        step = pair * 2
+        step = chunks + pair * 2
         odd_ref[...] = exponent(step + 1)
         add_blobs(step, even_ref)
         even_ref[...] = exponent(step + 2)
         add_blobs(step + 1, odd_ref)
         return carry
 
-    lax.fori_loop(0, steps // 2, density, 0)
+    lax.fori_loop(0, (steps - chunks) // 2, density, 0)
 
     sums = joined(sums_ref[...])
     live = weight > 0.0
@@ -165,36 +174,34 @@
     flux_ref[...] = weighted_rows(weight, score)
 
     place, score, live = place[:, 0:width], score[:, 0:width], live[:, 0:width]
-    own_ref[0] = -query_ref[:, 0:width]
-    own_ref[1] = along_query_features(place, score).astype(bf16)
+    own_along_ref[...] = along_query_features(place, score).astype(bf16)
     cubes_ref[...] = jnp.zeros_like(cubes_ref)
     linear_ref[...] = jnp.zeros_like(linear_ref)
 
-    def pair_products(chunk, square_ref, dot_ref):
+    def along(chunk):
         keys = slots(jnp.minimum(chunk, chunks - 1), CHUNK)
-        square_ref[...] = product(key_ref[keys, :], own_ref[0])
-        dot_ref[...] = product(along_ref[keys, :], own_ref[1])
-
-    def add_drift(chunk, square_ref, dot_ref):
+        return product(along_ref[keys, :], own_along_ref[...])
+
+    def add_drift(chunk, ref):
         keys = slots(chunk, CHUNK)
-        square = jnp.maximum(square_ref[...], TINY)
-        distance = square * lax.rsqrt(square)
-        cubes_ref[...] += split_product(flux_ref[:, keys], square * distance)
-        linear_ref[...] += split_product(moment_ref[:, keys], dot_ref[...] * distance)
-
-    pair_products(0, even_ref, even_along_ref)
+        negative = jnp.minimum(own_exponent_ref[keys, :], -TINY)
+        distance = negative * lax.rsqrt(-negative)
+        cubes_ref[...] += split_product(flux_ref[:, keys], negative * distance)
+        linear_ref[...] += split_product(moment_ref[:, keys], ref[...] * distance)
+
+    even_ref[...] = along(0)
 
     def drift_pair(pair, carry):
         chunk = pair * 2
-        pair_products(chunk + 1, odd_ref, odd_along_ref)
-        add_drift(chunk, even_ref, even_along_ref)
-        pair_products(chunk + 2, even_ref, even_along_ref)
-        add_drift(chunk + 1, odd_ref, odd_along_ref)
+        odd_ref[...] = along(chunk + 1)
+        add_drift(chunk, even_ref)
+        even_ref[...] = along(chunk + 2)
+        add_drift(chunk + 1, odd_ref)
         return carry
 
     lax.fori_loop(0, chunks // 2, drift_pair, 0)
     cubes, linear = joined(cubes_ref[...]), joined(linear_ref[...])
-    drift = score * cubes[0:1] - cubes[1:4] - place * linear[0:1] + linear[1:4]
+    drift = score * cubes[0:1] - cubes[1:4] + place * linear[0:1] - linear[1:4]
     drift = jnp.where(live, drift * (-1.0 / (SCALE * SCALE * SCALE * total_slots)), 0.0)
     largest = jnp.max(row_sum(drift * drift), axis=1, keepdims=True)
     speed_out[...] = jnp.broadcast_to(jnp.sqrt(largest), speed_out.shape)
@@ -227,11 +234,10 @@
             pltpu.VMEM((16, width), f32),
             pltpu.VMEM((CHUNK, width), f32),
             pltpu.VMEM((CHUNK, width), f32),
-            pltpu.VMEM((CHUNK, width), f32),
-            pltpu.VMEM((CHUNK, width), f32),
-            pltpu.VMEM((2, FEATURES, width), bf16),
+            pltpu.VMEM((slots, width), f32),
+            pltpu.VMEM((FEATURES, width), bf16),
         ],
-        compiler_params=pltpu.CompilerParams(vmem_limit_bytes=48 * 1024 * 1024),
+        compiler_params=pltpu.CompilerParams(vmem_limit_bytes=(16 << 20) + slots * 2688),
         name="sweep",
     )(counts, *blocks)
 

time: 32.9 us -> 32 us (0.973)
  Pallas kernels: 10.5 us -> 9.62 us
    pallas_call x1, Pallas kernels: 10.5 us -> 9.62 us  [sweep(): pl.pallas_call(functools.partial(sweep_kernel, order), out_shape=(parts,...]
where the time goes in v10:
time: 32 us; the launch traced here: 31.8 us
  blocking collectives  10.5 us (33%)
  Pallas kernels  9.62 us (30%)
  starting transfers between devices  5.76 us (18%)
  waiting for transfers between devices  3.26 us (10%)
  between operations  1.3 us (4%)
  local copies, waits for them, and re-layouts  0.7 us (2%)
  other arithmetic  0.66 us (2%)
    all_to_all x1, blocking collectives, local(): lax.all_to_all(speeds.reshape(copies, 1, 128), axes, 0, 0, tiled=True)  10.5 us
    pallas_call x1, Pallas kernels, sweep(): pl.pallas_call(functools.partial(sweep_kernel, order), out_shape=(parts,...  9.62 us
    ppermute x3, starting transfers between devices, swapped(): return lax.ppermute(value, axis, pairs)  5.76 us
    ppermute x3, waiting for transfers between devices, swapped(): return lax.ppermute(value, axis, pairs)  3.26 us
    unnamed x3, local copies, waits for them, and re-layouts  0.7 us
  transfers between devices with their start and end apart: 3, of which 3 were waited for; matrix products, arithmetic and copies ran while one was open for 0% of the time, Pallas kernels for 0%

profile of v10, /device:TPU:0, one launch (start us, length us, event | category | flops | bytes accessed | tf_op | source)
XLA Modules:
  0.0 31.8 jit_solution(9873762901057938462)
XLA Ops:
  0.6 0.0 copy-start
  0.6 0.7 %copy.11 = f32[1,3,512]{2,1,0:T(4,128)S(1)} copy(f32[1,3,512]{2,0,1:T(1,128)} %param.3) | data formatting | bytes 12288 | tf_op args[0]
  1.3 0.0 copy-done
  1.4 5.1 %collective-permute-start.2 = (f32[1,4,512]{2,1,0:T(4,128)S(1)}, f32[1,4,512]{2,1,0:T(4,128)S(1)}, u32[]{:S(2)}, u32[]{:S(2)}) collective-permute-start(f32[1,4,512]{2,1,0:T(4,128)S(1)} %pad_maximum_fusion.refs_1_), channel_id=1, source_target_pairs={{0,3},{1,2},{2,1},{3,0},{4,7},{5,6},{6,5},{7,4},{8,11},{9,10},{10,... | collective-permute-start | bytes 24584 | tf_op jit(solution)/shard_map/ppermute | solution.py:247
  6.5 0.0 collective-permute-start.1
  6.5 0.6 %collective-permute-start = (f32[1,4,512]{2,1,0:T(4,128)S(1)}, f32[1,4,512]{2,1,0:T(4,128)S(1)}, u32[]{:S(2)}, u32[]{:S(2)}) collective-permute-start(f32[1,4,512]{2,1,0:T(4,128)S(1)} %pad_maximum_fusion.refs_1_), channel_id=1, source_target_pairs={{0,2},{1,3},{2,0},{3,1},{4,6},{5,7},{6,4},{7,5},{8,10},{9,11},{10,... | collective-permute-start | bytes 24584 | tf_op jit(solution)/shard_map/ppermute | solution.py:247
  7.8 0.3 %collective-permute-done.2.refs_4_ = f32[1,4,512]{2,1,0:T(4,128)S(1)} collective-permute-done((f32[1,4,512]{2,1,0:T(4,128)S(1)}, f32[1,4,512]{2,1,0:T(4,128)S(1)}, u32[]{:S(2)}, u32[]{:S(2)}) %collective-permute-start.2) | collective-permute-done | bytes 8224 | tf_op jit(solution)/shard_map/ppermute | solution.py:247
  8.1 2.0 %collective-permute-done.1.refs_3_ = f32[1,4,512]{2,1,0:T(4,128)S(1)} collective-permute-done((f32[1,4,512]{2,1,0:T(4,128)S(1)}, f32[1,4,512]{2,1,0:T(4,128)S(1)}, u32[]{:S(2)}, u32[]{:S(2)}) %collective-permute-start.1) | collective-permute-done | bytes 8224 | tf_op jit(solution)/shard_map/ppermute | solution.py:247
  10.1 0.9 %collective-permute-done.refs_2_ = f32[1,4,512]{2,1,0:T(4,128)S(1)} collective-permute-done((f32[1,4,512]{2,1,0:T(4,128)S(1)}, f32[1,4,512]{2,1,0:T(4,128)S(1)}, u32[]{:S(2)}, u32[]{:S(2)}) %collective-permute-start) | collective-permute-done | bytes 8224 | tf_op jit(solution)/shard_map/ppermute | solution.py:247
  11.0 9.6 %sweep.1 = (f32[3,4,128]{2,1,0:T(4,128)}, f32[3,4,128]{2,1,0:T(4,128)S(1)}, f32[3,4,128]{2,1,0:T(4,128)S(1)}, f32[16,128]{1,0:T(8,128)S(1)}) custom-call(s32[1]{0:T(128)S(6)} %copy.15.refs_0_, f32[1,4,512]{2,1,0:T(4,128)S(1)} %pad_maximum_fusion.refs_1_, f32[1,4,512]{2,1,0:T(4,128)S(1)} %collective-permute-done.refs_2_, ...), custom_call_target="tpu_custom_call" | custom-call | tf_op jit(solution)/shard_map/sweep/pallas_call | solution.py:221
  20.6 10.5 %all_to_all.5 = f32[16,1,128]{2,1,0:T(1,128)S(1)} all-to-all(f32[16,1,128]{2,1,0:T(1,128)S(1)} %bitcast.6), channel_id=1, replica_groups=mesh['groups'=2,'cells'=4,'sharers'=4] {'cells','sharers'}, dimensions={0} | all-to-all | bytes 16384 | tf_op jit(solution)/shard_map/all_to_all | solution.py:269
  31.2 0.6 %multiply_add_fusion = f32[3,4,128]{2,1,0:T(4,128)} fusion(f32[3,4,128]{2,1,0:T(4,128)S(1)} %get-tuple-element.6, f32[3,4,128]{2,1,0:T(4,128)S(1)} %get-tuple-element.8, f32[128]{0:T(128)S(1)} %add_divide_fusion), kind=kLoop, calls=%fused_computation.1 | loop fusion | flops 3072 | bytes 18944 | tf_op jit(solution)/shard_map/add | solution.py:271
  (3 shorter events, 0.1 us)
Async XLA Ops:
  0.6 0.7 %copy-start = (f32[1,512]{1,0:T(1,128)S(1)}, f32[1,512]{1,0:T(1,128)}, u32[]{:S(2)}) copy-start(f32[1,512]{1,0:T(1,128)} %param.4) | copy-start | bytes 6148
  1.4 6.7 %collective-permute-start.2 = (f32[1,4,512]{2,1,0:T(4,128)S(1)}, f32[1,4,512]{2,1,0:T(4,128)S(1)}, u32[]{:S(2)}, u32[]{:S(2)}) collective-permute-start(f32[1,4,512]{2,1,0:T(4,128)S(1)} %pad_maximum_fusion.refs_1_), channel_id=1, source_target_pairs={{0,3},{1,2},{2,1},{3,0},{4,7},{5,6},{6,5},{7,4},{8,11},{9,10},{10,... | collective-permute-start | bytes 24584 | tf_op jit(solution)/shard_map/ppermute | solution.py:247
  6.5 3.7 %collective-permute-start.1 = (f32[1,4,512]{2,1,0:T(4,128)S(1)}, f32[1,4,512]{2,1,0:T(4,128)S(1)}, u32[]{:S(2)}, u32[]{:S(2)}) collective-permute-start(f32[1,4,512]{2,1,0:T(4,128)S(1)} %pad_maximum_fusion.refs_1_), channel_id=1, source_target_pairs={{0,1},{1,0},{2,3},{3,2},{4,5},{5,4},{6,7},{7,6},{8,9},{9,8},{10,11... | collective-permute-start | bytes 24584 | tf_op jit(solution)/shard_map/ppermute | solution.py:247
  6.5 4.5 %collective-permute-start = (f32[1,4,512]{2,1,0:T(4,128)S(1)}, f32[1,4,512]{2,1,0:T(4,128)S(1)}, u32[]{:S(2)}, u32[]{:S(2)}) collective-permute-start(f32[1,4,512]{2,1,0:T(4,128)S(1)} %pad_maximum_fusion.refs_1_), channel_id=1, source_target_pairs={{0,2},{1,3},{2,0},{3,1},{4,6},{5,7},{6,4},{7,5},{8,10},{9,11},{10,... | collective-permute-start | bytes 24584 | tf_op jit(solution)/shard_map/ppermute | solution.py:247

commit v11 on v10

--- a/solution.py
+++ b/solution.py
@@ -14,7 +14,8 @@
 GRID = 4.0
 TINY = 1e-30
 CHUNK = 512
-FEATURES = 48
+DISTANCE_ROWS = 96
+ALONG_ROWS = 112
 bf16, f32 = jnp.bfloat16, jnp.float32
 
 
@@ -31,16 +32,27 @@
     return parts
 
 
-def padded(rows, height):
-    filled = sum(row.shape[0] for row in rows)
-    width = rows[0].shape[1]
-    if filled < height:
-        rows = rows + [jnp.zeros((height - filled, width), f32)]
-    return jnp.concatenate(rows, axis=0)
-
-
-def row_sum(value):
-    return value[0:1] + value[1:2] + value[2:3]
+def row_of(value):
+    return lax.broadcasted_iota(jnp.int32, value.shape, 0)
+
+
+def rows_sum(value):
+    return jnp.sum(value, axis=0, keepdims=True)
+
+
+def stacked(groups):
+    if len(groups) % 2:
+        groups = groups + [jnp.zeros_like(groups[0])]
+    return jnp.concatenate(groups, axis=0).astype(bf16)
+
+
+def scalar_groups(value, like):
+    row = row_of(like)
+    first, second, third = pieces(value, 3)
+    low = jnp.where(row == 0, first, jnp.where(row == 1, second, jnp.where(row == 2, third, 0.0)))
+    high = jnp.where(row == 3, first, jnp.where(row == 4, second, jnp.where(row == 5, third, 0.0)))
+    ones_low, ones_high = row < 3, (row >= 3) & (row < 6)
+    return jnp.where(ones_high, 1.0, low), jnp.where(ones_low, 1.0, high)
 
 
 def grid_parts(place):
@@ -48,46 +60,33 @@
     return [coarse] + pieces(place - coarse, 2)
 
 
-def distance_features(place):
-    coarse, fine, rest = grid_parts(place)
-    minor = place - coarse
-    ones = jnp.ones_like(place)
-    coarse_norm = jnp.concatenate(pieces(-row_sum(coarse * coarse), 3), axis=0)
-    minor_norm = jnp.concatenate(
-        pieces(-row_sum(minor * (2.0 * coarse + minor)), 3), axis=0
-    )
-    key_rows = [coarse, ones, coarse_norm, coarse, coarse, fine, rest, ones, minor_norm]
-    key_rows += [fine, fine, rest, rest]
-    query_rows = [coarse, coarse_norm, ones, fine, rest, coarse, coarse, minor_norm, ones]
-    query_rows += [fine, rest, fine, rest]
-    doubled = (0, 3, 4, 5, 6, 9, 10, 11, 12)
-    query_rows = [row * 2.0 if i in doubled else row for i, row in enumerate(query_rows)]
-    return padded(key_rows, FEATURES), padded(query_rows, FEATURES)
-
-
-def along_key_features(place, score):
-    coarse, fine, rest = grid_parts(place)
-    first, second, third = pieces(score, 3)
-    ones = jnp.ones_like(place)
-    dot = jnp.concatenate(pieces(row_sum(place * score), 3), axis=0)
-    rows = [ones, dot, -first, -second, -third, -first, -second, -first]
-    rows += [coarse, coarse, coarse, fine, fine, rest]
-    return padded(rows, FEATURES)
-
-
-def along_query_features(place, score):
-    coarse, fine, rest = grid_parts(place)
-    first, second, third = pieces(score, 3)
-    ones = jnp.ones_like(place)
-    dot = jnp.concatenate(pieces(row_sum(place * score), 3), axis=0)
-    rows = [dot, ones, coarse, coarse, coarse, fine, fine, rest]
-    rows += [-first, -second, -third, -first, -second, -first]
-    return padded(rows, FEATURES)
+def distance_features(parts):
+    coarse, fine, rest = parts
+    minor = fine + rest
+    query_norm, key_norm = scalar_groups(-rows_sum(coarse * coarse), coarse)
+    query_less, key_less = scalar_groups(-rows_sum(minor * (2.0 * coarse + minor)), coarse)
+    key = [coarse, key_norm, coarse, coarse, fine, rest, key_less, fine, fine, rest, rest]
+    coarse, fine, rest = coarse * 2.0, fine * 2.0, rest * 2.0
+    query = [coarse, query_norm, fine, rest, coarse, coarse, query_less, fine, rest, fine, rest]
+    return stacked(key), stacked(query)
+
+
+def along_features(parts, score, is_key):
+    coarse, fine, rest = parts
+    first, second, third = pieces(-score, 3)
+    query_dot, key_dot = scalar_groups(rows_sum((coarse + fine + rest) * score), coarse)
+    places = [coarse, coarse, coarse, fine, fine, rest]
+    turns = [first, second, third, first, second, first]
+    if is_key:
+        return stacked([key_dot] + turns + places)
+    return stacked([query_dot] + places + turns)
 
 
 def weighted_rows(weight, value):
-    whole = jnp.concatenate([weight, weight * value], axis=0)
-    return padded(pieces(whole, 3), 16).astype(bf16)
+    row = row_of(value)
+    whole = jnp.where(row < 3, value, jnp.where(row == 3, 1.0, 0.0)) * weight
+    first, second, third = pieces(whole, 3)
+    return stacked([first, second + pltpu.roll(third, 4, 0)])
 
 
 def product(left, right):
@@ -103,7 +102,8 @@
 
 
 def joined(total):
-    return total[0:4] + total[4:8] + total[8:12]
+    upper, lower = total[0:8], total[8:16]
+    return upper + lower + pltpu.roll(lower, 4, 0)
 
 
 def sweep_kernel(order, *refs):
@@ -126,10 +126,13 @@
     weight = jnp.concatenate(
         [jnp.where(on, block[0, 3:4], 0.0) for on, block in zip(live, blocks)], axis=1
     )
-    place = jnp.concatenate([block[0, 0:3] for block in blocks], axis=1) * SCALE
-    key, query = distance_features(place)
-    key_ref[...] = key.T.astype(bf16)
-    query_ref[...] = query.astype(bf16)
+    whole = jnp.concatenate([block[0] for block in blocks], axis=1)
+    vector = row_of(whole) < 3
+    parts = grid_parts(jnp.where(vector, whole * SCALE, 0.0))
+    place = parts[0] + parts[1] + parts[2]
+    key, query = distance_features(parts)
+    key_ref[...] = key.T
+    query_ref[...] = query
     moment_ref[...] = weighted_rows(weight, place)
     sums_ref[...] = jnp.zeros_like(sums_ref)
 
@@ -167,14 +170,14 @@
 
     sums = joined(sums_ref[...])
     live = weight > 0.0
-    clamped = jnp.where(live, sums[0:1], 1.0)
-    pull = place * sums[0:1] - sums[1:4]
-    score = jnp.where(live, -pull / (SCALE * EPS * EPS * clamped), 0.0)
-    along_ref[...] = along_key_features(place, score).T.astype(bf16)
+    density_sum = jnp.where(live, sums[3:4], 1.0)
+    pull = place * density_sum - sums
+    score = jnp.where(vector & live, pull / (-SCALE * EPS * EPS * density_sum), 0.0)
+    along_ref[...] = along_features(parts, score, True).T
     flux_ref[...] = weighted_rows(weight, score)
 
     place, score, live = place[:, 0:width], score[:, 0:width], live[:, 0:width]
-    own_along_ref[...] = along_query_features(place, score).astype(bf16)
+    own_along_ref[...] = along_features([part[:, 0:width] for part in parts], score, False)
     cubes_ref[...] = jnp.zeros_like(cubes_ref)
     linear_ref[...] = jnp.zeros_like(linear_ref)
 
@@ -201,9 +204,10 @@
 
     lax.fori_loop(0, chunks // 2, drift_pair, 0)
     cubes, linear = joined(cubes_ref[...]), joined(linear_ref[...])
-    drift = score * cubes[0:1] - cubes[1:4] + place * linear[0:1] - linear[1:4]
-    drift = jnp.where(live, drift * (-1.0 / (SCALE * SCALE * SCALE * total_slots)), 0.0)
-    largest = jnp.max(row_sum(drift * drift), axis=1, keepdims=True)
+    drift = score * cubes[3:4] - cubes + place * linear[3:4] - linear
+    factor = -1.0 / (SCALE * SCALE * SCALE * total_slots)
+    drift = jnp.where(live & vector[:, 0:width], drift * factor, 0.0)
+    largest = jnp.max(rows_sum(drift * drift), axis=1, keepdims=True)
     speed_out[...] = jnp.broadcast_to(jnp.sqrt(largest), speed_out.shape)
     for part in range(width // 128):
         lanes = slice(part * 128, part * 128 + 128)
@@ -224,10 +228,10 @@
         in_specs=[pl.BlockSpec(memory_space=pltpu.SMEM)] + [whole] * count,
         out_specs=(whole, whole, whole, whole),
         scratch_shapes=[
-            pltpu.VMEM((slots, FEATURES), bf16),
-            pltpu.VMEM((FEATURES, slots), bf16),
+            pltpu.VMEM((slots, DISTANCE_ROWS), bf16),
+            pltpu.VMEM((DISTANCE_ROWS, slots), bf16),
             pltpu.VMEM((16, slots), bf16),
-            pltpu.VMEM((slots, FEATURES), bf16),
+            pltpu.VMEM((slots, ALONG_ROWS), bf16),
             pltpu.VMEM((16, slots), bf16),
             pltpu.VMEM((16, slots), f32),
             pltpu.VMEM((16, width), f32),
@@ -235,7 +239,7 @@
             pltpu.VMEM((CHUNK, width), f32),
             pltpu.VMEM((CHUNK, width), f32),
             pltpu.VMEM((slots, width), f32),
-            pltpu.VMEM((FEATURES, width), bf16),
+            pltpu.VMEM((ALONG_ROWS, width), bf16),
         ],
         compiler_params=pltpu.CompilerParams(vmem_limit_bytes=(16 << 20) + slots * 2688),
         name="sweep",
@@ -263,7 +267,9 @@
 
 def local(velocities, weights, counts):
     axes = ("cells", "sharers")
-    blocks, order = gathered(jnp.concatenate([velocities, weights[:, None]], axis=1))
+    blocks, order = gathered(
+        jnp.pad(jnp.concatenate([velocities, weights[:, None]], axis=1), ((0, 0), (0, 4), (0, 0)))
+    )
     copies = lax.axis_size(axes)
     scores, drift, start, speeds = sweep(counts, blocks, order, copies)
     speeds = lax.all_to_all(speeds.reshape(copies, 1, 128), axes, 0, 0, tiled=True)

time: 32 us -> 32.2 us (level)
  no operation moved by 1% of the time
where the time goes in v11:
time: 32.2 us; the launch traced here: 31.9 us
  blocking collectives  10.5 us (33%)
  Pallas kernels  9.66 us (30%)
  starting transfers between devices  5.76 us (18%)
  waiting for transfers between devices  3.35 us (10%)
  between operations  1.3 us (4%)
  local copies, waits for them, and re-layouts  0.7 us (2%)
  other arithmetic  0.66 us (2%)
    all_to_all x1, blocking collectives, local(): lax.all_to_all(speeds.reshape(copies, 1, 128), axes, 0, 0, tiled=True)  10.5 us
    pallas_call x1, Pallas kernels, sweep(): pl.pallas_call(functools.partial(sweep_kernel, order), out_shape=(parts,...  9.66 us
    ppermute x3, starting transfers between devices, swapped(): return lax.ppermute(value, axis, pairs)  5.76 us
    ppermute x3, waiting for transfers between devices, swapped(): return lax.ppermute(value, axis, pairs)  3.35 us
    unnamed x3, local copies, waits for them, and re-layouts  0.7 us
  transfers between devices with their start and end apart: 3, of which 3 were waited for; matrix products, arithmetic and copies ran while one was open for 0% of the time, Pallas kernels for 0%

profile of v11, /device:TPU:0, one launch (start us, length us, event | category | flops | bytes accessed | tf_op | source)
XLA Modules:
  0.0 31.9 jit_solution(10106699162534098231)
XLA Ops:
  0.6 0.0 copy-start
  0.6 0.7 %copy.11 = f32[1,3,512]{2,1,0:T(4,128)S(1)} copy(f32[1,3,512]{2,0,1:T(1,128)} %param.3) | data formatting | bytes 12288 | tf_op args[0]
  1.3 0.0 copy-done
  1.4 5.1 %collective-permute-start.2 = (f32[1,8,512]{2,1,0:T(8,128)S(1)}, f32[1,8,512]{2,1,0:T(8,128)S(1)}, u32[]{:S(2)}, u32[]{:S(2)}) collective-permute-start(f32[1,8,512]{2,1,0:T(8,128)S(1)} %select_maximum_fusion.refs_1_), channel_id=1, source_target_pairs={{0,3},{1,2},{2,1},{3,0},{4,7},{5,6},{6,5},{7,4},{8,11},{9,10},{10,... | collective-permute-start | bytes 49160 | tf_op jit(solution)/shard_map/ppermute | solution.py:251
  6.5 0.0 collective-permute-start.1
  6.5 0.6 %collective-permute-start = (f32[1,8,512]{2,1,0:T(8,128)S(1)}, f32[1,8,512]{2,1,0:T(8,128)S(1)}, u32[]{:S(2)}, u32[]{:S(2)}) collective-permute-start(f32[1,8,512]{2,1,0:T(8,128)S(1)} %select_maximum_fusion.refs_1_), channel_id=1, source_target_pairs={{0,2},{1,3},{2,0},{3,1},{4,6},{5,7},{6,4},{7,5},{8,10},{9,11},{10,... | collective-permute-start | bytes 49160 | tf_op jit(solution)/shard_map/ppermute | solution.py:251
  7.8 0.4 %collective-permute-done.2.refs_4_ = f32[1,8,512]{2,1,0:T(8,128)S(1)} collective-permute-done((f32[1,8,512]{2,1,0:T(8,128)S(1)}, f32[1,8,512]{2,1,0:T(8,128)S(1)}, u32[]{:S(2)}, u32[]{:S(2)}) %collective-permute-start.2) | collective-permute-done | bytes 16416 | tf_op jit(solution)/shard_map/ppermute | solution.py:251
  8.2 2.0 %collective-permute-done.1.refs_3_ = f32[1,8,512]{2,1,0:T(8,128)S(1)} collective-permute-done((f32[1,8,512]{2,1,0:T(8,128)S(1)}, f32[1,8,512]{2,1,0:T(8,128)S(1)}, u32[]{:S(2)}, u32[]{:S(2)}) %collective-permute-start.1) | collective-permute-done | bytes 16416 | tf_op jit(solution)/shard_map/ppermute | solution.py:251
  10.2 0.9 %collective-permute-done.refs_2_ = f32[1,8,512]{2,1,0:T(8,128)S(1)} collective-permute-done((f32[1,8,512]{2,1,0:T(8,128)S(1)}, f32[1,8,512]{2,1,0:T(8,128)S(1)}, u32[]{:S(2)}, u32[]{:S(2)}) %collective-permute-start) | collective-permute-done | bytes 16416 | tf_op jit(solution)/shard_map/ppermute | solution.py:251
  11.1 9.7 %sweep.1 = (f32[3,4,128]{2,1,0:T(4,128)}, f32[3,4,128]{2,1,0:T(4,128)S(1)}, f32[3,4,128]{2,1,0:T(4,128)S(1)}, f32[16,128]{1,0:T(8,128)S(1)}) custom-call(s32[1]{0:T(128)S(6)} %copy.15.refs_0_, f32[1,8,512]{2,1,0:T(8,128)S(1)} %select_maximum_fusion.refs_1_, f32[1,8,512]{2,1,0:T(8,128)S(1)} %collective-permute-done.refs_2_, ...), custom_call_target="tpu_custom_call" | custom-call | tf_op jit(solution)/shard_map/sweep/pallas_call | solution.py:225
  20.8 10.5 %all_to_all.5 = f32[16,1,128]{2,1,0:T(1,128)S(1)} all-to-all(f32[16,1,128]{2,1,0:T(1,128)S(1)} %bitcast.6), channel_id=1, replica_groups=mesh['groups'=2,'cells'=4,'sharers'=4] {'cells','sharers'}, dimensions={0} | all-to-all | bytes 16384 | tf_op jit(solution)/shard_map/all_to_all | solution.py:275
  31.3 0.6 %multiply_add_fusion = f32[3,4,128]{2,1,0:T(4,128)} fusion(f32[3,4,128]{2,1,0:T(4,128)S(1)} %get-tuple-element.6, f32[3,4,128]{2,1,0:T(4,128)S(1)} %get-tuple-element.8, f32[128]{0:T(128)S(1)} %add_divide_fusion), kind=kLoop, calls=%fused_computation.2 | loop fusion | flops 3072 | bytes 18944 | tf_op jit(solution)/shard_map/add | solution.py:277
  (3 shorter events, 0.1 us)
Async XLA Ops:
  0.6 0.7 %copy-start = (f32[1,512]{1,0:T(1,128)S(1)}, f32[1,512]{1,0:T(1,128)}, u32[]{:S(2)}) copy-start(f32[1,512]{1,0:T(1,128)} %param.4) | copy-start | bytes 6148
  1.4 6.8 %collective-permute-start.2 = (f32[1,8,512]{2,1,0:T(8,128)S(1)}, f32[1,8,512]{2,1,0:T(8,128)S(1)}, u32[]{:S(2)}, u32[]{:S(2)}) collective-permute-start(f32[1,8,512]{2,1,0:T(8,128)S(1)} %select_maximum_fusion.refs_1_), channel_id=1, source_target_pairs={{0,3},{1,2},{2,1},{3,0},{4,7},{5,6},{6,5},{7,4},{8,11},{9,10},{10,... | collective-permute-start | bytes 49160 | tf_op jit(solution)/shard_map/ppermute | solution.py:251
  6.5 3.7 %collective-permute-start.1 = (f32[1,8,512]{2,1,0:T(8,128)S(1)}, f32[1,8,512]{2,1,0:T(8,128)S(1)}, u32[]{:S(2)}, u32[]{:S(2)}) collective-permute-start(f32[1,8,512]{2,1,0:T(8,128)S(1)} %select_maximum_fusion.refs_1_), channel_id=1, source_target_pairs={{0,1},{1,0},{2,3},{3,2},{4,5},{5,4},{6,7},{7,6},{8,9},{9,8},{10,11... | collective-permute-start | bytes 49160 | tf_op jit(solution)/shard_map/ppermute | solution.py:251
  6.5 4.6 %collective-permute-start = (f32[1,8,512]{2,1,0:T(8,128)S(1)}, f32[1,8,512]{2,1,0:T(8,128)S(1)}, u32[]{:S(2)}, u32[]{:S(2)}) collective-permute-start(f32[1,8,512]{2,1,0:T(8,128)S(1)} %select_maximum_fusion.refs_1_), channel_id=1, source_target_pairs={{0,2},{1,3},{2,0},{3,1},{4,6},{5,7},{6,4},{7,5},{8,10},{9,11},{10,... | collective-permute-start | bytes 49160 | tf_op jit(solution)/shard_map/ppermute | solution.py:251

commit v12 on v11

--- a/solution.py
+++ b/solution.py
@@ -13,7 +13,9 @@
 SCALE = math.sqrt(math.log2(math.e) / (2.0 * EPS * EPS))
 GRID = 4.0
 TINY = 1e-30
+DEAD = -20000.0
 CHUNK = 512
+KEPT_BLOCKS = 4
 DISTANCE_ROWS = 96
 ALONG_ROWS = 112
 bf16, f32 = jnp.bfloat16, jnp.float32
@@ -60,7 +62,7 @@
     return [coarse] + pieces(place - coarse, 2)
 
 
-def distance_features(parts):
+def distance_features(parts, key_extra, query_extra):
     coarse, fine, rest = parts
     minor = fine + rest
     query_norm, key_norm = scalar_groups(-rows_sum(coarse * coarse), coarse)
@@ -68,7 +70,7 @@
     key = [coarse, key_norm, coarse, coarse, fine, rest, key_less, fine, fine, rest, rest]
     coarse, fine, rest = coarse * 2.0, fine * 2.0, rest * 2.0
     query = [coarse, query_norm, fine, rest, coarse, coarse, query_less, fine, rest, fine, rest]
-    return stacked(key), stacked(query)
+    return stacked(key + [key_extra]), stacked(query + [query_extra])
 
 
 def along_features(parts, score, is_key):
@@ -93,12 +95,15 @@
     return jnp.dot(left, right, preferred_element_type=f32)
 
 
-def split_product(left, matrix):
+def store_split(ref, rows, matrix):
     upper = matrix.astype(bf16)
-    lower = (matrix - upper.astype(f32)).astype(bf16)
-    return product(
-        jnp.concatenate([left, left], axis=1), jnp.concatenate([upper, lower], axis=0)
-    )
+    ref[rows, :] = upper
+    half = ref.shape[0] // 2
+    ref[pl.ds(half + rows.start, rows.size), :] = (matrix - upper.astype(f32)).astype(bf16)
+
+
+def split_product(left, ref):
+    return product(jnp.concatenate([left, left], axis=1), ref[...])
 
 
 def joined(total):
@@ -111,11 +116,13 @@
     filled, blocks, refs = refs[0], refs[1 : count + 1], refs[count + 1 :]
     scores_out, drift_out, start_out, speed_out, key_ref, query_ref, moment_ref = refs[:7]
     along_ref, flux_ref, sums_ref, cubes_ref, linear_ref, even_ref, odd_ref = refs[7:14]
-    own_exponent_ref, own_along_ref = refs[14:]
+    own_exponent_ref, own_along_ref, across_ref = refs[14:17]
+    even_cubes_ref, even_linear_ref, odd_cubes_ref, odd_linear_ref = refs[17:]
     width = blocks[0].shape[2]
     total_slots = count * width
     chunks = total_slots // CHUNK
     steps = chunks * count
+    kept = count <= KEPT_BLOCKS
     here = lax.axis_index("sharers")
 
     def slots(index, size):
@@ -130,9 +137,16 @@
     vector = row_of(whole) < 3
     parts = grid_parts(jnp.where(vector, whole * SCALE, 0.0))
     place = parts[0] + parts[1] + parts[2]
-    key, query = distance_features(parts)
+    live = weight > 0.0
+    row = row_of(whole)
+    log_weight = jnp.where(live, jnp.log2(jnp.where(live, weight, 1.0)), DEAD)
+    other = lax.broadcasted_iota(jnp.int32, whole.shape, 1) >= width
+    key, query = distance_features(
+        parts, scalar_groups(log_weight, whole)[0], jnp.where(other & (row < 3), 1.0, 0.0)
+    )
     key_ref[...] = key.T
     query_ref[...] = query
+    across_ref[...] = jnp.where(row == 3, weight, place).T
     moment_ref[...] = weighted_rows(weight, place)
     sums_ref[...] = jnp.zeros_like(sums_ref)
 
@@ -141,21 +155,43 @@
         tile, chunk = step // chunks, step % chunks
         return product(key_ref[slots(chunk, CHUNK), :], query_ref[:, slots(tile, width)])
 
-    def add_blobs(step, ref):
+    def add_blobs(step, ref, first=0, weigh=False):
         tile, chunk = step // chunks, step % chunks
-        sums_ref[:, slots(tile, width)] += split_product(
-            moment_ref[:, slots(chunk, CHUNK)], jnp.exp2(ref[...])
-        )
-
-    own_exponent_ref[slots(0, CHUNK), :] = exponent(0)
-
-    def own_density(chunk, carry):
-        later = jnp.minimum(chunk + 1, chunks - 1)
-        own_exponent_ref[slots(later, CHUNK), :] = exponent(later)
-        add_blobs(chunk, own_exponent_ref.at[slots(chunk, CHUNK), :])
-        return carry
-
-    lax.fori_loop(0, chunks, own_density, 0, unroll=count <= 4)
+        parts = width // 128
+        totals = [[jnp.zeros((8, 128), f32)] * 4 for _ in range(parts)]
+        for group in range(0, CHUNK, 8):
+            keys = pl.ds(pl.multiple_of(chunk * CHUNK + group, 8), 8)
+            across = across_ref[keys, :]
+            columns = [
+                jnp.broadcast_to(across[:, axis : axis + 1], (8, 128))
+                for axis in range(4 if weigh else 3)
+            ]
+            for part in range(parts):
+                rows = pl.ds(first + group, 8)
+                blob = jnp.exp2(ref[rows, part * 128 : part * 128 + 128])
+                if weigh:
+                    blob = blob * columns[3]
+                terms = [blob * column for column in columns[:3]] + [blob]
+                totals[part] = [total + term for total, term in zip(totals[part], terms)]
+        for part in range(parts):
+            lanes = pl.ds(pl.multiple_of(tile * width + part * 128, 128), 128)
+            for i in range(4):
+                sums_ref[i, :, lanes] += totals[part][i]
+
+    own_exponent_ref[0:CHUNK, :] = exponent(0)
+    if kept:
+        for chunk in range(chunks):
+            if chunk + 1 < chunks:
+                own_exponent_ref[slots(chunk + 1, CHUNK), :] = exponent(chunk + 1)
+            add_blobs(chunk, own_exponent_ref, chunk * CHUNK, True)
+    else:
+
+        def own_density(chunk, carry):
+            add_blobs(chunk, own_exponent_ref, 0, True)
+            own_exponent_ref[...] = exponent(chunk + 1)
+            return carry
+
+        lax.fori_loop(0, chunks, own_density, 0)
     even_ref[...] = exponent(chunks)
 
     def density(pair, carry):
@@ -168,9 +204,9 @@
 
     lax.fori_loop(0, (steps - chunks) // 2, density, 0)
 
-    sums = joined(sums_ref[...])
-    live = weight > 0.0
-    density_sum = jnp.where(live, sums[3:4], 1.0)
+    sums = [rows_sum(sums_ref[i]) for i in range(4)]
+    density_sum = jnp.where(live, sums[3], 1.0)
+    sums = jnp.where(row == 0, sums[0], jnp.where(row == 1, sums[1], sums[2]))
     pull = place * density_sum - sums
     score = jnp.where(vector & live, pull / (-SCALE * EPS * EPS * density_sum), 0.0)
     along_ref[...] = along_features(parts, score, True).T
@@ -185,21 +221,28 @@
         keys = slots(jnp.minimum(chunk, chunks - 1), CHUNK)
         return product(along_ref[keys, :], own_along_ref[...])
 
-    def add_drift(chunk, ref):
+    def add_drift(chunk, ref, cubes_split, linear_split):
+        if not kept:
+            own_exponent_ref[...] = exponent(chunk)
+        for group in range(0, CHUNK, 16):
+            rows = pl.ds(group, 16)
+            keys = pl.ds(pl.multiple_of(chunk * CHUNK + group, 16), 16)
+            negative = jnp.minimum(own_exponent_ref[keys if kept else rows, :], -TINY)
+            distance = negative * lax.rsqrt(-negative)
+            store_split(cubes_split, rows, negative * distance)
+            store_split(linear_split, rows, ref[rows, :] * distance)
         keys = slots(chunk, CHUNK)
-        negative = jnp.minimum(own_exponent_ref[keys, :], -TINY)
-        distance = negative * lax.rsqrt(-negative)
-        cubes_ref[...] += split_product(flux_ref[:, keys], negative * distance)
-        linear_ref[...] += split_product(moment_ref[:, keys], ref[...] * distance)
+        cubes_ref[...] += split_product(flux_ref[:, keys], cubes_split)
+        linear_ref[...] += split_product(moment_ref[:, keys], linear_split)
 
     even_ref[...] = along(0)
 
     def drift_pair(pair, carry):
         chunk = pair * 2
         odd_ref[...] = along(chunk + 1)
-        add_drift(chunk, even_ref)
+        add_drift(chunk, even_ref, even_cubes_ref, even_linear_ref)
         even_ref[...] = along(chunk + 2)
-        add_drift(chunk + 1, odd_ref)
+        add_drift(chunk + 1, odd_ref, odd_cubes_ref, odd_linear_ref)
         return carry
 
     lax.fori_loop(0, chunks // 2, drift_pair, 0)
@@ -233,13 +276,18 @@
             pltpu.VMEM((16, slots), bf16),
             pltpu.VMEM((slots, ALONG_ROWS), bf16),
             pltpu.VMEM((16, slots), bf16),
-            pltpu.VMEM((16, slots), f32),
+            pltpu.VMEM((4, 8, slots), f32),
             pltpu.VMEM((16, width), f32),
             pltpu.VMEM((16, width), f32),
             pltpu.VMEM((CHUNK, width), f32),
             pltpu.VMEM((CHUNK, width), f32),
-            pltpu.VMEM((slots, width), f32),
+            pltpu.VMEM((slots if count <= KEPT_BLOCKS else CHUNK, width), f32),
             pltpu.VMEM((ALONG_ROWS, width), bf16),
+            pltpu.VMEM((slots, 8), f32),
+            pltpu.VMEM((2 * CHUNK, width), bf16),
+            pltpu.VMEM((2 * CHUNK, width), bf16),
+            pltpu.VMEM((2 * CHUNK, width), bf16),
+            pltpu.VMEM((2 * CHUNK, width), bf16),
         ],
         compiler_params=pltpu.CompilerParams(vmem_limit_bytes=(16 << 20) + slots * 2688),
         name="sweep",

time: 32.2 us -> 33.8 us (1.050)
  Pallas kernels: 9.66 us -> 11.3 us
    pallas_call x1, Pallas kernels: 9.66 us -> 11.3 us  [sweep(): pl.pallas_call(functools.partial(sweep_kernel, order), out_shape=(parts,...]
where the time goes in v12:
time: 33.8 us; the launch traced here: 33.5 us
  Pallas kernels  11.3 us (33%)
  blocking collectives  10.5 us (31%)
  starting transfers between devices  5.76 us (17%)
  waiting for transfers between devices  3.35 us (10%)
  between operations  1.3 us (4%)
  local copies, waits for them, and re-layouts  0.7 us (2%)
  other arithmetic  0.66 us (2%)
    pallas_call x1, Pallas kernels, sweep(): pl.pallas_call(functools.partial(sweep_kernel, order), out_shape=(parts,...  11.3 us
    all_to_all x1, blocking collectives, local(): lax.all_to_all(speeds.reshape(copies, 1, 128), axes, 0, 0, tiled=True)  10.5 us
    ppermute x3, starting transfers between devices, swapped(): return lax.ppermute(value, axis, pairs)  5.76 us
    ppermute x3, waiting for transfers between devices, swapped(): return lax.ppermute(value, axis, pairs)  3.35 us
    unnamed x3, local copies, waits for them, and re-layouts  0.7 us
  transfers between devices with their start and end apart: 3, of which 3 were waited for; matrix products, arithmetic and copies ran while one was open for 0% of the time, Pallas kernels for 0%

profile of v12, /device:TPU:0, one launch (start us, length us, event | category | flops | bytes accessed | tf_op | source)
XLA Modules:
  0.0 33.5 jit_solution(17219520606007893433)
XLA Ops:
  0.6 0.0 copy-start
  0.6 0.7 %copy.11 = f32[1,3,512]{2,1,0:T(4,128)S(1)} copy(f32[1,3,512]{2,0,1:T(1,128)} %param.3) | data formatting | bytes 12288 | tf_op args[0]
  1.3 0.0 copy-done
  1.4 5.1 %collective-permute-start.2 = (f32[1,8,512]{2,1,0:T(8,128)S(1)}, f32[1,8,512]{2,1,0:T(8,128)S(1)}, u32[]{:S(2)}, u32[]{:S(2)}) collective-permute-start(f32[1,8,512]{2,1,0:T(8,128)S(1)} %select_maximum_fusion.refs_1_), channel_id=1, source_target_pairs={{0,3},{1,2},{2,1},{3,0},{4,7},{5,6},{6,5},{7,4},{8,11},{9,10},{10,... | collective-permute-start | bytes 49160 | tf_op jit(solution)/shard_map/ppermute | solution.py:299
  6.5 0.0 collective-permute-start.1
  6.5 0.6 %collective-permute-start = (f32[1,8,512]{2,1,0:T(8,128)S(1)}, f32[1,8,512]{2,1,0:T(8,128)S(1)}, u32[]{:S(2)}, u32[]{:S(2)}) collective-permute-start(f32[1,8,512]{2,1,0:T(8,128)S(1)} %select_maximum_fusion.refs_1_), channel_id=1, source_target_pairs={{0,2},{1,3},{2,0},{3,1},{4,6},{5,7},{6,4},{7,5},{8,10},{9,11},{10,... | collective-permute-start | bytes 49160 | tf_op jit(solution)/shard_map/ppermute | solution.py:299
  7.8 0.4 %collective-permute-done.2.refs_4_ = f32[1,8,512]{2,1,0:T(8,128)S(1)} collective-permute-done((f32[1,8,512]{2,1,0:T(8,128)S(1)}, f32[1,8,512]{2,1,0:T(8,128)S(1)}, u32[]{:S(2)}, u32[]{:S(2)}) %collective-permute-start.2) | collective-permute-done | bytes 16416 | tf_op jit(solution)/shard_map/ppermute | solution.py:299
  8.2 2.0 %collective-permute-done.1.refs_3_ = f32[1,8,512]{2,1,0:T(8,128)S(1)} collective-permute-done((f32[1,8,512]{2,1,0:T(8,128)S(1)}, f32[1,8,512]{2,1,0:T(8,128)S(1)}, u32[]{:S(2)}, u32[]{:S(2)}) %collective-permute-start.1) | collective-permute-done | bytes 16416 | tf_op jit(solution)/shard_map/ppermute | solution.py:299
  10.2 0.9 %collective-permute-done.refs_2_ = f32[1,8,512]{2,1,0:T(8,128)S(1)} collective-permute-done((f32[1,8,512]{2,1,0:T(8,128)S(1)}, f32[1,8,512]{2,1,0:T(8,128)S(1)}, u32[]{:S(2)}, u32[]{:S(2)}) %collective-permute-start) | collective-permute-done | bytes 16416 | tf_op jit(solution)/shard_map/ppermute | solution.py:299
  11.1 11.3 %sweep.1 = (f32[3,4,128]{2,1,0:T(4,128)}, f32[3,4,128]{2,1,0:T(4,128)S(1)}, f32[3,4,128]{2,1,0:T(4,128)S(1)}, f32[16,128]{1,0:T(8,128)S(1)}) custom-call(s32[1]{0:T(128)S(6)} %copy.15.refs_0_, f32[1,8,512]{2,1,0:T(8,128)S(1)} %select_maximum_fusion.refs_1_, f32[1,8,512]{2,1,0:T(8,128)S(1)} %collective-permute-done.refs_2_, ...), custom_call_target="tpu_custom_call" | custom-call | tf_op jit(solution)/shard_map/sweep/pallas_call | solution.py:268
  22.4 10.5 %all_to_all.5 = f32[16,1,128]{2,1,0:T(1,128)S(1)} all-to-all(f32[16,1,128]{2,1,0:T(1,128)S(1)} %bitcast.6), channel_id=1, replica_groups=mesh['groups'=2,'cells'=4,'sharers'=4] {'cells','sharers'}, dimensions={0} | all-to-all | bytes 16384 | tf_op jit(solution)/shard_map/all_to_all | solution.py:323
  32.9 0.6 %multiply_add_fusion = f32[3,4,128]{2,1,0:T(4,128)} fusion(f32[3,4,128]{2,1,0:T(4,128)S(1)} %get-tuple-element.6, f32[3,4,128]{2,1,0:T(4,128)S(1)} %get-tuple-element.8, f32[128]{0:T(128)S(1)} %add_divide_fusion), kind=kLoop, calls=%fused_computation.2 | loop fusion | flops 3072 | bytes 18944 | tf_op jit(solution)/shard_map/add | solution.py:325
  (3 shorter events, 0.1 us)
Async XLA Ops:
  0.6 0.7 %copy-start = (f32[1,512]{1,0:T(1,128)S(1)}, f32[1,512]{1,0:T(1,128)}, u32[]{:S(2)}) copy-start(f32[1,512]{1,0:T(1,128)} %param.4) | copy-start | bytes 6148
  1.4 6.8 %collective-permute-start.2 = (f32[1,8,512]{2,1,0:T(8,128)S(1)}, f32[1,8,512]{2,1,0:T(8,128)S(1)}, u32[]{:S(2)}, u32[]{:S(2)}) collective-permute-start(f32[1,8,512]{2,1,0:T(8,128)S(1)} %select_maximum_fusion.refs_1_), channel_id=1, source_target_pairs={{0,3},{1,2},{2,1},{3,0},{4,7},{5,6},{6,5},{7,4},{8,11},{9,10},{10,... | collective-permute-start | bytes 49160 | tf_op jit(solution)/shard_map/ppermute | solution.py:299
  6.5 3.7 %collective-permute-start.1 = (f32[1,8,512]{2,1,0:T(8,128)S(1)}, f32[1,8,512]{2,1,0:T(8,128)S(1)}, u32[]{:S(2)}, u32[]{:S(2)}) collective-permute-start(f32[1,8,512]{2,1,0:T(8,128)S(1)} %select_maximum_fusion.refs_1_), channel_id=1, source_target_pairs={{0,1},{1,0},{2,3},{3,2},{4,5},{5,4},{6,7},{7,6},{8,9},{9,8},{10,11... | collective-permute-start | bytes 49160 | tf_op jit(solution)/shard_map/ppermute | solution.py:299
  6.5 4.6 %collective-permute-start = (f32[1,8,512]{2,1,0:T(8,128)S(1)}, f32[1,8,512]{2,1,0:T(8,128)S(1)}, u32[]{:S(2)}, u32[]{:S(2)}) collective-permute-start(f32[1,8,512]{2,1,0:T(8,128)S(1)} %select_maximum_fusion.refs_1_), channel_id=1, source_target_pairs={{0,2},{1,3},{2,0},{3,1},{4,6},{5,7},{6,4},{7,5},{8,10},{9,11},{10,... | collective-permute-start | bytes 49160 | tf_op jit(solution)/shard_map/ppermute | solution.py:299

commit v13 on v11

--- a/solution.py
+++ b/solution.py
@@ -10,7 +10,7 @@
 from jax.sharding import PartitionSpec as P
 
 EPS = 0.35
-SCALE = math.sqrt(math.log2(math.e) / (2.0 * EPS * EPS))
+SCALE = math.sqrt(1.0 / (2.0 * EPS * EPS))
 GRID = 4.0
 TINY = 1e-30
 CHUNK = 512
@@ -144,7 +144,7 @@
     def add_blobs(step, ref):
         tile, chunk = step // chunks, step % chunks
         sums_ref[:, slots(tile, width)] += split_product(
-            moment_ref[:, slots(chunk, CHUNK)], jnp.exp2(ref[...])
+            moment_ref[:, slots(chunk, CHUNK)], jnp.exp(ref[...])
         )
 
     own_exponent_ref[slots(0, CHUNK), :] = exponent(0)

time: 32.2 us -> 32.4 us (level)
  no operation moved by 1% of the time
where the time goes in v13:
time: 32.4 us; the launch traced here: 32.1 us
  blocking collectives  10.5 us (32%)
  Pallas kernels  9.84 us (30%)
  starting transfers between devices  5.76 us (18%)
  waiting for transfers between devices  3.35 us (10%)
  between operations  1.3 us (4%)
  local copies, waits for them, and re-layouts  0.7 us (2%)
  other arithmetic  0.66 us (2%)
    all_to_all x1, blocking collectives, local(): lax.all_to_all(speeds.reshape(copies, 1, 128), axes, 0, 0, tiled=True)  10.5 us
    pallas_call x1, Pallas kernels, sweep(): pl.pallas_call(functools.partial(sweep_kernel, order), out_shape=(parts,...  9.84 us
    ppermute x3, starting transfers between devices, swapped(): return lax.ppermute(value, axis, pairs)  5.76 us
    ppermute x3, waiting for transfers between devices, swapped(): return lax.ppermute(value, axis, pairs)  3.35 us
    unnamed x3, local copies, waits for them, and re-layouts  0.7 us
  transfers between devices with their start and end apart: 3, of which 3 were waited for; matrix products, arithmetic and copies ran while one was open for 0% of the time, Pallas kernels for 0%

profile of v13, /device:TPU:0, one launch (start us, length us, event | category | flops | bytes accessed | tf_op | source)
XLA Modules:
  0.0 32.1 jit_solution(1249293595698001597)
XLA Ops:
  0.6 0.0 copy-start
  0.6 0.7 %copy.11 = f32[1,3,512]{2,1,0:T(4,128)S(1)} copy(f32[1,3,512]{2,0,1:T(1,128)} %param.3) | data formatting | bytes 12288 | tf_op args[0]
  1.3 0.0 copy-done
  1.4 5.1 %collective-permute-start.2 = (f32[1,8,512]{2,1,0:T(8,128)S(1)}, f32[1,8,512]{2,1,0:T(8,128)S(1)}, u32[]{:S(2)}, u32[]{:S(2)}) collective-permute-start(f32[1,8,512]{2,1,0:T(8,128)S(1)} %select_maximum_fusion.refs_1_), channel_id=1, source_target_pairs={{0,3},{1,2},{2,1},{3,0},{4,7},{5,6},{6,5},{7,4},{8,11},{9,10},{10,... | collective-permute-start | bytes 49160 | tf_op jit(solution)/shard_map/ppermute | solution.py:251
  6.5 0.0 collective-permute-start.1
  6.5 0.6 %collective-permute-start = (f32[1,8,512]{2,1,0:T(8,128)S(1)}, f32[1,8,512]{2,1,0:T(8,128)S(1)}, u32[]{:S(2)}, u32[]{:S(2)}) collective-permute-start(f32[1,8,512]{2,1,0:T(8,128)S(1)} %select_maximum_fusion.refs_1_), channel_id=1, source_target_pairs={{0,2},{1,3},{2,0},{3,1},{4,6},{5,7},{6,4},{7,5},{8,10},{9,11},{10,... | collective-permute-start | bytes 49160 | tf_op jit(solution)/shard_map/ppermute | solution.py:251
  7.8 0.4 %collective-permute-done.2.refs_4_ = f32[1,8,512]{2,1,0:T(8,128)S(1)} collective-permute-done((f32[1,8,512]{2,1,0:T(8,128)S(1)}, f32[1,8,512]{2,1,0:T(8,128)S(1)}, u32[]{:S(2)}, u32[]{:S(2)}) %collective-permute-start.2) | collective-permute-done | bytes 16416 | tf_op jit(solution)/shard_map/ppermute | solution.py:251
  8.2 2.0 %collective-permute-done.1.refs_3_ = f32[1,8,512]{2,1,0:T(8,128)S(1)} collective-permute-done((f32[1,8,512]{2,1,0:T(8,128)S(1)}, f32[1,8,512]{2,1,0:T(8,128)S(1)}, u32[]{:S(2)}, u32[]{:S(2)}) %collective-permute-start.1) | collective-permute-done | bytes 16416 | tf_op jit(solution)/shard_map/ppermute | solution.py:251
  10.2 0.9 %collective-permute-done.refs_2_ = f32[1,8,512]{2,1,0:T(8,128)S(1)} collective-permute-done((f32[1,8,512]{2,1,0:T(8,128)S(1)}, f32[1,8,512]{2,1,0:T(8,128)S(1)}, u32[]{:S(2)}, u32[]{:S(2)}) %collective-permute-start) | collective-permute-done | bytes 16416 | tf_op jit(solution)/shard_map/ppermute | solution.py:251
  11.1 9.8 %sweep.1 = (f32[3,4,128]{2,1,0:T(4,128)}, f32[3,4,128]{2,1,0:T(4,128)S(1)}, f32[3,4,128]{2,1,0:T(4,128)S(1)}, f32[16,128]{1,0:T(8,128)S(1)}) custom-call(s32[1]{0:T(128)S(6)} %copy.15.refs_0_, f32[1,8,512]{2,1,0:T(8,128)S(1)} %select_maximum_fusion.refs_1_, f32[1,8,512]{2,1,0:T(8,128)S(1)} %collective-permute-done.refs_2_, ...), custom_call_target="tpu_custom_call" | custom-call | tf_op jit(solution)/shard_map/sweep/pallas_call | solution.py:225
  21.0 10.5 %all_to_all.5 = f32[16,1,128]{2,1,0:T(1,128)S(1)} all-to-all(f32[16,1,128]{2,1,0:T(1,128)S(1)} %bitcast.6), channel_id=1, replica_groups=mesh['groups'=2,'cells'=4,'sharers'=4] {'cells','sharers'}, dimensions={0} | all-to-all | bytes 16384 | tf_op jit(solution)/shard_map/all_to_all | solution.py:275
  31.5 0.6 %multiply_add_fusion = f32[3,4,128]{2,1,0:T(4,128)} fusion(f32[3,4,128]{2,1,0:T(4,128)S(1)} %get-tuple-element.6, f32[3,4,128]{2,1,0:T(4,128)S(1)} %get-tuple-element.8, f32[128]{0:T(128)S(1)} %add_divide_fusion), kind=kLoop, calls=%fused_computation.2 | loop fusion | flops 3072 | bytes 18944 | tf_op jit(solution)/shard_map/add | solution.py:277
  (3 shorter events, 0.1 us)
Async XLA Ops:
  0.6 0.7 %copy-start = (f32[1,512]{1,0:T(1,128)S(1)}, f32[1,512]{1,0:T(1,128)}, u32[]{:S(2)}) copy-start(f32[1,512]{1,0:T(1,128)} %param.4) | copy-start | bytes 6148
  1.4 6.8 %collective-permute-start.2 = (f32[1,8,512]{2,1,0:T(8,128)S(1)}, f32[1,8,512]{2,1,0:T(8,128)S(1)}, u32[]{:S(2)}, u32[]{:S(2)}) collective-permute-start(f32[1,8,512]{2,1,0:T(8,128)S(1)} %select_maximum_fusion.refs_1_), channel_id=1, source_target_pairs={{0,3},{1,2},{2,1},{3,0},{4,7},{5,6},{6,5},{7,4},{8,11},{9,10},{10,... | collective-permute-start | bytes 49160 | tf_op jit(solution)/shard_map/ppermute | solution.py:251
  6.5 3.7 %collective-permute-start.1 = (f32[1,8,512]{2,1,0:T(8,128)S(1)}, f32[1,8,512]{2,1,0:T(8,128)S(1)}, u32[]{:S(2)}, u32[]{:S(2)}) collective-permute-start(f32[1,8,512]{2,1,0:T(8,128)S(1)} %select_maximum_fusion.refs_1_), channel_id=1, source_target_pairs={{0,1},{1,0},{2,3},{3,2},{4,5},{5,4},{6,7},{7,6},{8,9},{9,8},{10,11... | collective-permute-start | bytes 49160 | tf_op jit(solution)/shard_map/ppermute | solution.py:251
  6.5 4.6 %collective-permute-start = (f32[1,8,512]{2,1,0:T(8,128)S(1)}, f32[1,8,512]{2,1,0:T(8,128)S(1)}, u32[]{:S(2)}, u32[]{:S(2)}) collective-permute-start(f32[1,8,512]{2,1,0:T(8,128)S(1)} %select_maximum_fusion.refs_1_), channel_id=1, source_target_pairs={{0,2},{1,3},{2,0},{3,1},{4,6},{5,7},{6,4},{7,5},{8,10},{9,11},{10,... | collective-permute-start | bytes 49160 | tf_op jit(solution)/shard_map/ppermute | solution.py:251

commit v14 on v11

--- a/solution.py
+++ b/solution.py
@@ -13,7 +13,8 @@
 SCALE = math.sqrt(math.log2(math.e) / (2.0 * EPS * EPS))
 GRID = 4.0
 TINY = 1e-30
-CHUNK = 512
+GROUP = 16
+KEPT_BLOCKS = 4
 DISTANCE_ROWS = 96
 ALONG_ROWS = 112
 bf16, f32 = jnp.bfloat16, jnp.float32
@@ -93,12 +94,21 @@
     return jnp.dot(left, right, preferred_element_type=f32)
 
 
-def split_product(left, matrix):
+def store_split(ref, rows, matrix):
+    half = ref.shape[0] // 2
     upper = matrix.astype(bf16)
-    lower = (matrix - upper.astype(f32)).astype(bf16)
-    return product(
-        jnp.concatenate([left, left], axis=1), jnp.concatenate([upper, lower], axis=0)
-    )
+    ref[rows, :] = upper
+    ref[pl.ds(half + rows.start, rows.size), :] = (matrix - upper.astype(f32)).astype(bf16)
+
+
+def sum_rows(left, ref):
+    return product(jnp.concatenate([left, left], axis=1), ref[...])
+
+
+def sum_columns(left, ref):
+    both = lax.dot_general(left, ref[...], (((1,), (1,)), ((), ())), preferred_element_type=f32)
+    half = ref.shape[0] // 2
+    return both[:, :half] + both[:, half:]
 
 
 def joined(total):
@@ -111,11 +121,10 @@
     filled, blocks, refs = refs[0], refs[1 : count + 1], refs[count + 1 :]
     scores_out, drift_out, start_out, speed_out, key_ref, query_ref, moment_ref = refs[:7]
     along_ref, flux_ref, sums_ref, cubes_ref, linear_ref, even_ref, odd_ref = refs[7:14]
-    own_exponent_ref, own_along_ref = refs[14:]
+    own_exponent_ref, own_along_ref, *split_refs = refs[14:]
     width = blocks[0].shape[2]
     total_slots = count * width
-    chunks = total_slots // CHUNK
-    steps = chunks * count
+    kept = count <= KEPT_BLOCKS
     here = lax.axis_index("sharers")
 
     def slots(index, size):
@@ -136,37 +145,45 @@
     moment_ref[...] = weighted_rows(weight, place)
     sums_ref[...] = jnp.zeros_like(sums_ref)
 
-    def exponent(step):
-        step = jnp.minimum(step, steps - 1)
-        tile, chunk = step // chunks, step % chunks
-        return product(key_ref[slots(chunk, CHUNK), :], query_ref[:, slots(tile, width)])
-
-    def add_blobs(step, ref):
-        tile, chunk = step // chunks, step % chunks
-        sums_ref[:, slots(tile, width)] += split_product(
-            moment_ref[:, slots(chunk, CHUNK)], jnp.exp2(ref[...])
-        )
-
-    own_exponent_ref[slots(0, CHUNK), :] = exponent(0)
-
-    def own_density(chunk, carry):
-        later = jnp.minimum(chunk + 1, chunks - 1)
-        own_exponent_ref[slots(later, CHUNK), :] = exponent(later)
-        add_blobs(chunk, own_exponent_ref.at[slots(chunk, CHUNK), :])
-        return carry
-
-    lax.fori_loop(0, chunks, own_density, 0, unroll=count <= 4)
-    even_ref[...] = exponent(chunks)
-
-    def density(pair, carry):
-        step = chunks + pair * 2
-        odd_ref[...] = exponent(step + 1)
-        add_blobs(step, even_ref)
-        even_ref[...] = exponent(step + 2)
-        add_blobs(step + 1, odd_ref)
-        return carry
-
-    lax.fori_loop(0, (steps - chunks) // 2, density, 0)
+    def exponent(key_block, query_block):
+        return product(key_ref[slots(key_block, width), :], query_ref[:, slots(query_block, width)])
+
+    def add_blobs(key_block, query_block, ref, split, both):
+        for group in range(0, width, GROUP):
+            rows = pl.ds(group, GROUP)
+            store_split(split, rows, jnp.exp2(ref[rows, :]))
+        keys, queries = slots(key_block, width), slots(query_block, width)
+        sums_ref[:, queries] += sum_rows(moment_ref[:, keys], split)
+        if both:
+            sums_ref[:, keys] += sum_columns(moment_ref[:, queries], split)
+
+    if kept:
+        pairs = [(key, query) for query in range(count) for key in range(query, count)]
+        buffers = [even_ref, odd_ref]
+
+        def buffer(index):
+            key, query = pairs[index]
+            return own_exponent_ref.at[slots(key, width), :] if query == 0 else buffers[index % 2]
+
+        buffer(0)[...] = exponent(*pairs[0])
+        for index, (key, query) in enumerate(pairs):
+            if index + 1 < len(pairs):
+                buffer(index + 1)[...] = exponent(*pairs[index + 1])
+            add_blobs(key, query, buffer(index), split_refs[index % 2], key != query)
+    else:
+
+        def whole_row(query, carry):
+            even_ref[...] = exponent(query, query)
+            add_blobs(query, query, even_ref, split_refs[0], False)
+
+            def one(key, carry):
+                even_ref[...] = exponent(key, query)
+                add_blobs(key, query, even_ref, split_refs[0], True)
+                return carry
+
+            return lax.fori_loop(query + 1, count, one, carry)
+
+        lax.fori_loop(0, count, whole_row, 0)
 
     sums = joined(sums_ref[...])
     live = weight > 0.0
@@ -181,28 +198,38 @@
     cubes_ref[...] = jnp.zeros_like(cubes_ref)
     linear_ref[...] = jnp.zeros_like(linear_ref)
 
-    def along(chunk):
-        keys = slots(jnp.minimum(chunk, chunks - 1), CHUNK)
-        return product(along_ref[keys, :], own_along_ref[...])
-
-    def add_drift(chunk, ref):
-        keys = slots(chunk, CHUNK)
-        negative = jnp.minimum(own_exponent_ref[keys, :], -TINY)
-        distance = negative * lax.rsqrt(-negative)
-        cubes_ref[...] += split_product(flux_ref[:, keys], negative * distance)
-        linear_ref[...] += split_product(moment_ref[:, keys], ref[...] * distance)
-
-    even_ref[...] = along(0)
-
-    def drift_pair(pair, carry):
-        chunk = pair * 2
-        odd_ref[...] = along(chunk + 1)
-        add_drift(chunk, even_ref)
-        even_ref[...] = along(chunk + 2)
-        add_drift(chunk + 1, odd_ref)
-        return carry
-
-    lax.fori_loop(0, chunks // 2, drift_pair, 0)
+    def along(block):
+        return product(along_ref[slots(block, width), :], own_along_ref[...])
+
+    def add_drift(block, ref, cubes_split, linear_split):
+        if not kept:
+            own_exponent_ref[...] = exponent(block, 0)
+        for group in range(0, width, GROUP):
+            rows = pl.ds(group, GROUP)
+            first = block * width + group if kept else group
+            negative = jnp.minimum(own_exponent_ref[pl.ds(first, GROUP), :], -TINY)
+            distance = negative * lax.rsqrt(-negative)
+            store_split(cubes_split, rows, negative * distance)
+            store_split(linear_split, rows, ref[rows, :] * distance)
+        keys = slots(block, width)
+        cubes_ref[...] += sum_rows(flux_ref[:, keys], cubes_split)
+        linear_ref[...] += sum_rows(moment_ref[:, keys], linear_split)
+
+    if kept:
+        even_ref[...] = along(0)
+        for block in range(count):
+            if block + 1 < count:
+                buffers[(block + 1) % 2][...] = along(block + 1)
+            first = 2 * (block % 2)
+            add_drift(block, buffers[block % 2], *split_refs[first : first + 2])
+    else:
+
+        def drift_block(block, carry):
+            even_ref[...] = along(block)
+            add_drift(block, even_ref, *split_refs[0:2])
+            return carry
+
+        lax.fori_loop(0, count, drift_block, 0)
     cubes, linear = joined(cubes_ref[...]), joined(linear_ref[...])
     drift = score * cubes[3:4] - cubes + place * linear[3:4] - linear
     factor = -1.0 / (SCALE * SCALE * SCALE * total_slots)
@@ -236,11 +263,12 @@
             pltpu.VMEM((16, slots), f32),
             pltpu.VMEM((16, width), f32),
             pltpu.VMEM((16, width), f32),
-            pltpu.VMEM((CHUNK, width), f32),
-            pltpu.VMEM((CHUNK, width), f32),
-            pltpu.VMEM((slots, width), f32),
+            pltpu.VMEM((width, width), f32),
+            pltpu.VMEM((width, width), f32),
+            pltpu.VMEM((slots if count <= KEPT_BLOCKS else width, width), f32),
             pltpu.VMEM((ALONG_ROWS, width), bf16),
-        ],
+        ]
+        + [pltpu.VMEM((2 * width, width), bf16)] * 4,
         compiler_params=pltpu.CompilerParams(vmem_limit_bytes=(16 << 20) + slots * 2688),
         name="sweep",
     )(counts, *blocks)

time: 32.2 us -> 29.8 us (0.925)
  Pallas kernels: 9.66 us -> 7.31 us
    pallas_call x1, Pallas kernels: 9.66 us -> 7.31 us  [sweep(): pl.pallas_call(functools.partial(sweep_kernel, order), out_shape=(parts,...]
where the time goes in v14:
time: 29.8 us; the launch traced here: 29.6 us
  blocking collectives  10.5 us (35%)
  Pallas kernels  7.31 us (25%)
  starting transfers between devices  5.76 us (19%)
  waiting for transfers between devices  3.35 us (11%)
  between operations  1.3 us (4%)
  local copies, waits for them, and re-layouts  0.7 us (2%)
  other arithmetic  0.66 us (2%)
    all_to_all x1, blocking collectives, local(): lax.all_to_all(speeds.reshape(copies, 1, 128), axes, 0, 0, tiled=True)  10.5 us
    pallas_call x1, Pallas kernels, sweep(): pl.pallas_call(functools.partial(sweep_kernel, order), out_shape=(parts,...  7.31 us
    ppermute x3, starting transfers between devices, swapped(): return lax.ppermute(value, axis, pairs)  5.76 us
    ppermute x3, waiting for transfers between devices, swapped(): return lax.ppermute(value, axis, pairs)  3.35 us
    unnamed x3, local copies, waits for them, and re-layouts  0.7 us
    add x1, other arithmetic, local(): moved = start + time_step * drift  0.61 us
  transfers between devices with their start and end apart: 3, of which 3 were waited for; matrix products, arithmetic and copies ran while one was open for 0% of the time, Pallas kernels for 0%

profile of v14, /device:TPU:0, one launch (start us, length us, event | category | flops | bytes accessed | tf_op | source)
XLA Modules:
  0.0 29.6 jit_solution(2535359643189186737)
XLA Ops:
  0.6 0.0 copy-start
  0.6 0.7 %copy.11 = f32[1,3,512]{2,1,0:T(4,128)S(1)} copy(f32[1,3,512]{2,0,1:T(1,128)} %param.3) | data formatting | bytes 12288 | tf_op args[0]
  1.3 0.0 copy-done
  1.4 5.1 %collective-permute-start.2 = (f32[1,8,512]{2,1,0:T(8,128)S(1)}, f32[1,8,512]{2,1,0:T(8,128)S(1)}, u32[]{:S(2)}, u32[]{:S(2)}) collective-permute-start(f32[1,8,512]{2,1,0:T(8,128)S(1)} %select_maximum_fusion.refs_1_), channel_id=1, source_target_pairs={{0,3},{1,2},{2,1},{3,0},{4,7},{5,6},{6,5},{7,4},{8,11},{9,10},{10,... | collective-permute-start | bytes 49160 | tf_op jit(solution)/shard_map/ppermute | solution.py:279
  6.5 0.0 collective-permute-start.1
  6.5 0.6 %collective-permute-start = (f32[1,8,512]{2,1,0:T(8,128)S(1)}, f32[1,8,512]{2,1,0:T(8,128)S(1)}, u32[]{:S(2)}, u32[]{:S(2)}) collective-permute-start(f32[1,8,512]{2,1,0:T(8,128)S(1)} %select_maximum_fusion.refs_1_), channel_id=1, source_target_pairs={{0,2},{1,3},{2,0},{3,1},{4,6},{5,7},{6,4},{7,5},{8,10},{9,11},{10,... | collective-permute-start | bytes 49160 | tf_op jit(solution)/shard_map/ppermute | solution.py:279
  7.8 0.4 %collective-permute-done.2.refs_4_ = f32[1,8,512]{2,1,0:T(8,128)S(1)} collective-permute-done((f32[1,8,512]{2,1,0:T(8,128)S(1)}, f32[1,8,512]{2,1,0:T(8,128)S(1)}, u32[]{:S(2)}, u32[]{:S(2)}) %collective-permute-start.2) | collective-permute-done | bytes 16416 | tf_op jit(solution)/shard_map/ppermute | solution.py:279
  8.2 2.0 %collective-permute-done.1.refs_3_ = f32[1,8,512]{2,1,0:T(8,128)S(1)} collective-permute-done((f32[1,8,512]{2,1,0:T(8,128)S(1)}, f32[1,8,512]{2,1,0:T(8,128)S(1)}, u32[]{:S(2)}, u32[]{:S(2)}) %collective-permute-start.1) | collective-permute-done | bytes 16416 | tf_op jit(solution)/shard_map/ppermute | solution.py:279
  10.2 0.9 %collective-permute-done.refs_2_ = f32[1,8,512]{2,1,0:T(8,128)S(1)} collective-permute-done((f32[1,8,512]{2,1,0:T(8,128)S(1)}, f32[1,8,512]{2,1,0:T(8,128)S(1)}, u32[]{:S(2)}, u32[]{:S(2)}) %collective-permute-start) | collective-permute-done | bytes 16416 | tf_op jit(solution)/shard_map/ppermute | solution.py:279
  11.1 7.3 %sweep.1 = (f32[3,4,128]{2,1,0:T(4,128)}, f32[3,4,128]{2,1,0:T(4,128)S(1)}, f32[3,4,128]{2,1,0:T(4,128)S(1)}, f32[16,128]{1,0:T(8,128)S(1)}) custom-call(s32[1]{0:T(128)S(6)} %copy.15.refs_0_, f32[1,8,512]{2,1,0:T(8,128)S(1)} %select_maximum_fusion.refs_1_, f32[1,8,512]{2,1,0:T(8,128)S(1)} %collective-permute-done.refs_2_, ...), custom_call_target="tpu_custom_call" | custom-call | tf_op jit(solution)/shard_map/sweep/pallas_call | solution.py:252
  18.4 10.5 %all_to_all.5 = f32[16,1,128]{2,1,0:T(1,128)S(1)} all-to-all(f32[16,1,128]{2,1,0:T(1,128)S(1)} %bitcast.6), channel_id=1, replica_groups=mesh['groups'=2,'cells'=4,'sharers'=4] {'cells','sharers'}, dimensions={0} | all-to-all | bytes 16384 | tf_op jit(solution)/shard_map/all_to_all | solution.py:303
  29.0 0.6 %multiply_add_fusion = f32[3,4,128]{2,1,0:T(4,128)} fusion(f32[3,4,128]{2,1,0:T(4,128)S(1)} %get-tuple-element.6, f32[3,4,128]{2,1,0:T(4,128)S(1)} %get-tuple-element.8, f32[128]{0:T(128)S(1)} %add_divide_fusion), kind=kLoop, calls=%fused_computation.2 | loop fusion | flops 3072 | bytes 18944 | tf_op jit(solution)/shard_map/add | solution.py:305
  (3 shorter events, 0.1 us)
Async XLA Ops:
  0.6 0.7 %copy-start = (f32[1,512]{1,0:T(1,128)S(1)}, f32[1,512]{1,0:T(1,128)}, u32[]{:S(2)}) copy-start(f32[1,512]{1,0:T(1,128)} %param.4) | copy-start | bytes 6148
  1.4 6.8 %collective-permute-start.2 = (f32[1,8,512]{2,1,0:T(8,128)S(1)}, f32[1,8,512]{2,1,0:T(8,128)S(1)}, u32[]{:S(2)}, u32[]{:S(2)}) collective-permute-start(f32[1,8,512]{2,1,0:T(8,128)S(1)} %select_maximum_fusion.refs_1_), channel_id=1, source_target_pairs={{0,3},{1,2},{2,1},{3,0},{4,7},{5,6},{6,5},{7,4},{8,11},{9,10},{10,... | collective-permute-start | bytes 49160 | tf_op jit(solution)/shard_map/ppermute | solution.py:279
  6.5 3.7 %collective-permute-start.1 = (f32[1,8,512]{2,1,0:T(8,128)S(1)}, f32[1,8,512]{2,1,0:T(8,128)S(1)}, u32[]{:S(2)}, u32[]{:S(2)}) collective-permute-start(f32[1,8,512]{2,1,0:T(8,128)S(1)} %select_maximum_fusion.refs_1_), channel_id=1, source_target_pairs={{0,1},{1,0},{2,3},{3,2},{4,5},{5,4},{6,7},{7,6},{8,9},{9,8},{10,11... | collective-permute-start | bytes 49160 | tf_op jit(solution)/shard_map/ppermute | solution.py:279
  6.5 4.6 %collective-permute-start = (f32[1,8,512]{2,1,0:T(8,128)S(1)}, f32[1,8,512]{2,1,0:T(8,128)S(1)}, u32[]{:S(2)}, u32[]{:S(2)}) collective-permute-start(f32[1,8,512]{2,1,0:T(8,128)S(1)} %select_maximum_fusion.refs_1_), channel_id=1, source_target_pairs={{0,2},{1,3},{2,0},{3,1},{4,6},{5,7},{6,4},{7,5},{8,10},{9,11},{10,... | collective-permute-start | bytes 49160 | tf_op jit(solution)/shard_map/ppermute | solution.py:279

commit v15 on v14

--- a/solution.py
+++ b/solution.py
@@ -16,7 +16,7 @@
 GROUP = 16
 KEPT_BLOCKS = 4
 DISTANCE_ROWS = 96
-ALONG_ROWS = 112
+DRIFT_ROWS = 64
 bf16, f32 = jnp.bfloat16, jnp.float32
 
 
@@ -72,17 +72,6 @@
     return stacked(key), stacked(query)
 
 
-def along_features(parts, score, is_key):
-    coarse, fine, rest = parts
-    first, second, third = pieces(-score, 3)
-    query_dot, key_dot = scalar_groups(rows_sum((coarse + fine + rest) * score), coarse)
-    places = [coarse, coarse, coarse, fine, fine, rest]
-    turns = [first, second, third, first, second, first]
-    if is_key:
-        return stacked([key_dot] + turns + places)
-    return stacked([query_dot] + places + turns)
-
-
 def weighted_rows(weight, value):
     row = row_of(value)
     whole = jnp.where(row < 3, value, jnp.where(row == 3, 1.0, 0.0)) * weight
@@ -116,15 +105,47 @@
     return upper + lower + pltpu.roll(lower, 4, 0)
 
 
+def drift_rows(weight, place, score):
+    row = row_of(place)
+    base = place + jnp.where(row == 3, 1.0, 0.0) + pltpu.roll(score, 4, 0)
+    cubic = rows_sum(place * place) * score - rows_sum(place * score) * place
+    groups = [weight * base]
+    for i in range(3):
+        here = slice(i, i + 1)
+        groups.append(weight * jnp.where(row == 3, cubic[here], place[here] * base))
+    return stacked(sum(map(list, zip(*[pieces(group, 2) for group in groups])), []))
+
+
+def drift_sum(total, place, score):
+    row = row_of(place)
+    total = total[0:32] + total[32:64]
+    first, *rest = [total[8 * i : 8 * i + 8] for i in range(4)]
+    turned = [pltpu.roll(group, 4, 0) for group in rest]
+    count, scores = first[3:4], pltpu.roll(first, 4, 0)
+    square, both = rows_sum(place * place), rows_sum(place * score)
+    trace = rest[0][0:1] + rest[1][1:2] + rest[2][2:3]
+    cross = turned[0][0:1] + turned[1][1:2] + turned[2][2:3]
+    drift = score * (square * count - 2.0 * rows_sum(place * first) + trace) - square * scores
+    drift += both * first + place * (
+        rows_sum(place * scores) + rows_sum(score * first) - both * count - cross
+    )
+    ends = []
+    for i in range(3):
+        here = slice(i, i + 1)
+        drift += 2.0 * place[here] * turned[i] - score[here] * rest[i]
+        ends.append(rows_sum(place * turned[i]) + rest[i][3:4])
+    return drift - jnp.where(row == 0, ends[0], jnp.where(row == 1, ends[1], ends[2]))
+
+
 def sweep_kernel(order, *refs):
     count = len(order)
     filled, blocks, refs = refs[0], refs[1 : count + 1], refs[count + 1 :]
     scores_out, drift_out, start_out, speed_out, key_ref, query_ref, moment_ref = refs[:7]
-    along_ref, flux_ref, sums_ref, cubes_ref, linear_ref, even_ref, odd_ref = refs[7:14]
-    own_exponent_ref, own_along_ref, *split_refs = refs[14:]
+    flux_ref, sums_ref, totals_ref, exponent_ref, *split_refs = refs[7:]
     width = blocks[0].shape[2]
     total_slots = count * width
     kept = count <= KEPT_BLOCKS
+    pairs = [(key, query) for query in range(count) for key in range(query, count)]
     here = lax.axis_index("sharers")
 
     def slots(index, size):
@@ -143,6 +164,8 @@
     key_ref[...] = key.T
     query_ref[...] = query
     moment_ref[...] = weighted_rows(weight, place)
+    middle = jnp.sum(place * weight, axis=1, keepdims=True)
+    middle = middle / jnp.sum(weight, axis=1, keepdims=True)
     sums_ref[...] = jnp.zeros_like(sums_ref)
 
     def exponent(key_block, query_block):
@@ -158,27 +181,24 @@
             sums_ref[:, keys] += sum_columns(moment_ref[:, queries], split)
 
     if kept:
-        pairs = [(key, query) for query in range(count) for key in range(query, count)]
-        buffers = [even_ref, odd_ref]
-
-        def buffer(index):
-            key, query = pairs[index]
-            return own_exponent_ref.at[slots(key, width), :] if query == 0 else buffers[index % 2]
-
-        buffer(0)[...] = exponent(*pairs[0])
+
+        def tile(index):
+            return exponent_ref.at[slots(index, width), :]
+
+        tile(0)[...] = exponent(*pairs[0])
         for index, (key, query) in enumerate(pairs):
             if index + 1 < len(pairs):
-                buffer(index + 1)[...] = exponent(*pairs[index + 1])
-            add_blobs(key, query, buffer(index), split_refs[index % 2], key != query)
+                tile(index + 1)[...] = exponent(*pairs[index + 1])
+            add_blobs(key, query, tile(index), split_refs[index % 2], key != query)
     else:
 
         def whole_row(query, carry):
-            even_ref[...] = exponent(query, query)
-            add_blobs(query, query, even_ref, split_refs[0], False)
+            exponent_ref[...] = exponent(query, query)
+            add_blobs(query, query, exponent_ref, split_refs[0], False)
 
             def one(key, carry):
-                even_ref[...] = exponent(key, query)
-                add_blobs(key, query, even_ref, split_refs[0], True)
+                exponent_ref[...] = exponent(key, query)
+                add_blobs(key, query, exponent_ref, split_refs[0], True)
                 return carry
 
             return lax.fori_loop(query + 1, count, one, carry)
@@ -190,50 +210,37 @@
     density_sum = jnp.where(live, sums[3:4], 1.0)
     pull = place * density_sum - sums
     score = jnp.where(vector & live, pull / (-SCALE * EPS * EPS * density_sum), 0.0)
-    along_ref[...] = along_features(parts, score, True).T
-    flux_ref[...] = weighted_rows(weight, score)
-
-    place, score, live = place[:, 0:width], score[:, 0:width], live[:, 0:width]
-    own_along_ref[...] = along_features([part[:, 0:width] for part in parts], score, False)
-    cubes_ref[...] = jnp.zeros_like(cubes_ref)
-    linear_ref[...] = jnp.zeros_like(linear_ref)
-
-    def along(block):
-        return product(along_ref[slots(block, width), :], own_along_ref[...])
-
-    def add_drift(block, ref, cubes_split, linear_split):
-        if not kept:
-            own_exponent_ref[...] = exponent(block, 0)
+    centred = jnp.where(vector, place - middle, 0.0)
+    flux_ref[...] = drift_rows(weight, centred, score)
+    totals_ref[...] = jnp.zeros_like(totals_ref)
+
+    def add_distances(key_block, query_block, ref, split, both):
         for group in range(0, width, GROUP):
             rows = pl.ds(group, GROUP)
-            first = block * width + group if kept else group
-            negative = jnp.minimum(own_exponent_ref[pl.ds(first, GROUP), :], -TINY)
-            distance = negative * lax.rsqrt(-negative)
-            store_split(cubes_split, rows, negative * distance)
-            store_split(linear_split, rows, ref[rows, :] * distance)
-        keys = slots(block, width)
-        cubes_ref[...] += sum_rows(flux_ref[:, keys], cubes_split)
-        linear_ref[...] += sum_rows(moment_ref[:, keys], linear_split)
+            negative = jnp.minimum(ref[rows, :], -TINY)
+            store_split(split, rows, negative * lax.rsqrt(-negative))
+        keys, queries = slots(key_block, width), slots(query_block, width)
+        totals_ref[:, queries] += sum_rows(flux_ref[:, keys], split)
+        if both:
+            totals_ref[:, keys] += sum_columns(flux_ref[:, queries], split)
 
     if kept:
-        even_ref[...] = along(0)
-        for block in range(count):
-            if block + 1 < count:
-                buffers[(block + 1) % 2][...] = along(block + 1)
-            first = 2 * (block % 2)
-            add_drift(block, buffers[block % 2], *split_refs[first : first + 2])
+        for index, (key, query) in enumerate(pairs):
+            add_distances(key, query, tile(index), split_refs[index % 2], key != query)
+        spread = total_slots
     else:
 
-        def drift_block(block, carry):
-            even_ref[...] = along(block)
-            add_drift(block, even_ref, *split_refs[0:2])
+        def one_block(key, carry):
+            exponent_ref[...] = exponent(key, 0)
+            add_distances(key, 0, exponent_ref, split_refs[0], False)
             return carry
 
-        lax.fori_loop(0, count, drift_block, 0)
-    cubes, linear = joined(cubes_ref[...]), joined(linear_ref[...])
-    drift = score * cubes[3:4] - cubes + place * linear[3:4] - linear
-    factor = -1.0 / (SCALE * SCALE * SCALE * total_slots)
-    drift = jnp.where(live & vector[:, 0:width], drift * factor, 0.0)
+        lax.fori_loop(0, count, one_block, 0)
+        spread = width
+
+    drift = drift_sum(totals_ref[...], centred[:, 0:spread], score[:, 0:spread])
+    factor = 1.0 / (SCALE * SCALE * SCALE * total_slots)
+    drift = jnp.where((vector & live)[:, 0:spread], drift * factor, 0.0)
     largest = jnp.max(rows_sum(drift * drift), axis=1, keepdims=True)
     speed_out[...] = jnp.broadcast_to(jnp.sqrt(largest), speed_out.shape)
     for part in range(width // 128):
@@ -247,6 +254,7 @@
 def sweep(counts, blocks, order, copies):
     count, width = len(blocks), blocks[0].shape[2]
     slots = count * width
+    kept = count <= KEPT_BLOCKS
     parts = jax.ShapeDtypeStruct((3, width // 128, 128), f32)
     whole = pl.BlockSpec(memory_space=pltpu.VMEM)
     return pl.pallas_call(
@@ -258,17 +266,12 @@
             pltpu.VMEM((slots, DISTANCE_ROWS), bf16),
             pltpu.VMEM((DISTANCE_ROWS, slots), bf16),
             pltpu.VMEM((16, slots), bf16),
-            pltpu.VMEM((slots, ALONG_ROWS), bf16),
-            pltpu.VMEM((16, slots), bf16),
+            pltpu.VMEM((DRIFT_ROWS, slots), bf16),
             pltpu.VMEM((16, slots), f32),
-            pltpu.VMEM((16, width), f32),
-            pltpu.VMEM((16, width), f32),
-            pltpu.VMEM((width, width), f32),
-            pltpu.VMEM((width, width), f32),
-            pltpu.VMEM((slots if count <= KEPT_BLOCKS else width, width), f32),
-            pltpu.VMEM((ALONG_ROWS, width), bf16),
+            pltpu.VMEM((DRIFT_ROWS, slots if kept else width), f32),
+            pltpu.VMEM((count * (count + 1) // 2 * width if kept else width, width), f32),
         ]
-        + [pltpu.VMEM((2 * width, width), bf16)] * 4,
+        + [pltpu.VMEM((2 * width, width), bf16)] * 2,
         compiler_params=pltpu.CompilerParams(vmem_limit_bytes=(16 << 20) + slots * 2688),
         name="sweep",
     )(counts, *blocks)
@@ -293,16 +296,23 @@
     return [block[i : i + 1] for i in range(size)], list(range(size))
 
 
+def largest_speed(speeds, whole_cell):
+    if not whole_cell:
+        axes = ("cells", "sharers")
+        return jnp.max(lax.all_to_all(speeds[:, None], axes, 0, 0, tiled=True), axis=0)
+    for step in bits(lax.axis_size("cells")):
+        speeds = jnp.maximum(speeds, swapped(speeds, "cells", step))
+    return speeds[0:1]
+
+
 def local(velocities, weights, counts):
-    axes = ("cells", "sharers")
-    blocks, order = gathered(
-        jnp.pad(jnp.concatenate([velocities, weights[:, None]], axis=1), ((0, 0), (0, 4), (0, 0)))
-    )
-    copies = lax.axis_size(axes)
+    package = jnp.concatenate([velocities, weights[:, None]], axis=1)
+    blocks, order = gathered(jnp.pad(package, ((0, 0), (0, 4), (0, 0))))
+    whole_cell = len(blocks) <= KEPT_BLOCKS
+    copies = 8 if whole_cell else lax.axis_size(("cells", "sharers"))
     scores, drift, start, speeds = sweep(counts, blocks, order, copies)
-    speeds = lax.all_to_all(speeds.reshape(copies, 1, 128), axes, 0, 0, tiled=True)
-    time_step = 0.5 / (jnp.max(speeds, axis=0, keepdims=True) + 1e-06)
-    moved = start + time_step * drift
+    time_step = 0.5 / (largest_speed(speeds, whole_cell) + 1e-06)
+    moved = start + time_step[None] * drift
     return moved.reshape(velocities.shape), scores.reshape(velocities.shape)
 
 

time: 29.8 us -> 26.6 us (0.89)
  blocking collectives: 10.5 us -> 0 us
  waiting for transfers between devices: 3.35 us -> 6.63 us
  Pallas kernels: 7.31 us -> 9.88 us
  starting transfers between devices: 5.76 us -> 7.25 us
    all_to_all x1 -> x0, blocking collectives: 10.5 us -> none  [local(): lax.all_to_all(speeds.reshape(copies, 1, 128), axes, 0, 0, tiled=True)]
    ppermute x3 -> x5, waiting for transfers between devices: 3.35 us -> 6.63 us  [swapped(): return lax.ppermute(value, axis, pairs)]
    pallas_call x1, Pallas kernels: 7.31 us -> 9.88 us  [sweep(): pl.pallas_call(functools.partial(sweep_kernel, order), out_shape=(parts,...]
    ppermute x3 -> x5, starting transfers between devices: 5.76 us -> 7.25 us  [swapped(): return lax.ppermute(value, axis, pairs)]
  transfers between devices with their start and end apart: 3 -> 5, of which waited for: 3 -> 5; matrix products, arithmetic and copies ran while one was open for 0% -> 0% of each run, Pallas kernels for 0% -> 0%
where the time goes in v15:
time: 26.6 us; the launch traced here: 26.4 us
  Pallas kernels  9.88 us (37%)
  starting transfers between devices  7.25 us (27%)
  waiting for transfers between devices  6.63 us (25%)
  between operations  1.3 us (5%)
  local copies, waits for them, and re-layouts  0.7 us (3%)
  other arithmetic  0.63 us (2%)
    pallas_call x1, Pallas kernels, sweep(): pl.pallas_call(functools.partial(sweep_kernel, order), out_shape=(parts,...  9.88 us
    ppermute x5, starting transfers between devices, swapped(): return lax.ppermute(value, axis, pairs)  7.25 us
    ppermute x5, waiting for transfers between devices, swapped(): return lax.ppermute(value, axis, pairs)  6.63 us
    unnamed x3, local copies, waits for them, and re-layouts  0.7 us
    add x1, other arithmetic, local(): moved = start + time_step[None] * drift  0.61 us
  transfers between devices with their start and end apart: 5, of which 5 were waited for; matrix products, arithmetic and copies ran while one was open for 0% of the time, Pallas kernels for 0%

profile of v15, /device:TPU:0, one launch (start us, length us, event | category | flops | bytes accessed | tf_op | source)
XLA Modules:
  0.0 26.4 jit_solution(842325902438568513)
XLA Ops:
  0.6 0.0 copy-start
  0.6 0.7 %copy.8 = f32[1,3,512]{2,1,0:T(4,128)S(1)} copy(f32[1,3,512]{2,0,1:T(1,128)} %param.3) | data formatting | bytes 12288 | tf_op args[0]
  1.3 0.0 copy-done
  1.4 5.1 %collective-permute-start.2 = (f32[1,8,512]{2,1,0:T(8,128)S(1)}, f32[1,8,512]{2,1,0:T(8,128)S(1)}, u32[]{:S(2)}, u32[]{:S(2)}) collective-permute-start(f32[1,8,512]{2,1,0:T(8,128)S(1)} %select_maximum_fusion.refs_1_), channel_id=1, source_target_pairs={{0,3},{1,2},{2,1},{3,0},{4,7},{5,6},{6,5},{7,4},{8,11},{9,10},{10,... | collective-permute-start | bytes 49160 | tf_op jit(solution)/shard_map/ppermute | solution.py:282
  6.5 0.0 collective-permute-start.1
  6.5 0.6 %collective-permute-start = (f32[1,8,512]{2,1,0:T(8,128)S(1)}, f32[1,8,512]{2,1,0:T(8,128)S(1)}, u32[]{:S(2)}, u32[]{:S(2)}) collective-permute-start(f32[1,8,512]{2,1,0:T(8,128)S(1)} %select_maximum_fusion.refs_1_), channel_id=1, source_target_pairs={{0,2},{1,3},{2,0},{3,1},{4,6},{5,7},{6,4},{7,5},{8,10},{9,11},{10,... | collective-permute-start | bytes 49160 | tf_op jit(solution)/shard_map/ppermute | solution.py:282
  7.8 0.4 %collective-permute-done.2.refs_4_ = f32[1,8,512]{2,1,0:T(8,128)S(1)} collective-permute-done((f32[1,8,512]{2,1,0:T(8,128)S(1)}, f32[1,8,512]{2,1,0:T(8,128)S(1)}, u32[]{:S(2)}, u32[]{:S(2)}) %collective-permute-start.2) | collective-permute-done | bytes 16416 | tf_op jit(solution)/shard_map/ppermute | solution.py:282
  8.2 2.0 %collective-permute-done.1.refs_3_ = f32[1,8,512]{2,1,0:T(8,128)S(1)} collective-permute-done((f32[1,8,512]{2,1,0:T(8,128)S(1)}, f32[1,8,512]{2,1,0:T(8,128)S(1)}, u32[]{:S(2)}, u32[]{:S(2)}) %collective-permute-start.1) | collective-permute-done | bytes 16416 | tf_op jit(solution)/shard_map/ppermute | solution.py:282
  10.2 0.9 %collective-permute-done.refs_2_ = f32[1,8,512]{2,1,0:T(8,128)S(1)} collective-permute-done((f32[1,8,512]{2,1,0:T(8,128)S(1)}, f32[1,8,512]{2,1,0:T(8,128)S(1)}, u32[]{:S(2)}, u32[]{:S(2)}) %collective-permute-start) | collective-permute-done | bytes 16416 | tf_op jit(solution)/shard_map/ppermute | solution.py:282
  11.1 9.9 %sweep.1 = (f32[3,4,128]{2,1,0:T(4,128)}, f32[3,4,128]{2,1,0:T(4,128)S(1)}, f32[3,4,128]{2,1,0:T(4,128)S(1)}, f32[8,128]{1,0:T(8,128)S(1)}) custom-call(s32[1]{0:T(128)S(6)} %copy.11.refs_0_, f32[1,8,512]{2,1,0:T(8,128)S(1)} %select_maximum_fusion.refs_1_, f32[1,8,512]{2,1,0:T(8,128)S(1)} %collective-permute-done.refs_2_, ...), custom_call_target="tpu_custom_call" | custom-call | tf_op jit(solution)/shard_map/sweep/pallas_call | solution.py:260
  21.0 0.0 collective-permute-start.3
  21.0 1.2 %collective-permute-done.3 = f32[8,128]{1,0:T(8,128)S(1)} collective-permute-done((f32[8,128]{1,0:T(8,128)S(1)}, f32[8,128]{1,0:T(8,128)S(1)}, u32[]{:S(2)}, u32[]{:S(2)}) %collective-permute-start.3) | collective-permute-done | bytes 4128 | tf_op jit(solution)/shard_map/ppermute | solution.py:282
  22.2 1.5 %collective-permute-start.4 = (f32[8,128]{1,0:T(8,128)S(1)}, f32[8,128]{1,0:T(8,128)S(1)}, u32[]{:S(2)}, u32[]{:S(2)}) collective-permute-start(f32[8,128]{1,0:T(8,128)S(1)} %max.6), channel_id=1, source_target_pairs={{0,8},{4,12},{8,0},{12,4},{1,9},{5,13},{9,1},{13,5},{2,10},{6,14},... | collective-permute-start | bytes 12296 | tf_op jit(solution)/shard_map/ppermute | solution.py:282
  23.7 2.1 %collective-permute-done.4 = f32[8,128]{1,0:T(8,128)S(1)} collective-permute-done((f32[8,128]{1,0:T(8,128)S(1)}, f32[8,128]{1,0:T(8,128)S(1)}, u32[]{:S(2)}, u32[]{:S(2)}) %collective-permute-start.4) | collective-permute-done | bytes 4128 | tf_op jit(solution)/shard_map/ppermute | solution.py:282
  25.8 0.6 %multiply_add_fusion = f32[3,4,128]{2,1,0:T(4,128)} fusion(f32[3,4,128]{2,1,0:T(4,128)S(1)} %get-tuple-element.6, f32[3,4,128]{2,1,0:T(4,128)S(1)} %get-tuple-element.8, f32[128]{0:T(128)S(1)} %divide_bitcast_fusion), kind=kLoop, calls=%fused_computation.2 | loop fusion | flops 3072 | bytes 18944 | tf_op jit(solution)/shard_map/add | solution.py:315
  (4 shorter events, 0.0 us)
Async XLA Ops:
  0.6 0.7 %copy-start = (f32[1,512]{1,0:T(1,128)S(1)}, f32[1,512]{1,0:T(1,128)}, u32[]{:S(2)}) copy-start(f32[1,512]{1,0:T(1,128)} %param.4) | copy-start | bytes 6148
  1.4 6.8 %collective-permute-start.2 = (f32[1,8,512]{2,1,0:T(8,128)S(1)}, f32[1,8,512]{2,1,0:T(8,128)S(1)}, u32[]{:S(2)}, u32[]{:S(2)}) collective-permute-start(f32[1,8,512]{2,1,0:T(8,128)S(1)} %select_maximum_fusion.refs_1_), channel_id=1, source_target_pairs={{0,3},{1,2},{2,1},{3,0},{4,7},{5,6},{6,5},{7,4},{8,11},{9,10},{10,... | collective-permute-start | bytes 49160 | tf_op jit(solution)/shard_map/ppermute | solution.py:282
  6.5 3.7 %collective-permute-start.1 = (f32[1,8,512]{2,1,0:T(8,128)S(1)}, f32[1,8,512]{2,1,0:T(8,128)S(1)}, u32[]{:S(2)}, u32[]{:S(2)}) collective-permute-start(f32[1,8,512]{2,1,0:T(8,128)S(1)} %select_maximum_fusion.refs_1_), channel_id=1, source_target_pairs={{0,1},{1,0},{2,3},{3,2},{4,5},{5,4},{6,7},{7,6},{8,9},{9,8},{10,11... | collective-permute-start | bytes 49160 | tf_op jit(solution)/shard_map/ppermute | solution.py:282
  6.5 4.6 %collective-permute-start = (f32[1,8,512]{2,1,0:T(8,128)S(1)}, f32[1,8,512]{2,1,0:T(8,128)S(1)}, u32[]{:S(2)}, u32[]{:S(2)}) collective-permute-start(f32[1,8,512]{2,1,0:T(8,128)S(1)} %select_maximum_fusion.refs_1_), channel_id=1, source_target_pairs={{0,2},{1,3},{2,0},{3,1},{4,6},{5,7},{6,4},{7,5},{8,10},{9,11},{10,... | collective-permute-start | bytes 49160 | tf_op jit(solution)/shard_map/ppermute | solution.py:282
  21.0 1.2 %collective-permute-start.3 = (f32[8,128]{1,0:T(8,128)S(1)}, f32[8,128]{1,0:T(8,128)S(1)}, u32[]{:S(2)}, u32[]{:S(2)}) collective-permute-start(f32[8,128]{1,0:T(8,128)S(1)} %get-tuple-element.7), channel_id=1, source_target_pairs={{0,4},{4,0},{8,12},{12,8},{1,5},{5,1},{9,13},{13,9},{2,6},{6,2},{1... | collective-permute-start | bytes 12296 | tf_op jit(solution)/shard_map/ppermute | solution.py:282
  22.2 3.6 %collective-permute-start.4 = (f32[8,128]{1,0:T(8,128)S(1)}, f32[8,128]{1,0:T(8,128)S(1)}, u32[]{:S(2)}, u32[]{:S(2)}) collective-permute-start(f32[8,128]{1,0:T(8,128)S(1)} %max.6), channel_id=1, source_target_pairs={{0,8},{4,12},{8,0},{12,4},{1,9},{5,13},{9,1},{13,5},{2,10},{6,14},... | collective-permute-start | bytes 12296 | tf_op jit(solution)/shard_map/ppermute | solution.py:282

commit v16 on v15

--- a/solution.py
+++ b/solution.py
@@ -100,6 +100,21 @@
     return both[:, :half] + both[:, half:]
 
 
+def sum_rows_less(left, ref):
+    half = ref.shape[0] // 2
+    both = product(left, ref[:half, :])
+    few = left.shape[0] // 2
+    return both[:few] + product(left[:few], ref[half:, :]), both[few:]
+
+
+def sum_columns_less(left, ref):
+    half, few = ref.shape[0] // 2, left.shape[0] // 2
+    turned = (((1,), (1,)), ((), ()))
+    both = lax.dot_general(left, ref[:half, :], turned, preferred_element_type=f32)
+    less = lax.dot_general(left[:few], ref[half:, :], turned, preferred_element_type=f32)
+    return both[:few] + less, both[few:]
+
+
 def joined(total):
     upper, lower = total[0:8], total[8:16]
     return upper + lower + pltpu.roll(lower, 4, 0)
@@ -118,7 +133,6 @@
 
 def drift_sum(total, place, score):
     row = row_of(place)
-    total = total[0:32] + total[32:64]
     first, *rest = [total[8 * i : 8 * i + 8] for i in range(4)]
     turned = [pltpu.roll(group, 4, 0) for group in rest]
     count, scores = first[3:4], pltpu.roll(first, 4, 0)
@@ -137,8 +151,8 @@
     return drift - jnp.where(row == 0, ends[0], jnp.where(row == 1, ends[1], ends[2]))
 
 
-def sweep_kernel(order, *refs):
-    count = len(order)
+def sweep_kernel(sources, *refs):
+    count = len(sources)
     filled, blocks, refs = refs[0], refs[1 : count + 1], refs[count + 1 :]
     scores_out, drift_out, start_out, speed_out, key_ref, query_ref, moment_ref = refs[:7]
     flux_ref, sums_ref, totals_ref, exponent_ref, *split_refs = refs[7:]
@@ -152,7 +166,10 @@
         return pl.ds(pl.multiple_of(index * size, size), size)
 
     lane = lax.broadcasted_iota(jnp.int32, (1, width), 1)
-    live = [lane + (here ^ step) * width < filled[0] for step in order]
+    live = []
+    for source in sources:
+        owner = sum(jnp.where(here == i, source[i], 0) for i in range(count))
+        live.append(lane + owner * width < filled[0])
     weight = jnp.concatenate(
         [jnp.where(on, block[0, 3:4], 0.0) for on, block in zip(live, blocks)], axis=1
     )
@@ -220,9 +237,11 @@
             negative = jnp.minimum(ref[rows, :], -TINY)
             store_split(split, rows, negative * lax.rsqrt(-negative))
         keys, queries = slots(key_block, width), slots(query_block, width)
-        totals_ref[:, queries] += sum_rows(flux_ref[:, keys], split)
+        upper, lower = sum_rows_less(flux_ref[:, keys], split)
+        totals_ref[:, queries] += upper + lower
         if both:
-            totals_ref[:, keys] += sum_columns(flux_ref[:, queries], split)
+            upper, lower = sum_columns_less(flux_ref[:, queries], split)
+            totals_ref[:, keys] += upper + lower
 
     if kept:
         for index, (key, query) in enumerate(pairs):
@@ -243,23 +262,23 @@
     drift = jnp.where((vector & live)[:, 0:spread], drift * factor, 0.0)
     largest = jnp.max(rows_sum(drift * drift), axis=1, keepdims=True)
     speed_out[...] = jnp.broadcast_to(jnp.sqrt(largest), speed_out.shape)
+    scores_out[...] = score[:, 0:width]
     for part in range(width // 128):
         lanes = slice(part * 128, part * 128 + 128)
         for axis in range(3):
-            scores_out[axis, part : part + 1, :] = score[axis : axis + 1, lanes]
             drift_out[axis, part : part + 1, :] = drift[axis : axis + 1, lanes]
             start_out[axis, part : part + 1, :] = blocks[0][0, axis : axis + 1, lanes]
 
 
-def sweep(counts, blocks, order, copies):
+def sweep(counts, blocks, sources, copies):
     count, width = len(blocks), blocks[0].shape[2]
     slots = count * width
     kept = count <= KEPT_BLOCKS
     parts = jax.ShapeDtypeStruct((3, width // 128, 128), f32)
     whole = pl.BlockSpec(memory_space=pltpu.VMEM)
     return pl.pallas_call(
-        functools.partial(sweep_kernel, order),
-        out_shape=(parts, parts, parts, jax.ShapeDtypeStruct((copies, 128), f32)),
+        functools.partial(sweep_kernel, sources),
+        out_shape=(jax.ShapeDtypeStruct((8, width), f32), parts, parts, jax.ShapeDtypeStruct((copies, 128), f32)),
         in_specs=[pl.BlockSpec(memory_space=pltpu.SMEM)] + [whole] * count,
         out_specs=(whole, whole, whole, whole),
         scratch_shapes=[
@@ -268,7 +287,7 @@
             pltpu.VMEM((16, slots), bf16),
             pltpu.VMEM((DRIFT_ROWS, slots), bf16),
             pltpu.VMEM((16, slots), f32),
-            pltpu.VMEM((DRIFT_ROWS, slots if kept else width), f32),
+            pltpu.VMEM((DRIFT_ROWS // 2, slots if kept else width), f32),
             pltpu.VMEM((count * (count + 1) // 2 * width if kept else width, width), f32),
         ]
         + [pltpu.VMEM((2 * width, width), bf16)] * 2,
@@ -286,14 +305,21 @@
     return [1 << bit for bit in range(size.bit_length() - 1)]
 
 
+ROUNDS = ((2, 3, 1, 0), (3, 2, 0, 1), (1, 0, 3, 2))
+
+
 def gathered(block):
     size = lax.axis_size("sharers")
     if size == 4:
-        order = [0, 2, 1, 3]
-        return [block] + [swapped(block, "sharers", step) for step in order[1:]], order
+        blocks, sources = [block], [(0, 1, 2, 3)]
+        for targets in reversed(ROUNDS):
+            blocks.append(lax.ppermute(block, "sharers", list(enumerate(targets))))
+            sources.append(tuple(targets.index(i) for i in range(size)))
+        return blocks, sources
     for step in bits(size):
         block = jnp.concatenate([block, swapped(block, "sharers", step)], axis=0)
-    return [block[i : i + 1] for i in range(size)], list(range(size))
+    sources = [tuple(i ^ step for i in range(size)) for step in range(size)]
+    return [block[i : i + 1] for i in range(size)], sources
 
 
 def largest_speed(speeds, whole_cell):
@@ -307,13 +333,13 @@
 
 def local(velocities, weights, counts):
     package = jnp.concatenate([velocities, weights[:, None]], axis=1)
-    blocks, order = gathered(jnp.pad(package, ((0, 0), (0, 4), (0, 0))))
+    blocks, sources = gathered(jnp.pad(package, ((0, 0), (0, 4), (0, 0))))
     whole_cell = len(blocks) <= KEPT_BLOCKS
     copies = 8 if whole_cell else lax.axis_size(("cells", "sharers"))
-    scores, drift, start, speeds = sweep(counts, blocks, order, copies)
+    scores, drift, start, speeds = sweep(counts, blocks, sources, copies)
     time_step = 0.5 / (largest_speed(speeds, whole_cell) + 1e-06)
     moved = start + time_step[None] * drift
-    return moved.reshape(velocities.shape), scores.reshape(velocities.shape)
+    return moved.reshape(velocities.shape), scores[None, 0:3]
 
 
 def solution(mesh):

time: 26.6 us -> 25.6 us (0.962)
  waiting for transfers between devices: 6.63 us -> 5.11 us
  local copies, waits for them, and re-layouts: 0.7 us -> 1.31 us
    ppermute x0 -> x3, starting transfers between devices: none -> 5.67 us  [gathered(): blocks.append(lax.ppermute(block, 'sharers', list(enumerate(targets))))]
    ppermute x5 -> x2, starting transfers between devices: 7.25 us -> 1.65 us  [swapped(): return lax.ppermute(value, axis, pairs)]
    ppermute x5 -> x2, waiting for transfers between devices: 6.63 us -> 2.52 us  [swapped(): return lax.ppermute(value, axis, pairs)]
    ppermute x0 -> x3, waiting for transfers between devices: none -> 2.59 us  [gathered(): blocks.append(lax.ppermute(block, 'sharers', list(enumerate(targets))))]
    unnamed x3 -> x4, local copies, waits for them, and re-layouts: 0.7 us -> 1.31 us
  transfers between devices with their start and end apart: 5 -> 5, of which waited for: 5 -> 5; matrix products, arithmetic and copies ran while one was open for 0% -> 2% of each run, Pallas kernels for 0% -> 0%
where the time goes in v16:
time: 25.6 us; the launch traced here: 25.4 us
  Pallas kernels  9.77 us (38%)
  starting transfers between devices  7.32 us (29%)
  waiting for transfers between devices  5.11 us (20%)
  local copies, waits for them, and re-layouts  1.31 us (5%)
  between operations  1.3 us (5%)
  other arithmetic  0.63 us (2%)
    pallas_call x1, Pallas kernels, sweep(): pl.pallas_call(functools.partial(sweep_kernel, sources), out_shape=(jax.S...  9.77 us
    ppermute x3, starting transfers between devices, gathered(): blocks.append(lax.ppermute(block, 'sharers', list(enumerate(targets))))  5.67 us
    ppermute x3, waiting for transfers between devices, gathered(): blocks.append(lax.ppermute(block, 'sharers', list(enumerate(targets))))  2.59 us
    ppermute x2, waiting for transfers between devices, swapped(): return lax.ppermute(value, axis, pairs)  2.52 us
    ppermute x2, starting transfers between devices, swapped(): return lax.ppermute(value, axis, pairs)  1.65 us
    unnamed x4, local copies, waits for them, and re-layouts  1.31 us
    add x1, other arithmetic, local(): moved = start + time_step[None] * drift  0.61 us
  transfers between devices with their start and end apart: 5, of which 5 were waited for; matrix products, arithmetic and copies ran while one was open for 2% of the time, Pallas kernels for 0%

profile of v16, /device:TPU:0, one launch (start us, length us, event | category | flops | bytes accessed | tf_op | source)
XLA Modules:
  0.0 25.4 jit_solution(13384501972266690701)
XLA Ops:
  0.6 0.0 copy-start
  0.6 0.7 %copy.8 = f32[1,3,512]{2,1,0:T(4,128)S(1)} copy(f32[1,3,512]{2,0,1:T(1,128)} %param.3) | data formatting | bytes 12288 | tf_op args[0]
  1.3 0.0 copy-done
  1.4 4.1 %collective-permute-start.2 = (f32[1,8,512]{2,1,0:T(8,128)S(1)}, f32[1,8,512]{2,1,0:T(8,128)S(1)}, u32[]{:S(2)}, u32[]{:S(2)}) collective-permute-start(f32[1,8,512]{2,1,0:T(8,128)S(1)} %select_maximum_fusion.refs_1_), channel_id=1, source_target_pairs={{0,2},{1,3},{2,1},{3,0},{4,6},{5,7},{6,5},{7,4},{8,10},{9,11},{10,... | collective-permute-start | bytes 49160 | tf_op jit(solution)/shard_map/ppermute | solution.py:316
  5.4 1.1 %collective-permute-start.1 = (f32[1,8,512]{2,1,0:T(8,128)S(1)}, f32[1,8,512]{2,1,0:T(8,128)S(1)}, u32[]{:S(2)}, u32[]{:S(2)}) collective-permute-start(f32[1,8,512]{2,1,0:T(8,128)S(1)} %select_maximum_fusion.refs_1_), channel_id=1, source_target_pairs={{0,3},{1,2},{2,0},{3,1},{4,7},{5,6},{6,4},{7,5},{8,11},{9,10},{10,... | collective-permute-start | bytes 49160 | tf_op jit(solution)/shard_map/ppermute | solution.py:316
  6.5 0.5 %collective-permute-start = (f32[1,8,512]{2,1,0:T(8,128)S(1)}, f32[1,8,512]{2,1,0:T(8,128)S(1)}, u32[]{:S(2)}, u32[]{:S(2)}) collective-permute-start(f32[1,8,512]{2,1,0:T(8,128)S(1)} %select_maximum_fusion.refs_1_), channel_id=1, source_target_pairs={{0,1},{1,0},{2,3},{3,2},{4,5},{5,4},{6,7},{7,6},{8,9},{9,8},{10,11... | collective-permute-start | bytes 49160 | tf_op jit(solution)/shard_map/ppermute | solution.py:316
  7.7 0.5 %collective-permute-done.2.refs_4_ = f32[1,8,512]{2,1,0:T(8,128)S(1)} collective-permute-done((f32[1,8,512]{2,1,0:T(8,128)S(1)}, f32[1,8,512]{2,1,0:T(8,128)S(1)}, u32[]{:S(2)}, u32[]{:S(2)}) %collective-permute-start.2) | collective-permute-done | bytes 16416 | tf_op jit(solution)/shard_map/ppermute | solution.py:316
  8.2 1.9 %collective-permute-done.1.refs_3_ = f32[1,8,512]{2,1,0:T(8,128)S(1)} collective-permute-done((f32[1,8,512]{2,1,0:T(8,128)S(1)}, f32[1,8,512]{2,1,0:T(8,128)S(1)}, u32[]{:S(2)}, u32[]{:S(2)}) %collective-permute-start.1) | collective-permute-done | bytes 16416 | tf_op jit(solution)/shard_map/ppermute | solution.py:316
  10.1 0.2 collective-permute-done.refs_2_
  10.3 9.8 %sweep.1 = (f32[8,512]{1,0:T(8,128)S(1)}, f32[3,4,128]{2,1,0:T(4,128)S(1)}, f32[3,4,128]{2,1,0:T(4,128)S(1)}, f32[8,128]{1,0:T(8,128)S(1)}) custom-call(s32[1]{0:T(128)S(6)} %copy.11.refs_0_, f32[1,8,512]{2,1,0:T(8,128)S(1)} %select_maximum_fusion.refs_1_, f32[1,8,512]{2,1,0:T(8,128)S(1)} %collective-permute-done.refs_2_, ...), custom_call_target="tpu_custom_call" | custom-call | tf_op jit(solution)/shard_map/sweep/pallas_call | solution.py:279
  20.0 0.0 collective-permute-start.3
  20.0 1.2 %collective-permute-done.3 = f32[8,128]{1,0:T(8,128)S(1)} collective-permute-done((f32[8,128]{1,0:T(8,128)S(1)}, f32[8,128]{1,0:T(8,128)S(1)}, u32[]{:S(2)}, u32[]{:S(2)}) %collective-permute-start.3) | collective-permute-done | bytes 4128 | tf_op jit(solution)/shard_map/ppermute | solution.py:301
  21.2 1.6 %collective-permute-start.4 = (f32[8,128]{1,0:T(8,128)S(1)}, f32[8,128]{1,0:T(8,128)S(1)}, u32[]{:S(2)}, u32[]{:S(2)}) collective-permute-start(f32[8,128]{1,0:T(8,128)S(1)} %max.6), channel_id=1, source_target_pairs={{0,8},{4,12},{8,0},{12,4},{1,9},{5,13},{9,1},{13,5},{2,10},{6,14},... | collective-permute-start | bytes 12296 | tf_op jit(solution)/shard_map/ppermute | solution.py:301
  22.9 0.6 %copy.10 = f32[1,3,512]{2,0,1:T(1,128)} copy(f32[1,3,512]{2,1,0:T(4,128)S(1)} %slice_bitcast_fusion) | data formatting | bytes 12288
  23.5 1.4 %collective-permute-done.4 = f32[8,128]{1,0:T(8,128)S(1)} collective-permute-done((f32[8,128]{1,0:T(8,128)S(1)}, f32[8,128]{1,0:T(8,128)S(1)}, u32[]{:S(2)}, u32[]{:S(2)}) %collective-permute-start.4) | collective-permute-done | bytes 4128 | tf_op jit(solution)/shard_map/ppermute | solution.py:301
  24.8 0.6 %multiply_add_fusion = f32[3,4,128]{2,1,0:T(4,128)} fusion(f32[3,4,128]{2,1,0:T(4,128)S(1)} %get-tuple-element.6, f32[3,4,128]{2,1,0:T(4,128)S(1)} %get-tuple-element.8, f32[128]{0:T(128)S(1)} %divide_bitcast_fusion), kind=kLoop, calls=%fused_computation.3 | loop fusion | flops 3072 | bytes 18944 | tf_op jit(solution)/shard_map/add | solution.py:341
  (5 shorter events, 0.0 us)
Async XLA Ops:
  0.6 0.7 %copy-start = (f32[1,512]{1,0:T(1,128)S(1)}, f32[1,512]{1,0:T(1,128)}, u32[]{:S(2)}) copy-start(f32[1,512]{1,0:T(1,128)} %param.4) | copy-start | bytes 6148
  1.4 6.8 %collective-permute-start.2 = (f32[1,8,512]{2,1,0:T(8,128)S(1)}, f32[1,8,512]{2,1,0:T(8,128)S(1)}, u32[]{:S(2)}, u32[]{:S(2)}) collective-permute-start(f32[1,8,512]{2,1,0:T(8,128)S(1)} %select_maximum_fusion.refs_1_), channel_id=1, source_target_pairs={{0,2},{1,3},{2,1},{3,0},{4,6},{5,7},{6,5},{7,4},{8,10},{9,11},{10,... | collective-permute-start | bytes 49160 | tf_op jit(solution)/shard_map/ppermute | solution.py:316
  5.4 4.6 %collective-permute-start.1 = (f32[1,8,512]{2,1,0:T(8,128)S(1)}, f32[1,8,512]{2,1,0:T(8,128)S(1)}, u32[]{:S(2)}, u32[]{:S(2)}) collective-permute-start(f32[1,8,512]{2,1,0:T(8,128)S(1)} %select_maximum_fusion.refs_1_), channel_id=1, source_target_pairs={{0,3},{1,2},{2,0},{3,1},{4,7},{5,6},{6,4},{7,5},{8,11},{9,10},{10,... | collective-permute-start | bytes 49160 | tf_op jit(solution)/shard_map/ppermute | solution.py:316
  6.5 3.7 %collective-permute-start = (f32[1,8,512]{2,1,0:T(8,128)S(1)}, f32[1,8,512]{2,1,0:T(8,128)S(1)}, u32[]{:S(2)}, u32[]{:S(2)}) collective-permute-start(f32[1,8,512]{2,1,0:T(8,128)S(1)} %select_maximum_fusion.refs_1_), channel_id=1, source_target_pairs={{0,1},{1,0},{2,3},{3,2},{4,5},{5,4},{6,7},{7,6},{8,9},{9,8},{10,11... | collective-permute-start | bytes 49160 | tf_op jit(solution)/shard_map/ppermute | solution.py:316
  20.0 1.2 %collective-permute-start.3 = (f32[8,128]{1,0:T(8,128)S(1)}, f32[8,128]{1,0:T(8,128)S(1)}, u32[]{:S(2)}, u32[]{:S(2)}) collective-permute-start(f32[8,128]{1,0:T(8,128)S(1)} %get-tuple-element.7), channel_id=1, source_target_pairs={{0,4},{4,0},{8,12},{12,8},{1,5},{5,1},{9,13},{13,9},{2,6},{6,2},{1... | collective-permute-start | bytes 12296 | tf_op jit(solution)/shard_map/ppermute | solution.py:301
  21.2 3.6 %collective-permute-start.4 = (f32[8,128]{1,0:T(8,128)S(1)}, f32[8,128]{1,0:T(8,128)S(1)}, u32[]{:S(2)}, u32[]{:S(2)}) collective-permute-start(f32[8,128]{1,0:T(8,128)S(1)} %max.6), channel_id=1, source_target_pairs={{0,8},{4,12},{8,0},{12,4},{1,9},{5,13},{9,1},{13,5},{2,10},{6,14},... | collective-permute-start | bytes 12296 | tf_op jit(solution)/shard_map/ppermute | solution.py:301

commit v17 on v16

--- a/solution.py
+++ b/solution.py
@@ -159,11 +159,13 @@
     width = blocks[0].shape[2]
     total_slots = count * width
     kept = count <= KEPT_BLOCKS
-    pairs = [(key, query) for query in range(count) for key in range(query, count)]
+    half = width // 2
+    tiles = []
+    for query in range(count if kept else 0):
+        start = query * width
+        tiles += [(start, half, start, half, 0), (start + half, half, start, width, half)]
+        tiles += [(key * width, width, start, width, width) for key in range(query + 1, count)]
     here = lax.axis_index("sharers")
-
-    def slots(index, size):
-        return pl.ds(pl.multiple_of(index * size, size), size)
 
     lane = lax.broadcasted_iota(jnp.int32, (1, width), 1)
     live = []
@@ -185,40 +187,44 @@
     middle = middle / jnp.sum(weight, axis=1, keepdims=True)
     sums_ref[...] = jnp.zeros_like(sums_ref)
 
-    def exponent(key_block, query_block):
-        return product(key_ref[slots(key_block, width), :], query_ref[:, slots(query_block, width)])
-
-    def add_blobs(key_block, query_block, ref, split, both):
-        for group in range(0, width, GROUP):
+    def exponent(key, keys, query, queries):
+        return product(key_ref[pl.ds(key, keys), :], query_ref[:, pl.ds(query, queries)])
+
+    def add_blobs(tile, ref, split):
+        key, keys, query, queries, turned = tile
+        split = split.at[0 : 2 * keys, 0:queries]
+        for group in range(0, keys, GROUP):
             rows = pl.ds(group, GROUP)
             store_split(split, rows, jnp.exp2(ref[rows, :]))
-        keys, queries = slots(key_block, width), slots(query_block, width)
-        sums_ref[:, queries] += sum_rows(moment_ref[:, keys], split)
-        if both:
-            sums_ref[:, keys] += sum_columns(moment_ref[:, queries], split)
+        sums_ref[:, pl.ds(query, queries)] += sum_rows(moment_ref[:, pl.ds(key, keys)], split)
+        if turned:
+            left, right = moment_ref[:, pl.ds(query, turned)], split.at[:, 0:turned]
+            sums_ref[:, pl.ds(key, keys)] += sum_columns(left, right)
+
+    def block_tile(key, query, both):
+        start, first = (pl.multiple_of(block * width, width) for block in (key, query))
+        return (start, width, first, width, width if both else 0)
 
     if kept:
-
-        def tile(index):
-            return exponent_ref.at[slots(index, width), :]
-
-        tile(0)[...] = exponent(*pairs[0])
-        for index, (key, query) in enumerate(pairs):
-            if index + 1 < len(pairs):
-                tile(index + 1)[...] = exponent(*pairs[index + 1])
-            add_blobs(key, query, tile(index), split_refs[index % 2], key != query)
+        exponents = []
+        for index, (_, keys, _, queries, _) in enumerate(tiles):
+            exponents.append(exponent_ref.at[index, 0:keys, 0:queries])
+        exponents[0][...] = exponent(*tiles[0][:4])
+        for index, tile in enumerate(tiles):
+            if index + 1 < len(tiles):
+                exponents[index + 1][...] = exponent(*tiles[index + 1][:4])
+            add_blobs(tile, exponents[index], split_refs[index % 2])
     else:
 
         def whole_row(query, carry):
-            exponent_ref[...] = exponent(query, query)
-            add_blobs(query, query, exponent_ref, split_refs[0], False)
-
-            def one(key, carry):
-                exponent_ref[...] = exponent(key, query)
-                add_blobs(key, query, exponent_ref, split_refs[0], True)
+            def one(key, both, carry):
+                tile = block_tile(key, query, both)
+                exponent_ref[0] = exponent(*tile[:4])
+                add_blobs(tile, exponent_ref.at[0], split_refs[0])
                 return carry
 
-            return lax.fori_loop(query + 1, count, one, carry)
+            carry = one(query, False, carry)
+            return lax.fori_loop(query + 1, count, lambda key, c: one(key, True, c), carry)
 
         lax.fori_loop(0, count, whole_row, 0)
 
@@ -231,27 +237,30 @@
     flux_ref[...] = drift_rows(weight, centred, score)
     totals_ref[...] = jnp.zeros_like(totals_ref)
 
-    def add_distances(key_block, query_block, ref, split, both):
-        for group in range(0, width, GROUP):
+    def add_distances(tile, ref, split):
+        key, keys, query, queries, turned = tile
+        split = split.at[0 : 2 * keys, 0:queries]
+        for group in range(0, keys, GROUP):
             rows = pl.ds(group, GROUP)
             negative = jnp.minimum(ref[rows, :], -TINY)
             store_split(split, rows, negative * lax.rsqrt(-negative))
-        keys, queries = slots(key_block, width), slots(query_block, width)
-        upper, lower = sum_rows_less(flux_ref[:, keys], split)
-        totals_ref[:, queries] += upper + lower
-        if both:
-            upper, lower = sum_columns_less(flux_ref[:, queries], split)
-            totals_ref[:, keys] += upper + lower
+        upper, lower = sum_rows_less(flux_ref[:, pl.ds(key, keys)], split)
+        totals_ref[:, pl.ds(query, queries)] += upper + lower
+        if turned:
+            left, right = flux_ref[:, pl.ds(query, turned)], split.at[:, 0:turned]
+            upper, lower = sum_columns_less(left, right)
+            totals_ref[:, pl.ds(key, keys)] += upper + lower
 
     if kept:
-        for index, (key, query) in enumerate(pairs):
-            add_distances(key, query, tile(index), split_refs[index % 2], key != query)
+        for index, tile in enumerate(tiles):
+            add_distances(tile, exponents[index], split_refs[index % 2])
         spread = total_slots
     else:
 
         def one_block(key, carry):
-            exponent_ref[...] = exponent(key, 0)
-            add_distances(key, 0, exponent_ref, split_refs[0], False)
+            tile = block_tile(key, 0, False)
+            exponent_ref[0] = exponent(*tile[:4])
+            add_distances(tile, exponent_ref.at[0], split_refs[0])
             return carry
 
         lax.fori_loop(0, count, one_block, 0)
@@ -288,7 +297,7 @@
             pltpu.VMEM((DRIFT_ROWS, slots), bf16),
             pltpu.VMEM((16, slots), f32),
             pltpu.VMEM((DRIFT_ROWS // 2, slots if kept else width), f32),
-            pltpu.VMEM((count * (count + 1) // 2 * width if kept else width, width), f32),
+            pltpu.VMEM((count * (count + 3) // 2 if kept else 1, width, width), f32),
         ]
         + [pltpu.VMEM((2 * width, width), bf16)] * 2,
         compiler_params=pltpu.CompilerParams(vmem_limit_bytes=(16 << 20) + slots * 2688),
@@ -326,8 +335,13 @@
     if not whole_cell:
         axes = ("cells", "sharers")
         return jnp.max(lax.all_to_all(speeds[:, None], axes, 0, 0, tiled=True), axis=0)
-    for step in bits(lax.axis_size("cells")):
-        speeds = jnp.maximum(speeds, swapped(speeds, "cells", step))
+    size = lax.axis_size("cells")
+    if size == 4:
+        for other in [swapped(speeds, "cells", step) for step in (2, 3, 1)]:
+            speeds = jnp.maximum(speeds, other)
+    else:
+        for step in bits(size):
+            speeds = jnp.maximum(speeds, swapped(speeds, "cells", step))
     return speeds[0:1]
 
 

time: 25.6 us -> 25.6 us (level)
  Pallas kernels: 9.77 us -> 9.1 us
  starting transfers between devices: 7.32 us -> 7.81 us
    pallas_call x1, Pallas kernels: 9.77 us -> 9.1 us  [sweep(): pl.pallas_call(functools.partial(sweep_kernel, sources), out_shape=(jax.S...]
    ppermute x2 -> x3, starting transfers between devices: 1.65 us -> 2.14 us  [swapped(): return lax.ppermute(value, axis, pairs)]
    ppermute x2 -> x3, waiting for transfers between devices: 2.52 us -> 2.62 us  [swapped(): return lax.ppermute(value, axis, pairs)]
  transfers between devices with their start and end apart: 5 -> 6, of which waited for: 5 -> 5; matrix products, arithmetic and copies ran while one was open for 2% -> 2% of each run, Pallas kernels for 0% -> 0%
where the time goes in v17:
time: 25.6 us; the launch traced here: 25.4 us
  Pallas kernels  9.1 us (36%)
  starting transfers between devices  7.81 us (31%)
  waiting for transfers between devices  5.21 us (20%)
  local copies, waits for them, and re-layouts  1.31 us (5%)
  between operations  1.31 us (5%)
  other arithmetic  0.63 us (2%)
    pallas_call x1, Pallas kernels, sweep(): pl.pallas_call(functools.partial(sweep_kernel, sources), out_shape=(jax.S...  9.1 us
    ppermute x3, starting transfers between devices, gathered(): blocks.append(lax.ppermute(block, 'sharers', list(enumerate(targets))))  5.67 us
    ppermute x3, waiting for transfers between devices, swapped(): return lax.ppermute(value, axis, pairs)  2.62 us
    ppermute x3, waiting for transfers between devices, gathered(): blocks.append(lax.ppermute(block, 'sharers', list(enumerate(targets))))  2.59 us
    ppermute x3, starting transfers between devices, swapped(): return lax.ppermute(value, axis, pairs)  2.14 us
    unnamed x4, local copies, waits for them, and re-layouts  1.31 us
    add x1, other arithmetic, local(): moved = start + time_step[None] * drift  0.6 us
  transfers between devices with their start and end apart: 6, of which 5 were waited for; matrix products, arithmetic and copies ran while one was open for 2% of the time, Pallas kernels for 0%

profile of v17, /device:TPU:0, one launch (start us, length us, event | category | flops | bytes accessed | tf_op | source)
XLA Modules:
  0.0 25.4 jit_solution(16149519997374332586)
XLA Ops:
  0.6 0.0 copy-start
  0.6 0.7 %copy.8 = f32[1,3,512]{2,1,0:T(4,128)S(1)} copy(f32[1,3,512]{2,0,1:T(1,128)} %param.3) | data formatting | bytes 12288 | tf_op args[0]
  1.3 0.0 copy-done
  1.4 4.1 %collective-permute-start.2 = (f32[1,8,512]{2,1,0:T(8,128)S(1)}, f32[1,8,512]{2,1,0:T(8,128)S(1)}, u32[]{:S(2)}, u32[]{:S(2)}) collective-permute-start(f32[1,8,512]{2,1,0:T(8,128)S(1)} %select_maximum_fusion.refs_1_), channel_id=1, source_target_pairs={{0,2},{1,3},{2,1},{3,0},{4,6},{5,7},{6,5},{7,4},{8,10},{9,11},{10,... | collective-permute-start | bytes 49160 | tf_op jit(solution)/shard_map/ppermute | solution.py:325
  5.4 1.1 %collective-permute-start.1 = (f32[1,8,512]{2,1,0:T(8,128)S(1)}, f32[1,8,512]{2,1,0:T(8,128)S(1)}, u32[]{:S(2)}, u32[]{:S(2)}) collective-permute-start(f32[1,8,512]{2,1,0:T(8,128)S(1)} %select_maximum_fusion.refs_1_), channel_id=1, source_target_pairs={{0,3},{1,2},{2,0},{3,1},{4,7},{5,6},{6,4},{7,5},{8,11},{9,10},{10,... | collective-permute-start | bytes 49160 | tf_op jit(solution)/shard_map/ppermute | solution.py:325
  6.5 0.5 %collective-permute-start = (f32[1,8,512]{2,1,0:T(8,128)S(1)}, f32[1,8,512]{2,1,0:T(8,128)S(1)}, u32[]{:S(2)}, u32[]{:S(2)}) collective-permute-start(f32[1,8,512]{2,1,0:T(8,128)S(1)} %select_maximum_fusion.refs_1_), channel_id=1, source_target_pairs={{0,1},{1,0},{2,3},{3,2},{4,5},{5,4},{6,7},{7,6},{8,9},{9,8},{10,11... | collective-permute-start | bytes 49160 | tf_op jit(solution)/shard_map/ppermute | solution.py:325
  7.7 0.5 %collective-permute-done.2.refs_4_ = f32[1,8,512]{2,1,0:T(8,128)S(1)} collective-permute-done((f32[1,8,512]{2,1,0:T(8,128)S(1)}, f32[1,8,512]{2,1,0:T(8,128)S(1)}, u32[]{:S(2)}, u32[]{:S(2)}) %collective-permute-start.2) | collective-permute-done | bytes 16416 | tf_op jit(solution)/shard_map/ppermute | solution.py:325
  8.2 1.9 %collective-permute-done.1.refs_3_ = f32[1,8,512]{2,1,0:T(8,128)S(1)} collective-permute-done((f32[1,8,512]{2,1,0:T(8,128)S(1)}, f32[1,8,512]{2,1,0:T(8,128)S(1)}, u32[]{:S(2)}, u32[]{:S(2)}) %collective-permute-start.1) | collective-permute-done | bytes 16416 | tf_op jit(solution)/shard_map/ppermute | solution.py:325
  10.1 0.2 collective-permute-done.refs_2_
  10.3 9.1 %sweep.1 = (f32[8,512]{1,0:T(8,128)S(1)}, f32[3,4,128]{2,1,0:T(4,128)S(1)}, f32[3,4,128]{2,1,0:T(4,128)S(1)}, f32[8,128]{1,0:T(8,128)S(1)}) custom-call(s32[1]{0:T(128)S(6)} %copy.11.refs_0_, f32[1,8,512]{2,1,0:T(8,128)S(1)} %select_maximum_fusion.refs_1_, f32[1,8,512]{2,1,0:T(8,128)S(1)} %collective-permute-done.refs_2_, ...), custom_call_target="tpu_custom_call" | custom-call | tf_op jit(solution)/shard_map/sweep/pallas_call | solution.py:288
  19.4 0.0 collective-permute-start.5
  19.4 1.8 %collective-permute-start.4 = (f32[8,128]{1,0:T(8,128)S(1)}, f32[8,128]{1,0:T(8,128)S(1)}, u32[]{:S(2)}, u32[]{:S(2)}) collective-permute-start(f32[8,128]{1,0:T(8,128)S(1)} %get-tuple-element.7), channel_id=1, source_target_pairs={{0,12},{4,8},{8,4},{12,0},{1,13},{5,9},{9,5},{13,1},{2,14},{6,10},... | collective-permute-start | bytes 12296 | tf_op jit(solution)/shard_map/ppermute | solution.py:310
  21.1 0.4 %collective-permute-start.3 = (f32[8,128]{1,0:T(8,128)S(1)}, f32[8,128]{1,0:T(8,128)S(1)}, u32[]{:S(2)}, u32[]{:S(2)}) collective-permute-start(f32[8,128]{1,0:T(8,128)S(1)} %get-tuple-element.7), channel_id=1, source_target_pairs={{0,8},{4,12},{8,0},{12,4},{1,9},{5,13},{9,1},{13,5},{2,10},{6,14},... | collective-permute-start | bytes 12296 | tf_op jit(solution)/shard_map/ppermute | solution.py:310
  21.5 0.6 %copy.10 = f32[1,3,512]{2,0,1:T(1,128)} copy(f32[1,3,512]{2,1,0:T(4,128)S(1)} %slice_bitcast_fusion) | data formatting | bytes 12288
  22.1 0.0 collective-permute-done.5
  22.1 0.3 %collective-permute-done.4 = f32[8,128]{1,0:T(8,128)S(1)} collective-permute-done((f32[8,128]{1,0:T(8,128)S(1)}, f32[8,128]{1,0:T(8,128)S(1)}, u32[]{:S(2)}, u32[]{:S(2)}) %collective-permute-start.4) | collective-permute-done | bytes 4128 | tf_op jit(solution)/shard_map/ppermute | solution.py:310
  22.5 2.3 %collective-permute-done.3 = f32[8,128]{1,0:T(8,128)S(1)} collective-permute-done((f32[8,128]{1,0:T(8,128)S(1)}, f32[8,128]{1,0:T(8,128)S(1)}, u32[]{:S(2)}, u32[]{:S(2)}) %collective-permute-start.3) | collective-permute-done | bytes 4128 | tf_op jit(solution)/shard_map/ppermute | solution.py:310
  24.8 0.6 %multiply_add_fusion = f32[3,4,128]{2,1,0:T(4,128)} fusion(f32[3,4,128]{2,1,0:T(4,128)S(1)} %get-tuple-element.6, f32[3,4,128]{2,1,0:T(4,128)S(1)} %get-tuple-element.8, f32[128]{0:T(128)S(1)} %divide_bitcast_fusion), kind=kLoop, calls=%fused_computation.3 | loop fusion | flops 3072 | bytes 18944 | tf_op jit(solution)/shard_map/add | solution.py:355
  (4 shorter events, 0.0 us)
Async XLA Ops:
  0.6 0.7 %copy-start = (f32[1,512]{1,0:T(1,128)S(1)}, f32[1,512]{1,0:T(1,128)}, u32[]{:S(2)}) copy-start(f32[1,512]{1,0:T(1,128)} %param.4) | copy-start | bytes 6148
  1.4 6.8 %collective-permute-start.2 = (f32[1,8,512]{2,1,0:T(8,128)S(1)}, f32[1,8,512]{2,1,0:T(8,128)S(1)}, u32[]{:S(2)}, u32[]{:S(2)}) collective-permute-start(f32[1,8,512]{2,1,0:T(8,128)S(1)} %select_maximum_fusion.refs_1_), channel_id=1, source_target_pairs={{0,2},{1,3},{2,1},{3,0},{4,6},{5,7},{6,5},{7,4},{8,10},{9,11},{10,... | collective-permute-start | bytes 49160 | tf_op jit(solution)/shard_map/ppermute | solution.py:325
  5.4 4.6 %collective-permute-start.1 = (f32[1,8,512]{2,1,0:T(8,128)S(1)}, f32[1,8,512]{2,1,0:T(8,128)S(1)}, u32[]{:S(2)}, u32[]{:S(2)}) collective-permute-start(f32[1,8,512]{2,1,0:T(8,128)S(1)} %select_maximum_fusion.refs_1_), channel_id=1, source_target_pairs={{0,3},{1,2},{2,0},{3,1},{4,7},{5,6},{6,4},{7,5},{8,11},{9,10},{10,... | collective-permute-start | bytes 49160 | tf_op jit(solution)/shard_map/ppermute | solution.py:325
  6.5 3.7 %collective-permute-start = (f32[1,8,512]{2,1,0:T(8,128)S(1)}, f32[1,8,512]{2,1,0:T(8,128)S(1)}, u32[]{:S(2)}, u32[]{:S(2)}) collective-permute-start(f32[1,8,512]{2,1,0:T(8,128)S(1)} %select_maximum_fusion.refs_1_), channel_id=1, source_target_pairs={{0,1},{1,0},{2,3},{3,2},{4,5},{5,4},{6,7},{7,6},{8,9},{9,8},{10,11... | collective-permute-start | bytes 49160 | tf_op jit(solution)/shard_map/ppermute | solution.py:325
  19.4 2.8 %collective-permute-start.5 = (f32[8,128]{1,0:T(8,128)S(1)}, f32[8,128]{1,0:T(8,128)S(1)}, u32[]{:S(2)}, u32[]{:S(2)}) collective-permute-start(f32[8,128]{1,0:T(8,128)S(1)} %get-tuple-element.7), channel_id=1, source_target_pairs={{0,4},{4,0},{8,12},{12,8},{1,5},{5,1},{9,13},{13,9},{2,6},{6,2},{1... | collective-permute-start | bytes 12296 | tf_op jit(solution)/shard_map/ppermute | solution.py:310
  19.4 3.1 %collective-permute-start.4 = (f32[8,128]{1,0:T(8,128)S(1)}, f32[8,128]{1,0:T(8,128)S(1)}, u32[]{:S(2)}, u32[]{:S(2)}) collective-permute-start(f32[8,128]{1,0:T(8,128)S(1)} %get-tuple-element.7), channel_id=1, source_target_pairs={{0,12},{4,8},{8,4},{12,0},{1,13},{5,9},{9,5},{13,1},{2,14},{6,10},... | collective-permute-start | bytes 12296 | tf_op jit(solution)/shard_map/ppermute | solution.py:310
  21.1 3.6 %collective-permute-start.3 = (f32[8,128]{1,0:T(8,128)S(1)}, f32[8,128]{1,0:T(8,128)S(1)}, u32[]{:S(2)}, u32[]{:S(2)}) collective-permute-start(f32[8,128]{1,0:T(8,128)S(1)} %get-tuple-element.7), channel_id=1, source_target_pairs={{0,8},{4,12},{8,0},{12,4},{1,9},{5,13},{9,1},{13,5},{2,10},{6,14},... | collective-permute-start | bytes 12296 | tf_op jit(solution)/shard_map/ppermute | solution.py:310

commit v18 on v17

--- a/solution.py
+++ b/solution.py
@@ -151,20 +151,103 @@
     return drift - jnp.where(row == 0, ends[0], jnp.where(row == 1, ends[1], ends[2]))
 
 
+def prepared(whole, live):
+    weight = jnp.where(live, whole[3:4], 0.0)
+    parts = grid_parts(jnp.where(row_of(whole) < 3, whole * SCALE, 0.0))
+    place = parts[0] + parts[1] + parts[2]
+    key, query = distance_features(parts)
+    return weight, place, key.T, query, weighted_rows(weight, place)
+
+
+def split_blobs(exponent, split):
+    for group in range(0, exponent.shape[0], GROUP):
+        rows = pl.ds(group, GROUP)
+        store_split(split, rows, jnp.exp2(exponent[rows, :]))
+
+
+def split_distances(exponent, split):
+    for group in range(0, exponent.shape[0], GROUP):
+        rows = pl.ds(group, GROUP)
+        negative = jnp.minimum(exponent[rows, :], -TINY)
+        store_split(split, rows, negative * lax.rsqrt(-negative))
+
+
+def diagonal_tiles(start, width):
+    half = width // 2
+    return [(start, half, start, half, 0), (start + half, half, start, width, half)]
+
+
+def add_blobs(tile, split, moments, sums_ref):
+    key, keys, query, queries, turned = tile
+    sums_ref[:, pl.ds(query, queries)] += sum_rows(moments(key, keys), split)
+    if turned:
+        sums_ref[:, pl.ds(key, keys)] += sum_columns(moments(query, turned), split.at[:, 0:turned])
+
+
+def add_distances(tile, split, fluxes, totals_ref):
+    key, keys, query, queries, turned = tile
+    upper, lower = sum_rows_less(fluxes(key, keys), split)
+    totals_ref[:, pl.ds(query, queries)] += upper + lower
+    if turned:
+        upper, lower = sum_columns_less(fluxes(query, turned), split.at[:, 0:turned])
+        totals_ref[:, pl.ds(key, keys)] += upper + lower
+
+
+def own_kernel(filled, block, key_out, query_out, moment_out, sums_out, first_out, second_out,
+               exponent_ref, split_ref):
+    width = block.shape[2]
+    lane = lax.broadcasted_iota(jnp.int32, (1, width), 1)
+    live = lane + lax.axis_index("sharers") * width < filled[0]
+    _, _, key, query, moment = prepared(block[0], live)
+    key_out[...] = key
+    query_out[...] = query
+    moment_out[...] = moment
+    sums_out[...] = jnp.zeros_like(sums_out)
+
+    def moments(start, size):
+        return moment_out[:, pl.ds(start, size)]
+
+    for tile, distances in zip(diagonal_tiles(0, width), (first_out, second_out)):
+        first, keys, start, queries, _ = tile
+        exponent = exponent_ref.at[0:keys, 0:queries]
+        exponent[...] = product(key_out[pl.ds(first, keys), :], query_out[:, pl.ds(start, queries)])
+        split = split_ref.at[:, 0:queries]
+        split_blobs(exponent, split)
+        add_blobs(tile, split, moments, sums_out)
+        split_distances(exponent, distances)
+
+
+def own_part(counts, block):
+    width = block.shape[2]
+    half = width // 2
+    vector = pl.BlockSpec(memory_space=pltpu.VMEM)
+    return pl.pallas_call(
+        own_kernel,
+        out_shape=(
+            jax.ShapeDtypeStruct((width, DISTANCE_ROWS), bf16),
+            jax.ShapeDtypeStruct((DISTANCE_ROWS, width), bf16),
+            jax.ShapeDtypeStruct((16, width), bf16),
+            jax.ShapeDtypeStruct((16, width), f32),
+            jax.ShapeDtypeStruct((2 * half, half), bf16),
+            jax.ShapeDtypeStruct((2 * half, width), bf16),
+        ),
+        in_specs=[pl.BlockSpec(memory_space=pltpu.SMEM), vector],
+        out_specs=(vector,) * 6,
+        scratch_shapes=[pltpu.VMEM((half, width), f32), pltpu.VMEM((2 * half, width), bf16)],
+        compiler_params=pltpu.CompilerParams(vmem_limit_bytes=16 << 20),
+        name="own",
+    )(counts, block)
+
+
 def sweep_kernel(sources, *refs):
     count = len(sources)
+    kept = count <= KEPT_BLOCKS
     filled, blocks, refs = refs[0], refs[1 : count + 1], refs[count + 1 :]
+    early, refs = (refs[:6], refs[6:]) if kept else ((), refs)
     scores_out, drift_out, start_out, speed_out, key_ref, query_ref, moment_ref = refs[:7]
     flux_ref, sums_ref, totals_ref, exponent_ref, *split_refs = refs[7:]
     width = blocks[0].shape[2]
     total_slots = count * width
-    kept = count <= KEPT_BLOCKS
-    half = width // 2
-    tiles = []
-    for query in range(count if kept else 0):
-        start = query * width
-        tiles += [(start, half, start, half, 0), (start + half, half, start, width, half)]
-        tiles += [(key * width, width, start, width, width) for key in range(query + 1, count)]
     here = lax.axis_index("sharers")
 
     lane = lax.broadcasted_iota(jnp.int32, (1, width), 1)
@@ -172,55 +255,69 @@
     for source in sources:
         owner = sum(jnp.where(here == i, source[i], 0) for i in range(count))
         live.append(lane + owner * width < filled[0])
+    skipped = 1 if kept else 0
+    rest = [prepared(block[0], on) for block, on in zip(blocks[skipped:], live[skipped:])]
+    for index, (_, _, key, query, moment) in enumerate(rest):
+        lanes = pl.ds(index * width, width)
+        key_ref[lanes, :] = key
+        query_ref[:, lanes] = query
+        moment_ref[:, lanes] = moment
+    whole = jnp.concatenate([block[0] for block in blocks], axis=1)
+    vector = row_of(whole) < 3
     weight = jnp.concatenate(
         [jnp.where(on, block[0, 3:4], 0.0) for on, block in zip(live, blocks)], axis=1
     )
-    whole = jnp.concatenate([block[0] for block in blocks], axis=1)
-    vector = row_of(whole) < 3
-    parts = grid_parts(jnp.where(vector, whole * SCALE, 0.0))
-    place = parts[0] + parts[1] + parts[2]
-    key, query = distance_features(parts)
-    key_ref[...] = key.T
-    query_ref[...] = query
-    moment_ref[...] = weighted_rows(weight, place)
+    place = grid_parts(jnp.where(vector, whole * SCALE, 0.0))
+    place = place[0] + place[1] + place[2]
     middle = jnp.sum(place * weight, axis=1, keepdims=True)
     middle = middle / jnp.sum(weight, axis=1, keepdims=True)
-    sums_ref[...] = jnp.zeros_like(sums_ref)
-
-    def exponent(key, keys, query, queries):
-        return product(key_ref[pl.ds(key, keys), :], query_ref[:, pl.ds(query, queries)])
-
-    def add_blobs(tile, ref, split):
-        key, keys, query, queries, turned = tile
-        split = split.at[0 : 2 * keys, 0:queries]
-        for group in range(0, keys, GROUP):
-            rows = pl.ds(group, GROUP)
-            store_split(split, rows, jnp.exp2(ref[rows, :]))
-        sums_ref[:, pl.ds(query, queries)] += sum_rows(moment_ref[:, pl.ds(key, keys)], split)
-        if turned:
-            left, right = moment_ref[:, pl.ds(query, turned)], split.at[:, 0:turned]
-            sums_ref[:, pl.ds(key, keys)] += sum_columns(left, right)
+
+    def feature(index, start):
+        if kept and start < width:
+            return early[index], start
+        return (key_ref, query_ref, moment_ref)[index], start - skipped * width
+
+    def moments(start, size):
+        ref, start = feature(2, start)
+        return ref[:, pl.ds(start, size)]
+
+    def exponent(tile):
+        (keys, key), (queries, query) = feature(0, tile[0]), feature(1, tile[2])
+        return product(keys[pl.ds(key, tile[1]), :], queries[:, pl.ds(query, tile[3])])
 
     def block_tile(key, query, both):
         start, first = (pl.multiple_of(block * width, width) for block in (key, query))
         return (start, width, first, width, width if both else 0)
 
+    def piece(ref, tile):
+        return ref.at[0 : 2 * tile[1], 0 : tile[3]]
+
+    sums_ref[...] = jnp.zeros_like(sums_ref)
     if kept:
+        sums_ref[:, 0:width] = early[3][...]
+        tiles = [(key * width, width, 0, width, width) for key in range(1, count)]
+        for query in range(1, count):
+            start = query * width
+            tiles += diagonal_tiles(start, width)
+            tiles += [(key * width, width, start, width, width) for key in range(query + 1, count)]
         exponents = []
         for index, (_, keys, _, queries, _) in enumerate(tiles):
             exponents.append(exponent_ref.at[index, 0:keys, 0:queries])
-        exponents[0][...] = exponent(*tiles[0][:4])
+        exponents[0][...] = exponent(tiles[0])
         for index, tile in enumerate(tiles):
             if index + 1 < len(tiles):
-                exponents[index + 1][...] = exponent(*tiles[index + 1][:4])
-            add_blobs(tile, exponents[index], split_refs[index % 2])
+                exponents[index + 1][...] = exponent(tiles[index + 1])
+            split = piece(split_refs[index % 2], tile)
+            split_blobs(exponents[index], split)
+            add_blobs(tile, split, moments, sums_ref)
     else:
 
         def whole_row(query, carry):
             def one(key, both, carry):
                 tile = block_tile(key, query, both)
-                exponent_ref[0] = exponent(*tile[:4])
-                add_blobs(tile, exponent_ref.at[0], split_refs[0])
+                exponent_ref[0] = exponent(tile)
+                split_blobs(exponent_ref.at[0], split_refs[0])
+                add_blobs(tile, split_refs[0], moments, sums_ref)
                 return carry
 
             carry = one(query, False, carry)
@@ -237,30 +334,24 @@
     flux_ref[...] = drift_rows(weight, centred, score)
     totals_ref[...] = jnp.zeros_like(totals_ref)
 
-    def add_distances(tile, ref, split):
-        key, keys, query, queries, turned = tile
-        split = split.at[0 : 2 * keys, 0:queries]
-        for group in range(0, keys, GROUP):
-            rows = pl.ds(group, GROUP)
-            negative = jnp.minimum(ref[rows, :], -TINY)
-            store_split(split, rows, negative * lax.rsqrt(-negative))
-        upper, lower = sum_rows_less(flux_ref[:, pl.ds(key, keys)], split)
-        totals_ref[:, pl.ds(query, queries)] += upper + lower
-        if turned:
-            left, right = flux_ref[:, pl.ds(query, turned)], split.at[:, 0:turned]
-            upper, lower = sum_columns_less(left, right)
-            totals_ref[:, pl.ds(key, keys)] += upper + lower
+    def fluxes(start, size):
+        return flux_ref[:, pl.ds(start, size)]
 
     if kept:
+        for tile, split in zip(diagonal_tiles(0, width), early[4:6]):
+            add_distances(tile, split, fluxes, totals_ref)
         for index, tile in enumerate(tiles):
-            add_distances(tile, exponents[index], split_refs[index % 2])
+            split = piece(split_refs[index % 2], tile)
+            split_distances(exponents[index], split)
+            add_distances(tile, split, fluxes, totals_ref)
         spread = total_slots
     else:
 
         def one_block(key, carry):
             tile = block_tile(key, 0, False)
-            exponent_ref[0] = exponent(*tile[:4])
-            add_distances(tile, exponent_ref.at[0], split_refs[0])
+            exponent_ref[0] = exponent(tile)
+            split_distances(exponent_ref.at[0], split_refs[0])
+            add_distances(tile, split_refs[0], fluxes, totals_ref)
             return carry
 
         lax.fori_loop(0, count, one_block, 0)
@@ -279,30 +370,36 @@
             start_out[axis, part : part + 1, :] = blocks[0][0, axis : axis + 1, lanes]
 
 
-def sweep(counts, blocks, sources, copies):
+def sweep(counts, blocks, early, sources, copies):
     count, width = len(blocks), blocks[0].shape[2]
     slots = count * width
     kept = count <= KEPT_BLOCKS
+    built = slots - width if kept else slots
     parts = jax.ShapeDtypeStruct((3, width // 128, 128), f32)
-    whole = pl.BlockSpec(memory_space=pltpu.VMEM)
+    vector = pl.BlockSpec(memory_space=pltpu.VMEM)
     return pl.pallas_call(
         functools.partial(sweep_kernel, sources),
-        out_shape=(jax.ShapeDtypeStruct((8, width), f32), parts, parts, jax.ShapeDtypeStruct((copies, 128), f32)),
-        in_specs=[pl.BlockSpec(memory_space=pltpu.SMEM)] + [whole] * count,
-        out_specs=(whole, whole, whole, whole),
+        out_shape=(
+            jax.ShapeDtypeStruct((8, width), f32),
+            parts,
+            parts,
+            jax.ShapeDtypeStruct((copies, 128), f32),
+        ),
+        in_specs=[pl.BlockSpec(memory_space=pltpu.SMEM)] + [vector] * (count + len(early)),
+        out_specs=(vector,) * 4,
         scratch_shapes=[
-            pltpu.VMEM((slots, DISTANCE_ROWS), bf16),
-            pltpu.VMEM((DISTANCE_ROWS, slots), bf16),
-            pltpu.VMEM((16, slots), bf16),
+            pltpu.VMEM((built, DISTANCE_ROWS), bf16),
+            pltpu.VMEM((DISTANCE_ROWS, built), bf16),
+            pltpu.VMEM((16, built), bf16),
             pltpu.VMEM((DRIFT_ROWS, slots), bf16),
             pltpu.VMEM((16, slots), f32),
             pltpu.VMEM((DRIFT_ROWS // 2, slots if kept else width), f32),
-            pltpu.VMEM((count * (count + 3) // 2 if kept else 1, width, width), f32),
+            pltpu.VMEM(((count - 1) * (count + 4) // 2 if kept else 1, width, width), f32),
         ]
         + [pltpu.VMEM((2 * width, width), bf16)] * 2,
         compiler_params=pltpu.CompilerParams(vmem_limit_bytes=(16 << 20) + slots * 2688),
         name="sweep",
-    )(counts, *blocks)
+    )(counts, *blocks, *early)
 
 
 def swapped(value, axis, step):
@@ -335,13 +432,8 @@
     if not whole_cell:
         axes = ("cells", "sharers")
         return jnp.max(lax.all_to_all(speeds[:, None], axes, 0, 0, tiled=True), axis=0)
-    size = lax.axis_size("cells")
-    if size == 4:
-        for other in [swapped(speeds, "cells", step) for step in (2, 3, 1)]:
-            speeds = jnp.maximum(speeds, other)
-    else:
-        for step in bits(size):
-            speeds = jnp.maximum(speeds, swapped(speeds, "cells", step))
+    for step in bits(lax.axis_size("cells")):
+        speeds = jnp.maximum(speeds, swapped(speeds, "cells", 2 * step - 1))
     return speeds[0:1]
 
 
@@ -350,7 +442,8 @@
     blocks, sources = gathered(jnp.pad(package, ((0, 0), (0, 4), (0, 0))))
     whole_cell = len(blocks) <= KEPT_BLOCKS
     copies = 8 if whole_cell else lax.axis_size(("cells", "sharers"))
-    scores, drift, start, speeds = sweep(counts, blocks, sources, copies)
+    early = own_part(counts, blocks[0]) if whole_cell else ()
+    scores, drift, start, speeds = sweep(counts, blocks, early, sources, copies)
     time_step = 0.5 / (largest_speed(speeds, whole_cell) + 1e-06)
     moved = start + time_step[None] * drift
     return moved.reshape(velocities.shape), scores[None, 0:3]

time: 25.6 us -> 24 us (0.938)
  waiting for transfers between devices: 5.21 us -> 3.94 us
  starting transfers between devices: 7.81 us -> 7.09 us
  Pallas kernels: 9.1 us -> 9.49 us
    ppermute x3, waiting for transfers between devices: 2.59 us -> 1.77 us  [gathered(): blocks.append(lax.ppermute(block, 'sharers', list(enumerate(targets))))]
    pallas_call x0 -> x1, Pallas kernels: none -> 0.82 us  [own_part(): pl.pallas_call(own_kernel, out_shape=(jax.ShapeDtypeStruct((width, DISTAN...]
    ppermute x3 -> x2, starting transfers between devices: 2.14 us -> 1.42 us  [swapped(): return lax.ppermute(value, axis, pairs)]
    ppermute x3 -> x2, waiting for transfers between devices: 2.62 us -> 2.17 us  [swapped(): return lax.ppermute(value, axis, pairs)]
    pallas_call x1, Pallas kernels: 9.1 us -> 8.67 us  [sweep(): pl.pallas_call(functools.partial(sweep_kernel, sources), out_shape=(jax.S...]
  transfers between devices with their start and end apart: 6 -> 5, of which waited for: 5 -> 4; matrix products, arithmetic and copies ran while one was open for 2% -> 3% of each run, Pallas kernels for 0% -> 3%
where the time goes in v18:
time: 24 us; the launch traced here: 23.8 us
  Pallas kernels  9.49 us (40%)
  starting transfers between devices  7.09 us (30%)
  waiting for transfers between devices  3.94 us (16%)
  local copies, waits for them, and re-layouts  1.31 us (5%)
  between operations  1.31 us (5%)
  other arithmetic  0.63 us (3%)
    pallas_call x1, Pallas kernels, sweep(): pl.pallas_call(functools.partial(sweep_kernel, sources), out_shape=(jax.S...  8.67 us
    ppermute x3, starting transfers between devices, gathered(): blocks.append(lax.ppermute(block, 'sharers', list(enumerate(targets))))  5.67 us
    ppermute x2, waiting for transfers between devices, swapped(): return lax.ppermute(value, axis, pairs)  2.17 us
    ppermute x3, waiting for transfers between devices, gathered(): blocks.append(lax.ppermute(block, 'sharers', list(enumerate(targets))))  1.77 us
    ppermute x2, starting transfers between devices, swapped(): return lax.ppermute(value, axis, pairs)  1.42 us
    unnamed x4, local copies, waits for them, and re-layouts  1.31 us
    pallas_call x1, Pallas kernels, own_part(): pl.pallas_call(own_kernel, out_shape=(jax.ShapeDtypeStruct((width, DISTAN...  0.82 us
    add x1, other arithmetic, local(): moved = start + time_step[None] * drift  0.61 us
  transfers between devices with their start and end apart: 5, of which 4 were waited for; matrix products, arithmetic and copies ran while one was open for 3% of the time, Pallas kernels for 3%

profile of v18, /device:TPU:0, one launch (start us, length us, event | category | flops | bytes accessed | tf_op | source)
XLA Modules:
  0.0 23.8 jit_solution(11413196621128313986)
XLA Ops:
  0.6 0.0 copy-start
  0.6 0.7 %copy.8 = f32[1,3,512]{2,1,0:T(4,128)S(1)} copy(f32[1,3,512]{2,0,1:T(1,128)} %param.3) | data formatting | bytes 12288 | tf_op args[0]
  1.3 0.0 copy-done
  1.4 4.1 %collective-permute-start.2 = (f32[1,8,512]{2,1,0:T(8,128)S(1)}, f32[1,8,512]{2,1,0:T(8,128)S(1)}, u32[]{:S(2)}, u32[]{:S(2)}) collective-permute-start(f32[1,8,512]{2,1,0:T(8,128)S(1)} %select_maximum_fusion.block.refs_1_), channel_id=1, source_target_pairs={{0,2},{1,3},{2,1},{3,0},{4,6},{5,7},{6,5},{7,4},{8,10},{9,11},{10,... | collective-permute-start | bytes 49160 | tf_op jit(solution)/shard_map/ppermute | solution.py:422
  5.4 1.1 %collective-permute-start.1 = (f32[1,8,512]{2,1,0:T(8,128)S(1)}, f32[1,8,512]{2,1,0:T(8,128)S(1)}, u32[]{:S(2)}, u32[]{:S(2)}) collective-permute-start(f32[1,8,512]{2,1,0:T(8,128)S(1)} %select_maximum_fusion.block.refs_1_), channel_id=1, source_target_pairs={{0,3},{1,2},{2,0},{3,1},{4,7},{5,6},{6,4},{7,5},{8,11},{9,10},{10,... | collective-permute-start | bytes 49160 | tf_op jit(solution)/shard_map/ppermute | solution.py:422
  6.5 0.5 %collective-permute-start = (f32[1,8,512]{2,1,0:T(8,128)S(1)}, f32[1,8,512]{2,1,0:T(8,128)S(1)}, u32[]{:S(2)}, u32[]{:S(2)}) collective-permute-start(f32[1,8,512]{2,1,0:T(8,128)S(1)} %select_maximum_fusion.block.refs_1_), channel_id=1, source_target_pairs={{0,1},{1,0},{2,3},{3,2},{4,5},{5,4},{6,7},{7,6},{8,9},{9,8},{10,11... | collective-permute-start | bytes 49160 | tf_op jit(solution)/shard_map/ppermute | solution.py:422
  7.7 0.8 %own.1 = (bf16[512,96]{1,0:T(8,128)(2,1)S(1)}, bf16[96,512]{1,0:T(8,128)(2,1)S(1)}, bf16[16,512]{1,0:T(8,128)(2,1)S(1)}, f32[16,512]{1,0:T(8,128)S(1)}, bf16[512...) custom-call(s32[1]{0:T(128)S(6)} %copy.11.filled.refs_0_, f32[1,8,512]{2,1,0:T(8,128)S(1)} %select_maximum_fusion.block.refs_1_), custom_call_target="tpu_custom_call" | custom-call | tf_op jit(solution)/shard_map/own/pallas_call | solution.py:224
  8.5 0.0 collective-permute-done.2.refs_4_
  8.5 1.6 %collective-permute-done.1.refs_3_ = f32[1,8,512]{2,1,0:T(8,128)S(1)} collective-permute-done((f32[1,8,512]{2,1,0:T(8,128)S(1)}, f32[1,8,512]{2,1,0:T(8,128)S(1)}, u32[]{:S(2)}, u32[]{:S(2)}) %collective-permute-start.1) | collective-permute-done | bytes 16416 | tf_op jit(solution)/shard_map/ppermute | solution.py:422
  10.1 0.2 collective-permute-done.refs_2_
  10.3 8.7 %sweep.1 = (f32[8,512]{1,0:T(8,128)S(1)}, f32[3,4,128]{2,1,0:T(4,128)S(1)}, f32[3,4,128]{2,1,0:T(4,128)S(1)}, f32[8,128]{1,0:T(8,128)S(1)}) custom-call(s32[1]{0:T(128)S(6)} %copy.11.filled.refs_0_, f32[1,8,512]{2,1,0:T(8,128)S(1)} %select_maximum_fusion.block.refs_1_, f32[1,8,512]{2,1,0:T(8,128)S(1)} %collective-permute-done.refs_2_, ...), custom_call_target="tpu_custom_call" | custom-call | tf_op jit(solution)/shard_map/sweep/pallas_call | solution.py:380
  18.9 0.0 collective-permute-start.3
  18.9 1.2 %collective-permute-done.3 = f32[8,128]{1,0:T(8,128)S(1)} collective-permute-done((f32[8,128]{1,0:T(8,128)S(1)}, f32[8,128]{1,0:T(8,128)S(1)}, u32[]{:S(2)}, u32[]{:S(2)}) %collective-permute-start.3) | collective-permute-done | bytes 4128 | tf_op jit(solution)/shard_map/ppermute | solution.py:407
  20.1 1.4 %collective-permute-start.4 = (f32[8,128]{1,0:T(8,128)S(1)}, f32[8,128]{1,0:T(8,128)S(1)}, u32[]{:S(2)}, u32[]{:S(2)}) collective-permute-start(f32[8,128]{1,0:T(8,128)S(1)} %max.6), channel_id=1, source_target_pairs={{0,12},{4,8},{8,4},{12,0},{1,13},{5,9},{9,5},{13,1},{2,14},{6,10},... | collective-permute-start | bytes 12296 | tf_op jit(solution)/shard_map/ppermute | solution.py:407
  21.5 0.6 %copy.10 = f32[1,3,512]{2,0,1:T(1,128)} copy(f32[1,3,512]{2,1,0:T(4,128)S(1)} %slice_bitcast_fusion) | data formatting | bytes 12288
  22.1 1.0 %collective-permute-done.4 = f32[8,128]{1,0:T(8,128)S(1)} collective-permute-done((f32[8,128]{1,0:T(8,128)S(1)}, f32[8,128]{1,0:T(8,128)S(1)}, u32[]{:S(2)}, u32[]{:S(2)}) %collective-permute-start.4) | collective-permute-done | bytes 4128 | tf_op jit(solution)/shard_map/ppermute | solution.py:407
  23.2 0.6 %multiply_add_fusion = f32[3,4,128]{2,1,0:T(4,128)} fusion(f32[3,4,128]{2,1,0:T(4,128)S(1)} %get-tuple-element.18, f32[3,4,128]{2,1,0:T(4,128)S(1)} %get-tuple-element.20, f32[128]{0:T(128)S(1)} %divide_bitcast_fusion), kind=kLoop, calls=%fused_computation.3 | loop fusion | flops 3072 | bytes 18944 | tf_op jit(solution)/shard_map/add | solution.py:448
  (5 shorter events, 0.0 us)
Async XLA Ops:
  0.6 0.7 %copy-start = (f32[1,512]{1,0:T(1,128)S(1)}, f32[1,512]{1,0:T(1,128)}, u32[]{:S(2)}) copy-start(f32[1,512]{1,0:T(1,128)} %param.4) | copy-start | bytes 6148
  1.4 7.1 %collective-permute-start.2 = (f32[1,8,512]{2,1,0:T(8,128)S(1)}, f32[1,8,512]{2,1,0:T(8,128)S(1)}, u32[]{:S(2)}, u32[]{:S(2)}) collective-permute-start(f32[1,8,512]{2,1,0:T(8,128)S(1)} %select_maximum_fusion.block.refs_1_), channel_id=1, source_target_pairs={{0,2},{1,3},{2,1},{3,0},{4,6},{5,7},{6,5},{7,4},{8,10},{9,11},{10,... | collective-permute-start | bytes 49160 | tf_op jit(solution)/shard_map/ppermute | solution.py:422
  5.4 4.6 %collective-permute-start.1 = (f32[1,8,512]{2,1,0:T(8,128)S(1)}, f32[1,8,512]{2,1,0:T(8,128)S(1)}, u32[]{:S(2)}, u32[]{:S(2)}) collective-permute-start(f32[1,8,512]{2,1,0:T(8,128)S(1)} %select_maximum_fusion.block.refs_1_), channel_id=1, source_target_pairs={{0,3},{1,2},{2,0},{3,1},{4,7},{5,6},{6,4},{7,5},{8,11},{9,10},{10,... | collective-permute-start | bytes 49160 | tf_op jit(solution)/shard_map/ppermute | solution.py:422
  6.5 3.7 %collective-permute-start = (f32[1,8,512]{2,1,0:T(8,128)S(1)}, f32[1,8,512]{2,1,0:T(8,128)S(1)}, u32[]{:S(2)}, u32[]{:S(2)}) collective-permute-start(f32[1,8,512]{2,1,0:T(8,128)S(1)} %select_maximum_fusion.block.refs_1_), channel_id=1, source_target_pairs={{0,1},{1,0},{2,3},{3,2},{4,5},{5,4},{6,7},{7,6},{8,9},{9,8},{10,11... | collective-permute-start | bytes 49160 | tf_op jit(solution)/shard_map/ppermute | solution.py:422
  18.9 1.2 %collective-permute-start.3 = (f32[8,128]{1,0:T(8,128)S(1)}, f32[8,128]{1,0:T(8,128)S(1)}, u32[]{:S(2)}, u32[]{:S(2)}) collective-permute-start(f32[8,128]{1,0:T(8,128)S(1)} %get-tuple-element.19), channel_id=1, source_target_pairs={{0,4},{4,0},{8,12},{12,8},{1,5},{5,1},{9,13},{13,9},{2,6},{6,2},{1... | collective-permute-start | bytes 12296 | tf_op jit(solution)/shard_map/ppermute | solution.py:407
  20.1 3.0 %collective-permute-start.4 = (f32[8,128]{1,0:T(8,128)S(1)}, f32[8,128]{1,0:T(8,128)S(1)}, u32[]{:S(2)}, u32[]{:S(2)}) collective-permute-start(f32[8,128]{1,0:T(8,128)S(1)} %max.6), channel_id=1, source_target_pairs={{0,12},{4,8},{8,4},{12,0},{1,13},{5,9},{9,5},{13,1},{2,14},{6,10},... | collective-permute-start | bytes 12296 | tf_op jit(solution)/shard_map/ppermute | solution.py:407

commit v19 on v16

v19 whole, which is shorter than its diff:
```python
import functools
import functools
import math

import jax
import jax.numpy as jnp
from jax import lax
from jax.experimental import pallas as pl
from jax.experimental.pallas import tpu as pltpu
from jax.sharding import PartitionSpec as P

EPS = 0.35
SCALE = math.sqrt(math.log2(math.e) / (2.0 * EPS * EPS))
GRID = 4.0
TINY = 1e-30
GROUP = 16
DISTANCE_ROWS = 96
DRIFT_ROWS = 64
bf16, f32 = jnp.bfloat16, jnp.float32


def round_bf16(value):
    return value.astype(bf16).astype(f32)


def pieces(value, count):
    parts = []
    for _ in range(count):
        part = round_bf16(value)
        parts.append(part)
        value = value - part
    return parts


def row_of(value):
    return lax.broadcasted_iota(jnp.int32, value.shape, 0)


def rows_sum(value):
    return jnp.sum(value, axis=0, keepdims=True)


def stacked(groups):
    if len(groups) % 2:
        groups = groups + [jnp.zeros_like(groups[0])]
    return jnp.concatenate(groups, axis=0).astype(bf16)


def scalar_groups(value, like):
    row = row_of(like)
    first, second, third = pieces(value, 3)
    low = jnp.where(row == 0, first, jnp.where(row == 1, second, jnp.where(row == 2, third, 0.0)))
    high = jnp.where(row == 3, first, jnp.where(row == 4, second, jnp.where(row == 5, third, 0.0)))
    ones_low, ones_high = row < 3, (row >= 3) & (row < 6)
    return jnp.where(ones_high, 1.0, low), jnp.where(ones_low, 1.0, high)


def grid_parts(place):
    coarse = jnp.floor(place * GRID + 0.5) * (1.0 / GRID)
    return [coarse] + pieces(place - coarse, 2)


def distance_features(parts):
    coarse, fine, rest = parts
    minor = fine + rest
    query_norm, key_norm = scalar_groups(-rows_sum(coarse * coarse), coarse)
    query_less, key_less = scalar_groups(-rows_sum(minor * (2.0 * coarse + minor)), coarse)
    key = [coarse, key_norm, coarse, coarse, fine, rest, key_less, fine, fine, rest, rest]
    coarse, fine, rest = coarse * 2.0, fine * 2.0, rest * 2.0
    query = [coarse, query_norm, fine, rest, coarse, coarse, query_less, fine, rest, fine, rest]
    return stacked(key), stacked(query)


def weighted_rows(weight, value):
    row = row_of(value)
    whole = jnp.where(row < 3, value, jnp.where(row == 3, 1.0, 0.0)) * weight
    first, second, third = pieces(whole, 3)
    return stacked([first, second + pltpu.roll(third, 4, 0)])


def product(left, right):
    return jnp.dot(left, right, preferred_element_type=f32)


def store_split(ref, rows, matrix):
    half = ref.shape[0] // 2
    upper = matrix.astype(bf16)
    ref[rows, :] = upper
    ref[pl.ds(half + rows.start, rows.size), :] = (matrix - upper.astype(f32)).astype(bf16)


def sum_rows(left, ref):
    return product(jnp.concatenate([left, left], axis=1), ref[...])


def sum_columns(left, ref):
    both = lax.dot_general(left, ref[...], (((1,), (1,)), ((), ())), preferred_element_type=f32)
    half = ref.shape[0] // 2
    return both[:, :half] + both[:, half:]


def sum_rows_less(left, ref):
    half = ref.shape[0] // 2
    both = product(left, ref[:half, :])
    few = left.shape[0] // 2
    return both[:few] + product(left[:few], ref[half:, :]), both[few:]


def sum_columns_less(left, ref):
    half, few = ref.shape[0] // 2, left.shape[0] // 2
    turned = (((1,), (1,)), ((), ()))
    both = lax.dot_general(left, ref[:half, :], turned, preferred_element_type=f32)
    less = lax.dot_general(left[:few], ref[half:, :], turned, preferred_element_type=f32)
    return both[:few] + less, both[few:]


def joined(total):
    upper, lower = total[0:8], total[8:16]
    return upper + lower + pltpu.roll(lower, 4, 0)


def drift_rows(weight, place, score):
    row = row_of(place)
    base = place + jnp.where(row == 3, 1.0, 0.0) + pltpu.roll(score, 4, 0)
    cubic = rows_sum(place * place) * score - rows_sum(place * score) * place
    groups = [weight * base]
    for i in range(3):
        here = slice(i, i + 1)
        groups.append(weight * jnp.where(row == 3, cubic[here], place[here] * base))
    return stacked(sum(map(list, zip(*[pieces(group, 2) for group in groups])), []))


def drift_sum(total, place, score):
    row = row_of(place)
    first, *rest = [total[8 * i : 8 * i + 8] for i in range(4)]
    turned = [pltpu.roll(group, 4, 0) for group in rest]
    count, scores = first[3:4], pltpu.roll(first, 4, 0)
    square, both = rows_sum(place * place), rows_sum(place * score)
    trace = rest[0][0:1] + rest[1][1:2] + rest[2][2:3]
    cross = turned[0][0:1] + turned[1][1:2] + turned[2][2:3]
    drift = score * (square * count - 2.0 * rows_sum(place * first) + trace) - square * scores
    drift += both * first + place * (
        rows_sum(place * scores) + rows_sum(score * first) - both * count - cross
    )
    ends = []
    for i in range(3):
        here = slice(i, i + 1)
        drift += 2.0 * place[here] * turned[i] - score[here] * rest[i]
        ends.append(rows_sum(place * turned[i]) + rest[i][3:4])
    return drift - jnp.where(row == 0, ends[0], jnp.where(row == 1, ends[1], ends[2]))


def prepared(whole, live):
    weight = jnp.where(live, whole[3:4], 0.0)
    parts = grid_parts(jnp.where(row_of(whole) < 3, whole * SCALE, 0.0))
    place = parts[0] + parts[1] + parts[2]
    key, query = distance_features(parts)
    return weight, place, key.T, query, weighted_rows(weight, place)


def split_blobs(exponent, split):
    for group in range(0, exponent.shape[0], GROUP):
        rows = pl.ds(group, GROUP)
        store_split(split, rows, jnp.exp2(exponent[rows, :]))


def split_distances(exponent, split):
    for group in range(0, exponent.shape[0], GROUP):
        rows = pl.ds(group, GROUP)
        negative = jnp.minimum(exponent[rows, :], -TINY)
        store_split(split, rows, negative * lax.rsqrt(-negative))


def diagonal_tiles(start, width):
    half = width // 2
    return [(start, half, start, half, 0), (start + half, half, start, width, half)]


def add_blobs(tile, split, moments, sums_ref):
    key, keys, query, queries, turned = tile
    sums_ref[:, pl.ds(query, queries)] += sum_rows(moments(key, keys), split)
    if turned:
        sums_ref[:, pl.ds(key, keys)] += sum_columns(moments(query, turned), split.at[:, 0:turned])


def add_distances(tile, split, fluxes, totals_ref):
    key, keys, query, queries, turned = tile
    upper, lower = sum_rows_less(fluxes(key, keys), split)
    totals_ref[:, pl.ds(query, queries)] += upper + lower
    if turned:
        upper, lower = sum_columns_less(fluxes(query, turned), split.at[:, 0:turned])
        totals_ref[:, pl.ds(key, keys)] += upper + lower


def stage(tiles, exponent, moments, sums_ref, exponent_refs, split_refs, distance_refs):
    def buffer(index):
        _, keys, _, queries, _ = tiles[index]
        return exponent_refs[index % 2].at[0:keys, 0:queries]

    buffer(0)[...] = exponent(tiles[0])
    for index, tile in enumerate(tiles):
        if index + 1 < len(tiles):
            buffer(index + 1)[...] = exponent(tiles[index + 1])
        split = split_refs[index % 2].at[0 : 2 * tile[1], 0 : tile[3]]
        split_blobs(buffer(index), split)
        add_blobs(tile, split, moments, sums_ref)
        split_distances(buffer(index), distance_refs[index])


def looked_up(refs, width, axis):
    def read(start, size):
        at = pl.ds(start % width, size)
        ref = refs[start // width]
        return ref[at, :] if axis == 0 else ref[:, at]

    return read


def exponent_of(keys, queries):
    return lambda tile: product(keys(tile[0], tile[1]), queries(tile[2], tile[3]))


def lanes_of(source, width):
    return lax.broadcasted_iota(jnp.int32, (1, width), 1) + source * width


def owner_of(sources):
    here = lax.axis_index("sharers")
    return sum(jnp.where(here == i, source, 0) for i, source in enumerate(sources))


def own_kernel(filled_hbm, block, filled_out, key_out, query_out, moment_out, sums_out, first_out,
               second_out, filled_ref, filled_sem, *scratch):
    width = block.shape[2]
    fetch = pltpu.make_async_copy(filled_hbm, filled_ref, filled_sem)
    fetch.start()
    everything = lax.broadcasted_iota(jnp.int32, (1, width), 1) >= 0
    _, place, key, query, _ = prepared(block[0], everything)
    key_out[...] = key
    query_out[...] = query
    sums_out[...] = jnp.zeros_like(sums_out)
    fetch.wait()
    live = lanes_of(lax.axis_index("sharers"), width) < filled_ref[0]
    moment_out[...] = weighted_rows(jnp.where(live, block[0, 3:4], 0.0), place)
    filled_out[...] = jnp.full(filled_out.shape, filled_ref[0], jnp.int32)
    exponent = exponent_of(looked_up([key_out], width, 0), looked_up([query_out], width, 1))
    moments = looked_up([moment_out], width, 1)
    tiles = diagonal_tiles(0, width)
    stage(tiles, exponent, moments, sums_out, scratch[:2], scratch[2:], (first_out, second_out))


def next_kernel(sources, filled, block, own_key, own_query, own_moment, own_sums, key_out,
                query_out, moment_out, sums_out, tile_out, first_out, second_out, *scratch):
    width = block.shape[2]
    live = lanes_of(owner_of(sources), width) < filled[0:1, :]
    _, _, key, query, moment = prepared(block[0], live)
    key_out[...] = key
    query_out[...] = query
    moment_out[...] = moment
    sums_out[:, 0:width] = own_sums[...]
    sums_out[:, width:] = jnp.zeros_like(own_sums)
    exponent = exponent_of(
        looked_up([own_key, key_out], width, 0), looked_up([own_query, query_out], width, 1)
    )
    moments = looked_up([own_moment, moment_out], width, 1)
    tiles = [(width, width, 0, width, width)] + diagonal_tiles(width, width)
    distances = (tile_out, first_out, second_out)
    stage(tiles, exponent, moments, sums_out, scratch[:2], scratch[2:], distances)


def feature_shapes(width):
    return [
        jax.ShapeDtypeStruct((width, DISTANCE_ROWS), bf16),
        jax.ShapeDtypeStruct((DISTANCE_ROWS, width), bf16),
        jax.ShapeDtypeStruct((16, width), bf16),
    ]


def diagonal_shapes(width):
    half = width // 2
    return [
        jax.ShapeDtypeStruct((2 * half, half), bf16),
        jax.ShapeDtypeStruct((2 * half, width), bf16),
    ]


def stage_scratch(width):
    return [pltpu.VMEM((width, width), f32)] * 2 + [pltpu.VMEM((2 * width, width), bf16)] * 2


def own_part(counts, block):
    width = block.shape[2]
    vector = pl.BlockSpec(memory_space=pltpu.VMEM)
    shapes = [jax.ShapeDtypeStruct((8, width), jnp.int32)] + feature_shapes(width)
    shapes += [jax.ShapeDtypeStruct((16, width), f32)] + diagonal_shapes(width)
    return pl.pallas_call(
        own_kernel,
        out_shape=shapes,
        in_specs=[pl.BlockSpec(memory_space=pltpu.HBM), vector],
        out_specs=[vector] * len(shapes),
        scratch_shapes=[pltpu.SMEM((1,), jnp.int32), pltpu.SemaphoreType.DMA]
        + stage_scratch(width),
        compiler_params=pltpu.CompilerParams(vmem_limit_bytes=16 << 20),
        name="own",
    )(counts, block)


def next_part(filled, block, features, sums, sources):
    width = block.shape[2]
    vector = pl.BlockSpec(memory_space=pltpu.VMEM)
    shapes = feature_shapes(width) + [jax.ShapeDtypeStruct((16, 2 * width), f32)]
    shapes += [jax.ShapeDtypeStruct((2 * width, width), bf16)] + diagonal_shapes(width)
    return pl.pallas_call(
        functools.partial(next_kernel, sources),
        out_shape=shapes,
        in_specs=[vector] * 6,
        out_specs=[vector] * len(shapes),
        scratch_shapes=stage_scratch(width),
        compiler_params=pltpu.CompilerParams(vmem_limit_bytes=20 << 20),
        name="next",
    )(filled, block, *features, sums)


def late_tiles(count, width):
    tiles = []
    for query in range(count):
        first = max(query + 1, 2)
        tiles += diagonal_tiles(query * width, width) if query >= 2 else []
        tiles += [(key * width, width, query * width, width, width) for key in range(first, count)]
    return tiles


def scored(weight, place, sums):
    vector, live = row_of(place) < 3, weight > 0.0
    density_sum = jnp.where(live, sums[3:4], 1.0)
    pull = place * density_sum - sums
    return jnp.where(vector & live, pull / (-SCALE * EPS * EPS * density_sum), 0.0)


def whole_cell(blocks, live):
    weight = jnp.concatenate(
        [jnp.where(on, block[0, 3:4], 0.0) for on, block in zip(live, blocks)], axis=1
    )
    whole = jnp.concatenate([block[0] for block in blocks], axis=1)
    vector = row_of(whole) < 3
    parts = grid_parts(jnp.where(vector, whole * SCALE, 0.0))
    place = parts[0] + parts[1] + parts[2]
    middle = jnp.sum(place * weight, axis=1, keepdims=True)
    middle = middle / jnp.sum(weight, axis=1, keepdims=True)
    return weight, place, jnp.where(vector, place - middle, 0.0)


def finish(blocks, total_slots, weight, centred, score, totals, outs):
    scores_out, drift_out, start_out, speed_out = outs
    width = blocks[0].shape[2]
    spread = totals.shape[1]
    drift = drift_sum(totals, centred[:, 0:spread], score[:, 0:spread])
    factor = 1.0 / (SCALE * SCALE * SCALE * total_slots)
    live = (row_of(drift) < 3) & (weight[:, 0:spread] > 0.0)
    drift = jnp.where(live, drift * factor, 0.0)
    largest = jnp.max(rows_sum(drift * drift), axis=1, keepdims=True)
    speed_out[...] = jnp.broadcast_to(jnp.sqrt(largest), speed_out.shape)
    scores_out[...] = score[:, 0:width]
    for part in range(width // 128):
        lanes = slice(part * 128, part * 128 + 128)
        for axis in range(3):
            drift_out[axis, part : part + 1, :] = drift[axis : axis + 1, lanes]
            start_out[axis, part : part + 1, :] = blocks[0][0, axis : axis + 1, lanes]


def sweep_kernel(sources, *refs):
    count = len(sources)
    filled, blocks, refs = refs[0], refs[1 : count + 1], list(refs[count + 1 :])
    blocks = blocks[:2] + blocks[:1:-1]
    own, following, refs = refs[:5], refs[5:12], refs[12:]
    outs, (key_ref, query_ref, moment_ref, flux_ref, sums_ref, totals_ref), refs = (
        refs[:4], refs[4:10], refs[10:]
    )
    width = blocks[0].shape[2]
    half = 2 * width
    scratch, distance_refs = refs[:4], refs[4:]

    live = [lanes_of(owner_of(source), width) < filled[0:1, :] for source in sources]
    late = range(2, count)
    for index in late:
        _, _, key, query, moment = prepared(blocks[index][0], live[index])
        lanes = pl.ds((index - 2) * width, width)
        key_ref[lanes, :] = key
        query_ref[:, lanes] = query
        moment_ref[:, lanes] = moment
    weight, place, centred = whole_cell(blocks, live)
    lanes = [pl.ds((index - 2) * width, width) for index in late]
    keys = [own[0], following[0]] + [key_ref.at[lane, :] for lane in lanes]
    queries = [own[1], following[1]] + [query_ref.at[:, lane] for lane in lanes]
    moments = [own[2], following[2]] + [moment_ref.at[:, lane] for lane in lanes]
    exponent = exponent_of(looked_up(keys, width, 0), looked_up(queries, width, 1))

    sums_ref[:, 0:half] = following[3][...]
    sums_ref[:, half:] = jnp.zeros_like(sums_ref[:, half:])
    tiles = late_tiles(count, width)
    stage(
        tiles, exponent, looked_up(moments, width, 1), sums_ref, scratch[:2], scratch[2:],
        distance_refs,
    )
    score = scored(weight, place, joined(sums_ref[...]))
    flux_ref[...] = drift_rows(weight, centred, score)
    totals_ref[...] = jnp.zeros_like(totals_ref)

    def fluxes(start, size):
        return flux_ref[:, pl.ds(start, size)]

    early = diagonal_tiles(0, width) + [(width, width, 0, width, width)]
    early += diagonal_tiles(width, width)
    for tile, split in zip(early + tiles, own[3:5] + following[4:7] + distance_refs):
        add_distances(tile, split, fluxes, totals_ref)
    finish(blocks, count * width, weight, centred, score, totals_ref[...], outs)


def sweep_shapes(width, copies):
    parts = jax.ShapeDtypeStruct((3, width // 128, 128), f32)
    speeds = jax.ShapeDtypeStruct((copies, 128), f32)
    return [jax.ShapeDtypeStruct((8, width), f32), parts, parts, speeds]


def sweep(counts, blocks, sources):
    count, width = len(blocks), blocks[0].shape[2]
    slots, late = count * width, (count - 2) * width
    filled, *own = own_part(counts, blocks[0])
    following = next_part(filled, blocks[1], own[:3], own[3], sources[1])
    early = [*own[:3], *own[4:], *following]
    vector = pl.BlockSpec(memory_space=pltpu.VMEM)
    distances = [pltpu.VMEM((2 * tile[1], tile[3]), bf16) for tile in late_tiles(count, width)]
    return pl.pallas_call(
        functools.partial(sweep_kernel, sources),
        out_shape=sweep_shapes(width, 8),
        in_specs=[vector] * (1 + count + len(early)),
        out_specs=[vector] * 4,
        scratch_shapes=[
            pltpu.VMEM((late, DISTANCE_ROWS), bf16),
            pltpu.VMEM((DISTANCE_ROWS, late), bf16),
            pltpu.VMEM((16, late), bf16),
            pltpu.VMEM((DRIFT_ROWS, slots), bf16),
            pltpu.VMEM((16, slots), f32),
            pltpu.VMEM((DRIFT_ROWS // 2, slots), f32),
        ]
        + stage_scratch(width)
        + distances,
        compiler_params=pltpu.CompilerParams(vmem_limit_bytes=24 << 20),
        name="sweep",
    )(filled, *blocks[:2], *blocks[:1:-1], *early)


def long_kernel(sources, filled, *refs):
    count = len(sources)
    blocks, outs, refs = refs[:count], refs[count : count + 4], refs[count + 4 :]
    key_ref, query_ref, moment_ref, flux_ref, sums_ref, totals_ref, exponent_ref, split_ref = refs
    width = blocks[0].shape[2]
    live = [lanes_of(owner_of(source), width) < filled[0] for source in sources]
    for index, (block, on) in enumerate(zip(blocks, live)):
        _, _, key, query, moment = prepared(block[0], on)
        lanes = pl.ds(index * width, width)
        key_ref[lanes, :] = key
        query_ref[:, lanes] = query
        moment_ref[:, lanes] = moment
    weight, place, centred = whole_cell(blocks, live)
    sums_ref[...] = jnp.zeros_like(sums_ref)
    totals_ref[...] = jnp.zeros_like(totals_ref)

    def block_tile(key, query, both):
        start, first = (pl.multiple_of(block * width, width) for block in (key, query))
        return (start, width, first, width, width if both else 0)

    def fill(tile):
        key, keys, query, queries, _ = tile
        exponent_ref[...] = product(key_ref[pl.ds(key, keys), :], query_ref[:, pl.ds(query, queries)])

    def blobs(key, query, both):
        tile = block_tile(key, query, both)
        fill(tile)
        split_blobs(exponent_ref, split_ref)
        add_blobs(tile, split_ref, lambda at, size: moment_ref[:, pl.ds(at, size)], sums_ref)

    @pl.loop(0, count)
    def _(query):
        blobs(query, query, False)

        @pl.loop(query + 1, count)
        def _(key):
            blobs(key, query, True)

    score = scored(weight, place, joined(sums_ref[...]))
    flux_ref[...] = drift_rows(weight, centred, score)

    @pl.loop(0, count)
    def _(key):
        tile = block_tile(key, 0, False)
        fill(tile)
        split_distances(exponent_ref, split_ref)
        add_distances(tile, split_ref, lambda at, size: flux_ref[:, pl.ds(at, size)], totals_ref)

    finish(blocks, count * width, weight, centred, score, totals_ref[...], outs)


def long_sweep(counts, blocks, sources, copies):
    count, width = len(blocks), blocks[0].shape[2]
    slots = count * width
    vector = pl.BlockSpec(memory_space=pltpu.VMEM)
    return pl.pallas_call(
        functools.partial(long_kernel, sources),
        out_shape=sweep_shapes(width, copies),
        in_specs=[pl.BlockSpec(memory_space=pltpu.SMEM)] + [vector] * count,
        out_specs=[vector] * 4,
        scratch_shapes=[
            pltpu.VMEM((slots, DISTANCE_ROWS), bf16),
            pltpu.VMEM((DISTANCE_ROWS, slots), bf16),
            pltpu.VMEM((16, slots), bf16),
            pltpu.VMEM((DRIFT_ROWS, slots), bf16),
            pltpu.VMEM((16, slots), f32),
            pltpu.VMEM((DRIFT_ROWS // 2, width), f32),
            pltpu.VMEM((width, width), f32),
            pltpu.VMEM((2 * width, width), bf16),
        ],
        compiler_params=pltpu.CompilerParams(vmem_limit_bytes=(16 << 20) + slots * 2688),
        name="sweep",
    )(counts, *blocks)


def swapped(value, axis, step):
    pairs = [(i, i ^ step) for i in range(lax.axis_size(axis))]
    return lax.ppermute(value, axis, pairs)


def bits(size):
    return [1 << bit for bit in range(size.bit_length() - 1)]


ROUNDS = ((2, 3, 1, 0), (3, 2, 0, 1), (1, 0, 3, 2))


def gathered(block):
    size = lax.axis_size("sharers")
    if size == len(ROUNDS) + 1:
        blocks, sources = [block], [tuple(range(size))]
        for targets in ROUNDS:
            blocks.append(lax.ppermute(block, "sharers", list(enumerate(targets))))
            sources.append(tuple(targets.index(i) for i in range(size)))
        return blocks, sources
    for step in bits(size):
        block = jnp.concatenate([block, swapped(block, "sharers", step)], axis=0)
    sources = [tuple(i ^ step for i in range(size)) for step in range(size)]
    return [block[i : i + 1] for i in range(size)], sources


def local(velocities, weights, counts):
    package = jnp.concatenate([velocities, weights[:, None]], axis=1)
    blocks, sources = gathered(jnp.pad(package, ((0, 0), (0, 4), (0, 0))))
    if len(blocks) == len(ROUNDS) + 1:
        scores, drift, start, speeds = sweep(counts, blocks, sources)
        for step in bits(lax.axis_size("cells")):
            speeds = jnp.maximum(speeds, swapped(speeds, "cells", 2 * step - 1))
        largest = speeds[0:1]
    else:
        axes = ("cells", "sharers")
        scores, drift, start, speeds = long_sweep(counts, blocks, sources, lax.axis_size(axes))
        largest = jnp.max(lax.all_to_all(speeds[:, None], axes, 0, 0, tiled=True), axis=0)
    time_step = 0.5 / (largest + 1e-06)
    moved = start + time_step[None] * drift
    return moved.reshape(velocities.shape), scores[None, 0:3]


def solution(mesh):
    in_specs = (
        P(("groups", "cells"), None, "sharers"),
        P(("groups", "cells"), "sharers"),
        P(("groups", "cells")),
    )
    out_specs = (P(("groups", "cells"), None, "sharers"), P(("groups", "cells"), None, "sharers"))
    return jax.shard_map(local, mesh=mesh, in_specs=in_specs, out_specs=out_specs, check_vma=False)
```

time: 25.6 us -> 23.3 us (0.910)
  waiting for transfers between devices: 5.11 us -> 2.33 us
  Pallas kernels: 9.77 us -> 10.5 us
  starting transfers between devices: 7.32 us -> 6.95 us
    ppermute x3, waiting for transfers between devices: 2.59 us -> 0.01 us  [gathered(): blocks.append(lax.ppermute(block, 'sharers', list(enumerate(targets))))]
    pallas_call x1 -> x3, Pallas kernels: 9.77 us -> 10.5 us  [the longest x1 7.74 us: sweep(): pl.pallas_call(functools.partial(sweep_kernel, sources), out_shape=sweep_...]
    ppermute x2, starting transfers between devices: 1.65 us -> 1.28 us  [swapped(): return lax.ppermute(value, axis, pairs)]
  transfers between devices with their start and end apart: 5 -> 5, of which waited for: 5 -> 2; matrix products, arithmetic and copies ran while one was open for 2% -> 3% of each run, Pallas kernels for 0% -> 12%
where the time goes in v19:
time: 23.3 us; the launch traced here: 23.1 us
  Pallas kernels  10.5 us (45%)
  starting transfers between devices  6.95 us (30%)
  waiting for transfers between devices  2.33 us (10%)
  between operations  1.32 us (6%)
  local copies, waits for them, and re-layouts  1.31 us (6%)
  other arithmetic  0.63 us (3%)
    pallas_call x1, Pallas kernels, sweep(): pl.pallas_call(functools.partial(sweep_kernel, sources), out_shape=sweep_...  7.74 us
    ppermute x3, starting transfers between devices, gathered(): blocks.append(lax.ppermute(block, 'sharers', list(enumerate(targets))))  5.67 us
    ppermute x2, waiting for transfers between devices, swapped(): return lax.ppermute(value, axis, pairs)  2.32 us
    pallas_call x1, Pallas kernels, next_part(): pl.pallas_call(functools.partial(next_kernel, sources), out_shape=shapes,...  1.56 us
    unnamed x4, local copies, waits for them, and re-layouts  1.31 us
    ppermute x2, starting transfers between devices, swapped(): return lax.ppermute(value, axis, pairs)  1.28 us
    pallas_call x1, Pallas kernels, own_part(): pl.pallas_call(own_kernel, out_shape=shapes, in_specs=[pl.BlockSpec(memor...  1.23 us
    add x1, other arithmetic, local(): moved = start + time_step[None] * drift  0.61 us
  transfers between devices with their start and end apart: 5, of which 2 were waited for; matrix products, arithmetic and copies ran while one was open for 3% of the time, Pallas kernels for 12%

profile of v19, /device:TPU:0, one launch (start us, length us, event | category | flops | bytes accessed | tf_op | source)
XLA Modules:
  0.0 23.1 jit_solution(10043743590941949133)
XLA Ops:
  0.6 0.0 copy-start
  0.6 0.7 %copy.8 = f32[1,3,512]{2,1,0:T(4,128)S(1)} copy(f32[1,3,512]{2,0,1:T(1,128)} %param.3) | data formatting | bytes 12288 | tf_op args[0]
  1.3 0.0 copy-done
  1.4 4.1 %collective-permute-start = (f32[1,8,512]{2,1,0:T(8,128)S(1)}, f32[1,8,512]{2,1,0:T(8,128)S(1)}, u32[]{:S(2)}, u32[]{:S(2)}) collective-permute-start(f32[1,8,512]{2,1,0:T(8,128)S(1)} %select_maximum_fusion.block.refs_1_), channel_id=1, source_target_pairs={{0,2},{1,3},{2,1},{3,0},{4,6},{5,7},{6,5},{7,4},{8,10},{9,11},{10,... | collective-permute-start | bytes 49160 | tf_op jit(solution)/shard_map/ppermute | solution.py:545
  5.4 1.1 %collective-permute-start.2 = (f32[1,8,512]{2,1,0:T(8,128)S(1)}, f32[1,8,512]{2,1,0:T(8,128)S(1)}, u32[]{:S(2)}, u32[]{:S(2)}) collective-permute-start(f32[1,8,512]{2,1,0:T(8,128)S(1)} %select_maximum_fusion.block.refs_1_), channel_id=1, source_target_pairs={{0,3},{1,2},{2,0},{3,1},{4,7},{5,6},{6,4},{7,5},{8,11},{9,10},{10,... | collective-permute-start | bytes 49160 | tf_op jit(solution)/shard_map/ppermute | solution.py:545
  6.5 0.5 %collective-permute-start.1 = (f32[1,8,512]{2,1,0:T(8,128)S(1)}, f32[1,8,512]{2,1,0:T(8,128)S(1)}, u32[]{:S(2)}, u32[]{:S(2)}) collective-permute-start(f32[1,8,512]{2,1,0:T(8,128)S(1)} %select_maximum_fusion.block.refs_1_), channel_id=1, source_target_pairs={{0,1},{1,0},{2,3},{3,2},{4,5},{5,4},{6,7},{7,6},{8,9},{9,8},{10,11... | collective-permute-start | bytes 49160 | tf_op jit(solution)/shard_map/ppermute | solution.py:545
  7.7 1.2 %own.1 = (s32[8,512]{1,0:T(8,128)S(1)}, bf16[512,96]{1,0:T(8,128)(2,1)S(1)}, bf16[96,512]{1,0:T(8,128)(2,1)S(1)}, bf16[16,512]{1,0:T(8,128)(2,1)S(1)}, f32[16,51...) custom-call(s32[1]{0:T(128)S(6)} %copy.11.filled_hbm, ...), custom_call_target="tpu_custom_call" | custom-call | tf_op jit(solution)/shard_map/own/pallas_call | solution.py:296
  8.9 0.0 collective-permute-done.block.refs_2_
  8.9 1.6 %next.1 = (bf16[512,96]{1,0:T(8,128)(2,1)S(1)}, bf16[96,512]{1,0:T(8,128)(2,1)S(1)}, bf16[16,512]{1,0:T(8,128)(2,1)S(1)}, f32[16,1024]{1,0:T(8,128)S(1)}, bf16[1...) custom-call(s32[8,512]{1,0:T(8,128)S(1)} %get-tuple-element.20.filled.refs_0_, ...), custom_call_target="tpu_custom_call" | custom-call | tf_op jit(solution)/shard_map/next/pallas_call | solution.py:313
  10.5 0.0 collective-permute-done.2.refs_4_
  10.5 0.0 collective-permute-done.1.refs_3_
  10.5 7.7 %sweep.1 = (f32[8,512]{1,0:T(8,128)S(1)}, f32[3,4,128]{2,1,0:T(4,128)S(1)}, f32[3,4,128]{2,1,0:T(4,128)S(1)}, f32[8,128]{1,0:T(8,128)S(1)}) custom-call(s32[8,512]{1,0:T(8,128)S(1)} %get-tuple-element.20.filled.refs_0_, f32[1,8,512]{2,1,0:T(8,128)S(1)} %select_maximum_fusion.block.refs_1_, f32[1,8,512]{2,1,0:T(8,128)S(1)} %collective-permute-done.block.refs_2_, ...), custom_call_target="tpu_custom_call" | custom-call | tf_op jit(solution)/shard_map/sweep/pallas_call | solution.py:433
  18.2 0.0 collective-permute-start.3
  18.2 1.2 %collective-permute-done.3 = f32[8,128]{1,0:T(8,128)S(1)} collective-permute-done((f32[8,128]{1,0:T(8,128)S(1)}, f32[8,128]{1,0:T(8,128)S(1)}, u32[]{:S(2)}, u32[]{:S(2)}) %collective-permute-start.3) | collective-permute-done | bytes 4128 | tf_op jit(solution)/shard_map/ppermute | solution.py:530
  19.4 1.3 %collective-permute-start.4 = (f32[8,128]{1,0:T(8,128)S(1)}, f32[8,128]{1,0:T(8,128)S(1)}, u32[]{:S(2)}, u32[]{:S(2)}) collective-permute-start(f32[8,128]{1,0:T(8,128)S(1)} %max.6), channel_id=1, source_target_pairs={{0,12},{4,8},{8,4},{12,0},{1,13},{5,9},{9,5},{13,1},{2,14},{6,10},... | collective-permute-start | bytes 12296 | tf_op jit(solution)/shard_map/ppermute | solution.py:530
  20.7 0.6 %copy.10 = f32[1,3,512]{2,0,1:T(1,128)} copy(f32[1,3,512]{2,1,0:T(4,128)S(1)} %slice_bitcast_fusion) | data formatting | bytes 12288
  21.3 1.2 %collective-permute-done.4 = f32[8,128]{1,0:T(8,128)S(1)} collective-permute-done((f32[8,128]{1,0:T(8,128)S(1)}, f32[8,128]{1,0:T(8,128)S(1)}, u32[]{:S(2)}, u32[]{:S(2)}) %collective-permute-start.4) | collective-permute-done | bytes 4128 | tf_op jit(solution)/shard_map/ppermute | solution.py:530
  22.5 0.6 %multiply_add_fusion = f32[3,4,128]{2,1,0:T(4,128)} fusion(f32[3,4,128]{2,1,0:T(4,128)S(1)} %get-tuple-element.34, f32[3,4,128]{2,1,0:T(4,128)S(1)} %get-tuple-element.36, f32[128]{0:T(128)S(1)} %divide_bitcast_fusion), kind=kLoop, calls=%fused_computation.3 | loop fusion | flops 3072 | bytes 18944 | tf_op jit(solution)/shard_map/add | solution.py:567
  (5 shorter events, 0.0 us)
Async XLA Ops:
  0.6 0.7 %copy-start = (f32[1,512]{1,0:T(1,128)S(1)}, f32[1,512]{1,0:T(1,128)}, u32[]{:S(2)}) copy-start(f32[1,512]{1,0:T(1,128)} %param.4) | copy-start | bytes 6148
  1.4 7.6 %collective-permute-start = (f32[1,8,512]{2,1,0:T(8,128)S(1)}, f32[1,8,512]{2,1,0:T(8,128)S(1)}, u32[]{:S(2)}, u32[]{:S(2)}) collective-permute-start(f32[1,8,512]{2,1,0:T(8,128)S(1)} %select_maximum_fusion.block.refs_1_), channel_id=1, source_target_pairs={{0,2},{1,3},{2,1},{3,0},{4,6},{5,7},{6,5},{7,4},{8,10},{9,11},{10,... | collective-permute-start | bytes 49160 | tf_op jit(solution)/shard_map/ppermute | solution.py:545
  5.4 5.0 %collective-permute-start.2 = (f32[1,8,512]{2,1,0:T(8,128)S(1)}, f32[1,8,512]{2,1,0:T(8,128)S(1)}, u32[]{:S(2)}, u32[]{:S(2)}) collective-permute-start(f32[1,8,512]{2,1,0:T(8,128)S(1)} %select_maximum_fusion.block.refs_1_), channel_id=1, source_target_pairs={{0,3},{1,2},{2,0},{3,1},{4,7},{5,6},{6,4},{7,5},{8,11},{9,10},{10,... | collective-permute-start | bytes 49160 | tf_op jit(solution)/shard_map/ppermute | solution.py:545
  6.5 4.0 %collective-permute-start.1 = (f32[1,8,512]{2,1,0:T(8,128)S(1)}, f32[1,8,512]{2,1,0:T(8,128)S(1)}, u32[]{:S(2)}, u32[]{:S(2)}) collective-permute-start(f32[1,8,512]{2,1,0:T(8,128)S(1)} %select_maximum_fusion.block.refs_1_), channel_id=1, source_target_pairs={{0,1},{1,0},{2,3},{3,2},{4,5},{5,4},{6,7},{7,6},{8,9},{9,8},{10,11... | collective-permute-start | bytes 49160 | tf_op jit(solution)/shard_map/ppermute | solution.py:545
  18.2 1.2 %collective-permute-start.3 = (f32[8,128]{1,0:T(8,128)S(1)}, f32[8,128]{1,0:T(8,128)S(1)}, u32[]{:S(2)}, u32[]{:S(2)}) collective-permute-start(f32[8,128]{1,0:T(8,128)S(1)} %get-tuple-element.35), channel_id=1, source_target_pairs={{0,4},{4,0},{8,12},{12,8},{1,5},{5,1},{9,13},{13,9},{2,6},{6,2},{1... | collective-permute-start | bytes 12296 | tf_op jit(solution)/shard_map/ppermute | solution.py:530
  19.4 3.0 %collective-permute-start.4 = (f32[8,128]{1,0:T(8,128)S(1)}, f32[8,128]{1,0:T(8,128)S(1)}, u32[]{:S(2)}, u32[]{:S(2)}) collective-permute-start(f32[8,128]{1,0:T(8,128)S(1)} %max.6), channel_id=1, source_target_pairs={{0,12},{4,8},{8,4},{12,0},{1,13},{5,9},{9,5},{13,1},{2,14},{6,10},... | collective-permute-start | bytes 12296 | tf_op jit(solution)/shard_map/ppermute | solution.py:530

commit v20 on v19

--- a/solution.py
+++ b/solution.py
@@ -13,7 +13,7 @@
 SCALE = math.sqrt(math.log2(math.e) / (2.0 * EPS * EPS))
 GRID = 4.0
 TINY = 1e-30
-GROUP = 16
+GROUP = 32
 DISTANCE_ROWS = 96
 DRIFT_ROWS = 64
 bf16, f32 = jnp.bfloat16, jnp.float32
@@ -150,6 +150,10 @@
     return drift - jnp.where(row == 0, ends[0], jnp.where(row == 1, ends[1], ends[2]))
 
 
+def widened(block):
+    return jnp.concatenate([block[0], jnp.zeros_like(block[0])], axis=0)
+
+
 def prepared(whole, live):
     weight = jnp.where(live, whole[3:4], 0.0)
     parts = grid_parts(jnp.where(row_of(whole) < 3, whole * SCALE, 0.0))
@@ -229,20 +233,15 @@
     return sum(jnp.where(here == i, source, 0) for i, source in enumerate(sources))
 
 
-def own_kernel(filled_hbm, block, filled_out, key_out, query_out, moment_out, sums_out, first_out,
-               second_out, filled_ref, filled_sem, *scratch):
+def own_kernel(filled, block, key_out, query_out, moment_out, sums_out, first_out, second_out,
+               *scratch):
     width = block.shape[2]
-    fetch = pltpu.make_async_copy(filled_hbm, filled_ref, filled_sem)
-    fetch.start()
-    everything = lax.broadcasted_iota(jnp.int32, (1, width), 1) >= 0
-    _, place, key, query, _ = prepared(block[0], everything)
+    live = lanes_of(lax.axis_index("sharers"), width) < filled[...]
+    _, _, key, query, moment = prepared(widened(block), live)
     key_out[...] = key
     query_out[...] = query
+    moment_out[...] = moment
     sums_out[...] = jnp.zeros_like(sums_out)
-    fetch.wait()
-    live = lanes_of(lax.axis_index("sharers"), width) < filled_ref[0]
-    moment_out[...] = weighted_rows(jnp.where(live, block[0, 3:4], 0.0), place)
-    filled_out[...] = jnp.full(filled_out.shape, filled_ref[0], jnp.int32)
     exponent = exponent_of(looked_up([key_out], width, 0), looked_up([query_out], width, 1))
     moments = looked_up([moment_out], width, 1)
     tiles = diagonal_tiles(0, width)
@@ -252,8 +251,8 @@
 def next_kernel(sources, filled, block, own_key, own_query, own_moment, own_sums, key_out,
                 query_out, moment_out, sums_out, tile_out, first_out, second_out, *scratch):
     width = block.shape[2]
-    live = lanes_of(owner_of(sources), width) < filled[0:1, :]
-    _, _, key, query, moment = prepared(block[0], live)
+    live = lanes_of(owner_of(sources), width) < filled[...]
+    _, _, key, query, moment = prepared(widened(block), live)
     key_out[...] = key
     query_out[...] = query
     moment_out[...] = moment
@@ -288,21 +287,19 @@
     return [pltpu.VMEM((width, width), f32)] * 2 + [pltpu.VMEM((2 * width, width), bf16)] * 2
 
 
-def own_part(counts, block):
+def own_part(filled, block):
     width = block.shape[2]
     vector = pl.BlockSpec(memory_space=pltpu.VMEM)
-    shapes = [jax.ShapeDtypeStruct((8, width), jnp.int32)] + feature_shapes(width)
-    shapes += [jax.ShapeDtypeStruct((16, width), f32)] + diagonal_shapes(width)
+    shapes = feature_shapes(width) + [jax.ShapeDtypeStruct((16, width), f32)] + diagonal_shapes(width)
     return pl.pallas_call(
         own_kernel,
         out_shape=shapes,
-        in_specs=[pl.BlockSpec(memory_space=pltpu.HBM), vector],
+        in_specs=[vector] * 2,
         out_specs=[vector] * len(shapes),
-        scratch_shapes=[pltpu.SMEM((1,), jnp.int32), pltpu.SemaphoreType.DMA]
-        + stage_scratch(width),
+        scratch_shapes=stage_scratch(width),
         compiler_params=pltpu.CompilerParams(vmem_limit_bytes=16 << 20),
         name="own",
-    )(counts, block)
+    )(filled, block)
 
 
 def next_part(filled, block, features, sums, sources):
@@ -341,7 +338,7 @@
     weight = jnp.concatenate(
         [jnp.where(on, block[0, 3:4], 0.0) for on, block in zip(live, blocks)], axis=1
     )
-    whole = jnp.concatenate([block[0] for block in blocks], axis=1)
+    whole = jnp.concatenate([widened(block) for block in blocks], axis=1)
     vector = row_of(whole) < 3
     parts = grid_parts(jnp.where(vector, whole * SCALE, 0.0))
     place = parts[0] + parts[1] + parts[2]
@@ -380,10 +377,10 @@
     half = 2 * width
     scratch, distance_refs = refs[:4], refs[4:]
 
-    live = [lanes_of(owner_of(source), width) < filled[0:1, :] for source in sources]
+    live = [lanes_of(owner_of(source), width) < filled[...] for source in sources]
     late = range(2, count)
     for index in late:
-        _, _, key, query, moment = prepared(blocks[index][0], live[index])
+        _, _, key, query, moment = prepared(widened(blocks[index]), live[index])
         lanes = pl.ds((index - 2) * width, width)
         key_ref[lanes, :] = key
         query_ref[:, lanes] = query
@@ -422,17 +419,17 @@
     return [jax.ShapeDtypeStruct((8, width), f32), parts, parts, speeds]
 
 
-def sweep(counts, blocks, sources):
+def sweep(filled, blocks, sources):
     count, width = len(blocks), blocks[0].shape[2]
     slots, late = count * width, (count - 2) * width
-    filled, *own = own_part(counts, blocks[0])
+    own = own_part(filled, blocks[0])
     following = next_part(filled, blocks[1], own[:3], own[3], sources[1])
     early = [*own[:3], *own[4:], *following]
     vector = pl.BlockSpec(memory_space=pltpu.VMEM)
     distances = [pltpu.VMEM((2 * tile[1], tile[3]), bf16) for tile in late_tiles(count, width)]
     return pl.pallas_call(
         functools.partial(sweep_kernel, sources),
-        out_shape=sweep_shapes(width, 8),
+        out_shape=sweep_shapes(width, 1),
         in_specs=[vector] * (1 + count + len(early)),
         out_specs=[vector] * 4,
         scratch_shapes=[
@@ -455,9 +452,9 @@
     blocks, outs, refs = refs[:count], refs[count : count + 4], refs[count + 4 :]
     key_ref, query_ref, moment_ref, flux_ref, sums_ref, totals_ref, exponent_ref, split_ref = refs
     width = blocks[0].shape[2]
-    live = [lanes_of(owner_of(source), width) < filled[0] for source in sources]
+    live = [lanes_of(owner_of(source), width) < filled[...] for source in sources]
     for index, (block, on) in enumerate(zip(blocks, live)):
-        _, _, key, query, moment = prepared(block[0], on)
+        _, _, key, query, moment = prepared(widened(block), on)
         lanes = pl.ds(index * width, width)
         key_ref[lanes, :] = key
         query_ref[:, lanes] = query
@@ -501,14 +498,14 @@
     finish(blocks, count * width, weight, centred, score, totals_ref[...], outs)
 
 
-def long_sweep(counts, blocks, sources, copies):
+def long_sweep(filled, blocks, sources, copies):
     count, width = len(blocks), blocks[0].shape[2]
     slots = count * width
     vector = pl.BlockSpec(memory_space=pltpu.VMEM)
     return pl.pallas_call(
         functools.partial(long_kernel, sources),
         out_shape=sweep_shapes(width, copies),
-        in_specs=[pl.BlockSpec(memory_space=pltpu.SMEM)] + [vector] * count,
+        in_specs=[vector] * (1 + count),
         out_specs=[vector] * 4,
         scratch_shapes=[
             pltpu.VMEM((slots, DISTANCE_ROWS), bf16),
@@ -522,7 +519,7 @@
         ],
         compiler_params=pltpu.CompilerParams(vmem_limit_bytes=(16 << 20) + slots * 2688),
         name="sweep",
-    )(counts, *blocks)
+    )(filled, *blocks)
 
 
 def swapped(value, axis, step):
@@ -552,16 +549,16 @@
 
 
 def local(velocities, weights, counts):
-    package = jnp.concatenate([velocities, weights[:, None]], axis=1)
-    blocks, sources = gathered(jnp.pad(package, ((0, 0), (0, 4), (0, 0))))
+    filled = counts.reshape(1, 1)
+    blocks, sources = gathered(jnp.concatenate([velocities, weights[:, None]], axis=1))
     if len(blocks) == len(ROUNDS) + 1:
-        scores, drift, start, speeds = sweep(counts, blocks, sources)
+        scores, drift, start, speeds = sweep(filled, blocks, sources)
         for step in bits(lax.axis_size("cells")):
             speeds = jnp.maximum(speeds, swapped(speeds, "cells", 2 * step - 1))
-        largest = speeds[0:1]
+        largest = speeds
     else:
         axes = ("cells", "sharers")
-        scores, drift, start, speeds = long_sweep(counts, blocks, sources, lax.axis_size(axes))
+        scores, drift, start, speeds = long_sweep(filled, blocks, sources, lax.axis_size(axes))
         largest = jnp.max(lax.all_to_all(speeds[:, None], axes, 0, 0, tiled=True), axis=0)
     time_step = 0.5 / (largest + 1e-06)
     moved = start + time_step[None] * drift

time: 23.3 us -> 24.2 us (1.039)
  waiting for transfers between devices: 2.33 us -> 3.44 us
  Pallas kernels: 10.5 us -> 10 us
  starting transfers between devices: 6.95 us -> 7.31 us
    ppermute x3, waiting for transfers between devices: 0.01 us -> 1.26 us  [gathered(): blocks.append(lax.ppermute(block, 'sharers', list(enumerate(targets))))]
    pallas_call x1, Pallas kernels: 1.23 us -> 0.7 us  [own_part(): pl.pallas_call(own_kernel, out_shape=shapes, in_specs=[vector] * 2, out_s...]
    ppermute x3, starting transfers between devices: 5.67 us -> 6 us  [gathered(): blocks.append(lax.ppermute(block, 'sharers', list(enumerate(targets))))]
  transfers between devices with their start and end apart: 5 -> 5, of which waited for: 2 -> 3; matrix products, arithmetic and copies ran while one was open for 3% -> 3% of each run, Pallas kernels for 12% -> 10%
where the time goes in v20:
time: 24.2 us; the launch traced here: 24 us
  Pallas kernels  10 us (41%)
  starting transfers between devices  7.31 us (30%)
  waiting for transfers between devices  3.44 us (14%)
  local copies, waits for them, and re-layouts  1.31 us (5%)
  between operations  1.31 us (5%)
  other arithmetic  0.62 us (3%)
    pallas_call x1, Pallas kernels, sweep(): pl.pallas_call(functools.partial(sweep_kernel, sources), out_shape=sweep_...  7.75 us
    ppermute x3, starting transfers between devices, gathered(): blocks.append(lax.ppermute(block, 'sharers', list(enumerate(targets))))  6 us
    ppermute x2, waiting for transfers between devices, swapped(): return lax.ppermute(value, axis, pairs)  2.18 us
    pallas_call x1, Pallas kernels, next_part(): pl.pallas_call(functools.partial(next_kernel, sources), out_shape=shapes,...  1.6 us
    unnamed x4, local copies, waits for them, and re-layouts  1.31 us
    ppermute x2, starting transfers between devices, swapped(): return lax.ppermute(value, axis, pairs)  1.31 us
    ppermute x3, waiting for transfers between devices, gathered(): blocks.append(lax.ppermute(block, 'sharers', list(enumerate(targets))))  1.26 us
    pallas_call x1, Pallas kernels, own_part(): pl.pallas_call(own_kernel, out_shape=shapes, in_specs=[vector] * 2, out_s...  0.7 us
  transfers between devices with their start and end apart: 5, of which 3 were waited for; matrix products, arithmetic and copies ran while one was open for 3% of the time, Pallas kernels for 10%

profile of v20, /device:TPU:0, one launch (start us, length us, event | category | flops | bytes accessed | tf_op | source)
XLA Modules:
  0.0 24.0 jit_solution(346904497489649320)
XLA Ops:
  0.6 0.0 copy-start
  0.6 0.7 %copy.8 = f32[1,3,512]{2,1,0:T(4,128)S(1)} copy(f32[1,3,512]{2,0,1:T(1,128)} %param.3) | data formatting | bytes 12288 | tf_op args[0]
  1.3 0.0 copy-done
  1.4 4.1 %collective-permute-start = (f32[1,4,512]{2,1,0:T(4,128)S(1)}, f32[1,4,512]{2,1,0:T(4,128)S(1)}, u32[]{:S(2)}, u32[]{:S(2)}) collective-permute-start(f32[1,4,512]{2,1,0:T(4,128)S(1)} %pad_maximum_fusion.block.refs_1_), channel_id=1, source_target_pairs={{0,2},{1,3},{2,1},{3,0},{4,6},{5,7},{6,5},{7,4},{8,10},{9,11},{10,... | collective-permute-start | bytes 24584 | tf_op jit(solution)/shard_map/ppermute | solution.py:542
  5.4 1.6 %collective-permute-start.1 = (f32[1,4,512]{2,1,0:T(4,128)S(1)}, f32[1,4,512]{2,1,0:T(4,128)S(1)}, u32[]{:S(2)}, u32[]{:S(2)}) collective-permute-start(f32[1,4,512]{2,1,0:T(4,128)S(1)} %pad_maximum_fusion.block.refs_1_), channel_id=1, source_target_pairs={{0,1},{1,0},{2,3},{3,2},{4,5},{5,4},{6,7},{7,6},{8,9},{9,8},{10,11... | collective-permute-start | bytes 24584 | tf_op jit(solution)/shard_map/ppermute | solution.py:542
  7.0 0.3 %collective-permute-start.2 = (f32[1,4,512]{2,1,0:T(4,128)S(1)}, f32[1,4,512]{2,1,0:T(4,128)S(1)}, u32[]{:S(2)}, u32[]{:S(2)}) collective-permute-start(f32[1,4,512]{2,1,0:T(4,128)S(1)} %pad_maximum_fusion.block.refs_1_), channel_id=1, source_target_pairs={{0,3},{1,2},{2,0},{3,1},{4,7},{5,6},{6,4},{7,5},{8,11},{9,10},{10,... | collective-permute-start | bytes 24584 | tf_op jit(solution)/shard_map/ppermute | solution.py:542
  8.0 0.7 %own.1 = (bf16[512,96]{1,0:T(8,128)(2,1)S(1)}, bf16[96,512]{1,0:T(8,128)(2,1)S(1)}, bf16[16,512]{1,0:T(8,128)(2,1)S(1)}, f32[16,512]{1,0:T(8,128)S(1)}, bf16[512...) custom-call(s32[1,1]{1,0:T(1,128)} %bitcast.7.filled, f32[1,4,512]{2,1,0:T(4,128)S(1)} %pad_maximum_fusion.block.refs_1_), custom_call_target="tpu_custom_call" | custom-call | tf_op jit(solution)/shard_map/own/pallas_call | solution.py:294
  8.7 0.0 collective-permute-done.block.refs_2_
  8.7 1.6 %next.1 = (bf16[512,96]{1,0:T(8,128)(2,1)S(1)}, bf16[96,512]{1,0:T(8,128)(2,1)S(1)}, bf16[16,512]{1,0:T(8,128)(2,1)S(1)}, f32[16,1024]{1,0:T(8,128)S(1)}, bf16[1...) custom-call(s32[1,1]{1,0:T(1,128)} %bitcast.8.filled, ...), custom_call_target="tpu_custom_call" | custom-call | tf_op jit(solution)/shard_map/next/pallas_call | solution.py:310
  10.3 0.0 collective-permute-done.1.refs_3_
  10.3 1.3 %collective-permute-done.2.refs_4_ = f32[1,4,512]{2,1,0:T(4,128)S(1)} collective-permute-done((f32[1,4,512]{2,1,0:T(4,128)S(1)}, f32[1,4,512]{2,1,0:T(4,128)S(1)}, u32[]{:S(2)}, u32[]{:S(2)}) %collective-permute-start.2) | collective-permute-done | bytes 8224 | tf_op jit(solution)/shard_map/ppermute | solution.py:542
  11.6 7.7 %sweep.1 = (f32[8,512]{1,0:T(8,128)S(1)}, f32[3,4,128]{2,1,0:T(4,128)S(1)}, f32[3,4,128]{2,1,0:T(4,128)S(1)}, f32[1,128]{1,0:T(1,128)S(1)}) custom-call(s32[1,1]{1,0:T(1,128)} %bitcast.9.refs_0_, f32[1,4,512]{2,1,0:T(4,128)S(1)} %pad_maximum_fusion.block.refs_1_, f32[1,4,512]{2,1,0:T(4,128)S(1)} %collective-permute-done.block.refs_2_, ...), custom_call_target="tpu_custom_call" | custom-call | tf_op jit(solution)/shard_map/sweep/pallas_call | solution.py:430
  19.3 0.0 collective-permute-start.3
  19.3 1.1 %collective-permute-done.3 = f32[1,128]{1,0:T(1,128)S(1)} collective-permute-done((f32[1,128]{1,0:T(1,128)S(1)}, f32[1,128]{1,0:T(1,128)S(1)}, u32[]{:S(2)}, u32[]{:S(2)}) %collective-permute-start.3) | collective-permute-done | bytes 544 | tf_op jit(solution)/shard_map/ppermute | solution.py:527
  20.5 1.3 %collective-permute-start.4 = (f32[1,128]{1,0:T(1,128)S(1)}, f32[1,128]{1,0:T(1,128)S(1)}, u32[]{:S(2)}, u32[]{:S(2)}) collective-permute-start(f32[1,128]{1,0:T(1,128)S(1)} %max.6), channel_id=1, source_target_pairs={{0,12},{4,8},{8,4},{12,0},{1,13},{5,9},{9,5},{13,1},{2,14},{6,10},... | collective-permute-start | bytes 1544 | tf_op jit(solution)/shard_map/ppermute | solution.py:527
  21.8 0.6 %copy.10 = f32[1,3,512]{2,0,1:T(1,128)} copy(f32[1,3,512]{2,1,0:T(4,128)S(1)} %slice_bitcast_fusion) | data formatting | bytes 12288
  22.4 1.1 %collective-permute-done.4 = f32[1,128]{1,0:T(1,128)S(1)} collective-permute-done((f32[1,128]{1,0:T(1,128)S(1)}, f32[1,128]{1,0:T(1,128)S(1)}, u32[]{:S(2)}, u32[]{:S(2)}) %collective-permute-start.4) | collective-permute-done | bytes 544 | tf_op jit(solution)/shard_map/ppermute | solution.py:527
  23.4 0.6 %multiply_add_fusion = f32[3,4,128]{2,1,0:T(4,128)} fusion(f32[3,4,128]{2,1,0:T(4,128)S(1)} %get-tuple-element.32, f32[3,4,128]{2,1,0:T(4,128)S(1)} %get-tuple-element.34, f32[128]{0:T(128)S(1)} %divide_bitcast_fusion), kind=kLoop, calls=%fused_computation.2 | loop fusion | flops 3072 | bytes 18944 | tf_op jit(solution)/shard_map/add | solution.py:564
  (4 shorter events, 0.0 us)
Async XLA Ops:
  0.6 0.7 %copy-start = (f32[1,512]{1,0:T(1,128)S(1)}, f32[1,512]{1,0:T(1,128)}, u32[]{:S(2)}) copy-start(f32[1,512]{1,0:T(1,128)} %param.4) | copy-start | bytes 6148
  1.4 7.4 %collective-permute-start = (f32[1,4,512]{2,1,0:T(4,128)S(1)}, f32[1,4,512]{2,1,0:T(4,128)S(1)}, u32[]{:S(2)}, u32[]{:S(2)}) collective-permute-start(f32[1,4,512]{2,1,0:T(4,128)S(1)} %pad_maximum_fusion.block.refs_1_), channel_id=1, source_target_pairs={{0,2},{1,3},{2,1},{3,0},{4,6},{5,7},{6,5},{7,4},{8,10},{9,11},{10,... | collective-permute-start | bytes 24584 | tf_op jit(solution)/shard_map/ppermute | solution.py:542
  5.4 4.9 %collective-permute-start.1 = (f32[1,4,512]{2,1,0:T(4,128)S(1)}, f32[1,4,512]{2,1,0:T(4,128)S(1)}, u32[]{:S(2)}, u32[]{:S(2)}) collective-permute-start(f32[1,4,512]{2,1,0:T(4,128)S(1)} %pad_maximum_fusion.block.refs_1_), channel_id=1, source_target_pairs={{0,1},{1,0},{2,3},{3,2},{4,5},{5,4},{6,7},{7,6},{8,9},{9,8},{10,11... | collective-permute-start | bytes 24584 | tf_op jit(solution)/shard_map/ppermute | solution.py:542
  7.0 4.5 %collective-permute-start.2 = (f32[1,4,512]{2,1,0:T(4,128)S(1)}, f32[1,4,512]{2,1,0:T(4,128)S(1)}, u32[]{:S(2)}, u32[]{:S(2)}) collective-permute-start(f32[1,4,512]{2,1,0:T(4,128)S(1)} %pad_maximum_fusion.block.refs_1_), channel_id=1, source_target_pairs={{0,3},{1,2},{2,0},{3,1},{4,7},{5,6},{6,4},{7,5},{8,11},{9,10},{10,... | collective-permute-start | bytes 24584 | tf_op jit(solution)/shard_map/ppermute | solution.py:542
  19.3 1.1 %collective-permute-start.3 = (f32[1,128]{1,0:T(1,128)S(1)}, f32[1,128]{1,0:T(1,128)S(1)}, u32[]{:S(2)}, u32[]{:S(2)}) collective-permute-start(f32[1,128]{1,0:T(1,128)S(1)} %get-tuple-element.33), channel_id=1, source_target_pairs={{0,4},{4,0},{8,12},{12,8},{1,5},{5,1},{9,13},{13,9},{2,6},{6,2},{1... | collective-permute-start | bytes 1544 | tf_op jit(solution)/shard_map/ppermute | solution.py:527
  20.5 3.0 %collective-permute-start.4 = (f32[1,128]{1,0:T(1,128)S(1)}, f32[1,128]{1,0:T(1,128)S(1)}, u32[]{:S(2)}, u32[]{:S(2)}) collective-permute-start(f32[1,128]{1,0:T(1,128)S(1)} %max.6), channel_id=1, source_target_pairs={{0,12},{4,8},{8,4},{12,0},{1,13},{5,9},{9,5},{13,1},{2,14},{6,10},... | collective-permute-start | bytes 1544 | tf_op jit(solution)/shard_map/ppermute | solution.py:527

commit v21 on v20

--- a/solution.py
+++ b/solution.py
@@ -368,7 +368,6 @@
 def sweep_kernel(sources, *refs):
     count = len(sources)
     filled, blocks, refs = refs[0], refs[1 : count + 1], list(refs[count + 1 :])
-    blocks = blocks[:2] + blocks[:1:-1]
     own, following, refs = refs[:5], refs[5:12], refs[12:]
     outs, (key_ref, query_ref, moment_ref, flux_ref, sums_ref, totals_ref), refs = (
         refs[:4], refs[4:10], refs[10:]
@@ -444,7 +443,7 @@
         + distances,
         compiler_params=pltpu.CompilerParams(vmem_limit_bytes=24 << 20),
         name="sweep",
-    )(filled, *blocks[:2], *blocks[:1:-1], *early)
+    )(filled, *blocks, *early)
 
 
 def long_kernel(sources, filled, *refs):

time: 24.2 us -> 22.8 us (0.942)
  waiting for transfers between devices: 3.44 us -> 2.22 us
    ppermute x3, waiting for transfers between devices: 1.26 us -> 0.2 us  [gathered(): blocks.append(lax.ppermute(block, 'sharers', list(enumerate(targets))))]
    ppermute x3, starting transfers between devices: 6 us -> 5.67 us  [gathered(): blocks.append(lax.ppermute(block, 'sharers', list(enumerate(targets))))]
where the time goes in v21:
time: 22.8 us; the launch traced here: 22.6 us
  Pallas kernels  10 us (44%)
  starting transfers between devices  7.13 us (31%)
  waiting for transfers between devices  2.22 us (10%)
  local copies, waits for them, and re-layouts  1.31 us (6%)
  between operations  1.31 us (6%)
  other arithmetic  0.62 us (3%)
    pallas_call x1, Pallas kernels, sweep(): pl.pallas_call(functools.partial(sweep_kernel, sources), out_shape=sweep_...  7.75 us
    ppermute x3, starting transfers between devices, gathered(): blocks.append(lax.ppermute(block, 'sharers', list(enumerate(targets))))  5.67 us
    ppermute x2, waiting for transfers between devices, swapped(): return lax.ppermute(value, axis, pairs)  2.02 us
    pallas_call x1, Pallas kernels, next_part(): pl.pallas_call(functools.partial(next_kernel, sources), out_shape=shapes,...  1.6 us
    ppermute x2, starting transfers between devices, swapped(): return lax.ppermute(value, axis, pairs)  1.46 us
    unnamed x4, local copies, waits for them, and re-layouts  1.31 us
    pallas_call x1, Pallas kernels, own_part(): pl.pallas_call(own_kernel, out_shape=shapes, in_specs=[vector] * 2, out_s...  0.7 us
    add x1, other arithmetic, local(): moved = start + time_step[None] * drift  0.61 us
  transfers between devices with their start and end apart: 5, of which 3 were waited for; matrix products, arithmetic and copies ran while one was open for 3% of the time, Pallas kernels for 10%

profile of v21, /device:TPU:0, one launch (start us, length us, event | category | flops | bytes accessed | tf_op | source)
XLA Modules:
  0.0 22.6 jit_solution(16543262876721582344)
XLA Ops:
  0.6 0.0 copy-start
  0.6 0.7 %copy.8 = f32[1,3,512]{2,1,0:T(4,128)S(1)} copy(f32[1,3,512]{2,0,1:T(1,128)} %param.3) | data formatting | bytes 12288 | tf_op args[0]
  1.3 0.0 copy-done
  1.4 4.1 %collective-permute-start = (f32[1,4,512]{2,1,0:T(4,128)S(1)}, f32[1,4,512]{2,1,0:T(4,128)S(1)}, u32[]{:S(2)}, u32[]{:S(2)}) collective-permute-start(f32[1,4,512]{2,1,0:T(4,128)S(1)} %pad_maximum_fusion.block.refs_1_), channel_id=1, source_target_pairs={{0,2},{1,3},{2,1},{3,0},{4,6},{5,7},{6,5},{7,4},{8,10},{9,11},{10,... | collective-permute-start | bytes 24584 | tf_op jit(solution)/shard_map/ppermute | solution.py:541
  5.4 1.1 %collective-permute-start.1 = (f32[1,4,512]{2,1,0:T(4,128)S(1)}, f32[1,4,512]{2,1,0:T(4,128)S(1)}, u32[]{:S(2)}, u32[]{:S(2)}) collective-permute-start(f32[1,4,512]{2,1,0:T(4,128)S(1)} %pad_maximum_fusion.block.refs_1_), channel_id=1, source_target_pairs={{0,3},{1,2},{2,0},{3,1},{4,7},{5,6},{6,4},{7,5},{8,11},{9,10},{10,... | collective-permute-start | bytes 24584 | tf_op jit(solution)/shard_map/ppermute | solution.py:541
  6.5 0.5 %collective-permute-start.2 = (f32[1,4,512]{2,1,0:T(4,128)S(1)}, f32[1,4,512]{2,1,0:T(4,128)S(1)}, u32[]{:S(2)}, u32[]{:S(2)}) collective-permute-start(f32[1,4,512]{2,1,0:T(4,128)S(1)} %pad_maximum_fusion.block.refs_1_), channel_id=1, source_target_pairs={{0,1},{1,0},{2,3},{3,2},{4,5},{5,4},{6,7},{7,6},{8,9},{9,8},{10,11... | collective-permute-start | bytes 24584 | tf_op jit(solution)/shard_map/ppermute | solution.py:541
  7.7 0.7 %own.1 = (bf16[512,96]{1,0:T(8,128)(2,1)S(1)}, bf16[96,512]{1,0:T(8,128)(2,1)S(1)}, bf16[16,512]{1,0:T(8,128)(2,1)S(1)}, f32[16,512]{1,0:T(8,128)S(1)}, bf16[512...) custom-call(s32[1,1]{1,0:T(1,128)} %bitcast.7.filled, f32[1,4,512]{2,1,0:T(4,128)S(1)} %pad_maximum_fusion.block.refs_1_), custom_call_target="tpu_custom_call" | custom-call | tf_op jit(solution)/shard_map/own/pallas_call | solution.py:294
  8.4 0.0 collective-permute-done.block.refs_2_
  8.4 1.6 %next.1 = (bf16[512,96]{1,0:T(8,128)(2,1)S(1)}, bf16[96,512]{1,0:T(8,128)(2,1)S(1)}, bf16[16,512]{1,0:T(8,128)(2,1)S(1)}, f32[16,1024]{1,0:T(8,128)S(1)}, bf16[1...) custom-call(s32[1,1]{1,0:T(1,128)} %bitcast.8.filled, ...), custom_call_target="tpu_custom_call" | custom-call | tf_op jit(solution)/shard_map/next/pallas_call | solution.py:310
  10.0 0.0 collective-permute-done.1.refs_3_
  10.0 0.2 collective-permute-done.2.refs_4_
  10.2 7.7 %sweep.1 = (f32[8,512]{1,0:T(8,128)S(1)}, f32[3,4,128]{2,1,0:T(4,128)S(1)}, f32[3,4,128]{2,1,0:T(4,128)S(1)}, f32[1,128]{1,0:T(1,128)S(1)}) custom-call(s32[1,1]{1,0:T(1,128)} %bitcast.9.refs_0_, f32[1,4,512]{2,1,0:T(4,128)S(1)} %pad_maximum_fusion.block.refs_1_, f32[1,4,512]{2,1,0:T(4,128)S(1)} %collective-permute-done.block.refs_2_, ...), custom_call_target="tpu_custom_call" | custom-call | tf_op jit(solution)/shard_map/sweep/pallas_call | solution.py:429
  17.9 0.0 collective-permute-start.3
  17.9 1.1 %collective-permute-done.3 = f32[1,128]{1,0:T(1,128)S(1)} collective-permute-done((f32[1,128]{1,0:T(1,128)S(1)}, f32[1,128]{1,0:T(1,128)S(1)}, u32[]{:S(2)}, u32[]{:S(2)}) %collective-permute-start.3) | collective-permute-done | bytes 544 | tf_op jit(solution)/shard_map/ppermute | solution.py:526
  19.1 1.5 %collective-permute-start.4 = (f32[1,128]{1,0:T(1,128)S(1)}, f32[1,128]{1,0:T(1,128)S(1)}, u32[]{:S(2)}, u32[]{:S(2)}) collective-permute-start(f32[1,128]{1,0:T(1,128)S(1)} %max.6), channel_id=1, source_target_pairs={{0,12},{4,8},{8,4},{12,0},{1,13},{5,9},{9,5},{13,1},{2,14},{6,10},... | collective-permute-start | bytes 1544 | tf_op jit(solution)/shard_map/ppermute | solution.py:526
  20.5 0.6 %copy.10 = f32[1,3,512]{2,0,1:T(1,128)} copy(f32[1,3,512]{2,1,0:T(4,128)S(1)} %slice_bitcast_fusion) | data formatting | bytes 12288
  21.1 0.9 %collective-permute-done.4 = f32[1,128]{1,0:T(1,128)S(1)} collective-permute-done((f32[1,128]{1,0:T(1,128)S(1)}, f32[1,128]{1,0:T(1,128)S(1)}, u32[]{:S(2)}, u32[]{:S(2)}) %collective-permute-start.4) | collective-permute-done | bytes 544 | tf_op jit(solution)/shard_map/ppermute | solution.py:526
  22.0 0.6 %multiply_add_fusion = f32[3,4,128]{2,1,0:T(4,128)} fusion(f32[3,4,128]{2,1,0:T(4,128)S(1)} %get-tuple-element.32, f32[3,4,128]{2,1,0:T(4,128)S(1)} %get-tuple-element.34, f32[128]{0:T(128)S(1)} %divide_bitcast_fusion), kind=kLoop, calls=%fused_computation.2 | loop fusion | flops 3072 | bytes 18944 | tf_op jit(solution)/shard_map/add | solution.py:563
  (4 shorter events, 0.0 us)
Async XLA Ops:
  0.6 0.7 %copy-start = (f32[1,512]{1,0:T(1,128)S(1)}, f32[1,512]{1,0:T(1,128)}, u32[]{:S(2)}) copy-start(f32[1,512]{1,0:T(1,128)} %param.4) | copy-start | bytes 6148
  1.4 7.0 %collective-permute-start = (f32[1,4,512]{2,1,0:T(4,128)S(1)}, f32[1,4,512]{2,1,0:T(4,128)S(1)}, u32[]{:S(2)}, u32[]{:S(2)}) collective-permute-start(f32[1,4,512]{2,1,0:T(4,128)S(1)} %pad_maximum_fusion.block.refs_1_), channel_id=1, source_target_pairs={{0,2},{1,3},{2,1},{3,0},{4,6},{5,7},{6,5},{7,4},{8,10},{9,11},{10,... | collective-permute-start | bytes 24584 | tf_op jit(solution)/shard_map/ppermute | solution.py:541
  5.4 4.5 %collective-permute-start.1 = (f32[1,4,512]{2,1,0:T(4,128)S(1)}, f32[1,4,512]{2,1,0:T(4,128)S(1)}, u32[]{:S(2)}, u32[]{:S(2)}) collective-permute-start(f32[1,4,512]{2,1,0:T(4,128)S(1)} %pad_maximum_fusion.block.refs_1_), channel_id=1, source_target_pairs={{0,3},{1,2},{2,0},{3,1},{4,7},{5,6},{6,4},{7,5},{8,11},{9,10},{10,... | collective-permute-start | bytes 24584 | tf_op jit(solution)/shard_map/ppermute | solution.py:541
  6.5 3.7 %collective-permute-start.2 = (f32[1,4,512]{2,1,0:T(4,128)S(1)}, f32[1,4,512]{2,1,0:T(4,128)S(1)}, u32[]{:S(2)}, u32[]{:S(2)}) collective-permute-start(f32[1,4,512]{2,1,0:T(4,128)S(1)} %pad_maximum_fusion.block.refs_1_), channel_id=1, source_target_pairs={{0,1},{1,0},{2,3},{3,2},{4,5},{5,4},{6,7},{7,6},{8,9},{9,8},{10,11... | collective-permute-start | bytes 24584 | tf_op jit(solution)/shard_map/ppermute | solution.py:541
  17.9 1.1 %collective-permute-start.3 = (f32[1,128]{1,0:T(1,128)S(1)}, f32[1,128]{1,0:T(1,128)S(1)}, u32[]{:S(2)}, u32[]{:S(2)}) collective-permute-start(f32[1,128]{1,0:T(1,128)S(1)} %get-tuple-element.33), channel_id=1, source_target_pairs={{0,4},{4,0},{8,12},{12,8},{1,5},{5,1},{9,13},{13,9},{2,6},{6,2},{1... | collective-permute-start | bytes 1544 | tf_op jit(solution)/shard_map/ppermute | solution.py:526
  19.1 3.0 %collective-permute-start.4 = (f32[1,128]{1,0:T(1,128)S(1)}, f32[1,128]{1,0:T(1,128)S(1)}, u32[]{:S(2)}, u32[]{:S(2)}) collective-permute-start(f32[1,128]{1,0:T(1,128)S(1)} %max.6), channel_id=1, source_target_pairs={{0,12},{4,8},{8,4},{12,0},{1,13},{5,9},{9,5},{13,1},{2,14},{6,10},... | collective-permute-start | bytes 1544 | tf_op jit(solution)/shard_map/ppermute | solution.py:526

commit v22 on v21

--- a/solution.py
+++ b/solution.py
@@ -13,7 +13,7 @@
 SCALE = math.sqrt(math.log2(math.e) / (2.0 * EPS * EPS))
 GRID = 4.0
 TINY = 1e-30
-GROUP = 32
+GROUP = 16
 DISTANCE_ROWS = 96
 DRIFT_ROWS = 64
 bf16, f32 = jnp.bfloat16, jnp.float32
@@ -84,9 +84,10 @@
 
 def store_split(ref, rows, matrix):
     half = ref.shape[0] // 2
-    upper = matrix.astype(bf16)
-    ref[rows, :] = upper
-    ref[pl.ds(half + rows.start, rows.size), :] = (matrix - upper.astype(f32)).astype(bf16)
+    spread = matrix * 65537.0
+    upper = spread - (spread - matrix)
+    ref[rows, :] = upper.astype(bf16)
+    ref[pl.ds(half + rows.start, rows.size), :] = (matrix - upper).astype(bf16)
 
 
 def sum_rows(left, ref):
@@ -175,6 +176,15 @@
         store_split(split, rows, negative * lax.rsqrt(-negative))
 
 
+def split_both(exponent, blobs, distances):
+    for group in range(0, exponent.shape[0], GROUP):
+        rows = pl.ds(group, GROUP)
+        values = exponent[rows, :]
+        store_split(blobs, rows, jnp.exp2(values))
+        negative = jnp.minimum(values, -TINY)
+        store_split(distances, rows, negative * lax.rsqrt(-negative))
+
+
 def diagonal_tiles(start, width):
     half = width // 2
     return [(start, half, start, half, 0), (start + half, half, start, width, half)]
@@ -206,9 +216,8 @@
         if index + 1 < len(tiles):
             buffer(index + 1)[...] = exponent(tiles[index + 1])
         split = split_refs[index % 2].at[0 : 2 * tile[1], 0 : tile[3]]
-        split_blobs(buffer(index), split)
+        split_both(buffer(index), split, distance_refs[index])
         add_blobs(tile, split, moments, sums_ref)
-        split_distances(buffer(index), distance_refs[index])
 
 
 def looked_up(refs, width, axis):

time: 22.8 us -> 23.5 us (1.031)
  Pallas kernels: 10 us -> 10.9 us
    pallas_call x1, Pallas kernels: 7.75 us -> 8.26 us  [sweep(): pl.pallas_call(functools.partial(sweep_kernel, sources), out_shape=sweep_...]
  transfers between devices with their start and end apart: 5 -> 5, of which waited for: 3 -> 2; matrix products, arithmetic and copies ran while one was open for 3% -> 3% of each run, Pallas kernels for 10% -> 11%
where the time goes in v22:
time: 23.5 us; the launch traced here: 23.3 us
  Pallas kernels  10.9 us (46%)
  starting transfers between devices  6.97 us (30%)
  waiting for transfers between devices  2.19 us (9%)
  local copies, waits for them, and re-layouts  1.31 us (6%)
  between operations  1.31 us (6%)
  other arithmetic  0.62 us (3%)
    pallas_call x1, Pallas kernels, sweep(): pl.pallas_call(functools.partial(sweep_kernel, sources), out_shape=sweep_...  8.26 us
    ppermute x3, starting transfers between devices, gathered(): blocks.append(lax.ppermute(block, 'sharers', list(enumerate(targets))))  5.67 us
    ppermute x2, waiting for transfers between devices, swapped(): return lax.ppermute(value, axis, pairs)  2.18 us
    pallas_call x1, Pallas kernels, next_part(): pl.pallas_call(functools.partial(next_kernel, sources), out_shape=shapes,...  1.82 us
    unnamed x4, local copies, waits for them, and re-layouts  1.31 us
    ppermute x2, starting transfers between devices, swapped(): return lax.ppermute(value, axis, pairs)  1.3 us
    pallas_call x1, Pallas kernels, own_part(): pl.pallas_call(own_kernel, out_shape=shapes, in_specs=[vector] * 2, out_s...  0.79 us
    add x1, other arithmetic, local(): moved = start + time_step[None] * drift  0.61 us
  transfers between devices with their start and end apart: 5, of which 2 were waited for; matrix products, arithmetic and copies ran while one was open for 3% of the time, Pallas kernels for 11%

profile of v22, /device:TPU:0, one launch (start us, length us, event | category | flops | bytes accessed | tf_op | source)
XLA Modules:
  0.0 23.3 jit_solution(167263074237349880)
XLA Ops:
  0.6 0.0 copy-start
  0.6 0.7 %copy.8 = f32[1,3,512]{2,1,0:T(4,128)S(1)} copy(f32[1,3,512]{2,0,1:T(1,128)} %param.3) | data formatting | bytes 12288 | tf_op args[0]
  1.3 0.0 copy-done
  1.4 4.1 %collective-permute-start = (f32[1,4,512]{2,1,0:T(4,128)S(1)}, f32[1,4,512]{2,1,0:T(4,128)S(1)}, u32[]{:S(2)}, u32[]{:S(2)}) collective-permute-start(f32[1,4,512]{2,1,0:T(4,128)S(1)} %pad_maximum_fusion.block.refs_1_), channel_id=1, source_target_pairs={{0,2},{1,3},{2,1},{3,0},{4,6},{5,7},{6,5},{7,4},{8,10},{9,11},{10,... | collective-permute-start | bytes 24584 | tf_op jit(solution)/shard_map/ppermute | solution.py:550
  5.4 1.1 %collective-permute-start.1 = (f32[1,4,512]{2,1,0:T(4,128)S(1)}, f32[1,4,512]{2,1,0:T(4,128)S(1)}, u32[]{:S(2)}, u32[]{:S(2)}) collective-permute-start(f32[1,4,512]{2,1,0:T(4,128)S(1)} %pad_maximum_fusion.block.refs_1_), channel_id=1, source_target_pairs={{0,3},{1,2},{2,0},{3,1},{4,7},{5,6},{6,4},{7,5},{8,11},{9,10},{10,... | collective-permute-start | bytes 24584 | tf_op jit(solution)/shard_map/ppermute | solution.py:550
  6.5 0.5 %collective-permute-start.2 = (f32[1,4,512]{2,1,0:T(4,128)S(1)}, f32[1,4,512]{2,1,0:T(4,128)S(1)}, u32[]{:S(2)}, u32[]{:S(2)}) collective-permute-start(f32[1,4,512]{2,1,0:T(4,128)S(1)} %pad_maximum_fusion.block.refs_1_), channel_id=1, source_target_pairs={{0,1},{1,0},{2,3},{3,2},{4,5},{5,4},{6,7},{7,6},{8,9},{9,8},{10,11... | collective-permute-start | bytes 24584 | tf_op jit(solution)/shard_map/ppermute | solution.py:550
  7.7 0.8 %own.1 = (bf16[512,96]{1,0:T(8,128)(2,1)S(1)}, bf16[96,512]{1,0:T(8,128)(2,1)S(1)}, bf16[16,512]{1,0:T(8,128)(2,1)S(1)}, f32[16,512]{1,0:T(8,128)S(1)}, bf16[512...) custom-call(s32[1,1]{1,0:T(1,128)} %bitcast.7.filled, f32[1,4,512]{2,1,0:T(4,128)S(1)} %pad_maximum_fusion.block.refs_1_), custom_call_target="tpu_custom_call" | custom-call | tf_op jit(solution)/shard_map/own/pallas_call | solution.py:303
  8.5 0.0 collective-permute-done.block.refs_2_
  8.5 1.8 %next.1 = (bf16[512,96]{1,0:T(8,128)(2,1)S(1)}, bf16[96,512]{1,0:T(8,128)(2,1)S(1)}, bf16[16,512]{1,0:T(8,128)(2,1)S(1)}, f32[16,1024]{1,0:T(8,128)S(1)}, bf16[1...) custom-call(s32[1,1]{1,0:T(1,128)} %bitcast.8.filled, ...), custom_call_target="tpu_custom_call" | custom-call | tf_op jit(solution)/shard_map/next/pallas_call | solution.py:319
  10.3 0.0 collective-permute-done.1.refs_3_
  10.3 0.0 collective-permute-done.2.refs_4_
  10.3 8.3 %sweep.1 = (f32[8,512]{1,0:T(8,128)S(1)}, f32[3,4,128]{2,1,0:T(4,128)S(1)}, f32[3,4,128]{2,1,0:T(4,128)S(1)}, f32[1,128]{1,0:T(1,128)S(1)}) custom-call(s32[1,1]{1,0:T(1,128)} %bitcast.9.refs_0_, f32[1,4,512]{2,1,0:T(4,128)S(1)} %pad_maximum_fusion.block.refs_1_, f32[1,4,512]{2,1,0:T(4,128)S(1)} %collective-permute-done.block.refs_2_, ...), custom_call_target="tpu_custom_call" | custom-call | tf_op jit(solution)/shard_map/sweep/pallas_call | solution.py:438
  18.6 0.0 collective-permute-start.3
  18.6 1.1 %collective-permute-done.3 = f32[1,128]{1,0:T(1,128)S(1)} collective-permute-done((f32[1,128]{1,0:T(1,128)S(1)}, f32[1,128]{1,0:T(1,128)S(1)}, u32[]{:S(2)}, u32[]{:S(2)}) %collective-permute-start.3) | collective-permute-done | bytes 544 | tf_op jit(solution)/shard_map/ppermute | solution.py:535
  19.7 1.3 %collective-permute-start.4 = (f32[1,128]{1,0:T(1,128)S(1)}, f32[1,128]{1,0:T(1,128)S(1)}, u32[]{:S(2)}, u32[]{:S(2)}) collective-permute-start(f32[1,128]{1,0:T(1,128)S(1)} %max.6), channel_id=1, source_target_pairs={{0,12},{4,8},{8,4},{12,0},{1,13},{5,9},{9,5},{13,1},{2,14},{6,10},... | collective-permute-start | bytes 1544 | tf_op jit(solution)/shard_map/ppermute | solution.py:535
  21.0 0.6 %copy.10 = f32[1,3,512]{2,0,1:T(1,128)} copy(f32[1,3,512]{2,1,0:T(4,128)S(1)} %slice_bitcast_fusion) | data formatting | bytes 12288
  21.6 1.1 %collective-permute-done.4 = f32[1,128]{1,0:T(1,128)S(1)} collective-permute-done((f32[1,128]{1,0:T(1,128)S(1)}, f32[1,128]{1,0:T(1,128)S(1)}, u32[]{:S(2)}, u32[]{:S(2)}) %collective-permute-start.4) | collective-permute-done | bytes 544 | tf_op jit(solution)/shard_map/ppermute | solution.py:535
  22.7 0.6 %multiply_add_fusion = f32[3,4,128]{2,1,0:T(4,128)} fusion(f32[3,4,128]{2,1,0:T(4,128)S(1)} %get-tuple-element.32, f32[3,4,128]{2,1,0:T(4,128)S(1)} %get-tuple-element.34, f32[128]{0:T(128)S(1)} %divide_bitcast_fusion), kind=kLoop, calls=%fused_computation.2 | loop fusion | flops 3072 | bytes 18944 | tf_op jit(solution)/shard_map/add | solution.py:572
  (4 shorter events, 0.0 us)
Async XLA Ops:
  0.6 0.7 %copy-start = (f32[1,512]{1,0:T(1,128)S(1)}, f32[1,512]{1,0:T(1,128)}, u32[]{:S(2)}) copy-start(f32[1,512]{1,0:T(1,128)} %param.4) | copy-start | bytes 6148
  1.4 7.1 %collective-permute-start = (f32[1,4,512]{2,1,0:T(4,128)S(1)}, f32[1,4,512]{2,1,0:T(4,128)S(1)}, u32[]{:S(2)}, u32[]{:S(2)}) collective-permute-start(f32[1,4,512]{2,1,0:T(4,128)S(1)} %pad_maximum_fusion.block.refs_1_), channel_id=1, source_target_pairs={{0,2},{1,3},{2,1},{3,0},{4,6},{5,7},{6,5},{7,4},{8,10},{9,11},{10,... | collective-permute-start | bytes 24584 | tf_op jit(solution)/shard_map/ppermute | solution.py:550
  5.4 4.8 %collective-permute-start.1 = (f32[1,4,512]{2,1,0:T(4,128)S(1)}, f32[1,4,512]{2,1,0:T(4,128)S(1)}, u32[]{:S(2)}, u32[]{:S(2)}) collective-permute-start(f32[1,4,512]{2,1,0:T(4,128)S(1)} %pad_maximum_fusion.block.refs_1_), channel_id=1, source_target_pairs={{0,3},{1,2},{2,0},{3,1},{4,7},{5,6},{6,4},{7,5},{8,11},{9,10},{10,... | collective-permute-start | bytes 24584 | tf_op jit(solution)/shard_map/ppermute | solution.py:550
  6.5 3.8 %collective-permute-start.2 = (f32[1,4,512]{2,1,0:T(4,128)S(1)}, f32[1,4,512]{2,1,0:T(4,128)S(1)}, u32[]{:S(2)}, u32[]{:S(2)}) collective-permute-start(f32[1,4,512]{2,1,0:T(4,128)S(1)} %pad_maximum_fusion.block.refs_1_), channel_id=1, source_target_pairs={{0,1},{1,0},{2,3},{3,2},{4,5},{5,4},{6,7},{7,6},{8,9},{9,8},{10,11... | collective-permute-start | bytes 24584 | tf_op jit(solution)/shard_map/ppermute | solution.py:550
  18.6 1.1 %collective-permute-start.3 = (f32[1,128]{1,0:T(1,128)S(1)}, f32[1,128]{1,0:T(1,128)S(1)}, u32[]{:S(2)}, u32[]{:S(2)}) collective-permute-start(f32[1,128]{1,0:T(1,128)S(1)} %get-tuple-element.33), channel_id=1, source_target_pairs={{0,4},{4,0},{8,12},{12,8},{1,5},{5,1},{9,13},{13,9},{2,6},{6,2},{1... | collective-permute-start | bytes 1544 | tf_op jit(solution)/shard_map/ppermute | solution.py:535
  19.7 3.0 %collective-permute-start.4 = (f32[1,128]{1,0:T(1,128)S(1)}, f32[1,128]{1,0:T(1,128)S(1)}, u32[]{:S(2)}, u32[]{:S(2)}) collective-permute-start(f32[1,128]{1,0:T(1,128)S(1)} %max.6), channel_id=1, source_target_pairs={{0,12},{4,8},{8,4},{12,0},{1,13},{5,9},{9,5},{13,1},{2,14},{6,10},... | collective-permute-start | bytes 1544 | tf_op jit(solution)/shard_map/ppermute | solution.py:535

commit v23 on v21

--- a/solution.py
+++ b/solution.py
@@ -249,7 +249,7 @@
 
 
 def next_kernel(sources, filled, block, own_key, own_query, own_moment, own_sums, key_out,
-                query_out, moment_out, sums_out, tile_out, first_out, second_out, *scratch):
+                query_out, moment_out, sums_out, *refs):
     width = block.shape[2]
     live = lanes_of(owner_of(sources), width) < filled[...]
     _, _, key, query, moment = prepared(widened(block), live)
@@ -262,8 +262,8 @@
         looked_up([own_key, key_out], width, 0), looked_up([own_query, query_out], width, 1)
     )
     moments = looked_up([own_moment, moment_out], width, 1)
-    tiles = [(width, width, 0, width, width)] + diagonal_tiles(width, width)
-    distances = (tile_out, first_out, second_out)
+    tiles = square_tiles(width, 0, width) + diagonal_tiles(width, width)
+    distances, scratch = refs[: len(tiles)], refs[len(tiles) :]
     stage(tiles, exponent, moments, sums_out, scratch[:2], scratch[2:], distances)
 
 
@@ -284,7 +284,8 @@
 
 
 def stage_scratch(width):
-    return [pltpu.VMEM((width, width), f32)] * 2 + [pltpu.VMEM((2 * width, width), bf16)] * 2
+    half = width // 2
+    return [pltpu.VMEM((half, width), f32)] * 2 + [pltpu.VMEM((width, width), bf16)] * 2
 
 
 def own_part(filled, block):
@@ -306,7 +307,7 @@
     width = block.shape[2]
     vector = pl.BlockSpec(memory_space=pltpu.VMEM)
     shapes = feature_shapes(width) + [jax.ShapeDtypeStruct((16, 2 * width), f32)]
-    shapes += [jax.ShapeDtypeStruct((2 * width, width), bf16)] + diagonal_shapes(width)
+    shapes += [jax.ShapeDtypeStruct((width, width), bf16)] * 2 + diagonal_shapes(width)
     return pl.pallas_call(
         functools.partial(next_kernel, sources),
         out_shape=shapes,
@@ -318,12 +319,18 @@
     )(filled, block, *features, sums)
 
 
+def square_tiles(key, query, width):
+    half = width // 2
+    return [(key + part, half, query, width, width) for part in (0, half)]
+
+
 def late_tiles(count, width):
     tiles = []
     for query in range(count):
         first = max(query + 1, 2)
         tiles += diagonal_tiles(query * width, width) if query >= 2 else []
-        tiles += [(key * width, width, query * width, width, width) for key in range(first, count)]
+        for key in range(first, count):
+            tiles += square_tiles(key * width, query * width, width)
     return tiles
 
 
@@ -368,7 +375,7 @@
 def sweep_kernel(sources, *refs):
     count = len(sources)
     filled, blocks, refs = refs[0], refs[1 : count + 1], list(refs[count + 1 :])
-    own, following, refs = refs[:5], refs[5:12], refs[12:]
+    own, following, refs = refs[:5], refs[5:13], refs[13:]
     outs, (key_ref, query_ref, moment_ref, flux_ref, sums_ref, totals_ref), refs = (
         refs[:4], refs[4:10], refs[10:]
     )
@@ -405,9 +412,9 @@
     def fluxes(start, size):
         return flux_ref[:, pl.ds(start, size)]
 
-    early = diagonal_tiles(0, width) + [(width, width, 0, width, width)]
+    early = diagonal_tiles(0, width) + square_tiles(width, 0, width)
     early += diagonal_tiles(width, width)
-    for tile, split in zip(early + tiles, own[3:5] + following[4:7] + distance_refs):
+    for tile, split in zip(early + tiles, own[3:5] + following[4:8] + distance_refs):
         add_distances(tile, split, fluxes, totals_ref)
     finish(blocks, count * width, weight, centred, score, totals_ref[...], outs)
 

time: 22.8 us -> 22.7 us (level)
  Pallas kernels: 10 us -> 9.76 us
  transfers between devices with their start and end apart: 5 -> 5, of which waited for: 3 -> 4; matrix products, arithmetic and copies ran while one was open for 3% -> 3% of each run, Pallas kernels for 10% -> 10%
where the time goes in v23:
time: 22.7 us; the launch traced here: 22.5 us
  Pallas kernels  9.76 us (43%)
  starting transfers between devices  7.13 us (31%)
  waiting for transfers between devices  2.37 us (10%)
  local copies, waits for them, and re-layouts  1.31 us (6%)
  between operations  1.31 us (6%)
  other arithmetic  0.62 us (3%)
    pallas_call x1, Pallas kernels, sweep(): pl.pallas_call(functools.partial(sweep_kernel, sources), out_shape=sweep_...  7.61 us
    ppermute x3, starting transfers between devices, gathered(): blocks.append(lax.ppermute(block, 'sharers', list(enumerate(targets))))  5.67 us
    ppermute x2, waiting for transfers between devices, swapped(): return lax.ppermute(value, axis, pairs)  2.02 us
    ppermute x2, starting transfers between devices, swapped(): return lax.ppermute(value, axis, pairs)  1.46 us
    pallas_call x1, Pallas kernels, next_part(): pl.pallas_call(functools.partial(next_kernel, sources), out_shape=shapes,...  1.45 us
    unnamed x4, local copies, waits for them, and re-layouts  1.31 us
    pallas_call x1, Pallas kernels, own_part(): pl.pallas_call(own_kernel, out_shape=shapes, in_specs=[vector] * 2, out_s...  0.7 us
    add x1, other arithmetic, local(): moved = start + time_step[None] * drift  0.61 us
  transfers between devices with their start and end apart: 5, of which 4 were waited for; matrix products, arithmetic and copies ran while one was open for 3% of the time, Pallas kernels for 10%

profile of v23, /device:TPU:0, one launch (start us, length us, event | category | flops | bytes accessed | tf_op | source)
XLA Modules:
  0.0 22.5 jit_solution(6208775624370028450)
XLA Ops:
  0.6 0.0 copy-start
  0.6 0.7 %copy.8 = f32[1,3,512]{2,1,0:T(4,128)S(1)} copy(f32[1,3,512]{2,0,1:T(1,128)} %param.3) | data formatting | bytes 12288 | tf_op args[0]
  1.3 0.0 copy-done
  1.4 4.1 %collective-permute-start = (f32[1,4,512]{2,1,0:T(4,128)S(1)}, f32[1,4,512]{2,1,0:T(4,128)S(1)}, u32[]{:S(2)}, u32[]{:S(2)}) collective-permute-start(f32[1,4,512]{2,1,0:T(4,128)S(1)} %pad_maximum_fusion.block.refs_1_), channel_id=1, source_target_pairs={{0,2},{1,3},{2,1},{3,0},{4,6},{5,7},{6,5},{7,4},{8,10},{9,11},{10,... | collective-permute-start | bytes 24584 | tf_op jit(solution)/shard_map/ppermute | solution.py:548
  5.4 1.1 %collective-permute-start.1 = (f32[1,4,512]{2,1,0:T(4,128)S(1)}, f32[1,4,512]{2,1,0:T(4,128)S(1)}, u32[]{:S(2)}, u32[]{:S(2)}) collective-permute-start(f32[1,4,512]{2,1,0:T(4,128)S(1)} %pad_maximum_fusion.block.refs_1_), channel_id=1, source_target_pairs={{0,3},{1,2},{2,0},{3,1},{4,7},{5,6},{6,4},{7,5},{8,11},{9,10},{10,... | collective-permute-start | bytes 24584 | tf_op jit(solution)/shard_map/ppermute | solution.py:548
  6.5 0.5 %collective-permute-start.2 = (f32[1,4,512]{2,1,0:T(4,128)S(1)}, f32[1,4,512]{2,1,0:T(4,128)S(1)}, u32[]{:S(2)}, u32[]{:S(2)}) collective-permute-start(f32[1,4,512]{2,1,0:T(4,128)S(1)} %pad_maximum_fusion.block.refs_1_), channel_id=1, source_target_pairs={{0,1},{1,0},{2,3},{3,2},{4,5},{5,4},{6,7},{7,6},{8,9},{9,8},{10,11... | collective-permute-start | bytes 24584 | tf_op jit(solution)/shard_map/ppermute | solution.py:548
  7.7 0.7 %own.1 = (bf16[512,96]{1,0:T(8,128)(2,1)S(1)}, bf16[96,512]{1,0:T(8,128)(2,1)S(1)}, bf16[16,512]{1,0:T(8,128)(2,1)S(1)}, f32[16,512]{1,0:T(8,128)S(1)}, bf16[512...) custom-call(s32[1,1]{1,0:T(1,128)} %bitcast.7.filled, f32[1,4,512]{2,1,0:T(4,128)S(1)} %pad_maximum_fusion.block.refs_1_), custom_call_target="tpu_custom_call" | custom-call | tf_op jit(solution)/shard_map/own/pallas_call | solution.py:295
  8.4 0.0 collective-permute-done.block.refs_2_
  8.4 1.5 %next.1 = (bf16[512,96]{1,0:T(8,128)(2,1)S(1)}, bf16[96,512]{1,0:T(8,128)(2,1)S(1)}, bf16[16,512]{1,0:T(8,128)(2,1)S(1)}, f32[16,1024]{1,0:T(8,128)S(1)}, bf16[5...) custom-call(s32[1,1]{1,0:T(1,128)} %bitcast.8.filled, ...), custom_call_target="tpu_custom_call" | custom-call | tf_op jit(solution)/shard_map/next/pallas_call | solution.py:311
  9.8 0.2 collective-permute-done.1.refs_3_
  10.0 0.2 collective-permute-done.2.refs_4_
  10.2 7.6 %sweep.1 = (f32[8,512]{1,0:T(8,128)S(1)}, f32[3,4,128]{2,1,0:T(4,128)S(1)}, f32[3,4,128]{2,1,0:T(4,128)S(1)}, f32[1,128]{1,0:T(1,128)S(1)}) custom-call(s32[1,1]{1,0:T(1,128)} %bitcast.9.refs_0_, f32[1,4,512]{2,1,0:T(4,128)S(1)} %pad_maximum_fusion.block.refs_1_, f32[1,4,512]{2,1,0:T(4,128)S(1)} %collective-permute-done.block.refs_2_, ...), custom_call_target="tpu_custom_call" | custom-call | tf_op jit(solution)/shard_map/sweep/pallas_call | solution.py:436
  17.8 0.0 collective-permute-start.3
  17.8 1.1 %collective-permute-done.3 = f32[1,128]{1,0:T(1,128)S(1)} collective-permute-done((f32[1,128]{1,0:T(1,128)S(1)}, f32[1,128]{1,0:T(1,128)S(1)}, u32[]{:S(2)}, u32[]{:S(2)}) %collective-permute-start.3) | collective-permute-done | bytes 544 | tf_op jit(solution)/shard_map/ppermute | solution.py:533
  18.9 1.5 %collective-permute-start.4 = (f32[1,128]{1,0:T(1,128)S(1)}, f32[1,128]{1,0:T(1,128)S(1)}, u32[]{:S(2)}, u32[]{:S(2)}) collective-permute-start(f32[1,128]{1,0:T(1,128)S(1)} %max.6), channel_id=1, source_target_pairs={{0,12},{4,8},{8,4},{12,0},{1,13},{5,9},{9,5},{13,1},{2,14},{6,10},... | collective-permute-start | bytes 1544 | tf_op jit(solution)/shard_map/ppermute | solution.py:533
  20.4 0.6 %copy.10 = f32[1,3,512]{2,0,1:T(1,128)} copy(f32[1,3,512]{2,1,0:T(4,128)S(1)} %slice_bitcast_fusion) | data formatting | bytes 12288
  21.0 0.9 %collective-permute-done.4 = f32[1,128]{1,0:T(1,128)S(1)} collective-permute-done((f32[1,128]{1,0:T(1,128)S(1)}, f32[1,128]{1,0:T(1,128)S(1)}, u32[]{:S(2)}, u32[]{:S(2)}) %collective-permute-start.4) | collective-permute-done | bytes 544 | tf_op jit(solution)/shard_map/ppermute | solution.py:533
  21.9 0.6 %multiply_add_fusion = f32[3,4,128]{2,1,0:T(4,128)} fusion(f32[3,4,128]{2,1,0:T(4,128)S(1)} %get-tuple-element.34, f32[3,4,128]{2,1,0:T(4,128)S(1)} %get-tuple-element.36, f32[128]{0:T(128)S(1)} %divide_bitcast_fusion), kind=kLoop, calls=%fused_computation.2 | loop fusion | flops 3072 | bytes 18944 | tf_op jit(solution)/shard_map/add | solution.py:570
  (4 shorter events, 0.0 us)
Async XLA Ops:
  0.6 0.7 %copy-start = (f32[1,512]{1,0:T(1,128)S(1)}, f32[1,512]{1,0:T(1,128)}, u32[]{:S(2)}) copy-start(f32[1,512]{1,0:T(1,128)} %param.4) | copy-start | bytes 6148
  1.4 7.0 %collective-permute-start = (f32[1,4,512]{2,1,0:T(4,128)S(1)}, f32[1,4,512]{2,1,0:T(4,128)S(1)}, u32[]{:S(2)}, u32[]{:S(2)}) collective-permute-start(f32[1,4,512]{2,1,0:T(4,128)S(1)} %pad_maximum_fusion.block.refs_1_), channel_id=1, source_target_pairs={{0,2},{1,3},{2,1},{3,0},{4,6},{5,7},{6,5},{7,4},{8,10},{9,11},{10,... | collective-permute-start | bytes 24584 | tf_op jit(solution)/shard_map/ppermute | solution.py:548
  5.4 4.5 %collective-permute-start.1 = (f32[1,4,512]{2,1,0:T(4,128)S(1)}, f32[1,4,512]{2,1,0:T(4,128)S(1)}, u32[]{:S(2)}, u32[]{:S(2)}) collective-permute-start(f32[1,4,512]{2,1,0:T(4,128)S(1)} %pad_maximum_fusion.block.refs_1_), channel_id=1, source_target_pairs={{0,3},{1,2},{2,0},{3,1},{4,7},{5,6},{6,4},{7,5},{8,11},{9,10},{10,... | collective-permute-start | bytes 24584 | tf_op jit(solution)/shard_map/ppermute | solution.py:548
  6.5 3.7 %collective-permute-start.2 = (f32[1,4,512]{2,1,0:T(4,128)S(1)}, f32[1,4,512]{2,1,0:T(4,128)S(1)}, u32[]{:S(2)}, u32[]{:S(2)}) collective-permute-start(f32[1,4,512]{2,1,0:T(4,128)S(1)} %pad_maximum_fusion.block.refs_1_), channel_id=1, source_target_pairs={{0,1},{1,0},{2,3},{3,2},{4,5},{5,4},{6,7},{7,6},{8,9},{9,8},{10,11... | collective-permute-start | bytes 24584 | tf_op jit(solution)/shard_map/ppermute | solution.py:548
  17.8 1.1 %collective-permute-start.3 = (f32[1,128]{1,0:T(1,128)S(1)}, f32[1,128]{1,0:T(1,128)S(1)}, u32[]{:S(2)}, u32[]{:S(2)}) collective-permute-start(f32[1,128]{1,0:T(1,128)S(1)} %get-tuple-element.35), channel_id=1, source_target_pairs={{0,4},{4,0},{8,12},{12,8},{1,5},{5,1},{9,13},{13,9},{2,6},{6,2},{1... | collective-permute-start | bytes 1544 | tf_op jit(solution)/shard_map/ppermute | solution.py:533
  18.9 3.0 %collective-permute-start.4 = (f32[1,128]{1,0:T(1,128)S(1)}, f32[1,128]{1,0:T(1,128)S(1)}, u32[]{:S(2)}, u32[]{:S(2)}) collective-permute-start(f32[1,128]{1,0:T(1,128)S(1)} %max.6), channel_id=1, source_target_pairs={{0,12},{4,8},{8,4},{12,0},{1,13},{5,9},{9,5},{13,1},{2,14},{6,10},... | collective-permute-start | bytes 1544 | tf_op jit(solution)/shard_map/ppermute | solution.py:533

commit v24 on v23

--- a/solution.py
+++ b/solution.py
@@ -13,7 +13,7 @@
 SCALE = math.sqrt(math.log2(math.e) / (2.0 * EPS * EPS))
 GRID = 4.0
 TINY = 1e-30
-GROUP = 32
+GROUP = 16
 DISTANCE_ROWS = 96
 DRIFT_ROWS = 64
 bf16, f32 = jnp.bfloat16, jnp.float32
@@ -162,17 +162,13 @@
     return weight, place, key.T, query, weighted_rows(weight, place)
 
 
-def split_blobs(exponent, split):
-    for group in range(0, exponent.shape[0], GROUP):
-        rows = pl.ds(group, GROUP)
-        store_split(split, rows, jnp.exp2(exponent[rows, :]))
-
-
-def split_distances(exponent, split):
-    for group in range(0, exponent.shape[0], GROUP):
-        rows = pl.ds(group, GROUP)
-        negative = jnp.minimum(exponent[rows, :], -TINY)
-        store_split(split, rows, negative * lax.rsqrt(-negative))
+def split_both(exponent, blobs, distances, rows):
+    values = exponent[rows, :]
+    if blobs is not None:
+        store_split(blobs, rows, jnp.exp2(values))
+    if distances is not None:
+        negative = jnp.minimum(values, -TINY)
+        store_split(distances, rows, negative * lax.rsqrt(-negative))
 
 
 def diagonal_tiles(start, width):
@@ -182,9 +178,15 @@
 
 def add_blobs(tile, split, moments, sums_ref):
     key, keys, query, queries, turned = tile
-    sums_ref[:, pl.ds(query, queries)] += sum_rows(moments(key, keys), split)
-    if turned:
-        sums_ref[:, pl.ds(key, keys)] += sum_columns(moments(query, turned), split.at[:, 0:turned])
+
+    def rows():
+        sums_ref[:, pl.ds(query, queries)] += sum_rows(moments(key, keys), split)
+
+    def columns():
+        left, right = moments(query, turned), split.at[:, 0:turned]
+        sums_ref[:, pl.ds(key, keys)] += sum_columns(left, right)
+
+    return [rows, columns] if turned else [rows]
 
 
 def add_distances(tile, split, fluxes, totals_ref):
@@ -201,14 +203,28 @@
         _, keys, _, queries, _ = tiles[index]
         return exponent_refs[index % 2].at[0:keys, 0:queries]
 
-    buffer(0)[...] = exponent(tiles[0])
+    def split(index):
+        _, keys, _, queries, _ = tiles[index]
+        return split_refs[index % 2].at[0 : 2 * keys, 0:queries]
+
+    def fill(index):
+        buffer(index)[...] = exponent(tiles[index])
+
+    fill(0)
+    sums = []
     for index, tile in enumerate(tiles):
-        if index + 1 < len(tiles):
-            buffer(index + 1)[...] = exponent(tiles[index + 1])
-        split = split_refs[index % 2].at[0 : 2 * tile[1], 0 : tile[3]]
-        split_blobs(buffer(index), split)
-        add_blobs(tile, split, moments, sums_ref)
-        split_distances(buffer(index), distance_refs[index])
+        jobs = [functools.partial(fill, index + 1)] if index + 1 < len(tiles) else []
+        jobs += sums
+        groups = list(range(0, tile[1], GROUP))
+        for at, group in enumerate(groups):
+            if jobs and at * 4 % len(groups) == 0:
+                jobs.pop(0)()
+            split_both(buffer(index), split(index), distance_refs[index], pl.ds(group, GROUP))
+        for job in jobs:
+            job()
+        sums = add_blobs(tile, split(index), moments, sums_ref)
+    for job in sums:
+        job()
 
 
 def looked_up(refs, width, axis):
@@ -480,8 +496,12 @@
     def blobs(key, query, both):
         tile = block_tile(key, query, both)
         fill(tile)
-        split_blobs(exponent_ref, split_ref)
-        add_blobs(tile, split_ref, lambda at, size: moment_ref[:, pl.ds(at, size)], sums_ref)
+        for group in range(0, width, GROUP):
+            split_both(exponent_ref, split_ref, None, pl.ds(group, GROUP))
+        for job in add_blobs(
+            tile, split_ref, lambda at, size: moment_ref[:, pl.ds(at, size)], sums_ref
+        ):
+            job()
 
     @pl.loop(0, count)
     def _(query):
@@ -498,7 +518,8 @@
     def _(key):
         tile = block_tile(key, 0, False)
         fill(tile)
-        split_distances(exponent_ref, split_ref)
+        for group in range(0, width, GROUP):
+            split_both(exponent_ref, None, split_ref, pl.ds(group, GROUP))
         add_distances(tile, split_ref, lambda at, size: flux_ref[:, pl.ds(at, size)], totals_ref)
 
     finish(blocks, count * width, weight, centred, score, totals_ref[...], outs)
@@ -559,7 +580,7 @@
     blocks, sources = gathered(jnp.concatenate([velocities, weights[:, None]], axis=1))
     if len(blocks) == len(ROUNDS) + 1:
         scores, drift, start, speeds = sweep(filled, blocks, sources)
-        for step in bits(lax.axis_size("cells")):
+        for step in reversed(bits(lax.axis_size("cells"))):
             speeds = jnp.maximum(speeds, swapped(speeds, "cells", 2 * step - 1))
         largest = speeds
     else:

time: 22.7 us -> 23 us (1.013)
  waiting for transfers between devices: 2.37 us -> 3.84 us
  starting transfers between devices: 7.13 us -> 5.72 us
    ppermute x2, waiting for transfers between devices: 2.02 us -> 3.44 us  [swapped(): return lax.ppermute(value, axis, pairs)]
    ppermute x2, starting transfers between devices: 1.46 us -> 0.05 us  [swapped(): return lax.ppermute(value, axis, pairs)]
    pallas_call x1, Pallas kernels: 7.61 us -> 7.88 us  [sweep(): pl.pallas_call(functools.partial(sweep_kernel, sources), out_shape=sweep_...]
  transfers between devices with their start and end apart: 5 -> 5, of which waited for: 4 -> 4; matrix products, arithmetic and copies ran while one was open for 3% -> 3% of each run, Pallas kernels for 10% -> 9%
where the time goes in v24:
time: 23 us; the launch traced here: 22.8 us
  Pallas kernels  9.98 us (43%)
  starting transfers between devices  5.72 us (25%)
  waiting for transfers between devices  3.84 us (17%)
  local copies, waits for them, and re-layouts  1.31 us (6%)
  between operations  1.3 us (6%)
  other arithmetic  0.62 us (3%)
    pallas_call x1, Pallas kernels, sweep(): pl.pallas_call(functools.partial(sweep_kernel, sources), out_shape=sweep_...  7.88 us
    ppermute x3, starting transfers between devices, gathered(): blocks.append(lax.ppermute(block, 'sharers', list(enumerate(targets))))  5.67 us
    ppermute x2, waiting for transfers between devices, swapped(): return lax.ppermute(value, axis, pairs)  3.44 us
    pallas_call x1, Pallas kernels, next_part(): pl.pallas_call(functools.partial(next_kernel, sources), out_shape=shapes,...  1.4 us
    unnamed x4, local copies, waits for them, and re-layouts  1.31 us
    pallas_call x1, Pallas kernels, own_part(): pl.pallas_call(own_kernel, out_shape=shapes, in_specs=[vector] * 2, out_s...  0.7 us
    add x1, other arithmetic, local(): moved = start + time_step[None] * drift  0.61 us
  transfers between devices with their start and end apart: 5, of which 4 were waited for; matrix products, arithmetic and copies ran while one was open for 3% of the time, Pallas kernels for 9%

profile of v24, /device:TPU:0, one launch (start us, length us, event | category | flops | bytes accessed | tf_op | source)
XLA Modules:
  0.0 22.8 jit_solution(5074227427076241775)
XLA Ops:
  0.6 0.0 copy-start
  0.6 0.7 %copy.8 = f32[1,3,512]{2,1,0:T(4,128)S(1)} copy(f32[1,3,512]{2,0,1:T(1,128)} %param.3) | data formatting | bytes 12288 | tf_op args[0]
  1.3 0.0 copy-done
  1.4 4.1 %collective-permute-start = (f32[1,4,512]{2,1,0:T(4,128)S(1)}, f32[1,4,512]{2,1,0:T(4,128)S(1)}, u32[]{:S(2)}, u32[]{:S(2)}) collective-permute-start(f32[1,4,512]{2,1,0:T(4,128)S(1)} %pad_maximum_fusion.block.refs_1_), channel_id=1, source_target_pairs={{0,2},{1,3},{2,1},{3,0},{4,6},{5,7},{6,5},{7,4},{8,10},{9,11},{10,... | collective-permute-start | bytes 24584 | tf_op jit(solution)/shard_map/ppermute | solution.py:569
  5.4 1.1 %collective-permute-start.1 = (f32[1,4,512]{2,1,0:T(4,128)S(1)}, f32[1,4,512]{2,1,0:T(4,128)S(1)}, u32[]{:S(2)}, u32[]{:S(2)}) collective-permute-start(f32[1,4,512]{2,1,0:T(4,128)S(1)} %pad_maximum_fusion.block.refs_1_), channel_id=1, source_target_pairs={{0,3},{1,2},{2,0},{3,1},{4,7},{5,6},{6,4},{7,5},{8,11},{9,10},{10,... | collective-permute-start | bytes 24584 | tf_op jit(solution)/shard_map/ppermute | solution.py:569
  6.5 0.5 %collective-permute-start.2 = (f32[1,4,512]{2,1,0:T(4,128)S(1)}, f32[1,4,512]{2,1,0:T(4,128)S(1)}, u32[]{:S(2)}, u32[]{:S(2)}) collective-permute-start(f32[1,4,512]{2,1,0:T(4,128)S(1)} %pad_maximum_fusion.block.refs_1_), channel_id=1, source_target_pairs={{0,1},{1,0},{2,3},{3,2},{4,5},{5,4},{6,7},{7,6},{8,9},{9,8},{10,11... | collective-permute-start | bytes 24584 | tf_op jit(solution)/shard_map/ppermute | solution.py:569
  7.7 0.7 %own.1 = (bf16[512,96]{1,0:T(8,128)(2,1)S(1)}, bf16[96,512]{1,0:T(8,128)(2,1)S(1)}, bf16[16,512]{1,0:T(8,128)(2,1)S(1)}, f32[16,512]{1,0:T(8,128)S(1)}, bf16[512...) custom-call(s32[1,1]{1,0:T(1,128)} %bitcast.7.filled, f32[1,4,512]{2,1,0:T(4,128)S(1)} %pad_maximum_fusion.block.refs_1_), custom_call_target="tpu_custom_call" | custom-call | tf_op jit(solution)/shard_map/own/pallas_call | solution.py:311
  8.4 0.0 collective-permute-done.block.refs_2_
  8.4 1.4 %next.1 = (bf16[512,96]{1,0:T(8,128)(2,1)S(1)}, bf16[96,512]{1,0:T(8,128)(2,1)S(1)}, bf16[16,512]{1,0:T(8,128)(2,1)S(1)}, f32[16,1024]{1,0:T(8,128)S(1)}, bf16[5...) custom-call(s32[1,1]{1,0:T(1,128)} %bitcast.8.filled, ...), custom_call_target="tpu_custom_call" | custom-call | tf_op jit(solution)/shard_map/next/pallas_call | solution.py:327
  9.8 0.2 collective-permute-done.1.refs_3_
  10.0 0.2 collective-permute-done.2.refs_4_
  10.2 7.9 %sweep.1 = (f32[8,512]{1,0:T(8,128)S(1)}, f32[3,4,128]{2,1,0:T(4,128)S(1)}, f32[3,4,128]{2,1,0:T(4,128)S(1)}, f32[1,128]{1,0:T(1,128)S(1)}) custom-call(s32[1,1]{1,0:T(1,128)} %bitcast.9.refs_0_, f32[1,4,512]{2,1,0:T(4,128)S(1)} %pad_maximum_fusion.block.refs_1_, f32[1,4,512]{2,1,0:T(4,128)S(1)} %collective-permute-done.block.refs_2_, ...), custom_call_target="tpu_custom_call" | custom-call | tf_op jit(solution)/shard_map/sweep/pallas_call | solution.py:452
  18.1 0.0 collective-permute-start.3
  18.1 2.9 %collective-permute-done.3 = f32[1,128]{1,0:T(1,128)S(1)} collective-permute-done((f32[1,128]{1,0:T(1,128)S(1)}, f32[1,128]{1,0:T(1,128)S(1)}, u32[]{:S(2)}, u32[]{:S(2)}) %collective-permute-start.3) | collective-permute-done | bytes 544 | tf_op jit(solution)/shard_map/ppermute | solution.py:554
  21.0 0.0 collective-permute-start.4
  21.1 0.6 %copy.10 = f32[1,3,512]{2,0,1:T(1,128)} copy(f32[1,3,512]{2,1,0:T(4,128)S(1)} %slice_bitcast_fusion) | data formatting | bytes 12288
  21.7 0.5 %collective-permute-done.4 = f32[1,128]{1,0:T(1,128)S(1)} collective-permute-done((f32[1,128]{1,0:T(1,128)S(1)}, f32[1,128]{1,0:T(1,128)S(1)}, u32[]{:S(2)}, u32[]{:S(2)}) %collective-permute-start.4) | collective-permute-done | bytes 544 | tf_op jit(solution)/shard_map/ppermute | solution.py:554
  22.2 0.6 %multiply_add_fusion = f32[3,4,128]{2,1,0:T(4,128)} fusion(f32[3,4,128]{2,1,0:T(4,128)S(1)} %get-tuple-element.34, f32[3,4,128]{2,1,0:T(4,128)S(1)} %get-tuple-element.36, f32[128]{0:T(128)S(1)} %divide_bitcast_fusion), kind=kLoop, calls=%fused_computation.2 | loop fusion | flops 3072 | bytes 18944 | tf_op jit(solution)/shard_map/add | solution.py:591
  (4 shorter events, 0.0 us)
Async XLA Ops:
  0.6 0.7 %copy-start = (f32[1,512]{1,0:T(1,128)S(1)}, f32[1,512]{1,0:T(1,128)}, u32[]{:S(2)}) copy-start(f32[1,512]{1,0:T(1,128)} %param.4) | copy-start | bytes 6148
  1.4 7.0 %collective-permute-start = (f32[1,4,512]{2,1,0:T(4,128)S(1)}, f32[1,4,512]{2,1,0:T(4,128)S(1)}, u32[]{:S(2)}, u32[]{:S(2)}) collective-permute-start(f32[1,4,512]{2,1,0:T(4,128)S(1)} %pad_maximum_fusion.block.refs_1_), channel_id=1, source_target_pairs={{0,2},{1,3},{2,1},{3,0},{4,6},{5,7},{6,5},{7,4},{8,10},{9,11},{10,... | collective-permute-start | bytes 24584 | tf_op jit(solution)/shard_map/ppermute | solution.py:569
  5.4 4.5 %collective-permute-start.1 = (f32[1,4,512]{2,1,0:T(4,128)S(1)}, f32[1,4,512]{2,1,0:T(4,128)S(1)}, u32[]{:S(2)}, u32[]{:S(2)}) collective-permute-start(f32[1,4,512]{2,1,0:T(4,128)S(1)} %pad_maximum_fusion.block.refs_1_), channel_id=1, source_target_pairs={{0,3},{1,2},{2,0},{3,1},{4,7},{5,6},{6,4},{7,5},{8,11},{9,10},{10,... | collective-permute-start | bytes 24584 | tf_op jit(solution)/shard_map/ppermute | solution.py:569
  6.5 3.7 %collective-permute-start.2 = (f32[1,4,512]{2,1,0:T(4,128)S(1)}, f32[1,4,512]{2,1,0:T(4,128)S(1)}, u32[]{:S(2)}, u32[]{:S(2)}) collective-permute-start(f32[1,4,512]{2,1,0:T(4,128)S(1)} %pad_maximum_fusion.block.refs_1_), channel_id=1, source_target_pairs={{0,1},{1,0},{2,3},{3,2},{4,5},{5,4},{6,7},{7,6},{8,9},{9,8},{10,11... | collective-permute-start | bytes 24584 | tf_op jit(solution)/shard_map/ppermute | solution.py:569
  18.1 3.0 %collective-permute-start.3 = (f32[1,128]{1,0:T(1,128)S(1)}, f32[1,128]{1,0:T(1,128)S(1)}, u32[]{:S(2)}, u32[]{:S(2)}) collective-permute-start(f32[1,128]{1,0:T(1,128)S(1)} %get-tuple-element.35), channel_id=1, source_target_pairs={{0,12},{4,8},{8,4},{12,0},{1,13},{5,9},{9,5},{13,1},{2,14},{6,10},... | collective-permute-start | bytes 1544 | tf_op jit(solution)/shard_map/ppermute | solution.py:554
  21.0 1.1 %collective-permute-start.4 = (f32[1,128]{1,0:T(1,128)S(1)}, f32[1,128]{1,0:T(1,128)S(1)}, u32[]{:S(2)}, u32[]{:S(2)}) collective-permute-start(f32[1,128]{1,0:T(1,128)S(1)} %max.6), channel_id=1, source_target_pairs={{0,4},{4,0},{8,12},{12,8},{1,5},{5,1},{9,13},{13,9},{2,6},{6,2},{1... | collective-permute-start | bytes 1544 | tf_op jit(solution)/shard_map/ppermute | solution.py:554

commit v25 on v23

--- a/solution.py
+++ b/solution.py
@@ -324,16 +324,6 @@
     return [(key + part, half, query, width, width) for part in (0, half)]
 
 
-def late_tiles(count, width):
-    tiles = []
-    for query in range(count):
-        first = max(query + 1, 2)
-        tiles += diagonal_tiles(query * width, width) if query >= 2 else []
-        for key in range(first, count):
-            tiles += square_tiles(key * width, query * width, width)
-    return tiles
-
-
 def scored(weight, place, sums):
     vector, live = row_of(place) < 3, weight > 0.0
     density_sum = jnp.where(live, sums[3:4], 1.0)
@@ -372,6 +362,13 @@
             start_out[axis, part : part + 1, :] = blocks[0][0, axis : axis + 1, lanes]
 
 
+def pair_of(step):
+    return 2 + ((step & 1) | (step >> 2)), step >> 1
+
+
+LATE_PAIRS = 5
+
+
 def sweep_kernel(sources, *refs):
     count = len(sources)
     filled, blocks, refs = refs[0], refs[1 : count + 1], list(refs[count + 1 :])
@@ -380,30 +377,55 @@
         refs[:4], refs[4:10], refs[10:]
     )
     width = blocks[0].shape[2]
-    half = 2 * width
-    scratch, distance_refs = refs[:4], refs[4:]
+    half = width // 2
+    exponent_refs, split_refs, pair_ref, diagonal_refs = refs[:2], refs[2:4], refs[4], refs[5:]
 
     live = [lanes_of(owner_of(source), width) < filled[...] for source in sources]
-    late = range(2, count)
-    for index in late:
+    for index, early in enumerate((own, following)):
+        lanes = pl.ds(index * width, width)
+        query_ref[:, lanes] = early[1][...]
+        moment_ref[:, lanes] = early[2][...]
+    for index in range(2, count):
         _, _, key, query, moment = prepared(widened(blocks[index]), live[index])
-        lanes = pl.ds((index - 2) * width, width)
-        key_ref[lanes, :] = key
+        lanes = pl.ds(index * width, width)
+        key_ref[pl.ds((index - 2) * width, width), :] = key
         query_ref[:, lanes] = query
         moment_ref[:, lanes] = moment
     weight, place, centred = whole_cell(blocks, live)
-    lanes = [pl.ds((index - 2) * width, width) for index in late]
-    keys = [own[0], following[0]] + [key_ref.at[lane, :] for lane in lanes]
-    queries = [own[1], following[1]] + [query_ref.at[:, lane] for lane in lanes]
-    moments = [own[2], following[2]] + [moment_ref.at[:, lane] for lane in lanes]
-    exponent = exponent_of(looked_up(keys, width, 0), looked_up(queries, width, 1))
-
-    sums_ref[:, 0:half] = following[3][...]
-    sums_ref[:, half:] = jnp.zeros_like(sums_ref[:, half:])
-    tiles = late_tiles(count, width)
+
+    def exponent(key, keys, query, queries):
+        return product(key_ref[pl.ds(key - 2 * width, keys), :], query_ref[:, pl.ds(query, queries)])
+
+    def moments(start, size):
+        return moment_ref[:, pl.ds(start, size)]
+
+    sums_ref[:, 0 : 2 * width] = following[3][...]
+    sums_ref[:, 2 * width :] = jnp.zeros_like(sums_ref[:, 2 * width :])
+
+    def half_tile(step, part):
+        key, query = pair_of(step)
+        key = pl.multiple_of(key * width + part * half, half)
+        return (key, half, pl.multiple_of(query * width, width), width, width)
+
+    def work(tile, exponents, split, distances):
+        split_blobs(exponents, split)
+        add_blobs(tile, split, moments, sums_ref)
+        split_distances(exponents, distances)
+
+    exponent_refs[0][...] = exponent(*half_tile(0, 0)[:4])
+
+    @pl.loop(0, LATE_PAIRS)
+    def _(step):
+        exponent_refs[1][...] = exponent(*half_tile(step, 1)[:4])
+        work(half_tile(step, 0), exponent_refs[0], split_refs[0], pair_ref.at[2 * step])
+        following_step = jnp.minimum(step + 1, LATE_PAIRS - 1)
+        exponent_refs[0][...] = exponent(*half_tile(following_step, 0)[:4])
+        work(half_tile(step, 1), exponent_refs[1], split_refs[1], pair_ref.at[2 * step + 1])
+
+    diagonal = diagonal_tiles(2 * width, width) + diagonal_tiles(3 * width, width)
     stage(
-        tiles, exponent, looked_up(moments, width, 1), sums_ref, scratch[:2], scratch[2:],
-        distance_refs,
+        diagonal, lambda tile: exponent(*tile[:4]), moments, sums_ref, exponent_refs, split_refs,
+        diagonal_refs,
     )
     score = scored(weight, place, joined(sums_ref[...]))
     flux_ref[...] = drift_rows(weight, centred, score)
@@ -414,8 +436,14 @@
 
     early = diagonal_tiles(0, width) + square_tiles(width, 0, width)
     early += diagonal_tiles(width, width)
-    for tile, split in zip(early + tiles, own[3:5] + following[4:8] + distance_refs):
+    for tile, split in zip(early + diagonal, own[3:5] + following[4:8] + diagonal_refs):
         add_distances(tile, split, fluxes, totals_ref)
+
+    @pl.loop(0, LATE_PAIRS)
+    def _(step):
+        for part in range(2):
+            add_distances(half_tile(step, part), pair_ref.at[2 * step + part], fluxes, totals_ref)
+
     finish(blocks, count * width, weight, centred, score, totals_ref[...], outs)
 
 
@@ -427,27 +455,28 @@
 
 def sweep(filled, blocks, sources):
     count, width = len(blocks), blocks[0].shape[2]
-    slots, late = count * width, (count - 2) * width
+    slots = count * width
     own = own_part(filled, blocks[0])
     following = next_part(filled, blocks[1], own[:3], own[3], sources[1])
     early = [*own[:3], *own[4:], *following]
     vector = pl.BlockSpec(memory_space=pltpu.VMEM)
-    distances = [pltpu.VMEM((2 * tile[1], tile[3]), bf16) for tile in late_tiles(count, width)]
+    diagonal = diagonal_tiles(0, width) * 2
     return pl.pallas_call(
         functools.partial(sweep_kernel, sources),
         out_shape=sweep_shapes(width, 1),
         in_specs=[vector] * (1 + count + len(early)),
         out_specs=[vector] * 4,
         scratch_shapes=[
-            pltpu.VMEM((late, DISTANCE_ROWS), bf16),
-            pltpu.VMEM((DISTANCE_ROWS, late), bf16),
-            pltpu.VMEM((16, late), bf16),
+            pltpu.VMEM((slots - 2 * width, DISTANCE_ROWS), bf16),
+            pltpu.VMEM((DISTANCE_ROWS, slots), bf16),
+            pltpu.VMEM((16, slots), bf16),
             pltpu.VMEM((DRIFT_ROWS, slots), bf16),
             pltpu.VMEM((16, slots), f32),
             pltpu.VMEM((DRIFT_ROWS // 2, slots), f32),
         ]
         + stage_scratch(width)
-        + distances,
+        + [pltpu.VMEM((2 * LATE_PAIRS, width, width), bf16)]
+        + [pltpu.VMEM((2 * tile[1], tile[3]), bf16) for tile in diagonal],
         compiler_params=pltpu.CompilerParams(vmem_limit_bytes=24 << 20),
         name="sweep",
     )(filled, *blocks, *early)

time: 22.7 us -> 25.1 us (1.11)
  Pallas kernels: 9.76 us -> 12.1 us
    pallas_call x1, Pallas kernels: 7.61 us -> 9.94 us  [sweep(): pl.pallas_call(functools.partial(sweep_kernel, sources), out_shape=sweep_...]
  transfers between devices with their start and end apart: 5 -> 5, of which waited for: 4 -> 4; matrix products, arithmetic and copies ran while one was open for 3% -> 2% of each run, Pallas kernels for 10% -> 9%
where the time goes in v25:
time: 25.1 us; the launch traced here: 24.8 us
  Pallas kernels  12.1 us (48%)
  starting transfers between devices  7.13 us (28%)
  waiting for transfers between devices  2.37 us (9%)
  local copies, waits for them, and re-layouts  1.31 us (5%)
  between operations  1.31 us (5%)
  other arithmetic  0.62 us (2%)
    pallas_call x1, Pallas kernels, sweep(): pl.pallas_call(functools.partial(sweep_kernel, sources), out_shape=sweep_...  9.94 us
    ppermute x3, starting transfers between devices, gathered(): blocks.append(lax.ppermute(block, 'sharers', list(enumerate(targets))))  5.67 us
    ppermute x2, waiting for transfers between devices, swapped(): return lax.ppermute(value, axis, pairs)  2.02 us
    ppermute x2, starting transfers between devices, swapped(): return lax.ppermute(value, axis, pairs)  1.46 us
    pallas_call x1, Pallas kernels, next_part(): pl.pallas_call(functools.partial(next_kernel, sources), out_shape=shapes,...  1.45 us
    unnamed x4, local copies, waits for them, and re-layouts  1.31 us
    pallas_call x1, Pallas kernels, own_part(): pl.pallas_call(own_kernel, out_shape=shapes, in_specs=[vector] * 2, out_s...  0.7 us
    add x1, other arithmetic, local(): moved = start + time_step[None] * drift  0.61 us
  transfers between devices with their start and end apart: 5, of which 4 were waited for; matrix products, arithmetic and copies ran while one was open for 2% of the time, Pallas kernels for 9%

profile of v25, /device:TPU:0, one launch (start us, length us, event | category | flops | bytes accessed | tf_op | source)
XLA Modules:
  0.0 24.8 jit_solution(15633941861188175357)
XLA Ops:
  0.6 0.0 copy-start
  0.6 0.7 %copy.8 = f32[1,3,512]{2,1,0:T(4,128)S(1)} copy(f32[1,3,512]{2,0,1:T(1,128)} %param.3) | data formatting | bytes 12288 | tf_op args[0]
  1.3 0.0 copy-done
  1.4 4.1 %collective-permute-start = (f32[1,4,512]{2,1,0:T(4,128)S(1)}, f32[1,4,512]{2,1,0:T(4,128)S(1)}, u32[]{:S(2)}, u32[]{:S(2)}) collective-permute-start(f32[1,4,512]{2,1,0:T(4,128)S(1)} %pad_maximum_fusion.block.refs_1_), channel_id=1, source_target_pairs={{0,2},{1,3},{2,1},{3,0},{4,6},{5,7},{6,5},{7,4},{8,10},{9,11},{10,... | collective-permute-start | bytes 24584 | tf_op jit(solution)/shard_map/ppermute | solution.py:577
  5.4 1.1 %collective-permute-start.1 = (f32[1,4,512]{2,1,0:T(4,128)S(1)}, f32[1,4,512]{2,1,0:T(4,128)S(1)}, u32[]{:S(2)}, u32[]{:S(2)}) collective-permute-start(f32[1,4,512]{2,1,0:T(4,128)S(1)} %pad_maximum_fusion.block.refs_1_), channel_id=1, source_target_pairs={{0,3},{1,2},{2,0},{3,1},{4,7},{5,6},{6,4},{7,5},{8,11},{9,10},{10,... | collective-permute-start | bytes 24584 | tf_op jit(solution)/shard_map/ppermute | solution.py:577
  6.5 0.5 %collective-permute-start.2 = (f32[1,4,512]{2,1,0:T(4,128)S(1)}, f32[1,4,512]{2,1,0:T(4,128)S(1)}, u32[]{:S(2)}, u32[]{:S(2)}) collective-permute-start(f32[1,4,512]{2,1,0:T(4,128)S(1)} %pad_maximum_fusion.block.refs_1_), channel_id=1, source_target_pairs={{0,1},{1,0},{2,3},{3,2},{4,5},{5,4},{6,7},{7,6},{8,9},{9,8},{10,11... | collective-permute-start | bytes 24584 | tf_op jit(solution)/shard_map/ppermute | solution.py:577
  7.7 0.7 %own.1 = (bf16[512,96]{1,0:T(8,128)(2,1)S(1)}, bf16[96,512]{1,0:T(8,128)(2,1)S(1)}, bf16[16,512]{1,0:T(8,128)(2,1)S(1)}, f32[16,512]{1,0:T(8,128)S(1)}, bf16[512...) custom-call(s32[1,1]{1,0:T(1,128)} %bitcast.7.filled, f32[1,4,512]{2,1,0:T(4,128)S(1)} %pad_maximum_fusion.block.refs_1_), custom_call_target="tpu_custom_call" | custom-call | tf_op jit(solution)/shard_map/own/pallas_call | solution.py:295
  8.4 0.0 collective-permute-done.block.refs_2_
  8.4 1.5 %next.1 = (bf16[512,96]{1,0:T(8,128)(2,1)S(1)}, bf16[96,512]{1,0:T(8,128)(2,1)S(1)}, bf16[16,512]{1,0:T(8,128)(2,1)S(1)}, f32[16,1024]{1,0:T(8,128)S(1)}, bf16[5...) custom-call(s32[1,1]{1,0:T(1,128)} %bitcast.8.filled, ...), custom_call_target="tpu_custom_call" | custom-call | tf_op jit(solution)/shard_map/next/pallas_call | solution.py:311
  9.8 0.2 collective-permute-done.1.refs_3_
  10.0 0.2 collective-permute-done.2.refs_4_
  10.2 9.9 %sweep.1 = (f32[8,512]{1,0:T(8,128)S(1)}, f32[3,4,128]{2,1,0:T(4,128)S(1)}, f32[3,4,128]{2,1,0:T(4,128)S(1)}, f32[1,128]{1,0:T(1,128)S(1)}) custom-call(s32[1,1]{1,0:T(1,128)} %bitcast.9.refs_0_, f32[1,4,512]{2,1,0:T(4,128)S(1)} %pad_maximum_fusion.block.refs_1_, f32[1,4,512]{2,1,0:T(4,128)S(1)} %collective-permute-done.block.refs_2_, ...), custom_call_target="tpu_custom_call" | custom-call | tf_op jit(solution)/shard_map/sweep/pallas_call | solution.py:464
  20.1 0.0 collective-permute-start.3
  20.1 1.1 %collective-permute-done.3 = f32[1,128]{1,0:T(1,128)S(1)} collective-permute-done((f32[1,128]{1,0:T(1,128)S(1)}, f32[1,128]{1,0:T(1,128)S(1)}, u32[]{:S(2)}, u32[]{:S(2)}) %collective-permute-start.3) | collective-permute-done | bytes 544 | tf_op jit(solution)/shard_map/ppermute | solution.py:562
  21.3 1.5 %collective-permute-start.4 = (f32[1,128]{1,0:T(1,128)S(1)}, f32[1,128]{1,0:T(1,128)S(1)}, u32[]{:S(2)}, u32[]{:S(2)}) collective-permute-start(f32[1,128]{1,0:T(1,128)S(1)} %max.6), channel_id=1, source_target_pairs={{0,12},{4,8},{8,4},{12,0},{1,13},{5,9},{9,5},{13,1},{2,14},{6,10},... | collective-permute-start | bytes 1544 | tf_op jit(solution)/shard_map/ppermute | solution.py:562
  22.7 0.6 %copy.10 = f32[1,3,512]{2,0,1:T(1,128)} copy(f32[1,3,512]{2,1,0:T(4,128)S(1)} %slice_bitcast_fusion) | data formatting | bytes 12288
  23.3 0.9 %collective-permute-done.4 = f32[1,128]{1,0:T(1,128)S(1)} collective-permute-done((f32[1,128]{1,0:T(1,128)S(1)}, f32[1,128]{1,0:T(1,128)S(1)}, u32[]{:S(2)}, u32[]{:S(2)}) %collective-permute-start.4) | collective-permute-done | bytes 544 | tf_op jit(solution)/shard_map/ppermute | solution.py:562
  24.2 0.6 %multiply_add_fusion = f32[3,4,128]{2,1,0:T(4,128)} fusion(f32[3,4,128]{2,1,0:T(4,128)S(1)} %get-tuple-element.34, f32[3,4,128]{2,1,0:T(4,128)S(1)} %get-tuple-element.36, f32[128]{0:T(128)S(1)} %divide_bitcast_fusion), kind=kLoop, calls=%fused_computation.2 | loop fusion | flops 3072 | bytes 18944 | tf_op jit(solution)/shard_map/add | solution.py:599
  (4 shorter events, 0.0 us)
Async XLA Ops:
  0.6 0.7 %copy-start = (f32[1,512]{1,0:T(1,128)S(1)}, f32[1,512]{1,0:T(1,128)}, u32[]{:S(2)}) copy-start(f32[1,512]{1,0:T(1,128)} %param.4) | copy-start | bytes 6148
  1.4 7.0 %collective-permute-start = (f32[1,4,512]{2,1,0:T(4,128)S(1)}, f32[1,4,512]{2,1,0:T(4,128)S(1)}, u32[]{:S(2)}, u32[]{:S(2)}) collective-permute-start(f32[1,4,512]{2,1,0:T(4,128)S(1)} %pad_maximum_fusion.block.refs_1_), channel_id=1, source_target_pairs={{0,2},{1,3},{2,1},{3,0},{4,6},{5,7},{6,5},{7,4},{8,10},{9,11},{10,... | collective-permute-start | bytes 24584 | tf_op jit(solution)/shard_map/ppermute | solution.py:577
  5.4 4.5 %collective-permute-start.1 = (f32[1,4,512]{2,1,0:T(4,128)S(1)}, f32[1,4,512]{2,1,0:T(4,128)S(1)}, u32[]{:S(2)}, u32[]{:S(2)}) collective-permute-start(f32[1,4,512]{2,1,0:T(4,128)S(1)} %pad_maximum_fusion.block.refs_1_), channel_id=1, source_target_pairs={{0,3},{1,2},{2,0},{3,1},{4,7},{5,6},{6,4},{7,5},{8,11},{9,10},{10,... | collective-permute-start | bytes 24584 | tf_op jit(solution)/shard_map/ppermute | solution.py:577
  6.5 3.7 %collective-permute-start.2 = (f32[1,4,512]{2,1,0:T(4,128)S(1)}, f32[1,4,512]{2,1,0:T(4,128)S(1)}, u32[]{:S(2)}, u32[]{:S(2)}) collective-permute-start(f32[1,4,512]{2,1,0:T(4,128)S(1)} %pad_maximum_fusion.block.refs_1_), channel_id=1, source_target_pairs={{0,1},{1,0},{2,3},{3,2},{4,5},{5,4},{6,7},{7,6},{8,9},{9,8},{10,11... | collective-permute-start | bytes 24584 | tf_op jit(solution)/shard_map/ppermute | solution.py:577
  20.1 1.1 %collective-permute-start.3 = (f32[1,128]{1,0:T(1,128)S(1)}, f32[1,128]{1,0:T(1,128)S(1)}, u32[]{:S(2)}, u32[]{:S(2)}) collective-permute-start(f32[1,128]{1,0:T(1,128)S(1)} %get-tuple-element.35), channel_id=1, source_target_pairs={{0,4},{4,0},{8,12},{12,8},{1,5},{5,1},{9,13},{13,9},{2,6},{6,2},{1... | collective-permute-start | bytes 1544 | tf_op jit(solution)/shard_map/ppermute | solution.py:562
  21.3 3.0 %collective-permute-start.4 = (f32[1,128]{1,0:T(1,128)S(1)}, f32[1,128]{1,0:T(1,128)S(1)}, u32[]{:S(2)}, u32[]{:S(2)}) collective-permute-start(f32[1,128]{1,0:T(1,128)S(1)} %max.6), channel_id=1, source_target_pairs={{0,12},{4,8},{8,4},{12,0},{1,13},{5,9},{9,5},{13,1},{2,14},{6,10},... | collective-permute-start | bytes 1544 | tf_op jit(solution)/shard_map/ppermute | solution.py:562

commit v26 on v23

--- a/solution.py
+++ b/solution.py
@@ -199,7 +199,7 @@
 def stage(tiles, exponent, moments, sums_ref, exponent_refs, split_refs, distance_refs):
     def buffer(index):
         _, keys, _, queries, _ = tiles[index]
-        return exponent_refs[index % 2].at[0:keys, 0:queries]
+        return exponent_refs[index % len(exponent_refs)].at[0:keys, 0:queries]
 
     buffer(0)[...] = exponent(tiles[0])
     for index, tile in enumerate(tiles):
@@ -208,7 +208,8 @@
         split = split_refs[index % 2].at[0 : 2 * tile[1], 0 : tile[3]]
         split_blobs(buffer(index), split)
         add_blobs(tile, split, moments, sums_ref)
-        split_distances(buffer(index), distance_refs[index])
+        if distance_refs is not None:
+            split_distances(buffer(index), distance_refs[index])
 
 
 def looked_up(refs, width, axis):
@@ -381,7 +382,8 @@
     )
     width = blocks[0].shape[2]
     half = 2 * width
-    scratch, distance_refs = refs[:4], refs[4:]
+    split_refs, refs = refs[:2], refs[2:]
+    exponent_refs, distance_refs = refs[: len(refs) // 2], refs[len(refs) // 2 :]
 
     live = [lanes_of(owner_of(source), width) < filled[...] for source in sources]
     late = range(2, count)
@@ -402,8 +404,7 @@
     sums_ref[:, half:] = jnp.zeros_like(sums_ref[:, half:])
     tiles = late_tiles(count, width)
     stage(
-        tiles, exponent, looked_up(moments, width, 1), sums_ref, scratch[:2], scratch[2:],
-        distance_refs,
+        tiles, exponent, looked_up(moments, width, 1), sums_ref, exponent_refs, split_refs, None
     )
     score = scored(weight, place, joined(sums_ref[...]))
     flux_ref[...] = drift_rows(weight, centred, score)
@@ -414,8 +415,13 @@
 
     early = diagonal_tiles(0, width) + square_tiles(width, 0, width)
     early += diagonal_tiles(width, width)
-    for tile, split in zip(early + tiles, own[3:5] + following[4:8] + distance_refs):
-        add_distances(tile, split, fluxes, totals_ref)
+    ready = list(zip(early, own[3:5] + following[4:8]))
+    for tile, exponents, distances in zip(tiles, exponent_refs, distance_refs):
+        split_distances(exponents, distances)
+        add_distances(*ready.pop(0), fluxes, totals_ref)
+        ready.append((tile, distances))
+    for tile, distances in ready:
+        add_distances(tile, distances, fluxes, totals_ref)
     finish(blocks, count * width, weight, centred, score, totals_ref[...], outs)
 
 
@@ -446,7 +452,8 @@
             pltpu.VMEM((16, slots), f32),
             pltpu.VMEM((DRIFT_ROWS // 2, slots), f32),
         ]
-        + stage_scratch(width)
+        + [pltpu.VMEM((width, width), bf16)] * 2
+        + [pltpu.VMEM((tile[1], tile[3]), f32) for tile in late_tiles(count, width)]
         + distances,
         compiler_params=pltpu.CompilerParams(vmem_limit_bytes=24 << 20),
         name="sweep",

time: 22.7 us -> 22.7 us (level)
  no operation moved by 1% of the time
where the time goes in v26:
time: 22.7 us; the launch traced here: 22.5 us
  Pallas kernels  9.76 us (43%)
  starting transfers between devices  7.13 us (31%)
  waiting for transfers between devices  2.37 us (10%)
  local copies, waits for them, and re-layouts  1.31 us (6%)
  between operations  1.31 us (6%)
  other arithmetic  0.62 us (3%)
    pallas_call x1, Pallas kernels, sweep(): pl.pallas_call(functools.partial(sweep_kernel, sources), out_shape=sweep_...  7.61 us
    ppermute x3, starting transfers between devices, gathered(): blocks.append(lax.ppermute(block, 'sharers', list(enumerate(targets))))  5.67 us
    ppermute x2, waiting for transfers between devices, swapped(): return lax.ppermute(value, axis, pairs)  2.02 us
    ppermute x2, starting transfers between devices, swapped(): return lax.ppermute(value, axis, pairs)  1.46 us
    pallas_call x1, Pallas kernels, next_part(): pl.pallas_call(functools.partial(next_kernel, sources), out_shape=shapes,...  1.45 us
    unnamed x4, local copies, waits for them, and re-layouts  1.31 us
    pallas_call x1, Pallas kernels, own_part(): pl.pallas_call(own_kernel, out_shape=shapes, in_specs=[vector] * 2, out_s...  0.7 us
    add x1, other arithmetic, local(): moved = start + time_step[None] * drift  0.61 us
  transfers between devices with their start and end apart: 5, of which 4 were waited for; matrix products, arithmetic and copies ran while one was open for 3% of the time, Pallas kernels for 10%

profile of v26, /device:TPU:0, one launch (start us, length us, event | category | flops | bytes accessed | tf_op | source)
XLA Modules:
  0.0 22.5 jit_solution(6208775624370028450)
XLA Ops:
  0.6 0.0 copy-start
  0.6 0.7 %copy.8 = f32[1,3,512]{2,1,0:T(4,128)S(1)} copy(f32[1,3,512]{2,0,1:T(1,128)} %param.3) | data formatting | bytes 12288 | tf_op args[0]
  1.3 0.0 copy-done
  1.4 4.1 %collective-permute-start = (f32[1,4,512]{2,1,0:T(4,128)S(1)}, f32[1,4,512]{2,1,0:T(4,128)S(1)}, u32[]{:S(2)}, u32[]{:S(2)}) collective-permute-start(f32[1,4,512]{2,1,0:T(4,128)S(1)} %pad_maximum_fusion.block.refs_1_), channel_id=1, source_target_pairs={{0,2},{1,3},{2,1},{3,0},{4,6},{5,7},{6,5},{7,4},{8,10},{9,11},{10,... | collective-permute-start | bytes 24584 | tf_op jit(solution)/shard_map/ppermute | solution.py:555
  5.4 1.1 %collective-permute-start.1 = (f32[1,4,512]{2,1,0:T(4,128)S(1)}, f32[1,4,512]{2,1,0:T(4,128)S(1)}, u32[]{:S(2)}, u32[]{:S(2)}) collective-permute-start(f32[1,4,512]{2,1,0:T(4,128)S(1)} %pad_maximum_fusion.block.refs_1_), channel_id=1, source_target_pairs={{0,3},{1,2},{2,0},{3,1},{4,7},{5,6},{6,4},{7,5},{8,11},{9,10},{10,... | collective-permute-start | bytes 24584 | tf_op jit(solution)/shard_map/ppermute | solution.py:555
  6.5 0.5 %collective-permute-start.2 = (f32[1,4,512]{2,1,0:T(4,128)S(1)}, f32[1,4,512]{2,1,0:T(4,128)S(1)}, u32[]{:S(2)}, u32[]{:S(2)}) collective-permute-start(f32[1,4,512]{2,1,0:T(4,128)S(1)} %pad_maximum_fusion.block.refs_1_), channel_id=1, source_target_pairs={{0,1},{1,0},{2,3},{3,2},{4,5},{5,4},{6,7},{7,6},{8,9},{9,8},{10,11... | collective-permute-start | bytes 24584 | tf_op jit(solution)/shard_map/ppermute | solution.py:555
  7.7 0.7 %own.1 = (bf16[512,96]{1,0:T(8,128)(2,1)S(1)}, bf16[96,512]{1,0:T(8,128)(2,1)S(1)}, bf16[16,512]{1,0:T(8,128)(2,1)S(1)}, f32[16,512]{1,0:T(8,128)S(1)}, bf16[512...) custom-call(s32[1,1]{1,0:T(1,128)} %bitcast.7.filled, f32[1,4,512]{2,1,0:T(4,128)S(1)} %pad_maximum_fusion.block.refs_1_), custom_call_target="tpu_custom_call" | custom-call | tf_op jit(solution)/shard_map/own/pallas_call | solution.py:296
  8.4 0.0 collective-permute-done.block.refs_2_
  8.4 1.5 %next.1 = (bf16[512,96]{1,0:T(8,128)(2,1)S(1)}, bf16[96,512]{1,0:T(8,128)(2,1)S(1)}, bf16[16,512]{1,0:T(8,128)(2,1)S(1)}, f32[16,1024]{1,0:T(8,128)S(1)}, bf16[5...) custom-call(s32[1,1]{1,0:T(1,128)} %bitcast.8.filled, ...), custom_call_target="tpu_custom_call" | custom-call | tf_op jit(solution)/shard_map/next/pallas_call | solution.py:312
  9.8 0.2 collective-permute-done.1.refs_3_
  10.0 0.2 collective-permute-done.2.refs_4_
  10.2 7.6 %sweep.1 = (f32[8,512]{1,0:T(8,128)S(1)}, f32[3,4,128]{2,1,0:T(4,128)S(1)}, f32[3,4,128]{2,1,0:T(4,128)S(1)}, f32[1,128]{1,0:T(1,128)S(1)}) custom-call(s32[1,1]{1,0:T(1,128)} %bitcast.9.refs_0_, f32[1,4,512]{2,1,0:T(4,128)S(1)} %pad_maximum_fusion.block.refs_1_, f32[1,4,512]{2,1,0:T(4,128)S(1)} %collective-permute-done.block.refs_2_, ...), custom_call_target="tpu_custom_call" | custom-call | tf_op jit(solution)/shard_map/sweep/pallas_call | solution.py:442
  17.8 0.0 collective-permute-start.3
  17.8 1.1 %collective-permute-done.3 = f32[1,128]{1,0:T(1,128)S(1)} collective-permute-done((f32[1,128]{1,0:T(1,128)S(1)}, f32[1,128]{1,0:T(1,128)S(1)}, u32[]{:S(2)}, u32[]{:S(2)}) %collective-permute-start.3) | collective-permute-done | bytes 544 | tf_op jit(solution)/shard_map/ppermute | solution.py:540
  18.9 1.5 %collective-permute-start.4 = (f32[1,128]{1,0:T(1,128)S(1)}, f32[1,128]{1,0:T(1,128)S(1)}, u32[]{:S(2)}, u32[]{:S(2)}) collective-permute-start(f32[1,128]{1,0:T(1,128)S(1)} %max.6), channel_id=1, source_target_pairs={{0,12},{4,8},{8,4},{12,0},{1,13},{5,9},{9,5},{13,1},{2,14},{6,10},... | collective-permute-start | bytes 1544 | tf_op jit(solution)/shard_map/ppermute | solution.py:540
  20.4 0.6 %copy.10 = f32[1,3,512]{2,0,1:T(1,128)} copy(f32[1,3,512]{2,1,0:T(4,128)S(1)} %slice_bitcast_fusion) | data formatting | bytes 12288
  21.0 0.9 %collective-permute-done.4 = f32[1,128]{1,0:T(1,128)S(1)} collective-permute-done((f32[1,128]{1,0:T(1,128)S(1)}, f32[1,128]{1,0:T(1,128)S(1)}, u32[]{:S(2)}, u32[]{:S(2)}) %collective-permute-start.4) | collective-permute-done | bytes 544 | tf_op jit(solution)/shard_map/ppermute | solution.py:540
  21.9 0.6 %multiply_add_fusion = f32[3,4,128]{2,1,0:T(4,128)} fusion(f32[3,4,128]{2,1,0:T(4,128)S(1)} %get-tuple-element.34, f32[3,4,128]{2,1,0:T(4,128)S(1)} %get-tuple-element.36, f32[128]{0:T(128)S(1)} %divide_bitcast_fusion), kind=kLoop, calls=%fused_computation.2 | loop fusion | flops 3072 | bytes 18944 | tf_op jit(solution)/shard_map/add | solution.py:577
  (4 shorter events, 0.0 us)
Async XLA Ops:
  0.6 0.7 %copy-start = (f32[1,512]{1,0:T(1,128)S(1)}, f32[1,512]{1,0:T(1,128)}, u32[]{:S(2)}) copy-start(f32[1,512]{1,0:T(1,128)} %param.4) | copy-start | bytes 6148
  1.4 7.0 %collective-permute-start = (f32[1,4,512]{2,1,0:T(4,128)S(1)}, f32[1,4,512]{2,1,0:T(4,128)S(1)}, u32[]{:S(2)}, u32[]{:S(2)}) collective-permute-start(f32[1,4,512]{2,1,0:T(4,128)S(1)} %pad_maximum_fusion.block.refs_1_), channel_id=1, source_target_pairs={{0,2},{1,3},{2,1},{3,0},{4,6},{5,7},{6,5},{7,4},{8,10},{9,11},{10,... | collective-permute-start | bytes 24584 | tf_op jit(solution)/shard_map/ppermute | solution.py:555
  5.4 4.5 %collective-permute-start.1 = (f32[1,4,512]{2,1,0:T(4,128)S(1)}, f32[1,4,512]{2,1,0:T(4,128)S(1)}, u32[]{:S(2)}, u32[]{:S(2)}) collective-permute-start(f32[1,4,512]{2,1,0:T(4,128)S(1)} %pad_maximum_fusion.block.refs_1_), channel_id=1, source_target_pairs={{0,3},{1,2},{2,0},{3,1},{4,7},{5,6},{6,4},{7,5},{8,11},{9,10},{10,... | collective-permute-start | bytes 24584 | tf_op jit(solution)/shard_map/ppermute | solution.py:555
  6.5 3.7 %collective-permute-start.2 = (f32[1,4,512]{2,1,0:T(4,128)S(1)}, f32[1,4,512]{2,1,0:T(4,128)S(1)}, u32[]{:S(2)}, u32[]{:S(2)}) collective-permute-start(f32[1,4,512]{2,1,0:T(4,128)S(1)} %pad_maximum_fusion.block.refs_1_), channel_id=1, source_target_pairs={{0,1},{1,0},{2,3},{3,2},{4,5},{5,4},{6,7},{7,6},{8,9},{9,8},{10,11... | collective-permute-start | bytes 24584 | tf_op jit(solution)/shard_map/ppermute | solution.py:555
  17.8 1.1 %collective-permute-start.3 = (f32[1,128]{1,0:T(1,128)S(1)}, f32[1,128]{1,0:T(1,128)S(1)}, u32[]{:S(2)}, u32[]{:S(2)}) collective-permute-start(f32[1,128]{1,0:T(1,128)S(1)} %get-tuple-element.35), channel_id=1, source_target_pairs={{0,4},{4,0},{8,12},{12,8},{1,5},{5,1},{9,13},{13,9},{2,6},{6,2},{1... | collective-permute-start | bytes 1544 | tf_op jit(solution)/shard_map/ppermute | solution.py:540
  18.9 3.0 %collective-permute-start.4 = (f32[1,128]{1,0:T(1,128)S(1)}, f32[1,128]{1,0:T(1,128)S(1)}, u32[]{:S(2)}, u32[]{:S(2)}) collective-permute-start(f32[1,128]{1,0:T(1,128)S(1)} %max.6), channel_id=1, source_target_pairs={{0,12},{4,8},{8,4},{12,0},{1,13},{5,9},{9,5},{13,1},{2,14},{6,10},... | collective-permute-start | bytes 1544 | tf_op jit(solution)/shard_map/ppermute | solution.py:540

commit v27 on v26

--- a/solution.py
+++ b/solution.py
@@ -326,12 +326,15 @@
 
 
 def late_tiles(count, width):
-    tiles = []
-    for query in range(count):
-        first = max(query + 1, 2)
-        tiles += diagonal_tiles(query * width, width) if query >= 2 else []
-        for key in range(first, count):
+    tiles, late = [], range(2, count)
+    for query in late:
+        for key in range(2):
             tiles += square_tiles(key * width, query * width, width)
+    for query in late:
+        for key in range(2, query):
+            tiles += square_tiles(key * width, query * width, width)
+    for query in late:
+        tiles += diagonal_tiles(query * width, width)
     return tiles
 
 

time: 22.7 us -> 22.4 us (0.987)
  Pallas kernels: 9.76 us -> 9.42 us
    pallas_call x1, Pallas kernels: 7.61 us -> 7.27 us  [sweep(): pl.pallas_call(functools.partial(sweep_kernel, sources), out_shape=sweep_...]
where the time goes in v27:
time: 22.4 us; the launch traced here: 22.2 us
  Pallas kernels  9.42 us (42%)
  starting transfers between devices  7.13 us (32%)
  waiting for transfers between devices  2.37 us (11%)
  local copies, waits for them, and re-layouts  1.31 us (6%)
  between operations  1.31 us (6%)
  other arithmetic  0.62 us (3%)
    pallas_call x1, Pallas kernels, sweep(): pl.pallas_call(functools.partial(sweep_kernel, sources), out_shape=sweep_...  7.27 us
    ppermute x3, starting transfers between devices, gathered(): blocks.append(lax.ppermute(block, 'sharers', list(enumerate(targets))))  5.67 us
    ppermute x2, waiting for transfers between devices, swapped(): return lax.ppermute(value, axis, pairs)  2.02 us
    ppermute x2, starting transfers between devices, swapped(): return lax.ppermute(value, axis, pairs)  1.46 us
    pallas_call x1, Pallas kernels, next_part(): pl.pallas_call(functools.partial(next_kernel, sources), out_shape=shapes,...  1.45 us
    unnamed x4, local copies, waits for them, and re-layouts  1.31 us
    pallas_call x1, Pallas kernels, own_part(): pl.pallas_call(own_kernel, out_shape=shapes, in_specs=[vector] * 2, out_s...  0.7 us
    add x1, other arithmetic, local(): moved = start + time_step[None] * drift  0.61 us
  transfers between devices with their start and end apart: 5, of which 4 were waited for; matrix products, arithmetic and copies ran while one was open for 3% of the time, Pallas kernels for 10%

profile of v27, /device:TPU:0, one launch (start us, length us, event | category | flops | bytes accessed | tf_op | source)
XLA Modules:
  0.0 22.2 jit_solution(12781288462205162946)
XLA Ops:
  0.6 0.0 copy-start
  0.6 0.7 %copy.8 = f32[1,3,512]{2,1,0:T(4,128)S(1)} copy(f32[1,3,512]{2,0,1:T(1,128)} %param.3) | data formatting | bytes 12288 | tf_op args[0]
  1.3 0.0 copy-done
  1.4 4.1 %collective-permute-start = (f32[1,4,512]{2,1,0:T(4,128)S(1)}, f32[1,4,512]{2,1,0:T(4,128)S(1)}, u32[]{:S(2)}, u32[]{:S(2)}) collective-permute-start(f32[1,4,512]{2,1,0:T(4,128)S(1)} %pad_maximum_fusion.block.refs_1_), channel_id=1, source_target_pairs={{0,2},{1,3},{2,1},{3,0},{4,6},{5,7},{6,5},{7,4},{8,10},{9,11},{10,... | collective-permute-start | bytes 24584 | tf_op jit(solution)/shard_map/ppermute | solution.py:558
  5.4 1.1 %collective-permute-start.1 = (f32[1,4,512]{2,1,0:T(4,128)S(1)}, f32[1,4,512]{2,1,0:T(4,128)S(1)}, u32[]{:S(2)}, u32[]{:S(2)}) collective-permute-start(f32[1,4,512]{2,1,0:T(4,128)S(1)} %pad_maximum_fusion.block.refs_1_), channel_id=1, source_target_pairs={{0,3},{1,2},{2,0},{3,1},{4,7},{5,6},{6,4},{7,5},{8,11},{9,10},{10,... | collective-permute-start | bytes 24584 | tf_op jit(solution)/shard_map/ppermute | solution.py:558
  6.5 0.5 %collective-permute-start.2 = (f32[1,4,512]{2,1,0:T(4,128)S(1)}, f32[1,4,512]{2,1,0:T(4,128)S(1)}, u32[]{:S(2)}, u32[]{:S(2)}) collective-permute-start(f32[1,4,512]{2,1,0:T(4,128)S(1)} %pad_maximum_fusion.block.refs_1_), channel_id=1, source_target_pairs={{0,1},{1,0},{2,3},{3,2},{4,5},{5,4},{6,7},{7,6},{8,9},{9,8},{10,11... | collective-permute-start | bytes 24584 | tf_op jit(solution)/shard_map/ppermute | solution.py:558
  7.7 0.7 %own.1 = (bf16[512,96]{1,0:T(8,128)(2,1)S(1)}, bf16[96,512]{1,0:T(8,128)(2,1)S(1)}, bf16[16,512]{1,0:T(8,128)(2,1)S(1)}, f32[16,512]{1,0:T(8,128)S(1)}, bf16[512...) custom-call(s32[1,1]{1,0:T(1,128)} %bitcast.7.filled, f32[1,4,512]{2,1,0:T(4,128)S(1)} %pad_maximum_fusion.block.refs_1_), custom_call_target="tpu_custom_call" | custom-call | tf_op jit(solution)/shard_map/own/pallas_call | solution.py:296
  8.4 0.0 collective-permute-done.block.refs_2_
  8.4 1.5 %next.1 = (bf16[512,96]{1,0:T(8,128)(2,1)S(1)}, bf16[96,512]{1,0:T(8,128)(2,1)S(1)}, bf16[16,512]{1,0:T(8,128)(2,1)S(1)}, f32[16,1024]{1,0:T(8,128)S(1)}, bf16[5...) custom-call(s32[1,1]{1,0:T(1,128)} %bitcast.8.filled, ...), custom_call_target="tpu_custom_call" | custom-call | tf_op jit(solution)/shard_map/next/pallas_call | solution.py:312
  9.8 0.2 collective-permute-done.1.refs_3_
  10.0 0.2 collective-permute-done.2.refs_4_
  10.2 7.3 %sweep.1 = (f32[8,512]{1,0:T(8,128)S(1)}, f32[3,4,128]{2,1,0:T(4,128)S(1)}, f32[3,4,128]{2,1,0:T(4,128)S(1)}, f32[1,128]{1,0:T(1,128)S(1)}) custom-call(s32[1,1]{1,0:T(1,128)} %bitcast.9.refs_0_, f32[1,4,512]{2,1,0:T(4,128)S(1)} %pad_maximum_fusion.block.refs_1_, f32[1,4,512]{2,1,0:T(4,128)S(1)} %collective-permute-done.block.refs_2_, ...), custom_call_target="tpu_custom_call" | custom-call | tf_op jit(solution)/shard_map/sweep/pallas_call | solution.py:445
  17.4 0.0 collective-permute-start.3
  17.5 1.1 %collective-permute-done.3 = f32[1,128]{1,0:T(1,128)S(1)} collective-permute-done((f32[1,128]{1,0:T(1,128)S(1)}, f32[1,128]{1,0:T(1,128)S(1)}, u32[]{:S(2)}, u32[]{:S(2)}) %collective-permute-start.3) | collective-permute-done | bytes 544 | tf_op jit(solution)/shard_map/ppermute | solution.py:543
  18.6 1.5 %collective-permute-start.4 = (f32[1,128]{1,0:T(1,128)S(1)}, f32[1,128]{1,0:T(1,128)S(1)}, u32[]{:S(2)}, u32[]{:S(2)}) collective-permute-start(f32[1,128]{1,0:T(1,128)S(1)} %max.6), channel_id=1, source_target_pairs={{0,12},{4,8},{8,4},{12,0},{1,13},{5,9},{9,5},{13,1},{2,14},{6,10},... | collective-permute-start | bytes 1544 | tf_op jit(solution)/shard_map/ppermute | solution.py:543
  20.0 0.6 %copy.10 = f32[1,3,512]{2,0,1:T(1,128)} copy(f32[1,3,512]{2,1,0:T(4,128)S(1)} %slice_bitcast_fusion) | data formatting | bytes 12288
  20.6 0.9 %collective-permute-done.4 = f32[1,128]{1,0:T(1,128)S(1)} collective-permute-done((f32[1,128]{1,0:T(1,128)S(1)}, f32[1,128]{1,0:T(1,128)S(1)}, u32[]{:S(2)}, u32[]{:S(2)}) %collective-permute-start.4) | collective-permute-done | bytes 544 | tf_op jit(solution)/shard_map/ppermute | solution.py:543
  21.6 0.6 %multiply_add_fusion = f32[3,4,128]{2,1,0:T(4,128)} fusion(f32[3,4,128]{2,1,0:T(4,128)S(1)} %get-tuple-element.34, f32[3,4,128]{2,1,0:T(4,128)S(1)} %get-tuple-element.36, f32[128]{0:T(128)S(1)} %divide_bitcast_fusion), kind=kLoop, calls=%fused_computation.2 | loop fusion | flops 3072 | bytes 18944 | tf_op jit(solution)/shard_map/add | solution.py:580
  (4 shorter events, 0.0 us)
Async XLA Ops:
  0.6 0.7 %copy-start = (f32[1,512]{1,0:T(1,128)S(1)}, f32[1,512]{1,0:T(1,128)}, u32[]{:S(2)}) copy-start(f32[1,512]{1,0:T(1,128)} %param.4) | copy-start | bytes 6148
  1.4 7.0 %collective-permute-start = (f32[1,4,512]{2,1,0:T(4,128)S(1)}, f32[1,4,512]{2,1,0:T(4,128)S(1)}, u32[]{:S(2)}, u32[]{:S(2)}) collective-permute-start(f32[1,4,512]{2,1,0:T(4,128)S(1)} %pad_maximum_fusion.block.refs_1_), channel_id=1, source_target_pairs={{0,2},{1,3},{2,1},{3,0},{4,6},{5,7},{6,5},{7,4},{8,10},{9,11},{10,... | collective-permute-start | bytes 24584 | tf_op jit(solution)/shard_map/ppermute | solution.py:558
  5.4 4.5 %collective-permute-start.1 = (f32[1,4,512]{2,1,0:T(4,128)S(1)}, f32[1,4,512]{2,1,0:T(4,128)S(1)}, u32[]{:S(2)}, u32[]{:S(2)}) collective-permute-start(f32[1,4,512]{2,1,0:T(4,128)S(1)} %pad_maximum_fusion.block.refs_1_), channel_id=1, source_target_pairs={{0,3},{1,2},{2,0},{3,1},{4,7},{5,6},{6,4},{7,5},{8,11},{9,10},{10,... | collective-permute-start | bytes 24584 | tf_op jit(solution)/shard_map/ppermute | solution.py:558
  6.5 3.7 %collective-permute-start.2 = (f32[1,4,512]{2,1,0:T(4,128)S(1)}, f32[1,4,512]{2,1,0:T(4,128)S(1)}, u32[]{:S(2)}, u32[]{:S(2)}) collective-permute-start(f32[1,4,512]{2,1,0:T(4,128)S(1)} %pad_maximum_fusion.block.refs_1_), channel_id=1, source_target_pairs={{0,1},{1,0},{2,3},{3,2},{4,5},{5,4},{6,7},{7,6},{8,9},{9,8},{10,11... | collective-permute-start | bytes 24584 | tf_op jit(solution)/shard_map/ppermute | solution.py:558
  17.4 1.1 %collective-permute-start.3 = (f32[1,128]{1,0:T(1,128)S(1)}, f32[1,128]{1,0:T(1,128)S(1)}, u32[]{:S(2)}, u32[]{:S(2)}) collective-permute-start(f32[1,128]{1,0:T(1,128)S(1)} %get-tuple-element.35), channel_id=1, source_target_pairs={{0,4},{4,0},{8,12},{12,8},{1,5},{5,1},{9,13},{13,9},{2,6},{6,2},{1... | collective-permute-start | bytes 1544 | tf_op jit(solution)/shard_map/ppermute | solution.py:543
  18.6 3.0 %collective-permute-start.4 = (f32[1,128]{1,0:T(1,128)S(1)}, f32[1,128]{1,0:T(1,128)S(1)}, u32[]{:S(2)}, u32[]{:S(2)}) collective-permute-start(f32[1,128]{1,0:T(1,128)S(1)} %max.6), channel_id=1, source_target_pairs={{0,12},{4,8},{8,4},{12,0},{1,13},{5,9},{9,5},{13,1},{2,14},{6,10},... | collective-permute-start | bytes 1544 | tf_op jit(solution)/shard_map/ppermute | solution.py:543

commit v28 on v27

--- a/solution.py
+++ b/solution.py
@@ -189,14 +189,20 @@
 
 def add_distances(tile, split, fluxes, totals_ref):
     key, keys, query, queries, turned = tile
-    upper, lower = sum_rows_less(fluxes(key, keys), split)
-    totals_ref[:, pl.ds(query, queries)] += upper + lower
-    if turned:
+
+    def rows():
+        upper, lower = sum_rows_less(fluxes(key, keys), split)
+        totals_ref[:, pl.ds(query, queries)] += upper + lower
+
+    def columns():
         upper, lower = sum_columns_less(fluxes(query, turned), split.at[:, 0:turned])
         totals_ref[:, pl.ds(key, keys)] += upper + lower
 
-
-def stage(tiles, exponent, moments, sums_ref, exponent_refs, split_refs, distance_refs):
+    return rows, columns if turned else lambda: None
+
+
+def stage(tiles, exponent, moments, sums_ref, exponent_refs, split_refs, distance_refs,
+          after=lambda index: None):
     def buffer(index):
         _, keys, _, queries, _ = tiles[index]
         return exponent_refs[index % len(exponent_refs)].at[0:keys, 0:queries]
@@ -210,6 +216,7 @@
         add_blobs(tile, split, moments, sums_ref)
         if distance_refs is not None:
             split_distances(buffer(index), distance_refs[index])
+        after(index)
 
 
 def looked_up(refs, width, axis):
@@ -358,21 +365,23 @@
     return weight, place, jnp.where(vector, place - middle, 0.0)
 
 
-def finish(blocks, total_slots, weight, centred, score, totals, outs):
+def drift_of(total, centred, score, weight, total_slots):
+    drift = drift_sum(total, centred, score)
+    live = (row_of(drift) < 3) & (weight > 0.0)
+    return jnp.where(live, drift * (1.0 / (SCALE * SCALE * SCALE * total_slots)), 0.0)
+
+
+def finish(blocks, score, drifts, outs):
     scores_out, drift_out, start_out, speed_out = outs
     width = blocks[0].shape[2]
-    spread = totals.shape[1]
-    drift = drift_sum(totals, centred[:, 0:spread], score[:, 0:spread])
-    factor = 1.0 / (SCALE * SCALE * SCALE * total_slots)
-    live = (row_of(drift) < 3) & (weight[:, 0:spread] > 0.0)
-    drift = jnp.where(live, drift * factor, 0.0)
-    largest = jnp.max(rows_sum(drift * drift), axis=1, keepdims=True)
+    square = functools.reduce(jnp.maximum, [rows_sum(drift * drift) for drift in drifts])
+    largest = jnp.max(square, axis=1, keepdims=True)
     speed_out[...] = jnp.broadcast_to(jnp.sqrt(largest), speed_out.shape)
-    scores_out[...] = score[:, 0:width]
+    scores_out[...] = score
     for part in range(width // 128):
         lanes = slice(part * 128, part * 128 + 128)
         for axis in range(3):
-            drift_out[axis, part : part + 1, :] = drift[axis : axis + 1, lanes]
+            drift_out[axis, part : part + 1, :] = drifts[0][axis : axis + 1, lanes]
             start_out[axis, part : part + 1, :] = blocks[0][0, axis : axis + 1, lanes]
 
 
@@ -380,9 +389,10 @@
     count = len(sources)
     filled, blocks, refs = refs[0], refs[1 : count + 1], list(refs[count + 1 :])
     own, following, refs = refs[:5], refs[5:13], refs[13:]
-    outs, (key_ref, query_ref, moment_ref, flux_ref, sums_ref, totals_ref), refs = (
-        refs[:4], refs[4:10], refs[10:]
+    outs, (key_ref, query_ref, moment_ref, sums_ref, totals_ref), refs = (
+        refs[:4], refs[4:9], refs[9:]
     )
+    flux_refs, refs = refs[:count], refs[count:]
     width = blocks[0].shape[2]
     half = 2 * width
     split_refs, refs = refs[:2], refs[2:]
@@ -406,26 +416,61 @@
     sums_ref[:, 0:half] = following[3][...]
     sums_ref[:, half:] = jnp.zeros_like(sums_ref[:, half:])
     tiles = late_tiles(count, width)
+    totals_ref[...] = jnp.zeros_like(totals_ref)
+    lanes = [slice(index * width, index * width + width) for index in range(count)]
+    scores = [None] * count
+    fluxes = looked_up(flux_refs, width, 1)
+
+    def score_blocks(*indices):
+        for index in indices:
+            at = lanes[index]
+            scores[index] = scored(weight[:, at], place[:, at], joined(sums_ref[:, at]))
+            flux_refs[index][...] = drift_rows(weight[:, at], centred[:, at], scores[index])
+
+    mixed = sum(tile[0] < half for tile in tiles)
+
+    def after(index):
+        if index == mixed - 1:
+            score_blocks(0, 1)
+
     stage(
-        tiles, exponent, looked_up(moments, width, 1), sums_ref, exponent_refs, split_refs, None
+        tiles, exponent, looked_up(moments, width, 1), sums_ref, exponent_refs, split_refs, None,
+        after,
     )
-    score = scored(weight, place, joined(sums_ref[...]))
-    flux_ref[...] = drift_rows(weight, centred, score)
-    totals_ref[...] = jnp.zeros_like(totals_ref)
-
-    def fluxes(start, size):
-        return flux_ref[:, pl.ds(start, size)]
-
     early = diagonal_tiles(0, width) + square_tiles(width, 0, width)
     early += diagonal_tiles(width, width)
-    ready = list(zip(early, own[3:5] + following[4:8]))
-    for tile, exponents, distances in zip(tiles, exponent_refs, distance_refs):
-        split_distances(exponents, distances)
-        add_distances(*ready.pop(0), fluxes, totals_ref)
-        ready.append((tile, distances))
-    for tile, distances in ready:
-        add_distances(tile, distances, fluxes, totals_ref)
-    finish(blocks, count * width, weight, centred, score, totals_ref[...], outs)
+    for tile, distances in zip(early, own[3:5] + following[4:8]):
+        for job in add_distances(tile, distances, fluxes, totals_ref):
+            job()
+    score_blocks(*range(2, count))
+
+    total_slots = count * width
+    drifts = [None] * count
+
+    def drift_block(index):
+        at = lanes[index]
+        drifts[index] = drift_of(
+            totals_ref[:, at], centred[:, at], scores[index], weight[:, at], total_slots
+        )
+
+    turns = []
+    for index in range(mixed):
+        split_distances(exponent_refs[index], distance_refs[index])
+        rows, columns = add_distances(tiles[index], distance_refs[index], fluxes, totals_ref)
+        rows()
+        turns.append((tiles[index][0], columns))
+    for index in range(2):
+        for key, columns in turns:
+            if key // width == index:
+                columns()
+        drift_block(index)
+    for index in range(mixed, len(tiles)):
+        split_distances(exponent_refs[index], distance_refs[index])
+        for job in add_distances(tiles[index], distance_refs[index], fluxes, totals_ref):
+            job()
+    for index in range(2, count):
+        drift_block(index)
+    finish(blocks, scores[0], drifts, outs)
 
 
 def sweep_shapes(width, copies):
@@ -451,10 +496,10 @@
             pltpu.VMEM((late, DISTANCE_ROWS), bf16),
             pltpu.VMEM((DISTANCE_ROWS, late), bf16),
             pltpu.VMEM((16, late), bf16),
-            pltpu.VMEM((DRIFT_ROWS, slots), bf16),
             pltpu.VMEM((16, slots), f32),
             pltpu.VMEM((DRIFT_ROWS // 2, slots), f32),
         ]
+        + [pltpu.VMEM((DRIFT_ROWS, width), bf16)] * count
         + [pltpu.VMEM((width, width), bf16)] * 2
         + [pltpu.VMEM((tile[1], tile[3]), f32) for tile in late_tiles(count, width)]
         + distances,
@@ -509,9 +554,16 @@
         tile = block_tile(key, 0, False)
         fill(tile)
         split_distances(exponent_ref, split_ref)
-        add_distances(tile, split_ref, lambda at, size: flux_ref[:, pl.ds(at, size)], totals_ref)
-
-    finish(blocks, count * width, weight, centred, score, totals_ref[...], outs)
+        for job in add_distances(
+            tile, split_ref, lambda at, size: flux_ref[:, pl.ds(at, size)], totals_ref
+        ):
+            job()
+
+    own = slice(0, width)
+    drift = drift_of(
+        totals_ref[...], centred[:, own], score[:, own], weight[:, own], count * width
+    )
+    finish(blocks, score[:, own], [drift], outs)
 
 
 def long_sweep(filled, blocks, sources, copies):

time: 22.4 us -> 22.5 us (level)
  no operation moved by 1% of the time
where the time goes in v28:
time: 22.5 us; the launch traced here: 22.3 us
  Pallas kernels  9.52 us (42%)
  starting transfers between devices  7.12 us (32%)
  waiting for transfers between devices  2.38 us (11%)
  local copies, waits for them, and re-layouts  1.31 us (6%)
  between operations  1.31 us (6%)
  other arithmetic  0.62 us (3%)
    pallas_call x1, Pallas kernels, sweep(): pl.pallas_call(functools.partial(sweep_kernel, sources), out_shape=sweep_...  7.38 us
    ppermute x3, starting transfers between devices, gathered(): blocks.append(lax.ppermute(block, 'sharers', list(enumerate(targets))))  5.67 us
    ppermute x2, waiting for transfers between devices, swapped(): return lax.ppermute(value, axis, pairs)  2.03 us
    pallas_call x1, Pallas kernels, next_part(): pl.pallas_call(functools.partial(next_kernel, sources), out_shape=shapes,...  1.45 us
    ppermute x2, starting transfers between devices, swapped(): return lax.ppermute(value, axis, pairs)  1.45 us
    unnamed x4, local copies, waits for them, and re-layouts  1.31 us
    pallas_call x1, Pallas kernels, own_part(): pl.pallas_call(own_kernel, out_shape=shapes, in_specs=[vector] * 2, out_s...  0.7 us
    add x1, other arithmetic, local(): moved = start + time_step[None] * drift  0.61 us
  transfers between devices with their start and end apart: 5, of which 4 were waited for; matrix products, arithmetic and copies ran while one was open for 3% of the time, Pallas kernels for 10%

profile of v28, /device:TPU:0, one launch (start us, length us, event | category | flops | bytes accessed | tf_op | source)
XLA Modules:
  0.0 22.3 jit_solution(9292637332072719134)
XLA Ops:
  0.6 0.0 copy-start
  0.6 0.7 %copy.8 = f32[1,3,512]{2,1,0:T(4,128)S(1)} copy(f32[1,3,512]{2,0,1:T(1,128)} %param.3) | data formatting | bytes 12288 | tf_op args[0]
  1.3 0.0 copy-done
  1.4 4.1 %collective-permute-start = (f32[1,4,512]{2,1,0:T(4,128)S(1)}, f32[1,4,512]{2,1,0:T(4,128)S(1)}, u32[]{:S(2)}, u32[]{:S(2)}) collective-permute-start(f32[1,4,512]{2,1,0:T(4,128)S(1)} %pad_maximum_fusion.block.refs_1_), channel_id=1, source_target_pairs={{0,2},{1,3},{2,1},{3,0},{4,6},{5,7},{6,5},{7,4},{8,10},{9,11},{10,... | collective-permute-start | bytes 24584 | tf_op jit(solution)/shard_map/ppermute | solution.py:610
  5.4 1.1 %collective-permute-start.1 = (f32[1,4,512]{2,1,0:T(4,128)S(1)}, f32[1,4,512]{2,1,0:T(4,128)S(1)}, u32[]{:S(2)}, u32[]{:S(2)}) collective-permute-start(f32[1,4,512]{2,1,0:T(4,128)S(1)} %pad_maximum_fusion.block.refs_1_), channel_id=1, source_target_pairs={{0,3},{1,2},{2,0},{3,1},{4,7},{5,6},{6,4},{7,5},{8,11},{9,10},{10,... | collective-permute-start | bytes 24584 | tf_op jit(solution)/shard_map/ppermute | solution.py:610
  6.5 0.5 %collective-permute-start.2 = (f32[1,4,512]{2,1,0:T(4,128)S(1)}, f32[1,4,512]{2,1,0:T(4,128)S(1)}, u32[]{:S(2)}, u32[]{:S(2)}) collective-permute-start(f32[1,4,512]{2,1,0:T(4,128)S(1)} %pad_maximum_fusion.block.refs_1_), channel_id=1, source_target_pairs={{0,1},{1,0},{2,3},{3,2},{4,5},{5,4},{6,7},{7,6},{8,9},{9,8},{10,11... | collective-permute-start | bytes 24584 | tf_op jit(solution)/shard_map/ppermute | solution.py:610
  7.7 0.7 %own.1 = (bf16[512,96]{1,0:T(8,128)(2,1)S(1)}, bf16[96,512]{1,0:T(8,128)(2,1)S(1)}, bf16[16,512]{1,0:T(8,128)(2,1)S(1)}, f32[16,512]{1,0:T(8,128)S(1)}, bf16[512...) custom-call(s32[1,1]{1,0:T(1,128)} %bitcast.7.filled, f32[1,4,512]{2,1,0:T(4,128)S(1)} %pad_maximum_fusion.block.refs_1_), custom_call_target="tpu_custom_call" | custom-call | tf_op jit(solution)/shard_map/own/pallas_call | solution.py:303
  8.4 0.0 collective-permute-done.block.refs_2_
  8.4 1.5 %next.1 = (bf16[512,96]{1,0:T(8,128)(2,1)S(1)}, bf16[96,512]{1,0:T(8,128)(2,1)S(1)}, bf16[16,512]{1,0:T(8,128)(2,1)S(1)}, f32[16,1024]{1,0:T(8,128)S(1)}, bf16[5...) custom-call(s32[1,1]{1,0:T(1,128)} %bitcast.8.filled, ...), custom_call_target="tpu_custom_call" | custom-call | tf_op jit(solution)/shard_map/next/pallas_call | solution.py:319
  9.8 0.2 collective-permute-done.1.refs_3_
  10.0 0.2 collective-permute-done.2.refs_4_
  10.2 7.4 %sweep.1 = (f32[8,512]{1,0:T(8,128)S(1)}, f32[3,4,128]{2,1,0:T(4,128)S(1)}, f32[3,4,128]{2,1,0:T(4,128)S(1)}, f32[1,128]{1,0:T(1,128)S(1)}) custom-call(s32[1,1]{1,0:T(1,128)} %bitcast.9.refs_0_, f32[1,4,512]{2,1,0:T(4,128)S(1)} %pad_maximum_fusion.block.refs_1_, f32[1,4,512]{2,1,0:T(4,128)S(1)} %collective-permute-done.block.refs_2_, ...), custom_call_target="tpu_custom_call" | custom-call | tf_op jit(solution)/shard_map/sweep/pallas_call | solution.py:490
  17.5 0.0 collective-permute-start.3
  17.6 1.1 %collective-permute-done.3 = f32[1,128]{1,0:T(1,128)S(1)} collective-permute-done((f32[1,128]{1,0:T(1,128)S(1)}, f32[1,128]{1,0:T(1,128)S(1)}, u32[]{:S(2)}, u32[]{:S(2)}) %collective-permute-start.3) | collective-permute-done | bytes 544 | tf_op jit(solution)/shard_map/ppermute | solution.py:595
  18.7 1.4 %collective-permute-start.4 = (f32[1,128]{1,0:T(1,128)S(1)}, f32[1,128]{1,0:T(1,128)S(1)}, u32[]{:S(2)}, u32[]{:S(2)}) collective-permute-start(f32[1,128]{1,0:T(1,128)S(1)} %max.6), channel_id=1, source_target_pairs={{0,12},{4,8},{8,4},{12,0},{1,13},{5,9},{9,5},{13,1},{2,14},{6,10},... | collective-permute-start | bytes 1544 | tf_op jit(solution)/shard_map/ppermute | solution.py:595
  20.1 0.6 %copy.10 = f32[1,3,512]{2,0,1:T(1,128)} copy(f32[1,3,512]{2,1,0:T(4,128)S(1)} %slice_bitcast_fusion) | data formatting | bytes 12288
  20.7 0.9 %collective-permute-done.4 = f32[1,128]{1,0:T(1,128)S(1)} collective-permute-done((f32[1,128]{1,0:T(1,128)S(1)}, f32[1,128]{1,0:T(1,128)S(1)}, u32[]{:S(2)}, u32[]{:S(2)}) %collective-permute-start.4) | collective-permute-done | bytes 544 | tf_op jit(solution)/shard_map/ppermute | solution.py:595
  21.7 0.6 %multiply_add_fusion = f32[3,4,128]{2,1,0:T(4,128)} fusion(f32[3,4,128]{2,1,0:T(4,128)S(1)} %get-tuple-element.34, f32[3,4,128]{2,1,0:T(4,128)S(1)} %get-tuple-element.36, f32[128]{0:T(128)S(1)} %divide_bitcast_fusion), kind=kLoop, calls=%fused_computation.2 | loop fusion | flops 3072 | bytes 18944 | tf_op jit(solution)/shard_map/add | solution.py:632
  (4 shorter events, 0.0 us)
Async XLA Ops:
  0.6 0.7 %copy-start = (f32[1,512]{1,0:T(1,128)S(1)}, f32[1,512]{1,0:T(1,128)}, u32[]{:S(2)}) copy-start(f32[1,512]{1,0:T(1,128)} %param.4) | copy-start | bytes 6148
  1.4 7.0 %collective-permute-start = (f32[1,4,512]{2,1,0:T(4,128)S(1)}, f32[1,4,512]{2,1,0:T(4,128)S(1)}, u32[]{:S(2)}, u32[]{:S(2)}) collective-permute-start(f32[1,4,512]{2,1,0:T(4,128)S(1)} %pad_maximum_fusion.block.refs_1_), channel_id=1, source_target_pairs={{0,2},{1,3},{2,1},{3,0},{4,6},{5,7},{6,5},{7,4},{8,10},{9,11},{10,... | collective-permute-start | bytes 24584 | tf_op jit(solution)/shard_map/ppermute | solution.py:610
  5.4 4.5 %collective-permute-start.1 = (f32[1,4,512]{2,1,0:T(4,128)S(1)}, f32[1,4,512]{2,1,0:T(4,128)S(1)}, u32[]{:S(2)}, u32[]{:S(2)}) collective-permute-start(f32[1,4,512]{2,1,0:T(4,128)S(1)} %pad_maximum_fusion.block.refs_1_), channel_id=1, source_target_pairs={{0,3},{1,2},{2,0},{3,1},{4,7},{5,6},{6,4},{7,5},{8,11},{9,10},{10,... | collective-permute-start | bytes 24584 | tf_op jit(solution)/shard_map/ppermute | solution.py:610
  6.5 3.7 %collective-permute-start.2 = (f32[1,4,512]{2,1,0:T(4,128)S(1)}, f32[1,4,512]{2,1,0:T(4,128)S(1)}, u32[]{:S(2)}, u32[]{:S(2)}) collective-permute-start(f32[1,4,512]{2,1,0:T(4,128)S(1)} %pad_maximum_fusion.block.refs_1_), channel_id=1, source_target_pairs={{0,1},{1,0},{2,3},{3,2},{4,5},{5,4},{6,7},{7,6},{8,9},{9,8},{10,11... | collective-permute-start | bytes 24584 | tf_op jit(solution)/shard_map/ppermute | solution.py:610
  17.5 1.1 %collective-permute-start.3 = (f32[1,128]{1,0:T(1,128)S(1)}, f32[1,128]{1,0:T(1,128)S(1)}, u32[]{:S(2)}, u32[]{:S(2)}) collective-permute-start(f32[1,128]{1,0:T(1,128)S(1)} %get-tuple-element.35), channel_id=1, source_target_pairs={{0,4},{4,0},{8,12},{12,8},{1,5},{5,1},{9,13},{13,9},{2,6},{6,2},{1... | collective-permute-start | bytes 1544 | tf_op jit(solution)/shard_map/ppermute | solution.py:595
  18.7 3.0 %collective-permute-start.4 = (f32[1,128]{1,0:T(1,128)S(1)}, f32[1,128]{1,0:T(1,128)S(1)}, u32[]{:S(2)}, u32[]{:S(2)}) collective-permute-start(f32[1,128]{1,0:T(1,128)S(1)} %max.6), channel_id=1, source_target_pairs={{0,12},{4,8},{8,4},{12,0},{1,13},{5,9},{9,5},{13,1},{2,14},{6,10},... | collective-permute-start | bytes 1544 | tf_op jit(solution)/shard_map/ppermute | solution.py:595

commit v29 on v28

--- a/solution.py
+++ b/solution.py
@@ -93,10 +93,13 @@
     return product(jnp.concatenate([left, left], axis=1), ref[...])
 
 
+TURNED = (((1,), (1,)), ((), ()))
+
+
 def sum_columns(left, ref):
-    both = lax.dot_general(left, ref[...], (((1,), (1,)), ((), ())), preferred_element_type=f32)
+    both = lax.dot_general(ref[...], left, TURNED, preferred_element_type=f32)
     half = ref.shape[0] // 2
-    return both[:, :half] + both[:, half:]
+    return (both[:half] + both[half:]).T
 
 
 def sum_rows_less(left, ref):
@@ -108,9 +111,8 @@
 
 def sum_columns_less(left, ref):
     half, few = ref.shape[0] // 2, left.shape[0] // 2
-    turned = (((1,), (1,)), ((), ()))
-    both = lax.dot_general(left, ref[:half, :], turned, preferred_element_type=f32)
-    less = lax.dot_general(left[:few], ref[half:, :], turned, preferred_element_type=f32)
+    both = lax.dot_general(ref[:half, :], left, TURNED, preferred_element_type=f32).T
+    less = lax.dot_general(ref[half:, :], left[:few], TURNED, preferred_element_type=f32).T
     return both[:few] + less, both[few:]
 
 

time: 22.5 us -> 22.4 us (level)
  no operation moved by 1% of the time
where the time goes in v29:
time: 22.4 us; the launch traced here: 22.2 us
  Pallas kernels  9.52 us (42%)
  starting transfers between devices  7.13 us (32%)
  waiting for transfers between devices  2.32 us (10%)
  local copies, waits for them, and re-layouts  1.31 us (6%)
  between operations  1.3 us (6%)
  other arithmetic  0.62 us (3%)
    pallas_call x1, Pallas kernels, sweep(): pl.pallas_call(functools.partial(sweep_kernel, sources), out_shape=sweep_...  7.32 us
    ppermute x3, starting transfers between devices, gathered(): blocks.append(lax.ppermute(block, 'sharers', list(enumerate(targets))))  5.67 us
    ppermute x2, waiting for transfers between devices, swapped(): return lax.ppermute(value, axis, pairs)  2.02 us
    ppermute x2, starting transfers between devices, swapped(): return lax.ppermute(value, axis, pairs)  1.46 us
    pallas_call x1, Pallas kernels, next_part(): pl.pallas_call(functools.partial(next_kernel, sources), out_shape=shapes,...  1.44 us
    unnamed x4, local copies, waits for them, and re-layouts  1.31 us
    pallas_call x1, Pallas kernels, own_part(): pl.pallas_call(own_kernel, out_shape=shapes, in_specs=[vector] * 2, out_s...  0.76 us
    add x1, other arithmetic, local(): moved = start + time_step[None] * drift  0.61 us
  transfers between devices with their start and end apart: 5, of which 4 were waited for; matrix products, arithmetic and copies ran while one was open for 3% of the time, Pallas kernels for 10%

profile of v29, /device:TPU:0, one launch (start us, length us, event | category | flops | bytes accessed | tf_op | source)
XLA Modules:
  0.0 22.2 jit_solution(9667606093592270291)
XLA Ops:
  0.6 0.0 copy-start
  0.6 0.7 %copy.8 = f32[1,3,512]{2,1,0:T(4,128)S(1)} copy(f32[1,3,512]{2,0,1:T(1,128)} %param.3) | data formatting | bytes 12288 | tf_op args[0]
  1.3 0.0 copy-done
  1.4 4.1 %collective-permute-start = (f32[1,4,512]{2,1,0:T(4,128)S(1)}, f32[1,4,512]{2,1,0:T(4,128)S(1)}, u32[]{:S(2)}, u32[]{:S(2)}) collective-permute-start(f32[1,4,512]{2,1,0:T(4,128)S(1)} %pad_maximum_fusion.block.refs_1_), channel_id=1, source_target_pairs={{0,2},{1,3},{2,1},{3,0},{4,6},{5,7},{6,5},{7,4},{8,10},{9,11},{10,... | collective-permute-start | bytes 24584 | tf_op jit(solution)/shard_map/ppermute | solution.py:612
  5.4 1.1 %collective-permute-start.1 = (f32[1,4,512]{2,1,0:T(4,128)S(1)}, f32[1,4,512]{2,1,0:T(4,128)S(1)}, u32[]{:S(2)}, u32[]{:S(2)}) collective-permute-start(f32[1,4,512]{2,1,0:T(4,128)S(1)} %pad_maximum_fusion.block.refs_1_), channel_id=1, source_target_pairs={{0,3},{1,2},{2,0},{3,1},{4,7},{5,6},{6,4},{7,5},{8,11},{9,10},{10,... | collective-permute-start | bytes 24584 | tf_op jit(solution)/shard_map/ppermute | solution.py:612
  6.5 0.5 %collective-permute-start.2 = (f32[1,4,512]{2,1,0:T(4,128)S(1)}, f32[1,4,512]{2,1,0:T(4,128)S(1)}, u32[]{:S(2)}, u32[]{:S(2)}) collective-permute-start(f32[1,4,512]{2,1,0:T(4,128)S(1)} %pad_maximum_fusion.block.refs_1_), channel_id=1, source_target_pairs={{0,1},{1,0},{2,3},{3,2},{4,5},{5,4},{6,7},{7,6},{8,9},{9,8},{10,11... | collective-permute-start | bytes 24584 | tf_op jit(solution)/shard_map/ppermute | solution.py:612
  7.7 0.8 %own.1 = (bf16[512,96]{1,0:T(8,128)(2,1)S(1)}, bf16[96,512]{1,0:T(8,128)(2,1)S(1)}, bf16[16,512]{1,0:T(8,128)(2,1)S(1)}, f32[16,512]{1,0:T(8,128)S(1)}, bf16[512...) custom-call(s32[1,1]{1,0:T(1,128)} %bitcast.7.filled, f32[1,4,512]{2,1,0:T(4,128)S(1)} %pad_maximum_fusion.block.refs_1_), custom_call_target="tpu_custom_call" | custom-call | tf_op jit(solution)/shard_map/own/pallas_call | solution.py:305
  8.4 0.0 collective-permute-done.block.refs_2_
  8.4 1.4 %next.1 = (bf16[512,96]{1,0:T(8,128)(2,1)S(1)}, bf16[96,512]{1,0:T(8,128)(2,1)S(1)}, bf16[16,512]{1,0:T(8,128)(2,1)S(1)}, f32[16,1024]{1,0:T(8,128)S(1)}, bf16[5...) custom-call(s32[1,1]{1,0:T(1,128)} %bitcast.8.filled, ...), custom_call_target="tpu_custom_call" | custom-call | tf_op jit(solution)/shard_map/next/pallas_call | solution.py:321
  9.9 0.1 collective-permute-done.1.refs_3_
  10.0 0.2 collective-permute-done.2.refs_4_
  10.2 7.3 %sweep.1 = (f32[8,512]{1,0:T(8,128)S(1)}, f32[3,4,128]{2,1,0:T(4,128)S(1)}, f32[3,4,128]{2,1,0:T(4,128)S(1)}, f32[1,128]{1,0:T(1,128)S(1)}) custom-call(s32[1,1]{1,0:T(1,128)} %bitcast.9.refs_0_, f32[1,4,512]{2,1,0:T(4,128)S(1)} %pad_maximum_fusion.block.refs_1_, f32[1,4,512]{2,1,0:T(4,128)S(1)} %collective-permute-done.block.refs_2_, ...), custom_call_target="tpu_custom_call" | custom-call | tf_op jit(solution)/shard_map/sweep/pallas_call | solution.py:492
  17.5 0.0 collective-permute-start.3
  17.5 1.1 %collective-permute-done.3 = f32[1,128]{1,0:T(1,128)S(1)} collective-permute-done((f32[1,128]{1,0:T(1,128)S(1)}, f32[1,128]{1,0:T(1,128)S(1)}, u32[]{:S(2)}, u32[]{:S(2)}) %collective-permute-start.3) | collective-permute-done | bytes 544 | tf_op jit(solution)/shard_map/ppermute | solution.py:597
  18.6 1.5 %collective-permute-start.4 = (f32[1,128]{1,0:T(1,128)S(1)}, f32[1,128]{1,0:T(1,128)S(1)}, u32[]{:S(2)}, u32[]{:S(2)}) collective-permute-start(f32[1,128]{1,0:T(1,128)S(1)} %max.6), channel_id=1, source_target_pairs={{0,12},{4,8},{8,4},{12,0},{1,13},{5,9},{9,5},{13,1},{2,14},{6,10},... | collective-permute-start | bytes 1544 | tf_op jit(solution)/shard_map/ppermute | solution.py:597
  20.1 0.6 %copy.10 = f32[1,3,512]{2,0,1:T(1,128)} copy(f32[1,3,512]{2,1,0:T(4,128)S(1)} %slice_bitcast_fusion) | data formatting | bytes 12288
  20.7 0.9 %collective-permute-done.4 = f32[1,128]{1,0:T(1,128)S(1)} collective-permute-done((f32[1,128]{1,0:T(1,128)S(1)}, f32[1,128]{1,0:T(1,128)S(1)}, u32[]{:S(2)}, u32[]{:S(2)}) %collective-permute-start.4) | collective-permute-done | bytes 544 | tf_op jit(solution)/shard_map/ppermute | solution.py:597
  21.6 0.6 %multiply_add_fusion = f32[3,4,128]{2,1,0:T(4,128)} fusion(f32[3,4,128]{2,1,0:T(4,128)S(1)} %get-tuple-element.34, f32[3,4,128]{2,1,0:T(4,128)S(1)} %get-tuple-element.36, f32[128]{0:T(128)S(1)} %divide_bitcast_fusion), kind=kLoop, calls=%fused_computation.2 | loop fusion | flops 3072 | bytes 18944 | tf_op jit(solution)/shard_map/add | solution.py:634
  (4 shorter events, 0.0 us)
Async XLA Ops:
  0.6 0.7 %copy-start = (f32[1,512]{1,0:T(1,128)S(1)}, f32[1,512]{1,0:T(1,128)}, u32[]{:S(2)}) copy-start(f32[1,512]{1,0:T(1,128)} %param.4) | copy-start | bytes 6148
  1.4 7.1 %collective-permute-start = (f32[1,4,512]{2,1,0:T(4,128)S(1)}, f32[1,4,512]{2,1,0:T(4,128)S(1)}, u32[]{:S(2)}, u32[]{:S(2)}) collective-permute-start(f32[1,4,512]{2,1,0:T(4,128)S(1)} %pad_maximum_fusion.block.refs_1_), channel_id=1, source_target_pairs={{0,2},{1,3},{2,1},{3,0},{4,6},{5,7},{6,5},{7,4},{8,10},{9,11},{10,... | collective-permute-start | bytes 24584 | tf_op jit(solution)/shard_map/ppermute | solution.py:612
  5.4 4.5 %collective-permute-start.1 = (f32[1,4,512]{2,1,0:T(4,128)S(1)}, f32[1,4,512]{2,1,0:T(4,128)S(1)}, u32[]{:S(2)}, u32[]{:S(2)}) collective-permute-start(f32[1,4,512]{2,1,0:T(4,128)S(1)} %pad_maximum_fusion.block.refs_1_), channel_id=1, source_target_pairs={{0,3},{1,2},{2,0},{3,1},{4,7},{5,6},{6,4},{7,5},{8,11},{9,10},{10,... | collective-permute-start | bytes 24584 | tf_op jit(solution)/shard_map/ppermute | solution.py:612
  6.5 3.7 %collective-permute-start.2 = (f32[1,4,512]{2,1,0:T(4,128)S(1)}, f32[1,4,512]{2,1,0:T(4,128)S(1)}, u32[]{:S(2)}, u32[]{:S(2)}) collective-permute-start(f32[1,4,512]{2,1,0:T(4,128)S(1)} %pad_maximum_fusion.block.refs_1_), channel_id=1, source_target_pairs={{0,1},{1,0},{2,3},{3,2},{4,5},{5,4},{6,7},{7,6},{8,9},{9,8},{10,11... | collective-permute-start | bytes 24584 | tf_op jit(solution)/shard_map/ppermute | solution.py:612
  17.5 1.1 %collective-permute-start.3 = (f32[1,128]{1,0:T(1,128)S(1)}, f32[1,128]{1,0:T(1,128)S(1)}, u32[]{:S(2)}, u32[]{:S(2)}) collective-permute-start(f32[1,128]{1,0:T(1,128)S(1)} %get-tuple-element.35), channel_id=1, source_target_pairs={{0,4},{4,0},{8,12},{12,8},{1,5},{5,1},{9,13},{13,9},{2,6},{6,2},{1... | collective-permute-start | bytes 1544 | tf_op jit(solution)/shard_map/ppermute | solution.py:597
  18.6 3.0 %collective-permute-start.4 = (f32[1,128]{1,0:T(1,128)S(1)}, f32[1,128]{1,0:T(1,128)S(1)}, u32[]{:S(2)}, u32[]{:S(2)}) collective-permute-start(f32[1,128]{1,0:T(1,128)S(1)} %max.6), channel_id=1, source_target_pairs={{0,12},{4,8},{8,4},{12,0},{1,13},{5,9},{9,5},{13,1},{2,14},{6,10},... | collective-permute-start | bytes 1544 | tf_op jit(solution)/shard_map/ppermute | solution.py:597

commit v30 on v28

--- a/solution.py
+++ b/solution.py
@@ -13,7 +13,7 @@
 SCALE = math.sqrt(math.log2(math.e) / (2.0 * EPS * EPS))
 GRID = 4.0
 TINY = 1e-30
-GROUP = 32
+GROUP = 16
 DISTANCE_ROWS = 96
 DRIFT_ROWS = 64
 bf16, f32 = jnp.bfloat16, jnp.float32
@@ -168,11 +168,15 @@
         store_split(split, rows, jnp.exp2(exponent[rows, :]))
 
 
+def negative_distance(exponent):
+    negative = jnp.minimum(exponent, -TINY)
+    return negative * lax.rsqrt(-negative)
+
+
 def split_distances(exponent, split):
     for group in range(0, exponent.shape[0], GROUP):
         rows = pl.ds(group, GROUP)
-        negative = jnp.minimum(exponent[rows, :], -TINY)
-        store_split(split, rows, negative * lax.rsqrt(-negative))
+        store_split(split, rows, negative_distance(exponent[rows, :]))
 
 
 def diagonal_tiles(start, width):
@@ -201,21 +205,15 @@
     return rows, columns if turned else lambda: None
 
 
-def stage(tiles, exponent, moments, sums_ref, exponent_refs, split_refs, distance_refs,
-          after=lambda index: None):
-    def buffer(index):
-        _, keys, _, queries, _ = tiles[index]
-        return exponent_refs[index % len(exponent_refs)].at[0:keys, 0:queries]
-
-    buffer(0)[...] = exponent(tiles[0])
+def stage(tiles, exponent, moments, sums_ref, split_refs, distance_refs, after=lambda index: None):
     for index, tile in enumerate(tiles):
-        if index + 1 < len(tiles):
-            buffer(index + 1)[...] = exponent(tiles[index + 1])
         split = split_refs[index % 2].at[0 : 2 * tile[1], 0 : tile[3]]
-        split_blobs(buffer(index), split)
+        values = exponent(tile)
+        for group in range(0, tile[1], GROUP):
+            rows, part = pl.ds(group, GROUP), values[group : group + GROUP]
+            store_split(split, rows, jnp.exp2(part))
+            store_split(distance_refs[index], rows, negative_distance(part))
         add_blobs(tile, split, moments, sums_ref)
-        if distance_refs is not None:
-            split_distances(buffer(index), distance_refs[index])
         after(index)
 
 
@@ -253,7 +251,7 @@
     exponent = exponent_of(looked_up([key_out], width, 0), looked_up([query_out], width, 1))
     moments = looked_up([moment_out], width, 1)
     tiles = diagonal_tiles(0, width)
-    stage(tiles, exponent, moments, sums_out, scratch[:2], scratch[2:], (first_out, second_out))
+    stage(tiles, exponent, moments, sums_out, scratch, (first_out, second_out))
 
 
 def next_kernel(sources, filled, block, own_key, own_query, own_moment, own_sums, key_out,
@@ -272,7 +270,7 @@
     moments = looked_up([own_moment, moment_out], width, 1)
     tiles = square_tiles(width, 0, width) + diagonal_tiles(width, width)
     distances, scratch = refs[: len(tiles)], refs[len(tiles) :]
-    stage(tiles, exponent, moments, sums_out, scratch[:2], scratch[2:], distances)
+    stage(tiles, exponent, moments, sums_out, scratch, distances)
 
 
 def feature_shapes(width):
@@ -292,8 +290,7 @@
 
 
 def stage_scratch(width):
-    half = width // 2
-    return [pltpu.VMEM((half, width), f32)] * 2 + [pltpu.VMEM((width, width), bf16)] * 2
+    return [pltpu.VMEM((width, width), bf16)] * 2
 
 
 def own_part(filled, block):
@@ -395,8 +392,7 @@
     flux_refs, refs = refs[:count], refs[count:]
     width = blocks[0].shape[2]
     half = 2 * width
-    split_refs, refs = refs[:2], refs[2:]
-    exponent_refs, distance_refs = refs[: len(refs) // 2], refs[len(refs) // 2 :]
+    split_refs, distance_refs = refs[:2], refs[2:]
 
     live = [lanes_of(owner_of(source), width) < filled[...] for source in sources]
     late = range(2, count)
@@ -433,10 +429,8 @@
         if index == mixed - 1:
             score_blocks(0, 1)
 
-    stage(
-        tiles, exponent, looked_up(moments, width, 1), sums_ref, exponent_refs, split_refs, None,
-        after,
-    )
+    moments = looked_up(moments, width, 1)
+    stage(tiles, exponent, moments, sums_ref, split_refs, distance_refs, after)
     early = diagonal_tiles(0, width) + square_tiles(width, 0, width)
     early += diagonal_tiles(width, width)
     for tile, distances in zip(early, own[3:5] + following[4:8]):
@@ -455,7 +449,6 @@
 
     turns = []
     for index in range(mixed):
-        split_distances(exponent_refs[index], distance_refs[index])
         rows, columns = add_distances(tiles[index], distance_refs[index], fluxes, totals_ref)
         rows()
         turns.append((tiles[index][0], columns))
@@ -465,7 +458,6 @@
                 columns()
         drift_block(index)
     for index in range(mixed, len(tiles)):
-        split_distances(exponent_refs[index], distance_refs[index])
         for job in add_distances(tiles[index], distance_refs[index], fluxes, totals_ref):
             job()
     for index in range(2, count):
@@ -501,7 +493,6 @@
         ]
         + [pltpu.VMEM((DRIFT_ROWS, width), bf16)] * count
         + [pltpu.VMEM((width, width), bf16)] * 2
-        + [pltpu.VMEM((tile[1], tile[3]), f32) for tile in late_tiles(count, width)]
         + distances,
         compiler_params=pltpu.CompilerParams(vmem_limit_bytes=24 << 20),
         name="sweep",

time: 22.5 us -> 23.5 us (1.044)
  Pallas kernels: 9.52 us -> 10.9 us
  waiting for transfers between devices: 2.38 us -> 2.14 us
    pallas_call x1, Pallas kernels: 7.38 us -> 8.31 us  [sweep(): pl.pallas_call(functools.partial(sweep_kernel, sources), out_shape=sweep_...]
    ppermute x3, waiting for transfers between devices: 0.35 us -> 0.01 us  [gathered(): blocks.append(lax.ppermute(block, 'sharers', list(enumerate(targets))))]
    pallas_call x1, Pallas kernels: 1.45 us -> 1.74 us  [next_part(): pl.pallas_call(functools.partial(next_kernel, sources), out_shape=shapes,...]
  transfers between devices with their start and end apart: 5 -> 5, of which waited for: 4 -> 2; matrix products, arithmetic and copies ran while one was open for 3% -> 3% of each run, Pallas kernels for 10% -> 11%
where the time goes in v30:
time: 23.5 us; the launch traced here: 23.3 us
  Pallas kernels  10.9 us (46%)
  starting transfers between devices  7.02 us (30%)
  waiting for transfers between devices  2.14 us (9%)
  local copies, waits for them, and re-layouts  1.31 us (6%)
  between operations  1.31 us (6%)
  other arithmetic  0.62 us (3%)
    pallas_call x1, Pallas kernels, sweep(): pl.pallas_call(functools.partial(sweep_kernel, sources), out_shape=sweep_...  8.31 us
    ppermute x3, starting transfers between devices, gathered(): blocks.append(lax.ppermute(block, 'sharers', list(enumerate(targets))))  5.67 us
    ppermute x2, waiting for transfers between devices, swapped(): return lax.ppermute(value, axis, pairs)  2.13 us
    pallas_call x1, Pallas kernels, next_part(): pl.pallas_call(functools.partial(next_kernel, sources), out_shape=shapes,...  1.74 us
    ppermute x2, starting transfers between devices, swapped(): return lax.ppermute(value, axis, pairs)  1.35 us
    unnamed x4, local copies, waits for them, and re-layouts  1.31 us
    pallas_call x1, Pallas kernels, own_part(): pl.pallas_call(own_kernel, out_shape=shapes, in_specs=[vector] * 2, out_s...  0.82 us
    add x1, other arithmetic, local(): moved = start + time_step[None] * drift  0.61 us
  transfers between devices with their start and end apart: 5, of which 2 were waited for; matrix products, arithmetic and copies ran while one was open for 3% of the time, Pallas kernels for 11%

profile of v30, /device:TPU:0, one launch (start us, length us, event | category | flops | bytes accessed | tf_op | source)
XLA Modules:
  0.0 23.3 jit_solution(14190507593763337442)
XLA Ops:
  0.6 0.0 copy-start
  0.6 0.7 %copy.8 = f32[1,3,512]{2,1,0:T(4,128)S(1)} copy(f32[1,3,512]{2,0,1:T(1,128)} %param.3) | data formatting | bytes 12288 | tf_op args[0]
  1.3 0.0 copy-done
  1.4 4.1 %collective-permute-start = (f32[1,4,512]{2,1,0:T(4,128)S(1)}, f32[1,4,512]{2,1,0:T(4,128)S(1)}, u32[]{:S(2)}, u32[]{:S(2)}) collective-permute-start(f32[1,4,512]{2,1,0:T(4,128)S(1)} %pad_maximum_fusion.block.refs_1_), channel_id=1, source_target_pairs={{0,2},{1,3},{2,1},{3,0},{4,6},{5,7},{6,5},{7,4},{8,10},{9,11},{10,... | collective-permute-start | bytes 24584 | tf_op jit(solution)/shard_map/ppermute | solution.py:601
  5.4 1.1 %collective-permute-start.1 = (f32[1,4,512]{2,1,0:T(4,128)S(1)}, f32[1,4,512]{2,1,0:T(4,128)S(1)}, u32[]{:S(2)}, u32[]{:S(2)}) collective-permute-start(f32[1,4,512]{2,1,0:T(4,128)S(1)} %pad_maximum_fusion.block.refs_1_), channel_id=1, source_target_pairs={{0,3},{1,2},{2,0},{3,1},{4,7},{5,6},{6,4},{7,5},{8,11},{9,10},{10,... | collective-permute-start | bytes 24584 | tf_op jit(solution)/shard_map/ppermute | solution.py:601
  6.5 0.5 %collective-permute-start.2 = (f32[1,4,512]{2,1,0:T(4,128)S(1)}, f32[1,4,512]{2,1,0:T(4,128)S(1)}, u32[]{:S(2)}, u32[]{:S(2)}) collective-permute-start(f32[1,4,512]{2,1,0:T(4,128)S(1)} %pad_maximum_fusion.block.refs_1_), channel_id=1, source_target_pairs={{0,1},{1,0},{2,3},{3,2},{4,5},{5,4},{6,7},{7,6},{8,9},{9,8},{10,11... | collective-permute-start | bytes 24584 | tf_op jit(solution)/shard_map/ppermute | solution.py:601
  7.7 0.8 %own.1 = (bf16[512,96]{1,0:T(8,128)(2,1)S(1)}, bf16[96,512]{1,0:T(8,128)(2,1)S(1)}, bf16[16,512]{1,0:T(8,128)(2,1)S(1)}, f32[16,512]{1,0:T(8,128)S(1)}, bf16[512...) custom-call(s32[1,1]{1,0:T(1,128)} %bitcast.7.filled, f32[1,4,512]{2,1,0:T(4,128)S(1)} %pad_maximum_fusion.block.refs_1_), custom_call_target="tpu_custom_call" | custom-call | tf_op jit(solution)/shard_map/own/pallas_call | solution.py:300
  8.5 0.0 collective-permute-done.block.refs_2_
  8.5 1.7 %next.1 = (bf16[512,96]{1,0:T(8,128)(2,1)S(1)}, bf16[96,512]{1,0:T(8,128)(2,1)S(1)}, bf16[16,512]{1,0:T(8,128)(2,1)S(1)}, f32[16,1024]{1,0:T(8,128)S(1)}, bf16[5...) custom-call(s32[1,1]{1,0:T(1,128)} %bitcast.8.filled, ...), custom_call_target="tpu_custom_call" | custom-call | tf_op jit(solution)/shard_map/next/pallas_call | solution.py:316
  10.2 0.0 collective-permute-done.1.refs_3_
  10.2 0.0 collective-permute-done.2.refs_4_
  10.2 8.3 %sweep.1 = (f32[8,512]{1,0:T(8,128)S(1)}, f32[3,4,128]{2,1,0:T(4,128)S(1)}, f32[3,4,128]{2,1,0:T(4,128)S(1)}, f32[1,128]{1,0:T(1,128)S(1)}) custom-call(s32[1,1]{1,0:T(1,128)} %bitcast.9.refs_0_, f32[1,4,512]{2,1,0:T(4,128)S(1)} %pad_maximum_fusion.block.refs_1_, f32[1,4,512]{2,1,0:T(4,128)S(1)} %collective-permute-done.block.refs_2_, ...), custom_call_target="tpu_custom_call" | custom-call | tf_op jit(solution)/shard_map/sweep/pallas_call | solution.py:482
  18.6 0.0 collective-permute-start.3
  18.6 1.1 %collective-permute-done.3 = f32[1,128]{1,0:T(1,128)S(1)} collective-permute-done((f32[1,128]{1,0:T(1,128)S(1)}, f32[1,128]{1,0:T(1,128)S(1)}, u32[]{:S(2)}, u32[]{:S(2)}) %collective-permute-start.3) | collective-permute-done | bytes 544 | tf_op jit(solution)/shard_map/ppermute | solution.py:586
  19.7 1.3 %collective-permute-start.4 = (f32[1,128]{1,0:T(1,128)S(1)}, f32[1,128]{1,0:T(1,128)S(1)}, u32[]{:S(2)}, u32[]{:S(2)}) collective-permute-start(f32[1,128]{1,0:T(1,128)S(1)} %max.6), channel_id=1, source_target_pairs={{0,12},{4,8},{8,4},{12,0},{1,13},{5,9},{9,5},{13,1},{2,14},{6,10},... | collective-permute-start | bytes 1544 | tf_op jit(solution)/shard_map/ppermute | solution.py:586
  21.0 0.6 %copy.10 = f32[1,3,512]{2,0,1:T(1,128)} copy(f32[1,3,512]{2,1,0:T(4,128)S(1)} %slice_bitcast_fusion) | data formatting | bytes 12288
  21.6 1.0 %collective-permute-done.4 = f32[1,128]{1,0:T(1,128)S(1)} collective-permute-done((f32[1,128]{1,0:T(1,128)S(1)}, f32[1,128]{1,0:T(1,128)S(1)}, u32[]{:S(2)}, u32[]{:S(2)}) %collective-permute-start.4) | collective-permute-done | bytes 544 | tf_op jit(solution)/shard_map/ppermute | solution.py:586
  22.7 0.6 %multiply_add_fusion = f32[3,4,128]{2,1,0:T(4,128)} fusion(f32[3,4,128]{2,1,0:T(4,128)S(1)} %get-tuple-element.34, f32[3,4,128]{2,1,0:T(4,128)S(1)} %get-tuple-element.36, f32[128]{0:T(128)S(1)} %divide_bitcast_fusion), kind=kLoop, calls=%fused_computation.2 | loop fusion | flops 3072 | bytes 18944 | tf_op jit(solution)/shard_map/add | solution.py:623
  (4 shorter events, 0.0 us)
Async XLA Ops:
  0.6 0.7 %copy-start = (f32[1,512]{1,0:T(1,128)S(1)}, f32[1,512]{1,0:T(1,128)}, u32[]{:S(2)}) copy-start(f32[1,512]{1,0:T(1,128)} %param.4) | copy-start | bytes 6148
  1.4 7.1 %collective-permute-start = (f32[1,4,512]{2,1,0:T(4,128)S(1)}, f32[1,4,512]{2,1,0:T(4,128)S(1)}, u32[]{:S(2)}, u32[]{:S(2)}) collective-permute-start(f32[1,4,512]{2,1,0:T(4,128)S(1)} %pad_maximum_fusion.block.refs_1_), channel_id=1, source_target_pairs={{0,2},{1,3},{2,1},{3,0},{4,6},{5,7},{6,5},{7,4},{8,10},{9,11},{10,... | collective-permute-start | bytes 24584 | tf_op jit(solution)/shard_map/ppermute | solution.py:601
  5.4 4.8 %collective-permute-start.1 = (f32[1,4,512]{2,1,0:T(4,128)S(1)}, f32[1,4,512]{2,1,0:T(4,128)S(1)}, u32[]{:S(2)}, u32[]{:S(2)}) collective-permute-start(f32[1,4,512]{2,1,0:T(4,128)S(1)} %pad_maximum_fusion.block.refs_1_), channel_id=1, source_target_pairs={{0,3},{1,2},{2,0},{3,1},{4,7},{5,6},{6,4},{7,5},{8,11},{9,10},{10,... | collective-permute-start | bytes 24584 | tf_op jit(solution)/shard_map/ppermute | solution.py:601
  6.5 3.7 %collective-permute-start.2 = (f32[1,4,512]{2,1,0:T(4,128)S(1)}, f32[1,4,512]{2,1,0:T(4,128)S(1)}, u32[]{:S(2)}, u32[]{:S(2)}) collective-permute-start(f32[1,4,512]{2,1,0:T(4,128)S(1)} %pad_maximum_fusion.block.refs_1_), channel_id=1, source_target_pairs={{0,1},{1,0},{2,3},{3,2},{4,5},{5,4},{6,7},{7,6},{8,9},{9,8},{10,11... | collective-permute-start | bytes 24584 | tf_op jit(solution)/shard_map/ppermute | solution.py:601
  18.6 1.1 %collective-permute-start.3 = (f32[1,128]{1,0:T(1,128)S(1)}, f32[1,128]{1,0:T(1,128)S(1)}, u32[]{:S(2)}, u32[]{:S(2)}) collective-permute-start(f32[1,128]{1,0:T(1,128)S(1)} %get-tuple-element.35), channel_id=1, source_target_pairs={{0,4},{4,0},{8,12},{12,8},{1,5},{5,1},{9,13},{13,9},{2,6},{6,2},{1... | collective-permute-start | bytes 1544 | tf_op jit(solution)/shard_map/ppermute | solution.py:586
  19.7 3.0 %collective-permute-start.4 = (f32[1,128]{1,0:T(1,128)S(1)}, f32[1,128]{1,0:T(1,128)S(1)}, u32[]{:S(2)}, u32[]{:S(2)}) collective-permute-start(f32[1,128]{1,0:T(1,128)S(1)} %max.6), channel_id=1, source_target_pairs={{0,12},{4,8},{8,4},{12,0},{1,13},{5,9},{9,5},{13,1},{2,14},{6,10},... | collective-permute-start | bytes 1544 | tf_op jit(solution)/shard_map/ppermute | solution.py:586

commit v31 on v28

--- a/solution.py
+++ b/solution.py
@@ -84,9 +84,10 @@
 
 def store_split(ref, rows, matrix):
     half = ref.shape[0] // 2
-    upper = matrix.astype(bf16)
-    ref[rows, :] = upper
-    ref[pl.ds(half + rows.start, rows.size), :] = (matrix - upper.astype(f32)).astype(bf16)
+    spread = matrix * 65537.0
+    upper = spread - (spread - matrix)
+    ref[rows, :] = upper.astype(bf16)
+    ref[pl.ds(half + rows.start, rows.size), :] = (matrix - upper).astype(bf16)
 
 
 def sum_rows(left, ref):

time: 22.5 us -> 22.8 us (1.013)
  Pallas kernels: 9.52 us -> 10.1 us
  waiting for transfers between devices: 2.38 us -> 2.08 us
    pallas_call x1, Pallas kernels: 7.38 us -> 7.67 us  [sweep(): pl.pallas_call(functools.partial(sweep_kernel, sources), out_shape=sweep_...]
    ppermute x3, waiting for transfers between devices: 0.35 us -> 0.06 us  [gathered(): blocks.append(lax.ppermute(block, 'sharers', list(enumerate(targets))))]
  transfers between devices with their start and end apart: 5 -> 5, of which waited for: 4 -> 3; matrix products, arithmetic and copies ran while one was open for 3% -> 3% of each run, Pallas kernels for 10% -> 11%
where the time goes in v31:
time: 22.8 us; the launch traced here: 22.6 us
  Pallas kernels  10.1 us (44%)
  starting transfers between devices  7.13 us (31%)
  waiting for transfers between devices  2.08 us (9%)
  local copies, waits for them, and re-layouts  1.31 us (6%)
  between operations  1.31 us (6%)
  other arithmetic  0.62 us (3%)
    pallas_call x1, Pallas kernels, sweep(): pl.pallas_call(functools.partial(sweep_kernel, sources), out_shape=sweep_...  7.67 us
    ppermute x3, starting transfers between devices, gathered(): blocks.append(lax.ppermute(block, 'sharers', list(enumerate(targets))))  5.67 us
    ppermute x2, waiting for transfers between devices, swapped(): return lax.ppermute(value, axis, pairs)  2.02 us
    pallas_call x1, Pallas kernels, next_part(): pl.pallas_call(functools.partial(next_kernel, sources), out_shape=shapes,...  1.64 us
    ppermute x2, starting transfers between devices, swapped(): return lax.ppermute(value, axis, pairs)  1.46 us
    unnamed x4, local copies, waits for them, and re-layouts  1.31 us
    pallas_call x1, Pallas kernels, own_part(): pl.pallas_call(own_kernel, out_shape=shapes, in_specs=[vector] * 2, out_s...  0.79 us
    add x1, other arithmetic, local(): moved = start + time_step[None] * drift  0.61 us
  transfers between devices with their start and end apart: 5, of which 3 were waited for; matrix products, arithmetic and copies ran while one was open for 3% of the time, Pallas kernels for 11%

profile of v31, /device:TPU:0, one launch (start us, length us, event | category | flops | bytes accessed | tf_op | source)
XLA Modules:
  0.0 22.6 jit_solution(12913491123201182305)
XLA Ops:
  0.6 0.0 copy-start
  0.6 0.7 %copy.8 = f32[1,3,512]{2,1,0:T(4,128)S(1)} copy(f32[1,3,512]{2,0,1:T(1,128)} %param.3) | data formatting | bytes 12288 | tf_op args[0]
  1.3 0.0 copy-done
  1.4 4.1 %collective-permute-start = (f32[1,4,512]{2,1,0:T(4,128)S(1)}, f32[1,4,512]{2,1,0:T(4,128)S(1)}, u32[]{:S(2)}, u32[]{:S(2)}) collective-permute-start(f32[1,4,512]{2,1,0:T(4,128)S(1)} %pad_maximum_fusion.block.refs_1_), channel_id=1, source_target_pairs={{0,2},{1,3},{2,1},{3,0},{4,6},{5,7},{6,5},{7,4},{8,10},{9,11},{10,... | collective-permute-start | bytes 24584 | tf_op jit(solution)/shard_map/ppermute | solution.py:611
  5.4 1.1 %collective-permute-start.1 = (f32[1,4,512]{2,1,0:T(4,128)S(1)}, f32[1,4,512]{2,1,0:T(4,128)S(1)}, u32[]{:S(2)}, u32[]{:S(2)}) collective-permute-start(f32[1,4,512]{2,1,0:T(4,128)S(1)} %pad_maximum_fusion.block.refs_1_), channel_id=1, source_target_pairs={{0,3},{1,2},{2,0},{3,1},{4,7},{5,6},{6,4},{7,5},{8,11},{9,10},{10,... | collective-permute-start | bytes 24584 | tf_op jit(solution)/shard_map/ppermute | solution.py:611
  6.5 0.5 %collective-permute-start.2 = (f32[1,4,512]{2,1,0:T(4,128)S(1)}, f32[1,4,512]{2,1,0:T(4,128)S(1)}, u32[]{:S(2)}, u32[]{:S(2)}) collective-permute-start(f32[1,4,512]{2,1,0:T(4,128)S(1)} %pad_maximum_fusion.block.refs_1_), channel_id=1, source_target_pairs={{0,1},{1,0},{2,3},{3,2},{4,5},{5,4},{6,7},{7,6},{8,9},{9,8},{10,11... | collective-permute-start | bytes 24584 | tf_op jit(solution)/shard_map/ppermute | solution.py:611
  7.7 0.8 %own.1 = (bf16[512,96]{1,0:T(8,128)(2,1)S(1)}, bf16[96,512]{1,0:T(8,128)(2,1)S(1)}, bf16[16,512]{1,0:T(8,128)(2,1)S(1)}, f32[16,512]{1,0:T(8,128)S(1)}, bf16[512...) custom-call(s32[1,1]{1,0:T(1,128)} %bitcast.7.filled, f32[1,4,512]{2,1,0:T(4,128)S(1)} %pad_maximum_fusion.block.refs_1_), custom_call_target="tpu_custom_call" | custom-call | tf_op jit(solution)/shard_map/own/pallas_call | solution.py:304
  8.5 0.0 collective-permute-done.block.refs_2_
  8.5 1.6 %next.1 = (bf16[512,96]{1,0:T(8,128)(2,1)S(1)}, bf16[96,512]{1,0:T(8,128)(2,1)S(1)}, bf16[16,512]{1,0:T(8,128)(2,1)S(1)}, f32[16,1024]{1,0:T(8,128)S(1)}, bf16[5...) custom-call(s32[1,1]{1,0:T(1,128)} %bitcast.8.filled, ...), custom_call_target="tpu_custom_call" | custom-call | tf_op jit(solution)/shard_map/next/pallas_call | solution.py:320
  10.1 0.0 collective-permute-done.1.refs_3_
  10.1 0.1 collective-permute-done.2.refs_4_
  10.2 7.7 %sweep.1 = (f32[8,512]{1,0:T(8,128)S(1)}, f32[3,4,128]{2,1,0:T(4,128)S(1)}, f32[3,4,128]{2,1,0:T(4,128)S(1)}, f32[1,128]{1,0:T(1,128)S(1)}) custom-call(s32[1,1]{1,0:T(1,128)} %bitcast.9.refs_0_, f32[1,4,512]{2,1,0:T(4,128)S(1)} %pad_maximum_fusion.block.refs_1_, f32[1,4,512]{2,1,0:T(4,128)S(1)} %collective-permute-done.block.refs_2_, ...), custom_call_target="tpu_custom_call" | custom-call | tf_op jit(solution)/shard_map/sweep/pallas_call | solution.py:491
  17.8 0.0 collective-permute-start.3
  17.9 1.1 %collective-permute-done.3 = f32[1,128]{1,0:T(1,128)S(1)} collective-permute-done((f32[1,128]{1,0:T(1,128)S(1)}, f32[1,128]{1,0:T(1,128)S(1)}, u32[]{:S(2)}, u32[]{:S(2)}) %collective-permute-start.3) | collective-permute-done | bytes 544 | tf_op jit(solution)/shard_map/ppermute | solution.py:596
  19.0 1.5 %collective-permute-start.4 = (f32[1,128]{1,0:T(1,128)S(1)}, f32[1,128]{1,0:T(1,128)S(1)}, u32[]{:S(2)}, u32[]{:S(2)}) collective-permute-start(f32[1,128]{1,0:T(1,128)S(1)} %max.6), channel_id=1, source_target_pairs={{0,12},{4,8},{8,4},{12,0},{1,13},{5,9},{9,5},{13,1},{2,14},{6,10},... | collective-permute-start | bytes 1544 | tf_op jit(solution)/shard_map/ppermute | solution.py:596
  20.4 0.6 %copy.10 = f32[1,3,512]{2,0,1:T(1,128)} copy(f32[1,3,512]{2,1,0:T(4,128)S(1)} %slice_bitcast_fusion) | data formatting | bytes 12288
  21.0 0.9 %collective-permute-done.4 = f32[1,128]{1,0:T(1,128)S(1)} collective-permute-done((f32[1,128]{1,0:T(1,128)S(1)}, f32[1,128]{1,0:T(1,128)S(1)}, u32[]{:S(2)}, u32[]{:S(2)}) %collective-permute-start.4) | collective-permute-done | bytes 544 | tf_op jit(solution)/shard_map/ppermute | solution.py:596
  21.9 0.6 %multiply_add_fusion = f32[3,4,128]{2,1,0:T(4,128)} fusion(f32[3,4,128]{2,1,0:T(4,128)S(1)} %get-tuple-element.34, f32[3,4,128]{2,1,0:T(4,128)S(1)} %get-tuple-element.36, f32[128]{0:T(128)S(1)} %divide_bitcast_fusion), kind=kLoop, calls=%fused_computation.2 | loop fusion | flops 3072 | bytes 18944 | tf_op jit(solution)/shard_map/add | solution.py:633
  (4 shorter events, 0.0 us)
Async XLA Ops:
  0.6 0.7 %copy-start = (f32[1,512]{1,0:T(1,128)S(1)}, f32[1,512]{1,0:T(1,128)}, u32[]{:S(2)}) copy-start(f32[1,512]{1,0:T(1,128)} %param.4) | copy-start | bytes 6148
  1.4 7.1 %collective-permute-start = (f32[1,4,512]{2,1,0:T(4,128)S(1)}, f32[1,4,512]{2,1,0:T(4,128)S(1)}, u32[]{:S(2)}, u32[]{:S(2)}) collective-permute-start(f32[1,4,512]{2,1,0:T(4,128)S(1)} %pad_maximum_fusion.block.refs_1_), channel_id=1, source_target_pairs={{0,2},{1,3},{2,1},{3,0},{4,6},{5,7},{6,5},{7,4},{8,10},{9,11},{10,... | collective-permute-start | bytes 24584 | tf_op jit(solution)/shard_map/ppermute | solution.py:611
  5.4 4.7 %collective-permute-start.1 = (f32[1,4,512]{2,1,0:T(4,128)S(1)}, f32[1,4,512]{2,1,0:T(4,128)S(1)}, u32[]{:S(2)}, u32[]{:S(2)}) collective-permute-start(f32[1,4,512]{2,1,0:T(4,128)S(1)} %pad_maximum_fusion.block.refs_1_), channel_id=1, source_target_pairs={{0,3},{1,2},{2,0},{3,1},{4,7},{5,6},{6,4},{7,5},{8,11},{9,10},{10,... | collective-permute-start | bytes 24584 | tf_op jit(solution)/shard_map/ppermute | solution.py:611
  6.5 3.7 %collective-permute-start.2 = (f32[1,4,512]{2,1,0:T(4,128)S(1)}, f32[1,4,512]{2,1,0:T(4,128)S(1)}, u32[]{:S(2)}, u32[]{:S(2)}) collective-permute-start(f32[1,4,512]{2,1,0:T(4,128)S(1)} %pad_maximum_fusion.block.refs_1_), channel_id=1, source_target_pairs={{0,1},{1,0},{2,3},{3,2},{4,5},{5,4},{6,7},{7,6},{8,9},{9,8},{10,11... | collective-permute-start | bytes 24584 | tf_op jit(solution)/shard_map/ppermute | solution.py:611
  17.8 1.1 %collective-permute-start.3 = (f32[1,128]{1,0:T(1,128)S(1)}, f32[1,128]{1,0:T(1,128)S(1)}, u32[]{:S(2)}, u32[]{:S(2)}) collective-permute-start(f32[1,128]{1,0:T(1,128)S(1)} %get-tuple-element.35), channel_id=1, source_target_pairs={{0,4},{4,0},{8,12},{12,8},{1,5},{5,1},{9,13},{13,9},{2,6},{6,2},{1... | collective-permute-start | bytes 1544 | tf_op jit(solution)/shard_map/ppermute | solution.py:596
  19.0 3.0 %collective-permute-start.4 = (f32[1,128]{1,0:T(1,128)S(1)}, f32[1,128]{1,0:T(1,128)S(1)}, u32[]{:S(2)}, u32[]{:S(2)}) collective-permute-start(f32[1,128]{1,0:T(1,128)S(1)} %max.6), channel_id=1, source_target_pairs={{0,12},{4,8},{8,4},{12,0},{1,13},{5,9},{9,5},{13,1},{2,14},{6,10},... | collective-permute-start | bytes 1544 | tf_op jit(solution)/shard_map/ppermute | solution.py:596

commit v32 on v28

--- a/solution.py
+++ b/solution.py
@@ -99,21 +99,6 @@
     return both[:, :half] + both[:, half:]
 
 
-def sum_rows_less(left, ref):
-    half = ref.shape[0] // 2
-    both = product(left, ref[:half, :])
-    few = left.shape[0] // 2
-    return both[:few] + product(left[:few], ref[half:, :]), both[few:]
-
-
-def sum_columns_less(left, ref):
-    half, few = ref.shape[0] // 2, left.shape[0] // 2
-    turned = (((1,), (1,)), ((), ()))
-    both = lax.dot_general(left, ref[:half, :], turned, preferred_element_type=f32)
-    less = lax.dot_general(left[:few], ref[half:, :], turned, preferred_element_type=f32)
-    return both[:few] + less, both[few:]
-
-
 def joined(total):
     upper, lower = total[0:8], total[8:16]
     return upper + lower + pltpu.roll(lower, 4, 0)
@@ -132,6 +117,7 @@
 
 def drift_sum(total, place, score):
     row = row_of(place)
+    total = total[: DRIFT_ROWS // 2] + total[DRIFT_ROWS // 2 :]
     first, *rest = [total[8 * i : 8 * i + 8] for i in range(4)]
     turned = [pltpu.roll(group, 4, 0) for group in rest]
     count, scores = first[3:4], pltpu.roll(first, 4, 0)
@@ -191,12 +177,11 @@
     key, keys, query, queries, turned = tile
 
     def rows():
-        upper, lower = sum_rows_less(fluxes(key, keys), split)
-        totals_ref[:, pl.ds(query, queries)] += upper + lower
+        totals_ref[:, pl.ds(query, queries)] += sum_rows(fluxes(key, keys), split)
 
     def columns():
-        upper, lower = sum_columns_less(fluxes(query, turned), split.at[:, 0:turned])
-        totals_ref[:, pl.ds(key, keys)] += upper + lower
+        left, right = fluxes(query, turned), split.at[:, 0:turned]
+        totals_ref[:, pl.ds(key, keys)] += sum_columns(left, right)
 
     return rows, columns if turned else lambda: None
 
@@ -497,7 +482,7 @@
             pltpu.VMEM((DISTANCE_ROWS, late), bf16),
             pltpu.VMEM((16, late), bf16),
             pltpu.VMEM((16, slots), f32),
-            pltpu.VMEM((DRIFT_ROWS // 2, slots), f32),
+            pltpu.VMEM((DRIFT_ROWS, slots), f32),
         ]
         + [pltpu.VMEM((DRIFT_ROWS, width), bf16)] * count
         + [pltpu.VMEM((width, width), bf16)] * 2
@@ -581,7 +566,7 @@
             pltpu.VMEM((16, slots), bf16),
             pltpu.VMEM((DRIFT_ROWS, slots), bf16),
             pltpu.VMEM((16, slots), f32),
-            pltpu.VMEM((DRIFT_ROWS // 2, width), f32),
+            pltpu.VMEM((DRIFT_ROWS, width), f32),
             pltpu.VMEM((width, width), f32),
             pltpu.VMEM((2 * width, width), bf16),
         ],

time: 22.5 us -> 22.6 us (level)
  no operation moved by 1% of the time
where the time goes in v32:
time: 22.6 us; the launch traced here: 22.4 us
  Pallas kernels  9.62 us (43%)
  starting transfers between devices  7.13 us (32%)
  waiting for transfers between devices  2.37 us (10%)
  local copies, waits for them, and re-layouts  1.31 us (6%)
  between operations  1.31 us (6%)
  other arithmetic  0.62 us (3%)
    pallas_call x1, Pallas kernels, sweep(): pl.pallas_call(functools.partial(sweep_kernel, sources), out_shape=sweep_...  7.47 us
    ppermute x3, starting transfers between devices, gathered(): blocks.append(lax.ppermute(block, 'sharers', list(enumerate(targets))))  5.67 us
    ppermute x2, waiting for transfers between devices, swapped(): return lax.ppermute(value, axis, pairs)  2.02 us
    ppermute x2, starting transfers between devices, swapped(): return lax.ppermute(value, axis, pairs)  1.46 us
    pallas_call x1, Pallas kernels, next_part(): pl.pallas_call(functools.partial(next_kernel, sources), out_shape=shapes,...  1.45 us
    unnamed x4, local copies, waits for them, and re-layouts  1.31 us
    pallas_call x1, Pallas kernels, own_part(): pl.pallas_call(own_kernel, out_shape=shapes, in_specs=[vector] * 2, out_s...  0.7 us
    add x1, other arithmetic, local(): moved = start + time_step[None] * drift  0.61 us
  transfers between devices with their start and end apart: 5, of which 4 were waited for; matrix products, arithmetic and copies ran while one was open for 3% of the time, Pallas kernels for 10%

profile of v32, /device:TPU:0, one launch (start us, length us, event | category | flops | bytes accessed | tf_op | source)
XLA Modules:
  0.0 22.4 jit_solution(10947775654821049733)
XLA Ops:
  0.6 0.0 copy-start
  0.6 0.7 %copy.8 = f32[1,3,512]{2,1,0:T(4,128)S(1)} copy(f32[1,3,512]{2,0,1:T(1,128)} %param.3) | data formatting | bytes 12288 | tf_op args[0]
  1.3 0.0 copy-done
  1.4 4.1 %collective-permute-start = (f32[1,4,512]{2,1,0:T(4,128)S(1)}, f32[1,4,512]{2,1,0:T(4,128)S(1)}, u32[]{:S(2)}, u32[]{:S(2)}) collective-permute-start(f32[1,4,512]{2,1,0:T(4,128)S(1)} %pad_maximum_fusion.block.refs_1_), channel_id=1, source_target_pairs={{0,2},{1,3},{2,1},{3,0},{4,6},{5,7},{6,5},{7,4},{8,10},{9,11},{10,... | collective-permute-start | bytes 24584 | tf_op jit(solution)/shard_map/ppermute | solution.py:595
  5.4 1.1 %collective-permute-start.1 = (f32[1,4,512]{2,1,0:T(4,128)S(1)}, f32[1,4,512]{2,1,0:T(4,128)S(1)}, u32[]{:S(2)}, u32[]{:S(2)}) collective-permute-start(f32[1,4,512]{2,1,0:T(4,128)S(1)} %pad_maximum_fusion.block.refs_1_), channel_id=1, source_target_pairs={{0,3},{1,2},{2,0},{3,1},{4,7},{5,6},{6,4},{7,5},{8,11},{9,10},{10,... | collective-permute-start | bytes 24584 | tf_op jit(solution)/shard_map/ppermute | solution.py:595
  6.5 0.5 %collective-permute-start.2 = (f32[1,4,512]{2,1,0:T(4,128)S(1)}, f32[1,4,512]{2,1,0:T(4,128)S(1)}, u32[]{:S(2)}, u32[]{:S(2)}) collective-permute-start(f32[1,4,512]{2,1,0:T(4,128)S(1)} %pad_maximum_fusion.block.refs_1_), channel_id=1, source_target_pairs={{0,1},{1,0},{2,3},{3,2},{4,5},{5,4},{6,7},{7,6},{8,9},{9,8},{10,11... | collective-permute-start | bytes 24584 | tf_op jit(solution)/shard_map/ppermute | solution.py:595
  7.7 0.7 %own.1 = (bf16[512,96]{1,0:T(8,128)(2,1)S(1)}, bf16[96,512]{1,0:T(8,128)(2,1)S(1)}, bf16[16,512]{1,0:T(8,128)(2,1)S(1)}, f32[16,512]{1,0:T(8,128)S(1)}, bf16[512...) custom-call(s32[1,1]{1,0:T(1,128)} %bitcast.7.filled, f32[1,4,512]{2,1,0:T(4,128)S(1)} %pad_maximum_fusion.block.refs_1_), custom_call_target="tpu_custom_call" | custom-call | tf_op jit(solution)/shard_map/own/pallas_call | solution.py:288
  8.4 0.0 collective-permute-done.block.refs_2_
  8.4 1.5 %next.1 = (bf16[512,96]{1,0:T(8,128)(2,1)S(1)}, bf16[96,512]{1,0:T(8,128)(2,1)S(1)}, bf16[16,512]{1,0:T(8,128)(2,1)S(1)}, f32[16,1024]{1,0:T(8,128)S(1)}, bf16[5...) custom-call(s32[1,1]{1,0:T(1,128)} %bitcast.8.filled, ...), custom_call_target="tpu_custom_call" | custom-call | tf_op jit(solution)/shard_map/next/pallas_call | solution.py:304
  9.8 0.2 collective-permute-done.1.refs_3_
  10.0 0.2 collective-permute-done.2.refs_4_
  10.2 7.5 %sweep.1 = (f32[8,512]{1,0:T(8,128)S(1)}, f32[3,4,128]{2,1,0:T(4,128)S(1)}, f32[3,4,128]{2,1,0:T(4,128)S(1)}, f32[1,128]{1,0:T(1,128)S(1)}) custom-call(s32[1,1]{1,0:T(1,128)} %bitcast.9.refs_0_, f32[1,4,512]{2,1,0:T(4,128)S(1)} %pad_maximum_fusion.block.refs_1_, f32[1,4,512]{2,1,0:T(4,128)S(1)} %collective-permute-done.block.refs_2_, ...), custom_call_target="tpu_custom_call" | custom-call | tf_op jit(solution)/shard_map/sweep/pallas_call | solution.py:475
  17.6 0.0 collective-permute-start.3
  17.6 1.1 %collective-permute-done.3 = f32[1,128]{1,0:T(1,128)S(1)} collective-permute-done((f32[1,128]{1,0:T(1,128)S(1)}, f32[1,128]{1,0:T(1,128)S(1)}, u32[]{:S(2)}, u32[]{:S(2)}) %collective-permute-start.3) | collective-permute-done | bytes 544 | tf_op jit(solution)/shard_map/ppermute | solution.py:580
  18.8 1.5 %collective-permute-start.4 = (f32[1,128]{1,0:T(1,128)S(1)}, f32[1,128]{1,0:T(1,128)S(1)}, u32[]{:S(2)}, u32[]{:S(2)}) collective-permute-start(f32[1,128]{1,0:T(1,128)S(1)} %max.6), channel_id=1, source_target_pairs={{0,12},{4,8},{8,4},{12,0},{1,13},{5,9},{9,5},{13,1},{2,14},{6,10},... | collective-permute-start | bytes 1544 | tf_op jit(solution)/shard_map/ppermute | solution.py:580
  20.2 0.6 %copy.10 = f32[1,3,512]{2,0,1:T(1,128)} copy(f32[1,3,512]{2,1,0:T(4,128)S(1)} %slice_bitcast_fusion) | data formatting | bytes 12288
  20.8 0.9 %collective-permute-done.4 = f32[1,128]{1,0:T(1,128)S(1)} collective-permute-done((f32[1,128]{1,0:T(1,128)S(1)}, f32[1,128]{1,0:T(1,128)S(1)}, u32[]{:S(2)}, u32[]{:S(2)}) %collective-permute-start.4) | collective-permute-done | bytes 544 | tf_op jit(solution)/shard_map/ppermute | solution.py:580
  21.7 0.6 %multiply_add_fusion = f32[3,4,128]{2,1,0:T(4,128)} fusion(f32[3,4,128]{2,1,0:T(4,128)S(1)} %get-tuple-element.34, f32[3,4,128]{2,1,0:T(4,128)S(1)} %get-tuple-element.36, f32[128]{0:T(128)S(1)} %divide_bitcast_fusion), kind=kLoop, calls=%fused_computation.2 | loop fusion | flops 3072 | bytes 18944 | tf_op jit(solution)/shard_map/add | solution.py:617
  (4 shorter events, 0.0 us)
Async XLA Ops:
  0.6 0.7 %copy-start = (f32[1,512]{1,0:T(1,128)S(1)}, f32[1,512]{1,0:T(1,128)}, u32[]{:S(2)}) copy-start(f32[1,512]{1,0:T(1,128)} %param.4) | copy-start | bytes 6148
  1.4 7.0 %collective-permute-start = (f32[1,4,512]{2,1,0:T(4,128)S(1)}, f32[1,4,512]{2,1,0:T(4,128)S(1)}, u32[]{:S(2)}, u32[]{:S(2)}) collective-permute-start(f32[1,4,512]{2,1,0:T(4,128)S(1)} %pad_maximum_fusion.block.refs_1_), channel_id=1, source_target_pairs={{0,2},{1,3},{2,1},{3,0},{4,6},{5,7},{6,5},{7,4},{8,10},{9,11},{10,... | collective-permute-start | bytes 24584 | tf_op jit(solution)/shard_map/ppermute | solution.py:595
  5.4 4.5 %collective-permute-start.1 = (f32[1,4,512]{2,1,0:T(4,128)S(1)}, f32[1,4,512]{2,1,0:T(4,128)S(1)}, u32[]{:S(2)}, u32[]{:S(2)}) collective-permute-start(f32[1,4,512]{2,1,0:T(4,128)S(1)} %pad_maximum_fusion.block.refs_1_), channel_id=1, source_target_pairs={{0,3},{1,2},{2,0},{3,1},{4,7},{5,6},{6,4},{7,5},{8,11},{9,10},{10,... | collective-permute-start | bytes 24584 | tf_op jit(solution)/shard_map/ppermute | solution.py:595
  6.5 3.7 %collective-permute-start.2 = (f32[1,4,512]{2,1,0:T(4,128)S(1)}, f32[1,4,512]{2,1,0:T(4,128)S(1)}, u32[]{:S(2)}, u32[]{:S(2)}) collective-permute-start(f32[1,4,512]{2,1,0:T(4,128)S(1)} %pad_maximum_fusion.block.refs_1_), channel_id=1, source_target_pairs={{0,1},{1,0},{2,3},{3,2},{4,5},{5,4},{6,7},{7,6},{8,9},{9,8},{10,11... | collective-permute-start | bytes 24584 | tf_op jit(solution)/shard_map/ppermute | solution.py:595
  17.6 1.1 %collective-permute-start.3 = (f32[1,128]{1,0:T(1,128)S(1)}, f32[1,128]{1,0:T(1,128)S(1)}, u32[]{:S(2)}, u32[]{:S(2)}) collective-permute-start(f32[1,128]{1,0:T(1,128)S(1)} %get-tuple-element.35), channel_id=1, source_target_pairs={{0,4},{4,0},{8,12},{12,8},{1,5},{5,1},{9,13},{13,9},{2,6},{6,2},{1... | collective-permute-start | bytes 1544 | tf_op jit(solution)/shard_map/ppermute | solution.py:580
  18.8 3.0 %collective-permute-start.4 = (f32[1,128]{1,0:T(1,128)S(1)}, f32[1,128]{1,0:T(1,128)S(1)}, u32[]{:S(2)}, u32[]{:S(2)}) collective-permute-start(f32[1,128]{1,0:T(1,128)S(1)} %max.6), channel_id=1, source_target_pairs={{0,12},{4,8},{8,4},{12,0},{1,13},{5,9},{9,5},{13,1},{2,14},{6,10},... | collective-permute-start | bytes 1544 | tf_op jit(solution)/shard_map/ppermute | solution.py:580

commit v33 on v28

--- a/solution.py
+++ b/solution.py
@@ -327,19 +327,19 @@
     )(filled, block, *features, sums)
 
 
-def square_tiles(key, query, width):
-    half = width // 2
-    return [(key + part, half, query, width, width) for part in (0, half)]
+def square_tiles(key, query, width, cuts=2):
+    part = width // cuts
+    return [(key + at, part, query, width, width) for at in range(0, width, part)]
 
 
 def late_tiles(count, width):
     tiles, late = [], range(2, count)
     for query in late:
         for key in range(2):
-            tiles += square_tiles(key * width, query * width, width)
+            tiles += square_tiles(key * width, query * width, width, 4)
     for query in late:
         for key in range(2, query):
-            tiles += square_tiles(key * width, query * width, width)
+            tiles += square_tiles(key * width, query * width, width, 4)
     for query in late:
         tiles += diagonal_tiles(query * width, width)
     return tiles

time: 22.5 us -> 22.5 us (level)
  no operation moved by 1% of the time
where the time goes in v33:
time: 22.5 us; the launch traced here: 22.3 us
  Pallas kernels  9.59 us (43%)
  starting transfers between devices  7.13 us (32%)
  waiting for transfers between devices  2.37 us (11%)
  local copies, waits for them, and re-layouts  1.31 us (6%)
  between operations  1.31 us (6%)
  other arithmetic  0.62 us (3%)
    pallas_call x1, Pallas kernels, sweep(): pl.pallas_call(functools.partial(sweep_kernel, sources), out_shape=sweep_...  7.44 us
    ppermute x3, starting transfers between devices, gathered(): blocks.append(lax.ppermute(block, 'sharers', list(enumerate(targets))))  5.67 us
    ppermute x2, waiting for transfers between devices, swapped(): return lax.ppermute(value, axis, pairs)  2.02 us
    ppermute x2, starting transfers between devices, swapped(): return lax.ppermute(value, axis, pairs)  1.46 us
    pallas_call x1, Pallas kernels, next_part(): pl.pallas_call(functools.partial(next_kernel, sources), out_shape=shapes,...  1.45 us
    unnamed x4, local copies, waits for them, and re-layouts  1.31 us
    pallas_call x1, Pallas kernels, own_part(): pl.pallas_call(own_kernel, out_shape=shapes, in_specs=[vector] * 2, out_s...  0.7 us
    add x1, other arithmetic, local(): moved = start + time_step[None] * drift  0.61 us
  transfers between devices with their start and end apart: 5, of which 4 were waited for; matrix products, arithmetic and copies ran while one was open for 3% of the time, Pallas kernels for 10%

profile of v33, /device:TPU:0, one launch (start us, length us, event | category | flops | bytes accessed | tf_op | source)
XLA Modules:
  0.0 22.3 jit_solution(14321522514972540456)
XLA Ops:
  0.6 0.0 copy-start
  0.6 0.7 %copy.8 = f32[1,3,512]{2,1,0:T(4,128)S(1)} copy(f32[1,3,512]{2,0,1:T(1,128)} %param.3) | data formatting | bytes 12288 | tf_op args[0]
  1.3 0.0 copy-done
  1.4 4.1 %collective-permute-start = (f32[1,4,512]{2,1,0:T(4,128)S(1)}, f32[1,4,512]{2,1,0:T(4,128)S(1)}, u32[]{:S(2)}, u32[]{:S(2)}) collective-permute-start(f32[1,4,512]{2,1,0:T(4,128)S(1)} %pad_maximum_fusion.block.refs_1_), channel_id=1, source_target_pairs={{0,2},{1,3},{2,1},{3,0},{4,6},{5,7},{6,5},{7,4},{8,10},{9,11},{10,... | collective-permute-start | bytes 24584 | tf_op jit(solution)/shard_map/ppermute | solution.py:610
  5.4 1.1 %collective-permute-start.1 = (f32[1,4,512]{2,1,0:T(4,128)S(1)}, f32[1,4,512]{2,1,0:T(4,128)S(1)}, u32[]{:S(2)}, u32[]{:S(2)}) collective-permute-start(f32[1,4,512]{2,1,0:T(4,128)S(1)} %pad_maximum_fusion.block.refs_1_), channel_id=1, source_target_pairs={{0,3},{1,2},{2,0},{3,1},{4,7},{5,6},{6,4},{7,5},{8,11},{9,10},{10,... | collective-permute-start | bytes 24584 | tf_op jit(solution)/shard_map/ppermute | solution.py:610
  6.5 0.5 %collective-permute-start.2 = (f32[1,4,512]{2,1,0:T(4,128)S(1)}, f32[1,4,512]{2,1,0:T(4,128)S(1)}, u32[]{:S(2)}, u32[]{:S(2)}) collective-permute-start(f32[1,4,512]{2,1,0:T(4,128)S(1)} %pad_maximum_fusion.block.refs_1_), channel_id=1, source_target_pairs={{0,1},{1,0},{2,3},{3,2},{4,5},{5,4},{6,7},{7,6},{8,9},{9,8},{10,11... | collective-permute-start | bytes 24584 | tf_op jit(solution)/shard_map/ppermute | solution.py:610
  7.7 0.7 %own.1 = (bf16[512,96]{1,0:T(8,128)(2,1)S(1)}, bf16[96,512]{1,0:T(8,128)(2,1)S(1)}, bf16[16,512]{1,0:T(8,128)(2,1)S(1)}, f32[16,512]{1,0:T(8,128)S(1)}, bf16[512...) custom-call(s32[1,1]{1,0:T(1,128)} %bitcast.7.filled, f32[1,4,512]{2,1,0:T(4,128)S(1)} %pad_maximum_fusion.block.refs_1_), custom_call_target="tpu_custom_call" | custom-call | tf_op jit(solution)/shard_map/own/pallas_call | solution.py:303
  8.4 0.0 collective-permute-done.block.refs_2_
  8.4 1.5 %next.1 = (bf16[512,96]{1,0:T(8,128)(2,1)S(1)}, bf16[96,512]{1,0:T(8,128)(2,1)S(1)}, bf16[16,512]{1,0:T(8,128)(2,1)S(1)}, f32[16,1024]{1,0:T(8,128)S(1)}, bf16[5...) custom-call(s32[1,1]{1,0:T(1,128)} %bitcast.8.filled, ...), custom_call_target="tpu_custom_call" | custom-call | tf_op jit(solution)/shard_map/next/pallas_call | solution.py:319
  9.8 0.2 collective-permute-done.1.refs_3_
  10.0 0.2 collective-permute-done.2.refs_4_
  10.2 7.4 %sweep.1 = (f32[8,512]{1,0:T(8,128)S(1)}, f32[3,4,128]{2,1,0:T(4,128)S(1)}, f32[3,4,128]{2,1,0:T(4,128)S(1)}, f32[1,128]{1,0:T(1,128)S(1)}) custom-call(s32[1,1]{1,0:T(1,128)} %bitcast.9.refs_0_, f32[1,4,512]{2,1,0:T(4,128)S(1)} %pad_maximum_fusion.block.refs_1_, f32[1,4,512]{2,1,0:T(4,128)S(1)} %collective-permute-done.block.refs_2_, ...), custom_call_target="tpu_custom_call" | custom-call | tf_op jit(solution)/shard_map/sweep/pallas_call | solution.py:490
  17.6 0.0 collective-permute-start.3
  17.6 1.1 %collective-permute-done.3 = f32[1,128]{1,0:T(1,128)S(1)} collective-permute-done((f32[1,128]{1,0:T(1,128)S(1)}, f32[1,128]{1,0:T(1,128)S(1)}, u32[]{:S(2)}, u32[]{:S(2)}) %collective-permute-start.3) | collective-permute-done | bytes 544 | tf_op jit(solution)/shard_map/ppermute | solution.py:595
  18.8 1.5 %collective-permute-start.4 = (f32[1,128]{1,0:T(1,128)S(1)}, f32[1,128]{1,0:T(1,128)S(1)}, u32[]{:S(2)}, u32[]{:S(2)}) collective-permute-start(f32[1,128]{1,0:T(1,128)S(1)} %max.6), channel_id=1, source_target_pairs={{0,12},{4,8},{8,4},{12,0},{1,13},{5,9},{9,5},{13,1},{2,14},{6,10},... | collective-permute-start | bytes 1544 | tf_op jit(solution)/shard_map/ppermute | solution.py:595
  20.2 0.6 %copy.10 = f32[1,3,512]{2,0,1:T(1,128)} copy(f32[1,3,512]{2,1,0:T(4,128)S(1)} %slice_bitcast_fusion) | data formatting | bytes 12288
  20.8 0.9 %collective-permute-done.4 = f32[1,128]{1,0:T(1,128)S(1)} collective-permute-done((f32[1,128]{1,0:T(1,128)S(1)}, f32[1,128]{1,0:T(1,128)S(1)}, u32[]{:S(2)}, u32[]{:S(2)}) %collective-permute-start.4) | collective-permute-done | bytes 544 | tf_op jit(solution)/shard_map/ppermute | solution.py:595
  21.7 0.6 %multiply_add_fusion = f32[3,4,128]{2,1,0:T(4,128)} fusion(f32[3,4,128]{2,1,0:T(4,128)S(1)} %get-tuple-element.34, f32[3,4,128]{2,1,0:T(4,128)S(1)} %get-tuple-element.36, f32[128]{0:T(128)S(1)} %divide_bitcast_fusion), kind=kLoop, calls=%fused_computation.2 | loop fusion | flops 3072 | bytes 18944 | tf_op jit(solution)/shard_map/add | solution.py:632
  (4 shorter events, 0.0 us)
Async XLA Ops:
  0.6 0.7 %copy-start = (f32[1,512]{1,0:T(1,128)S(1)}, f32[1,512]{1,0:T(1,128)}, u32[]{:S(2)}) copy-start(f32[1,512]{1,0:T(1,128)} %param.4) | copy-start | bytes 6148
  1.4 7.0 %collective-permute-start = (f32[1,4,512]{2,1,0:T(4,128)S(1)}, f32[1,4,512]{2,1,0:T(4,128)S(1)}, u32[]{:S(2)}, u32[]{:S(2)}) collective-permute-start(f32[1,4,512]{2,1,0:T(4,128)S(1)} %pad_maximum_fusion.block.refs_1_), channel_id=1, source_target_pairs={{0,2},{1,3},{2,1},{3,0},{4,6},{5,7},{6,5},{7,4},{8,10},{9,11},{10,... | collective-permute-start | bytes 24584 | tf_op jit(solution)/shard_map/ppermute | solution.py:610
  5.4 4.5 %collective-permute-start.1 = (f32[1,4,512]{2,1,0:T(4,128)S(1)}, f32[1,4,512]{2,1,0:T(4,128)S(1)}, u32[]{:S(2)}, u32[]{:S(2)}) collective-permute-start(f32[1,4,512]{2,1,0:T(4,128)S(1)} %pad_maximum_fusion.block.refs_1_), channel_id=1, source_target_pairs={{0,3},{1,2},{2,0},{3,1},{4,7},{5,6},{6,4},{7,5},{8,11},{9,10},{10,... | collective-permute-start | bytes 24584 | tf_op jit(solution)/shard_map/ppermute | solution.py:610
  6.5 3.7 %collective-permute-start.2 = (f32[1,4,512]{2,1,0:T(4,128)S(1)}, f32[1,4,512]{2,1,0:T(4,128)S(1)}, u32[]{:S(2)}, u32[]{:S(2)}) collective-permute-start(f32[1,4,512]{2,1,0:T(4,128)S(1)} %pad_maximum_fusion.block.refs_1_), channel_id=1, source_target_pairs={{0,1},{1,0},{2,3},{3,2},{4,5},{5,4},{6,7},{7,6},{8,9},{9,8},{10,11... | collective-permute-start | bytes 24584 | tf_op jit(solution)/shard_map/ppermute | solution.py:610
  17.6 1.1 %collective-permute-start.3 = (f32[1,128]{1,0:T(1,128)S(1)}, f32[1,128]{1,0:T(1,128)S(1)}, u32[]{:S(2)}, u32[]{:S(2)}) collective-permute-start(f32[1,128]{1,0:T(1,128)S(1)} %get-tuple-element.35), channel_id=1, source_target_pairs={{0,4},{4,0},{8,12},{12,8},{1,5},{5,1},{9,13},{13,9},{2,6},{6,2},{1... | collective-permute-start | bytes 1544 | tf_op jit(solution)/shard_map/ppermute | solution.py:595
  18.8 3.0 %collective-permute-start.4 = (f32[1,128]{1,0:T(1,128)S(1)}, f32[1,128]{1,0:T(1,128)S(1)}, u32[]{:S(2)}, u32[]{:S(2)}) collective-permute-start(f32[1,128]{1,0:T(1,128)S(1)} %max.6), channel_id=1, source_target_pairs={{0,12},{4,8},{8,4},{12,0},{1,13},{5,9},{9,5},{13,1},{2,14},{6,10},... | collective-permute-start | bytes 1544 | tf_op jit(solution)/shard_map/ppermute | solution.py:595

commit v34 on v28

--- a/solution.py
+++ b/solution.py
@@ -211,7 +211,7 @@
     for index, tile in enumerate(tiles):
         if index + 1 < len(tiles):
             buffer(index + 1)[...] = exponent(tiles[index + 1])
-        split = split_refs[index % 2].at[0 : 2 * tile[1], 0 : tile[3]]
+        split = split_refs[index % len(split_refs)].at[0 : 2 * tile[1], 0 : tile[3]]
         split_blobs(buffer(index), split)
         add_blobs(tile, split, moments, sums_ref)
         if distance_refs is not None:
@@ -395,7 +395,7 @@
     flux_refs, refs = refs[:count], refs[count:]
     width = blocks[0].shape[2]
     half = 2 * width
-    split_refs, refs = refs[:2], refs[2:]
+    split_refs, refs = refs[:4], refs[4:]
     exponent_refs, distance_refs = refs[: len(refs) // 2], refs[len(refs) // 2 :]
 
     live = [lanes_of(owner_of(source), width) < filled[...] for source in sources]
@@ -500,7 +500,7 @@
             pltpu.VMEM((DRIFT_ROWS // 2, slots), f32),
         ]
         + [pltpu.VMEM((DRIFT_ROWS, width), bf16)] * count
-        + [pltpu.VMEM((width, width), bf16)] * 2
+        + [pltpu.VMEM((width, width), bf16)] * 4
         + [pltpu.VMEM((tile[1], tile[3]), f32) for tile in late_tiles(count, width)]
         + distances,
         compiler_params=pltpu.CompilerParams(vmem_limit_bytes=24 << 20),

time: 22.5 us -> 22.5 us (level)
  no operation moved by 1% of the time
where the time goes in v34:
time: 22.5 us; the launch traced here: 22.3 us
  Pallas kernels  9.52 us (42%)
  starting transfers between devices  7.12 us (32%)
  waiting for transfers between devices  2.38 us (11%)
  local copies, waits for them, and re-layouts  1.31 us (6%)
  between operations  1.31 us (6%)
  other arithmetic  0.62 us (3%)
    pallas_call x1, Pallas kernels, sweep(): pl.pallas_call(functools.partial(sweep_kernel, sources), out_shape=sweep_...  7.38 us
    ppermute x3, starting transfers between devices, gathered(): blocks.append(lax.ppermute(block, 'sharers', list(enumerate(targets))))  5.67 us
    ppermute x2, waiting for transfers between devices, swapped(): return lax.ppermute(value, axis, pairs)  2.03 us
    pallas_call x1, Pallas kernels, next_part(): pl.pallas_call(functools.partial(next_kernel, sources), out_shape=shapes,...  1.45 us
    ppermute x2, starting transfers between devices, swapped(): return lax.ppermute(value, axis, pairs)  1.45 us
    unnamed x4, local copies, waits for them, and re-layouts  1.31 us
    pallas_call x1, Pallas kernels, own_part(): pl.pallas_call(own_kernel, out_shape=shapes, in_specs=[vector] * 2, out_s...  0.7 us
    add x1, other arithmetic, local(): moved = start + time_step[None] * drift  0.61 us
  transfers between devices with their start and end apart: 5, of which 4 were waited for; matrix products, arithmetic and copies ran while one was open for 3% of the time, Pallas kernels for 10%

profile of v34, /device:TPU:0, one launch (start us, length us, event | category | flops | bytes accessed | tf_op | source)
XLA Modules:
  0.0 22.3 jit_solution(9292637332072719134)
XLA Ops:
  0.6 0.0 copy-start
  0.6 0.7 %copy.8 = f32[1,3,512]{2,1,0:T(4,128)S(1)} copy(f32[1,3,512]{2,0,1:T(1,128)} %param.3) | data formatting | bytes 12288 | tf_op args[0]
  1.3 0.0 copy-done
  1.4 4.1 %collective-permute-start = (f32[1,4,512]{2,1,0:T(4,128)S(1)}, f32[1,4,512]{2,1,0:T(4,128)S(1)}, u32[]{:S(2)}, u32[]{:S(2)}) collective-permute-start(f32[1,4,512]{2,1,0:T(4,128)S(1)} %pad_maximum_fusion.block.refs_1_), channel_id=1, source_target_pairs={{0,2},{1,3},{2,1},{3,0},{4,6},{5,7},{6,5},{7,4},{8,10},{9,11},{10,... | collective-permute-start | bytes 24584 | tf_op jit(solution)/shard_map/ppermute | solution.py:610
  5.4 1.1 %collective-permute-start.1 = (f32[1,4,512]{2,1,0:T(4,128)S(1)}, f32[1,4,512]{2,1,0:T(4,128)S(1)}, u32[]{:S(2)}, u32[]{:S(2)}) collective-permute-start(f32[1,4,512]{2,1,0:T(4,128)S(1)} %pad_maximum_fusion.block.refs_1_), channel_id=1, source_target_pairs={{0,3},{1,2},{2,0},{3,1},{4,7},{5,6},{6,4},{7,5},{8,11},{9,10},{10,... | collective-permute-start | bytes 24584 | tf_op jit(solution)/shard_map/ppermute | solution.py:610
  6.5 0.5 %collective-permute-start.2 = (f32[1,4,512]{2,1,0:T(4,128)S(1)}, f32[1,4,512]{2,1,0:T(4,128)S(1)}, u32[]{:S(2)}, u32[]{:S(2)}) collective-permute-start(f32[1,4,512]{2,1,0:T(4,128)S(1)} %pad_maximum_fusion.block.refs_1_), channel_id=1, source_target_pairs={{0,1},{1,0},{2,3},{3,2},{4,5},{5,4},{6,7},{7,6},{8,9},{9,8},{10,11... | collective-permute-start | bytes 24584 | tf_op jit(solution)/shard_map/ppermute | solution.py:610
  7.7 0.7 %own.1 = (bf16[512,96]{1,0:T(8,128)(2,1)S(1)}, bf16[96,512]{1,0:T(8,128)(2,1)S(1)}, bf16[16,512]{1,0:T(8,128)(2,1)S(1)}, f32[16,512]{1,0:T(8,128)S(1)}, bf16[512...) custom-call(s32[1,1]{1,0:T(1,128)} %bitcast.7.filled, f32[1,4,512]{2,1,0:T(4,128)S(1)} %pad_maximum_fusion.block.refs_1_), custom_call_target="tpu_custom_call" | custom-call | tf_op jit(solution)/shard_map/own/pallas_call | solution.py:303
  8.4 0.0 collective-permute-done.block.refs_2_
  8.4 1.5 %next.1 = (bf16[512,96]{1,0:T(8,128)(2,1)S(1)}, bf16[96,512]{1,0:T(8,128)(2,1)S(1)}, bf16[16,512]{1,0:T(8,128)(2,1)S(1)}, f32[16,1024]{1,0:T(8,128)S(1)}, bf16[5...) custom-call(s32[1,1]{1,0:T(1,128)} %bitcast.8.filled, ...), custom_call_target="tpu_custom_call" | custom-call | tf_op jit(solution)/shard_map/next/pallas_call | solution.py:319
  9.8 0.2 collective-permute-done.1.refs_3_
  10.0 0.2 collective-permute-done.2.refs_4_
  10.2 7.4 %sweep.1 = (f32[8,512]{1,0:T(8,128)S(1)}, f32[3,4,128]{2,1,0:T(4,128)S(1)}, f32[3,4,128]{2,1,0:T(4,128)S(1)}, f32[1,128]{1,0:T(1,128)S(1)}) custom-call(s32[1,1]{1,0:T(1,128)} %bitcast.9.refs_0_, f32[1,4,512]{2,1,0:T(4,128)S(1)} %pad_maximum_fusion.block.refs_1_, f32[1,4,512]{2,1,0:T(4,128)S(1)} %collective-permute-done.block.refs_2_, ...), custom_call_target="tpu_custom_call" | custom-call | tf_op jit(solution)/shard_map/sweep/pallas_call | solution.py:490
  17.5 0.0 collective-permute-start.3
  17.6 1.1 %collective-permute-done.3 = f32[1,128]{1,0:T(1,128)S(1)} collective-permute-done((f32[1,128]{1,0:T(1,128)S(1)}, f32[1,128]{1,0:T(1,128)S(1)}, u32[]{:S(2)}, u32[]{:S(2)}) %collective-permute-start.3) | collective-permute-done | bytes 544 | tf_op jit(solution)/shard_map/ppermute | solution.py:595
  18.7 1.4 %collective-permute-start.4 = (f32[1,128]{1,0:T(1,128)S(1)}, f32[1,128]{1,0:T(1,128)S(1)}, u32[]{:S(2)}, u32[]{:S(2)}) collective-permute-start(f32[1,128]{1,0:T(1,128)S(1)} %max.6), channel_id=1, source_target_pairs={{0,12},{4,8},{8,4},{12,0},{1,13},{5,9},{9,5},{13,1},{2,14},{6,10},... | collective-permute-start | bytes 1544 | tf_op jit(solution)/shard_map/ppermute | solution.py:595
  20.1 0.6 %copy.10 = f32[1,3,512]{2,0,1:T(1,128)} copy(f32[1,3,512]{2,1,0:T(4,128)S(1)} %slice_bitcast_fusion) | data formatting | bytes 12288
  20.7 0.9 %collective-permute-done.4 = f32[1,128]{1,0:T(1,128)S(1)} collective-permute-done((f32[1,128]{1,0:T(1,128)S(1)}, f32[1,128]{1,0:T(1,128)S(1)}, u32[]{:S(2)}, u32[]{:S(2)}) %collective-permute-start.4) | collective-permute-done | bytes 544 | tf_op jit(solution)/shard_map/ppermute | solution.py:595
  21.7 0.6 %multiply_add_fusion = f32[3,4,128]{2,1,0:T(4,128)} fusion(f32[3,4,128]{2,1,0:T(4,128)S(1)} %get-tuple-element.34, f32[3,4,128]{2,1,0:T(4,128)S(1)} %get-tuple-element.36, f32[128]{0:T(128)S(1)} %divide_bitcast_fusion), kind=kLoop, calls=%fused_computation.2 | loop fusion | flops 3072 | bytes 18944 | tf_op jit(solution)/shard_map/add | solution.py:632
  (4 shorter events, 0.0 us)
Async XLA Ops:
  0.6 0.7 %copy-start = (f32[1,512]{1,0:T(1,128)S(1)}, f32[1,512]{1,0:T(1,128)}, u32[]{:S(2)}) copy-start(f32[1,512]{1,0:T(1,128)} %param.4) | copy-start | bytes 6148
  1.4 7.0 %collective-permute-start = (f32[1,4,512]{2,1,0:T(4,128)S(1)}, f32[1,4,512]{2,1,0:T(4,128)S(1)}, u32[]{:S(2)}, u32[]{:S(2)}) collective-permute-start(f32[1,4,512]{2,1,0:T(4,128)S(1)} %pad_maximum_fusion.block.refs_1_), channel_id=1, source_target_pairs={{0,2},{1,3},{2,1},{3,0},{4,6},{5,7},{6,5},{7,4},{8,10},{9,11},{10,... | collective-permute-start | bytes 24584 | tf_op jit(solution)/shard_map/ppermute | solution.py:610
  5.4 4.5 %collective-permute-start.1 = (f32[1,4,512]{2,1,0:T(4,128)S(1)}, f32[1,4,512]{2,1,0:T(4,128)S(1)}, u32[]{:S(2)}, u32[]{:S(2)}) collective-permute-start(f32[1,4,512]{2,1,0:T(4,128)S(1)} %pad_maximum_fusion.block.refs_1_), channel_id=1, source_target_pairs={{0,3},{1,2},{2,0},{3,1},{4,7},{5,6},{6,4},{7,5},{8,11},{9,10},{10,... | collective-permute-start | bytes 24584 | tf_op jit(solution)/shard_map/ppermute | solution.py:610
  6.5 3.7 %collective-permute-start.2 = (f32[1,4,512]{2,1,0:T(4,128)S(1)}, f32[1,4,512]{2,1,0:T(4,128)S(1)}, u32[]{:S(2)}, u32[]{:S(2)}) collective-permute-start(f32[1,4,512]{2,1,0:T(4,128)S(1)} %pad_maximum_fusion.block.refs_1_), channel_id=1, source_target_pairs={{0,1},{1,0},{2,3},{3,2},{4,5},{5,4},{6,7},{7,6},{8,9},{9,8},{10,11... | collective-permute-start | bytes 24584 | tf_op jit(solution)/shard_map/ppermute | solution.py:610
  17.5 1.1 %collective-permute-start.3 = (f32[1,128]{1,0:T(1,128)S(1)}, f32[1,128]{1,0:T(1,128)S(1)}, u32[]{:S(2)}, u32[]{:S(2)}) collective-permute-start(f32[1,128]{1,0:T(1,128)S(1)} %get-tuple-element.35), channel_id=1, source_target_pairs={{0,4},{4,0},{8,12},{12,8},{1,5},{5,1},{9,13},{13,9},{2,6},{6,2},{1... | collective-permute-start | bytes 1544 | tf_op jit(solution)/shard_map/ppermute | solution.py:595
  18.7 3.0 %collective-permute-start.4 = (f32[1,128]{1,0:T(1,128)S(1)}, f32[1,128]{1,0:T(1,128)S(1)}, u32[]{:S(2)}, u32[]{:S(2)}) collective-permute-start(f32[1,128]{1,0:T(1,128)S(1)} %max.6), channel_id=1, source_target_pairs={{0,12},{4,8},{8,4},{12,0},{1,13},{5,9},{9,5},{13,1},{2,14},{6,10},... | collective-permute-start | bytes 1544 | tf_op jit(solution)/shard_map/ppermute | solution.py:595

commit v35 on v28

--- a/solution.py
+++ b/solution.py
@@ -14,7 +14,7 @@
 GRID = 4.0
 TINY = 1e-30
 GROUP = 32
-DISTANCE_ROWS = 96
+DISTANCE_ROWS = 64
 DRIFT_ROWS = 64
 bf16, f32 = jnp.bfloat16, jnp.float32
 
@@ -65,10 +65,16 @@
     minor = fine + rest
     query_norm, key_norm = scalar_groups(-rows_sum(coarse * coarse), coarse)
     query_less, key_less = scalar_groups(-rows_sum(minor * (2.0 * coarse + minor)), coarse)
-    key = [coarse, key_norm, coarse, coarse, fine, rest, key_less, fine, fine, rest, rest]
+    key = [coarse, key_norm, paired(coarse, coarse), paired(fine, rest), key_less]
+    key += [paired(fine, fine), paired(rest, rest)]
     coarse, fine, rest = coarse * 2.0, fine * 2.0, rest * 2.0
-    query = [coarse, query_norm, fine, rest, coarse, coarse, query_less, fine, rest, fine, rest]
+    query = [coarse, query_norm, paired(fine, rest), paired(coarse, coarse), query_less]
+    query += [paired(fine, rest)] * 2
     return stacked(key), stacked(query)
+
+
+def paired(first, second):
+    return first + pltpu.roll(second, 4, 0)
 
 
 def weighted_rows(weight, value):

time: 22.5 us -> 22.5 us (level)
  no operation moved by 1% of the time
where the time goes in v35:
time: 22.5 us; the launch traced here: 22.3 us
  Pallas kernels  9.52 us (42%)
  starting transfers between devices  7.13 us (32%)
  waiting for transfers between devices  2.37 us (11%)
  local copies, waits for them, and re-layouts  1.31 us (6%)
  between operations  1.31 us (6%)
  other arithmetic  0.62 us (3%)
    pallas_call x1, Pallas kernels, sweep(): pl.pallas_call(functools.partial(sweep_kernel, sources), out_shape=sweep_...  7.38 us
    ppermute x3, starting transfers between devices, gathered(): blocks.append(lax.ppermute(block, 'sharers', list(enumerate(targets))))  5.67 us
    ppermute x2, waiting for transfers between devices, swapped(): return lax.ppermute(value, axis, pairs)  2.03 us
    ppermute x2, starting transfers between devices, swapped(): return lax.ppermute(value, axis, pairs)  1.46 us
    pallas_call x1, Pallas kernels, next_part(): pl.pallas_call(functools.partial(next_kernel, sources), out_shape=shapes,...  1.45 us
    unnamed x4, local copies, waits for them, and re-layouts  1.31 us
    pallas_call x1, Pallas kernels, own_part(): pl.pallas_call(own_kernel, out_shape=shapes, in_specs=[vector] * 2, out_s...  0.7 us
    add x1, other arithmetic, local(): moved = start + time_step[None] * drift  0.61 us
  transfers between devices with their start and end apart: 5, of which 4 were waited for; matrix products, arithmetic and copies ran while one was open for 3% of the time, Pallas kernels for 10%

profile of v35, /device:TPU:0, one launch (start us, length us, event | category | flops | bytes accessed | tf_op | source)
XLA Modules:
  0.0 22.3 jit_solution(2580718795063451008)
XLA Ops:
  0.6 0.0 copy-start
  0.6 0.7 %copy.8 = f32[1,3,512]{2,1,0:T(4,128)S(1)} copy(f32[1,3,512]{2,0,1:T(1,128)} %param.3) | data formatting | bytes 12288 | tf_op args[0]
  1.3 0.0 copy-done
  1.4 4.1 %collective-permute-start = (f32[1,4,512]{2,1,0:T(4,128)S(1)}, f32[1,4,512]{2,1,0:T(4,128)S(1)}, u32[]{:S(2)}, u32[]{:S(2)}) collective-permute-start(f32[1,4,512]{2,1,0:T(4,128)S(1)} %pad_maximum_fusion.block.refs_1_), channel_id=1, source_target_pairs={{0,2},{1,3},{2,1},{3,0},{4,6},{5,7},{6,5},{7,4},{8,10},{9,11},{10,... | collective-permute-start | bytes 24584 | tf_op jit(solution)/shard_map/ppermute | solution.py:616
  5.4 1.1 %collective-permute-start.1 = (f32[1,4,512]{2,1,0:T(4,128)S(1)}, f32[1,4,512]{2,1,0:T(4,128)S(1)}, u32[]{:S(2)}, u32[]{:S(2)}) collective-permute-start(f32[1,4,512]{2,1,0:T(4,128)S(1)} %pad_maximum_fusion.block.refs_1_), channel_id=1, source_target_pairs={{0,3},{1,2},{2,0},{3,1},{4,7},{5,6},{6,4},{7,5},{8,11},{9,10},{10,... | collective-permute-start | bytes 24584 | tf_op jit(solution)/shard_map/ppermute | solution.py:616
  6.5 0.5 %collective-permute-start.2 = (f32[1,4,512]{2,1,0:T(4,128)S(1)}, f32[1,4,512]{2,1,0:T(4,128)S(1)}, u32[]{:S(2)}, u32[]{:S(2)}) collective-permute-start(f32[1,4,512]{2,1,0:T(4,128)S(1)} %pad_maximum_fusion.block.refs_1_), channel_id=1, source_target_pairs={{0,1},{1,0},{2,3},{3,2},{4,5},{5,4},{6,7},{7,6},{8,9},{9,8},{10,11... | collective-permute-start | bytes 24584 | tf_op jit(solution)/shard_map/ppermute | solution.py:616
  7.7 0.7 %own.1 = (bf16[512,64]{1,0:T(8,128)(2,1)S(1)}, bf16[64,512]{1,0:T(8,128)(2,1)S(1)}, bf16[16,512]{1,0:T(8,128)(2,1)S(1)}, f32[16,512]{1,0:T(8,128)S(1)}, bf16[512...) custom-call(s32[1,1]{1,0:T(1,128)} %bitcast.7.filled, f32[1,4,512]{2,1,0:T(4,128)S(1)} %pad_maximum_fusion.block.refs_1_), custom_call_target="tpu_custom_call" | custom-call | tf_op jit(solution)/shard_map/own/pallas_call | solution.py:309
  8.4 0.0 collective-permute-done.block.refs_2_
  8.4 1.4 %next.1 = (bf16[512,64]{1,0:T(8,128)(2,1)S(1)}, bf16[64,512]{1,0:T(8,128)(2,1)S(1)}, bf16[16,512]{1,0:T(8,128)(2,1)S(1)}, f32[16,1024]{1,0:T(8,128)S(1)}, bf16[5...) custom-call(s32[1,1]{1,0:T(1,128)} %bitcast.8.filled, ...), custom_call_target="tpu_custom_call" | custom-call | tf_op jit(solution)/shard_map/next/pallas_call | solution.py:325
  9.8 0.2 collective-permute-done.1.refs_3_
  10.0 0.2 collective-permute-done.2.refs_4_
  10.2 7.4 %sweep.1 = (f32[8,512]{1,0:T(8,128)S(1)}, f32[3,4,128]{2,1,0:T(4,128)S(1)}, f32[3,4,128]{2,1,0:T(4,128)S(1)}, f32[1,128]{1,0:T(1,128)S(1)}) custom-call(s32[1,1]{1,0:T(1,128)} %bitcast.9.refs_0_, f32[1,4,512]{2,1,0:T(4,128)S(1)} %pad_maximum_fusion.block.refs_1_, f32[1,4,512]{2,1,0:T(4,128)S(1)} %collective-permute-done.block.refs_2_, ...), custom_call_target="tpu_custom_call" | custom-call | tf_op jit(solution)/shard_map/sweep/pallas_call | solution.py:496
  17.5 0.0 collective-permute-start.3
  17.6 1.1 %collective-permute-done.3 = f32[1,128]{1,0:T(1,128)S(1)} collective-permute-done((f32[1,128]{1,0:T(1,128)S(1)}, f32[1,128]{1,0:T(1,128)S(1)}, u32[]{:S(2)}, u32[]{:S(2)}) %collective-permute-start.3) | collective-permute-done | bytes 544 | tf_op jit(solution)/shard_map/ppermute | solution.py:601
  18.7 1.5 %collective-permute-start.4 = (f32[1,128]{1,0:T(1,128)S(1)}, f32[1,128]{1,0:T(1,128)S(1)}, u32[]{:S(2)}, u32[]{:S(2)}) collective-permute-start(f32[1,128]{1,0:T(1,128)S(1)} %max.6), channel_id=1, source_target_pairs={{0,12},{4,8},{8,4},{12,0},{1,13},{5,9},{9,5},{13,1},{2,14},{6,10},... | collective-permute-start | bytes 1544 | tf_op jit(solution)/shard_map/ppermute | solution.py:601
  20.1 0.6 %copy.10 = f32[1,3,512]{2,0,1:T(1,128)} copy(f32[1,3,512]{2,1,0:T(4,128)S(1)} %slice_bitcast_fusion) | data formatting | bytes 12288
  20.7 0.9 %collective-permute-done.4 = f32[1,128]{1,0:T(1,128)S(1)} collective-permute-done((f32[1,128]{1,0:T(1,128)S(1)}, f32[1,128]{1,0:T(1,128)S(1)}, u32[]{:S(2)}, u32[]{:S(2)}) %collective-permute-start.4) | collective-permute-done | bytes 544 | tf_op jit(solution)/shard_map/ppermute | solution.py:601
  21.7 0.6 %multiply_add_fusion = f32[3,4,128]{2,1,0:T(4,128)} fusion(f32[3,4,128]{2,1,0:T(4,128)S(1)} %get-tuple-element.34, f32[3,4,128]{2,1,0:T(4,128)S(1)} %get-tuple-element.36, f32[128]{0:T(128)S(1)} %divide_bitcast_fusion), kind=kLoop, calls=%fused_computation.2 | loop fusion | flops 3072 | bytes 18944 | tf_op jit(solution)/shard_map/add | solution.py:638
  (4 shorter events, 0.0 us)
Async XLA Ops:
  0.6 0.7 %copy-start = (f32[1,512]{1,0:T(1,128)S(1)}, f32[1,512]{1,0:T(1,128)}, u32[]{:S(2)}) copy-start(f32[1,512]{1,0:T(1,128)} %param.4) | copy-start | bytes 6148
  1.4 7.0 %collective-permute-start = (f32[1,4,512]{2,1,0:T(4,128)S(1)}, f32[1,4,512]{2,1,0:T(4,128)S(1)}, u32[]{:S(2)}, u32[]{:S(2)}) collective-permute-start(f32[1,4,512]{2,1,0:T(4,128)S(1)} %pad_maximum_fusion.block.refs_1_), channel_id=1, source_target_pairs={{0,2},{1,3},{2,1},{3,0},{4,6},{5,7},{6,5},{7,4},{8,10},{9,11},{10,... | collective-permute-start | bytes 24584 | tf_op jit(solution)/shard_map/ppermute | solution.py:616
  5.4 4.5 %collective-permute-start.1 = (f32[1,4,512]{2,1,0:T(4,128)S(1)}, f32[1,4,512]{2,1,0:T(4,128)S(1)}, u32[]{:S(2)}, u32[]{:S(2)}) collective-permute-start(f32[1,4,512]{2,1,0:T(4,128)S(1)} %pad_maximum_fusion.block.refs_1_), channel_id=1, source_target_pairs={{0,3},{1,2},{2,0},{3,1},{4,7},{5,6},{6,4},{7,5},{8,11},{9,10},{10,... | collective-permute-start | bytes 24584 | tf_op jit(solution)/shard_map/ppermute | solution.py:616
  6.5 3.7 %collective-permute-start.2 = (f32[1,4,512]{2,1,0:T(4,128)S(1)}, f32[1,4,512]{2,1,0:T(4,128)S(1)}, u32[]{:S(2)}, u32[]{:S(2)}) collective-permute-start(f32[1,4,512]{2,1,0:T(4,128)S(1)} %pad_maximum_fusion.block.refs_1_), channel_id=1, source_target_pairs={{0,1},{1,0},{2,3},{3,2},{4,5},{5,4},{6,7},{7,6},{8,9},{9,8},{10,11... | collective-permute-start | bytes 24584 | tf_op jit(solution)/shard_map/ppermute | solution.py:616
  17.5 1.1 %collective-permute-start.3 = (f32[1,128]{1,0:T(1,128)S(1)}, f32[1,128]{1,0:T(1,128)S(1)}, u32[]{:S(2)}, u32[]{:S(2)}) collective-permute-start(f32[1,128]{1,0:T(1,128)S(1)} %get-tuple-element.35), channel_id=1, source_target_pairs={{0,4},{4,0},{8,12},{12,8},{1,5},{5,1},{9,13},{13,9},{2,6},{6,2},{1... | collective-permute-start | bytes 1544 | tf_op jit(solution)/shard_map/ppermute | solution.py:601
  18.7 3.0 %collective-permute-start.4 = (f32[1,128]{1,0:T(1,128)S(1)}, f32[1,128]{1,0:T(1,128)S(1)}, u32[]{:S(2)}, u32[]{:S(2)}) collective-permute-start(f32[1,128]{1,0:T(1,128)S(1)} %max.6), channel_id=1, source_target_pairs={{0,12},{4,8},{8,4},{12,0},{1,13},{5,9},{9,5},{13,1},{2,14},{6,10},... | collective-permute-start | bytes 1544 | tf_op jit(solution)/shard_map/ppermute | solution.py:601

commit v36 on v28

--- a/solution.py
+++ b/solution.py
@@ -207,10 +207,12 @@
         _, keys, _, queries, _ = tiles[index]
         return exponent_refs[index % len(exponent_refs)].at[0:keys, 0:queries]
 
-    buffer(0)[...] = exponent(tiles[0])
+    ahead = 2 if len(exponent_refs) > 2 else 1
+    for index in range(ahead):
+        buffer(index)[...] = exponent(tiles[index])
     for index, tile in enumerate(tiles):
-        if index + 1 < len(tiles):
-            buffer(index + 1)[...] = exponent(tiles[index + 1])
+        if index + ahead < len(tiles):
+            buffer(index + ahead)[...] = exponent(tiles[index + ahead])
         split = split_refs[index % 2].at[0 : 2 * tile[1], 0 : tile[3]]
         split_blobs(buffer(index), split)
         add_blobs(tile, split, moments, sums_ref)

time: 22.5 us -> 22.6 us (level)
  no operation moved by 1% of the time
where the time goes in v36:
time: 22.6 us; the launch traced here: 22.4 us
  Pallas kernels  9.67 us (43%)
  starting transfers between devices  7.13 us (32%)
  waiting for transfers between devices  2.37 us (10%)
  local copies, waits for them, and re-layouts  1.31 us (6%)
  between operations  1.31 us (6%)
  other arithmetic  0.62 us (3%)
    pallas_call x1, Pallas kernels, sweep(): pl.pallas_call(functools.partial(sweep_kernel, sources), out_shape=sweep_...  7.52 us
    ppermute x3, starting transfers between devices, gathered(): blocks.append(lax.ppermute(block, 'sharers', list(enumerate(targets))))  5.67 us
    ppermute x2, waiting for transfers between devices, swapped(): return lax.ppermute(value, axis, pairs)  2.02 us
    ppermute x2, starting transfers between devices, swapped(): return lax.ppermute(value, axis, pairs)  1.46 us
    pallas_call x1, Pallas kernels, next_part(): pl.pallas_call(functools.partial(next_kernel, sources), out_shape=shapes,...  1.45 us
    unnamed x4, local copies, waits for them, and re-layouts  1.31 us
    pallas_call x1, Pallas kernels, own_part(): pl.pallas_call(own_kernel, out_shape=shapes, in_specs=[vector] * 2, out_s...  0.7 us
    add x1, other arithmetic, local(): moved = start + time_step[None] * drift  0.61 us
  transfers between devices with their start and end apart: 5, of which 4 were waited for; matrix products, arithmetic and copies ran while one was open for 3% of the time, Pallas kernels for 10%

profile of v36, /device:TPU:0, one launch (start us, length us, event | category | flops | bytes accessed | tf_op | source)
XLA Modules:
  0.0 22.4 jit_solution(14564813041152066288)
XLA Ops:
  0.6 0.0 copy-start
  0.6 0.7 %copy.8 = f32[1,3,512]{2,1,0:T(4,128)S(1)} copy(f32[1,3,512]{2,0,1:T(1,128)} %param.3) | data formatting | bytes 12288 | tf_op args[0]
  1.3 0.0 copy-done
  1.4 4.1 %collective-permute-start = (f32[1,4,512]{2,1,0:T(4,128)S(1)}, f32[1,4,512]{2,1,0:T(4,128)S(1)}, u32[]{:S(2)}, u32[]{:S(2)}) collective-permute-start(f32[1,4,512]{2,1,0:T(4,128)S(1)} %pad_maximum_fusion.block.refs_1_), channel_id=1, source_target_pairs={{0,2},{1,3},{2,1},{3,0},{4,6},{5,7},{6,5},{7,4},{8,10},{9,11},{10,... | collective-permute-start | bytes 24584 | tf_op jit(solution)/shard_map/ppermute | solution.py:612
  5.4 1.1 %collective-permute-start.1 = (f32[1,4,512]{2,1,0:T(4,128)S(1)}, f32[1,4,512]{2,1,0:T(4,128)S(1)}, u32[]{:S(2)}, u32[]{:S(2)}) collective-permute-start(f32[1,4,512]{2,1,0:T(4,128)S(1)} %pad_maximum_fusion.block.refs_1_), channel_id=1, source_target_pairs={{0,3},{1,2},{2,0},{3,1},{4,7},{5,6},{6,4},{7,5},{8,11},{9,10},{10,... | collective-permute-start | bytes 24584 | tf_op jit(solution)/shard_map/ppermute | solution.py:612
  6.5 0.5 %collective-permute-start.2 = (f32[1,4,512]{2,1,0:T(4,128)S(1)}, f32[1,4,512]{2,1,0:T(4,128)S(1)}, u32[]{:S(2)}, u32[]{:S(2)}) collective-permute-start(f32[1,4,512]{2,1,0:T(4,128)S(1)} %pad_maximum_fusion.block.refs_1_), channel_id=1, source_target_pairs={{0,1},{1,0},{2,3},{3,2},{4,5},{5,4},{6,7},{7,6},{8,9},{9,8},{10,11... | collective-permute-start | bytes 24584 | tf_op jit(solution)/shard_map/ppermute | solution.py:612
  7.7 0.7 %own.1 = (bf16[512,96]{1,0:T(8,128)(2,1)S(1)}, bf16[96,512]{1,0:T(8,128)(2,1)S(1)}, bf16[16,512]{1,0:T(8,128)(2,1)S(1)}, f32[16,512]{1,0:T(8,128)S(1)}, bf16[512...) custom-call(s32[1,1]{1,0:T(1,128)} %bitcast.7.filled, f32[1,4,512]{2,1,0:T(4,128)S(1)} %pad_maximum_fusion.block.refs_1_), custom_call_target="tpu_custom_call" | custom-call | tf_op jit(solution)/shard_map/own/pallas_call | solution.py:305
  8.4 0.0 collective-permute-done.block.refs_2_
  8.4 1.5 %next.1 = (bf16[512,96]{1,0:T(8,128)(2,1)S(1)}, bf16[96,512]{1,0:T(8,128)(2,1)S(1)}, bf16[16,512]{1,0:T(8,128)(2,1)S(1)}, f32[16,1024]{1,0:T(8,128)S(1)}, bf16[5...) custom-call(s32[1,1]{1,0:T(1,128)} %bitcast.8.filled, ...), custom_call_target="tpu_custom_call" | custom-call | tf_op jit(solution)/shard_map/next/pallas_call | solution.py:321
  9.8 0.2 collective-permute-done.1.refs_3_
  10.0 0.2 collective-permute-done.2.refs_4_
  10.2 7.5 %sweep.1 = (f32[8,512]{1,0:T(8,128)S(1)}, f32[3,4,128]{2,1,0:T(4,128)S(1)}, f32[3,4,128]{2,1,0:T(4,128)S(1)}, f32[1,128]{1,0:T(1,128)S(1)}) custom-call(s32[1,1]{1,0:T(1,128)} %bitcast.9.refs_0_, f32[1,4,512]{2,1,0:T(4,128)S(1)} %pad_maximum_fusion.block.refs_1_, f32[1,4,512]{2,1,0:T(4,128)S(1)} %collective-permute-done.block.refs_2_, ...), custom_call_target="tpu_custom_call" | custom-call | tf_op jit(solution)/shard_map/sweep/pallas_call | solution.py:492
  17.7 0.0 collective-permute-start.3
  17.7 1.1 %collective-permute-done.3 = f32[1,128]{1,0:T(1,128)S(1)} collective-permute-done((f32[1,128]{1,0:T(1,128)S(1)}, f32[1,128]{1,0:T(1,128)S(1)}, u32[]{:S(2)}, u32[]{:S(2)}) %collective-permute-start.3) | collective-permute-done | bytes 544 | tf_op jit(solution)/shard_map/ppermute | solution.py:597
  18.8 1.5 %collective-permute-start.4 = (f32[1,128]{1,0:T(1,128)S(1)}, f32[1,128]{1,0:T(1,128)S(1)}, u32[]{:S(2)}, u32[]{:S(2)}) collective-permute-start(f32[1,128]{1,0:T(1,128)S(1)} %max.6), channel_id=1, source_target_pairs={{0,12},{4,8},{8,4},{12,0},{1,13},{5,9},{9,5},{13,1},{2,14},{6,10},... | collective-permute-start | bytes 1544 | tf_op jit(solution)/shard_map/ppermute | solution.py:597
  20.3 0.6 %copy.10 = f32[1,3,512]{2,0,1:T(1,128)} copy(f32[1,3,512]{2,1,0:T(4,128)S(1)} %slice_bitcast_fusion) | data formatting | bytes 12288
  20.9 0.9 %collective-permute-done.4 = f32[1,128]{1,0:T(1,128)S(1)} collective-permute-done((f32[1,128]{1,0:T(1,128)S(1)}, f32[1,128]{1,0:T(1,128)S(1)}, u32[]{:S(2)}, u32[]{:S(2)}) %collective-permute-start.4) | collective-permute-done | bytes 544 | tf_op jit(solution)/shard_map/ppermute | solution.py:597
  21.8 0.6 %multiply_add_fusion = f32[3,4,128]{2,1,0:T(4,128)} fusion(f32[3,4,128]{2,1,0:T(4,128)S(1)} %get-tuple-element.34, f32[3,4,128]{2,1,0:T(4,128)S(1)} %get-tuple-element.36, f32[128]{0:T(128)S(1)} %divide_bitcast_fusion), kind=kLoop, calls=%fused_computation.2 | loop fusion | flops 3072 | bytes 18944 | tf_op jit(solution)/shard_map/add | solution.py:634
  (4 shorter events, 0.0 us)
Async XLA Ops:
  0.6 0.7 %copy-start = (f32[1,512]{1,0:T(1,128)S(1)}, f32[1,512]{1,0:T(1,128)}, u32[]{:S(2)}) copy-start(f32[1,512]{1,0:T(1,128)} %param.4) | copy-start | bytes 6148
  1.4 7.0 %collective-permute-start = (f32[1,4,512]{2,1,0:T(4,128)S(1)}, f32[1,4,512]{2,1,0:T(4,128)S(1)}, u32[]{:S(2)}, u32[]{:S(2)}) collective-permute-start(f32[1,4,512]{2,1,0:T(4,128)S(1)} %pad_maximum_fusion.block.refs_1_), channel_id=1, source_target_pairs={{0,2},{1,3},{2,1},{3,0},{4,6},{5,7},{6,5},{7,4},{8,10},{9,11},{10,... | collective-permute-start | bytes 24584 | tf_op jit(solution)/shard_map/ppermute | solution.py:612
  5.4 4.5 %collective-permute-start.1 = (f32[1,4,512]{2,1,0:T(4,128)S(1)}, f32[1,4,512]{2,1,0:T(4,128)S(1)}, u32[]{:S(2)}, u32[]{:S(2)}) collective-permute-start(f32[1,4,512]{2,1,0:T(4,128)S(1)} %pad_maximum_fusion.block.refs_1_), channel_id=1, source_target_pairs={{0,3},{1,2},{2,0},{3,1},{4,7},{5,6},{6,4},{7,5},{8,11},{9,10},{10,... | collective-permute-start | bytes 24584 | tf_op jit(solution)/shard_map/ppermute | solution.py:612
  6.5 3.7 %collective-permute-start.2 = (f32[1,4,512]{2,1,0:T(4,128)S(1)}, f32[1,4,512]{2,1,0:T(4,128)S(1)}, u32[]{:S(2)}, u32[]{:S(2)}) collective-permute-start(f32[1,4,512]{2,1,0:T(4,128)S(1)} %pad_maximum_fusion.block.refs_1_), channel_id=1, source_target_pairs={{0,1},{1,0},{2,3},{3,2},{4,5},{5,4},{6,7},{7,6},{8,9},{9,8},{10,11... | collective-permute-start | bytes 24584 | tf_op jit(solution)/shard_map/ppermute | solution.py:612
  17.7 1.1 %collective-permute-start.3 = (f32[1,128]{1,0:T(1,128)S(1)}, f32[1,128]{1,0:T(1,128)S(1)}, u32[]{:S(2)}, u32[]{:S(2)}) collective-permute-start(f32[1,128]{1,0:T(1,128)S(1)} %get-tuple-element.35), channel_id=1, source_target_pairs={{0,4},{4,0},{8,12},{12,8},{1,5},{5,1},{9,13},{13,9},{2,6},{6,2},{1... | collective-permute-start | bytes 1544 | tf_op jit(solution)/shard_map/ppermute | solution.py:597
  18.8 3.0 %collective-permute-start.4 = (f32[1,128]{1,0:T(1,128)S(1)}, f32[1,128]{1,0:T(1,128)S(1)}, u32[]{:S(2)}, u32[]{:S(2)}) collective-permute-start(f32[1,128]{1,0:T(1,128)S(1)} %max.6), channel_id=1, source_target_pairs={{0,12},{4,8},{8,4},{12,0},{1,13},{5,9},{9,5},{13,1},{2,14},{6,10},... | collective-permute-start | bytes 1544 | tf_op jit(solution)/shard_map/ppermute | solution.py:597

commit v37 on v28

--- a/solution.py
+++ b/solution.py
@@ -13,7 +13,7 @@
 SCALE = math.sqrt(math.log2(math.e) / (2.0 * EPS * EPS))
 GRID = 4.0
 TINY = 1e-30
-GROUP = 32
+GROUP = 16
 DISTANCE_ROWS = 96
 DRIFT_ROWS = 64
 bf16, f32 = jnp.bfloat16, jnp.float32

time: 22.5 us -> 22.5 us (level)
  no operation moved by 1% of the time
where the time goes in v37:
time: 22.5 us; the launch traced here: 22.3 us
  Pallas kernels  9.52 us (42%)
  starting transfers between devices  7.12 us (32%)
  waiting for transfers between devices  2.38 us (11%)
  local copies, waits for them, and re-layouts  1.31 us (6%)
  between operations  1.31 us (6%)
  other arithmetic  0.62 us (3%)
    pallas_call x1, Pallas kernels, sweep(): pl.pallas_call(functools.partial(sweep_kernel, sources), out_shape=sweep_...  7.38 us
    ppermute x3, starting transfers between devices, gathered(): blocks.append(lax.ppermute(block, 'sharers', list(enumerate(targets))))  5.67 us
    ppermute x2, waiting for transfers between devices, swapped(): return lax.ppermute(value, axis, pairs)  2.03 us
    pallas_call x1, Pallas kernels, next_part(): pl.pallas_call(functools.partial(next_kernel, sources), out_shape=shapes,...  1.45 us
    ppermute x2, starting transfers between devices, swapped(): return lax.ppermute(value, axis, pairs)  1.45 us
    unnamed x4, local copies, waits for them, and re-layouts  1.31 us
    pallas_call x1, Pallas kernels, own_part(): pl.pallas_call(own_kernel, out_shape=shapes, in_specs=[vector] * 2, out_s...  0.7 us
    add x1, other arithmetic, local(): moved = start + time_step[None] * drift  0.61 us
  transfers between devices with their start and end apart: 5, of which 4 were waited for; matrix products, arithmetic and copies ran while one was open for 3% of the time, Pallas kernels for 10%

profile of v37, /device:TPU:0, one launch (start us, length us, event | category | flops | bytes accessed | tf_op | source)
XLA Modules:
  0.0 22.3 jit_solution(9292637332072719134)
XLA Ops:
  0.6 0.0 copy-start
  0.6 0.7 %copy.8 = f32[1,3,512]{2,1,0:T(4,128)S(1)} copy(f32[1,3,512]{2,0,1:T(1,128)} %param.3) | data formatting | bytes 12288 | tf_op args[0]
  1.3 0.0 copy-done
  1.4 4.1 %collective-permute-start = (f32[1,4,512]{2,1,0:T(4,128)S(1)}, f32[1,4,512]{2,1,0:T(4,128)S(1)}, u32[]{:S(2)}, u32[]{:S(2)}) collective-permute-start(f32[1,4,512]{2,1,0:T(4,128)S(1)} %pad_maximum_fusion.block.refs_1_), channel_id=1, source_target_pairs={{0,2},{1,3},{2,1},{3,0},{4,6},{5,7},{6,5},{7,4},{8,10},{9,11},{10,... | collective-permute-start | bytes 24584 | tf_op jit(solution)/shard_map/ppermute | solution.py:610
  5.4 1.1 %collective-permute-start.1 = (f32[1,4,512]{2,1,0:T(4,128)S(1)}, f32[1,4,512]{2,1,0:T(4,128)S(1)}, u32[]{:S(2)}, u32[]{:S(2)}) collective-permute-start(f32[1,4,512]{2,1,0:T(4,128)S(1)} %pad_maximum_fusion.block.refs_1_), channel_id=1, source_target_pairs={{0,3},{1,2},{2,0},{3,1},{4,7},{5,6},{6,4},{7,5},{8,11},{9,10},{10,... | collective-permute-start | bytes 24584 | tf_op jit(solution)/shard_map/ppermute | solution.py:610
  6.5 0.5 %collective-permute-start.2 = (f32[1,4,512]{2,1,0:T(4,128)S(1)}, f32[1,4,512]{2,1,0:T(4,128)S(1)}, u32[]{:S(2)}, u32[]{:S(2)}) collective-permute-start(f32[1,4,512]{2,1,0:T(4,128)S(1)} %pad_maximum_fusion.block.refs_1_), channel_id=1, source_target_pairs={{0,1},{1,0},{2,3},{3,2},{4,5},{5,4},{6,7},{7,6},{8,9},{9,8},{10,11... | collective-permute-start | bytes 24584 | tf_op jit(solution)/shard_map/ppermute | solution.py:610
  7.7 0.7 %own.1 = (bf16[512,96]{1,0:T(8,128)(2,1)S(1)}, bf16[96,512]{1,0:T(8,128)(2,1)S(1)}, bf16[16,512]{1,0:T(8,128)(2,1)S(1)}, f32[16,512]{1,0:T(8,128)S(1)}, bf16[512...) custom-call(s32[1,1]{1,0:T(1,128)} %bitcast.7.filled, f32[1,4,512]{2,1,0:T(4,128)S(1)} %pad_maximum_fusion.block.refs_1_), custom_call_target="tpu_custom_call" | custom-call | tf_op jit(solution)/shard_map/own/pallas_call | solution.py:303
  8.4 0.0 collective-permute-done.block.refs_2_
  8.4 1.5 %next.1 = (bf16[512,96]{1,0:T(8,128)(2,1)S(1)}, bf16[96,512]{1,0:T(8,128)(2,1)S(1)}, bf16[16,512]{1,0:T(8,128)(2,1)S(1)}, f32[16,1024]{1,0:T(8,128)S(1)}, bf16[5...) custom-call(s32[1,1]{1,0:T(1,128)} %bitcast.8.filled, ...), custom_call_target="tpu_custom_call" | custom-call | tf_op jit(solution)/shard_map/next/pallas_call | solution.py:319
  9.8 0.2 collective-permute-done.1.refs_3_
  10.0 0.2 collective-permute-done.2.refs_4_
  10.2 7.4 %sweep.1 = (f32[8,512]{1,0:T(8,128)S(1)}, f32[3,4,128]{2,1,0:T(4,128)S(1)}, f32[3,4,128]{2,1,0:T(4,128)S(1)}, f32[1,128]{1,0:T(1,128)S(1)}) custom-call(s32[1,1]{1,0:T(1,128)} %bitcast.9.refs_0_, f32[1,4,512]{2,1,0:T(4,128)S(1)} %pad_maximum_fusion.block.refs_1_, f32[1,4,512]{2,1,0:T(4,128)S(1)} %collective-permute-done.block.refs_2_, ...), custom_call_target="tpu_custom_call" | custom-call | tf_op jit(solution)/shard_map/sweep/pallas_call | solution.py:490
  17.5 0.0 collective-permute-start.3
  17.6 1.1 %collective-permute-done.3 = f32[1,128]{1,0:T(1,128)S(1)} collective-permute-done((f32[1,128]{1,0:T(1,128)S(1)}, f32[1,128]{1,0:T(1,128)S(1)}, u32[]{:S(2)}, u32[]{:S(2)}) %collective-permute-start.3) | collective-permute-done | bytes 544 | tf_op jit(solution)/shard_map/ppermute | solution.py:595
  18.7 1.4 %collective-permute-start.4 = (f32[1,128]{1,0:T(1,128)S(1)}, f32[1,128]{1,0:T(1,128)S(1)}, u32[]{:S(2)}, u32[]{:S(2)}) collective-permute-start(f32[1,128]{1,0:T(1,128)S(1)} %max.6), channel_id=1, source_target_pairs={{0,12},{4,8},{8,4},{12,0},{1,13},{5,9},{9,5},{13,1},{2,14},{6,10},... | collective-permute-start | bytes 1544 | tf_op jit(solution)/shard_map/ppermute | solution.py:595
  20.1 0.6 %copy.10 = f32[1,3,512]{2,0,1:T(1,128)} copy(f32[1,3,512]{2,1,0:T(4,128)S(1)} %slice_bitcast_fusion) | data formatting | bytes 12288
  20.7 0.9 %collective-permute-done.4 = f32[1,128]{1,0:T(1,128)S(1)} collective-permute-done((f32[1,128]{1,0:T(1,128)S(1)}, f32[1,128]{1,0:T(1,128)S(1)}, u32[]{:S(2)}, u32[]{:S(2)}) %collective-permute-start.4) | collective-permute-done | bytes 544 | tf_op jit(solution)/shard_map/ppermute | solution.py:595
  21.7 0.6 %multiply_add_fusion = f32[3,4,128]{2,1,0:T(4,128)} fusion(f32[3,4,128]{2,1,0:T(4,128)S(1)} %get-tuple-element.34, f32[3,4,128]{2,1,0:T(4,128)S(1)} %get-tuple-element.36, f32[128]{0:T(128)S(1)} %divide_bitcast_fusion), kind=kLoop, calls=%fused_computation.2 | loop fusion | flops 3072 | bytes 18944 | tf_op jit(solution)/shard_map/add | solution.py:632
  (4 shorter events, 0.0 us)
Async XLA Ops:
  0.6 0.7 %copy-start = (f32[1,512]{1,0:T(1,128)S(1)}, f32[1,512]{1,0:T(1,128)}, u32[]{:S(2)}) copy-start(f32[1,512]{1,0:T(1,128)} %param.4) | copy-start | bytes 6148
  1.4 7.0 %collective-permute-start = (f32[1,4,512]{2,1,0:T(4,128)S(1)}, f32[1,4,512]{2,1,0:T(4,128)S(1)}, u32[]{:S(2)}, u32[]{:S(2)}) collective-permute-start(f32[1,4,512]{2,1,0:T(4,128)S(1)} %pad_maximum_fusion.block.refs_1_), channel_id=1, source_target_pairs={{0,2},{1,3},{2,1},{3,0},{4,6},{5,7},{6,5},{7,4},{8,10},{9,11},{10,... | collective-permute-start | bytes 24584 | tf_op jit(solution)/shard_map/ppermute | solution.py:610
  5.4 4.5 %collective-permute-start.1 = (f32[1,4,512]{2,1,0:T(4,128)S(1)}, f32[1,4,512]{2,1,0:T(4,128)S(1)}, u32[]{:S(2)}, u32[]{:S(2)}) collective-permute-start(f32[1,4,512]{2,1,0:T(4,128)S(1)} %pad_maximum_fusion.block.refs_1_), channel_id=1, source_target_pairs={{0,3},{1,2},{2,0},{3,1},{4,7},{5,6},{6,4},{7,5},{8,11},{9,10},{10,... | collective-permute-start | bytes 24584 | tf_op jit(solution)/shard_map/ppermute | solution.py:610
  6.5 3.7 %collective-permute-start.2 = (f32[1,4,512]{2,1,0:T(4,128)S(1)}, f32[1,4,512]{2,1,0:T(4,128)S(1)}, u32[]{:S(2)}, u32[]{:S(2)}) collective-permute-start(f32[1,4,512]{2,1,0:T(4,128)S(1)} %pad_maximum_fusion.block.refs_1_), channel_id=1, source_target_pairs={{0,1},{1,0},{2,3},{3,2},{4,5},{5,4},{6,7},{7,6},{8,9},{9,8},{10,11... | collective-permute-start | bytes 24584 | tf_op jit(solution)/shard_map/ppermute | solution.py:610
  17.5 1.1 %collective-permute-start.3 = (f32[1,128]{1,0:T(1,128)S(1)}, f32[1,128]{1,0:T(1,128)S(1)}, u32[]{:S(2)}, u32[]{:S(2)}) collective-permute-start(f32[1,128]{1,0:T(1,128)S(1)} %get-tuple-element.35), channel_id=1, source_target_pairs={{0,4},{4,0},{8,12},{12,8},{1,5},{5,1},{9,13},{13,9},{2,6},{6,2},{1... | collective-permute-start | bytes 1544 | tf_op jit(solution)/shard_map/ppermute | solution.py:595
  18.7 3.0 %collective-permute-start.4 = (f32[1,128]{1,0:T(1,128)S(1)}, f32[1,128]{1,0:T(1,128)S(1)}, u32[]{:S(2)}, u32[]{:S(2)}) collective-permute-start(f32[1,128]{1,0:T(1,128)S(1)} %max.6), channel_id=1, source_target_pairs={{0,12},{4,8},{8,4},{12,0},{1,13},{5,9},{9,5},{13,1},{2,14},{6,10},... | collective-permute-start | bytes 1544 | tf_op jit(solution)/shard_map/ppermute | solution.py:595
